TPU v7x, 256 devices: a whole 4x4x8 slice. The times are simulated.
256 devices in a mesh: pole: 8 (over z_lo, y), row: 4 (over x), col: 8 (over z_hi, core).
Axes of the slice: x: 4, y: 4, z: 8 (z_hi: 4, z_lo: 2; z = z_hi * 2 + z_lo), core: 2. Of those that a mesh axis runs over, the one named last changes fastest.
Arguments:
- inverse: bfloat16 [8, 2, 8192, 8192], P('pole', None, None, ('row', 'col')), may hold values from -0.0625 to 0.0625
- factor: bfloat16 [8, 2, 8192, 768], P('pole', None, ('row', 'col')), may hold values from -1 to 1
- diag_inverse: bfloat16 [8, 2, 768, 256], P('pole', None, ('row', 'col')), may hold values from -6 to 6
- widths: int32 [3], replicated, may hold values from 1 to 256, 512 in all
- pattern: int32 [32, 3], replicated, may hold values 0 or 1
- owner: int32 [32], replicated, may hold values from 0 to 31, each once
- assign: int32 [8], P('pole'), may hold values from 0 to 19
- pole_weights: float32 [20, 2], replicated, may hold values from -4 to 4
Outputs:
- rho_panel: float32 [8192, 768], P(('row', 'col'))
- rho_diag: float32 [768, 256], P(('row', 'col'))
Inputs may be any that keep to these rules, and one draw needn't show every extreme that they name: The widths sum to 512 and the largest is exactly 256. `owner`: each piece number appears once.
All inputs are finite; a program needn't handle non-finite values.
Results may differ from a plain program's by a relative error of at most 0.0027.
Values may be sent and summed in bfloat16 or wider, within the bound.
No kernel may reach another device: no remote copies, remote signals or barrier semaphores. Data moves between devices by JAX's collectives and lax.ppermute only.
A program may use at most 192 MiB of HBM per device.

v0:
```python
import jax
import jax.numpy as jnp
from jax import lax
from jax.sharding import PartitionSpec as P


def inner_dot(left, right):
    return lax.dot_general(
        left, right, (((0,), (0,)), ((), ())), preferred_element_type=jnp.float32
    )


def block_product(left, right):
    return jnp.einsum("wka,wkb->kab", left, right, preferred_element_type=jnp.float32)


def accumulate(totals, shard_rows, columns_inverse, own_start):
    sum_real, sum_imag, picked = totals
    row_count = shard_rows.shape[1]
    sum_real = inner_dot(columns_inverse[0], shard_rows[0]) - inner_dot(
        columns_inverse[1], shard_rows[1]
    )
    sum_imag = inner_dot(columns_inverse[0], shard_rows[1]) + inner_dot(
        columns_inverse[1], shard_rows[0]
    )
    own_width = picked.shape[1]
    inside = (own_start >= 0) & (own_start < row_count)
    slice_start = jnp.clip(own_start, 0, row_count - own_width)
    picked = lax.cond(
        inside,
        lambda: lax.dynamic_slice_in_dim(shard_rows, slice_start, own_width, 1),
        lambda: picked,
    )
    return (sum_real, sum_imag, picked)


def lookup_small(keys, table_keys, values):
    return jnp.sum(jnp.where(keys[:, None] == table_keys[None, :], values[None, :], 0), axis=1)


def local(inverse, factor, diag_inverse, widths, pattern, owner, assign, pole_weights):
    devices = lax.axis_size(("row", "col"))
    device = lax.axis_index(("row", "col"))
    local_width = factor.shape[2]
    total_cols = factor.shape[3]
    block = diag_inverse.shape[3]
    blocks_k = total_cols // block
    blocks_a = pattern.shape[0]
    block_ids = jnp.arange(blocks_k, dtype=jnp.int32)
    row_ids = device * local_width + jnp.arange(local_width, dtype=jnp.int32)
    row_onehot = (
        row_ids[:, None] // block == jnp.arange(blocks_a, dtype=jnp.int32)[None, :]
    ).astype(jnp.float32)
    block_mask = jnp.dot(row_onehot, pattern.astype(jnp.float32), precision=lax.Precision.HIGHEST)
    col_ids = jnp.arange(total_cols, dtype=jnp.int32)
    col_block = col_ids // block
    col_pos = col_ids % block
    col_width = lookup_small(col_block, block_ids, widths)
    col_live = col_pos < col_width
    full_mask = jnp.repeat(block_mask, block, axis=1) * col_live.astype(jnp.float32)[None, :]
    masked = factor[0] * full_mask.astype(jnp.bfloat16)[None]
    pole_onehot = (
        assign[:, None] == jnp.arange(pole_weights.shape[0], dtype=jnp.int32)[None, :]
    ).astype(jnp.float32)
    weight = jnp.dot(pole_onehot, pole_weights, precision=lax.Precision.HIGHEST)[0]
    weight_real = weight[0]
    weight_imag = weight[1]
    own_piece = jnp.sum(jnp.where(jnp.arange(devices, dtype=jnp.int32) == device, owner, 0))
    own_start = own_piece * local_width
    columns_inverse = inverse[0]
    zero_sum = jnp.zeros((local_width, total_cols), jnp.float32)
    zero_pick = jnp.zeros((2, local_width, total_cols), jnp.bfloat16)
    sum_real, sum_imag, picked = accumulate(
        (zero_sum, zero_sum, zero_pick),
        lax.all_gather(masked, ("row", "col"), axis=1, tiled=True),
        columns_inverse,
        own_start,
    )
    x_real = -sum_real
    x_imag = -sum_imag
    panel_local = weight_real * x_imag + weight_imag * x_real
    x_bf = jnp.stack([x_real, x_imag]).astype(jnp.bfloat16)
    own_blocks = picked.reshape(2, local_width, blocks_k, block)
    x_blocks = x_bf.reshape(2, local_width, blocks_k, block)
    part_real = (
        block_product(own_blocks[0], x_blocks[0]) - block_product(own_blocks[1], x_blocks[1])
    ).reshape(total_cols, block)
    part_imag = (
        block_product(own_blocks[0], x_blocks[1]) + block_product(own_blocks[1], x_blocks[0])
    ).reshape(total_cols, block)
    inverse_diag = diag_inverse[0].astype(jnp.float32)
    shared = lax.psum_scatter(
        jnp.stack([part_real, part_imag]), ("row", "col"), scatter_dimension=1, tiled=True
    )
    diag_real = inverse_diag[0] - shared[0]
    diag_imag = inverse_diag[1] - shared[1]
    diag_local = weight_real * diag_imag + weight_imag * diag_real
    panel_total, diag_total = lax.psum((panel_local, diag_local), "pole")
    return (panel_total, diag_total)


def solution(mesh):
    placed = (
        P("pole", None, None, ("row", "col")),
        P("pole", None, ("row", "col"), None),
        P("pole", None, ("row", "col"), None),
        P(),
        P(),
        P(),
        P("pole"),
        P(),
    )
    return jax.shard_map(
        local,
        mesh=mesh,
        in_specs=placed,
        out_specs=(P(("row", "col"), None), P(("row", "col"), None)),
        check_vma=False,
    )
```

profile of v0, /device:TPU:2, one launch (start us, length us, event | category | flops | bytes accessed | tf_op | source)
XLA Modules:
  0.0 436.8 jit_solution(4128939970164663476)
XLA Ops:
  7.2 0.0 copy-start
  7.2 0.0 all-gather.2.cloned.1.call-start
  7.3 0.7 select_reduce_fusion
  8.0 1.4 copy.26
  9.4 0.9 fusion.25
  10.3 0.2 fusion.24
  10.5 1.0 bitcast_multiply_fusion.1
  11.5 0.0 all-gather.2.cloned.1.call-update
  11.5 0.0 all-reduce.2.cloned.1.call-start
  12.2 1.3 fusion.39
  14.2 0.0 copy-done
  14.2 0.1 convolution_bitcast_fusion
  14.3 0.6 fusion.43
  14.9 172.1 %all-gather.2.cloned.1.call-done = bf16[2,8192,768]{1,2,0:T(8,128)(2,1)} async-done(((bf16[2,256,768]{1,2,0:T(8,128)(2,1)}), bf16[2,8192,768]{1,2,0:T(8,128)(2,1)}) %all-gather.2.cloned.1.call-update) | async-done | bytes 25165840 | tf_op jit(solution)/shard_map/all_gather | solution.py:75
  187.0 0.0 slice-start
  187.0 9.3 %fusion.1 = f32[768,256]{1,0:T(8,128)S(1)} fusion(bf16[2,8192,768]{1,2,0:T(8,128)(2,1)} %all-gather.2.cloned.1.call-done, bf16[1,2,8192,256]{3,2,1,0:T(8,128)(2,1)} %param.10), kind=kOutput, calls=%fused_computation.5 | convolution fusion | flops 3221225472 | bytes 17563648 | tf_op jit(solution)/shard_map/dot_general | solution.py:8
  196.3 0.0 slice-start.1
  196.3 7.8 %fusion = f32[768,256]{1,0:T(8,128)S(1)} fusion(bf16[2,8192,768]{1,2,0:T(8,128)(2,1)} %all-gather.2.cloned.1.call-done, bf16[1,2,8192,256]{3,2,1,0:T(8,128)(2,1)} %param.10), kind=kOutput, calls=%fused_computation.4 | convolution fusion | flops 3221225472 | bytes 17563648 | tf_op jit(solution)/shard_map/dot_general | solution.py:8
  204.1 0.0 slice-done
  204.1 0.0 slice-done.1
  204.1 6.5 %fusion.15 = f32[768,256]{1,0:T(8,128)S(1)} fusion(f32[768,256]{1,0:T(8,128)S(1)} %fusion.1, bf16[1,2,8192,256]{3,2,1,0:T(8,128)(2,1)S(1)} %bitcast.93, bf16[2,8192,768]{1,2,0:T(8,128)(2,1)} %all-gather.2.cloned.1.call-done), kind=kOutput, calls=%fused_computation.20 | convolution fusion | flops 3221618688 | bytes 18350080 | tf_op jit(solution)/shard_map/dot_general | solution.py:8
  210.6 10.2 %fusion.42 = (bf16[768,256]{1,0:T(8,128)(2,1)S(1)}, f32[256,768]{0,1:T(8,128)}, bf16[768,256]{1,0:T(8,128)(2,1)S(1)}) fusion(f32[]{:T(128)} %bitcast.12, f32[768,256]{1,0:T(8,128)S(1)} %fusion.15, f32[]{:T(128)} %bitcast.5, f32[768,256]{1,0:T(8,128)S(1)} %fusion, bf16[1,2,8192,256]{3,2,1,0:T(8,128)(2,1)S(1)} %bitcast.93, ...), kind=kOutput, calls=%fused_computation.63 | convolution fusion | flops 3222601728 | bytes 19923968 | tf_op jit(solution)/shard_map/dot_general | solution.py:8
  220.8 0.0 copy-start.1
  220.8 0.0 all-reduce.2.cloned.1.call-update
  220.8 0.0 reduce-scatter.2.cloned.1.call-start
  220.9 1.6 conditional.1
  220.9 1.6 constant_dynamic-slice_fusion.1
  222.5 0.3 fusion.46
  222.8 0.3 fusion.47
  223.1 0.3 convolution_subtract_fusion
  223.4 0.3 convolution_add_fusion
  223.7 1.3 pad_maximum_fusion
  225.0 0.0 reduce-scatter.2.cloned.1.call-update
  225.0 0.0 copy-done.1
  225.0 76.1 %all-reduce.2.cloned.1.call-done = f32[256,768]{0,1:T(8,128)} async-done(((f32[256,768]{0,1:T(8,128)}), f32[256,768]{0,1:T(8,128)}) %all-reduce.2.cloned.1.call-update) | async-done | bytes 786448 | tf_op jit(solution)/shard_map/psum | solution.py:98
  301.1 2.3 copy.31
  303.4 90.9 %reduce-scatter.2.cloned.1.call-done = f32[2,24,256]{2,1,0:T(8,128)} async-done(((f32[2,768,256]{2,1,0:T(8,128)}), f32[2,24,256]{2,1,0:T(8,128)}) %reduce-scatter.2.cloned.1.call-update) | async-done | bytes 49168 | tf_op jit(solution)/shard_map/reduce_scatter | solution.py:92
  394.3 2.0 fusion.29
  396.3 33.9 %psum.15 = f32[24,256]{1,0:T(8,128)} all-reduce(f32[24,256]{1,0:T(8,128)S(1)} %fusion.29), channel_id=1, replica_groups=mesh['pole'=8,'row'=4,'col'=8] {'pole'}, use_global_device_ids=true, to_apply=%region_6.7 | all-reduce | flops 6144 | bytes 49152 | tf_op jit(solution)/shard_map/psum | solution.py:98
  (5 shorter events, 0.0 us)
Async XLA Ops:
  7.2 7.0 %copy-start = (f32[20,2]{0,1:T(2,128)S(1)}, f32[20,2]{0,1:T(2,128)}, u32[]{:S(2)}) copy-start(f32[20,2]{0,1:T(2,128)} %param.17) | copy-start | bytes 484
  7.2 179.8 %all-gather.2.cloned.1.call-start = ((), (), s32[]{:S(2)}) async-start(), calls=%async_computation.1 | async-start | bytes 25952256 | tf_op jit(solution)/shard_map/all_gather | solution.py:75
  11.5 289.5 %all-reduce.2.cloned.1.call-start = ((), (), s32[]{:S(2)}) async-start(), calls=%async_computation.2 | async-start | bytes 1572864 | tf_op jit(solution)/shard_map/psum | solution.py:98
  187.0 17.1 %slice-start = ((s8[8388608]{0:T(1024)(128)(4,1)}), s8[4194304]{0:T(1024)(128)(4,1)S(1)}, s32[]{:S(2)}) async-start(s8[8388608]{0:T(1024)(128)(4,1)} %bitcast.92), calls=%async_computation.4 | async-start | bytes 8388608
  196.3 7.8 %slice-start.1 = ((s8[8388608]{0:T(1024)(128)(4,1)}), s8[4194304]{0:T(1024)(128)(4,1)S(1)}, s32[]{:S(2)}) async-start(s8[8388608]{0:T(1024)(128)(4,1)} %bitcast.92), calls=%async_computation.5 | async-start | bytes 8388608
  220.8 4.2 copy-start.1
  220.8 173.5 %reduce-scatter.2.cloned.1.call-start = ((), (), s32[]{:S(2)}) async-start(), calls=%async_computation.3 | async-start | bytes 1622016 | tf_op jit(solution)/shard_map/reduce_scatter | solution.py:92
Sparse Core Ops, SparseCore 0:
  11.6 175.2 all-gather.1
  220.9 80.0 all-reduce.1
  305.4 88.8 reduce-scatter.1
where the time goes:
time: 437 us
  waiting for transfers between devices  339 us (78%)
  matrix products  35.9 us (8%)
  blocking collectives  33.9 us (8%)
  between operations  15.2 us (3%)
  other arithmetic  6.54 us (1%)
  local copies, waits for them, and re-layouts  5.93 us (1%)
    all_gather x1, waiting for transfers between devices, local(): lax.all_gather(masked, ('row', 'col'), axis=1, tiled=True)  172 us
    reduce_scatter x1, waiting for transfers between devices, local(): lax.psum_scatter(jnp.stack([part_real, part_imag]), ('row', 'col'), scatt...  90.9 us
    psum x1, waiting for transfers between devices, local(): panel_total, diag_total = lax.psum((panel_local, diag_local), 'pole')  76.1 us
    psum x1, blocking collectives, local(): panel_total, diag_total = lax.psum((panel_local, diag_local), 'pole')  33.9 us
    dot_general x4, matrix products, inner_dot(): lax.dot_general(left, right, (((0,), (0,)), ((), ())), preferred_element_...  33.7 us
  transfers between devices with their start and end apart: 3, of which 3 were waited for; matrix products, arithmetic and copies ran while one was open for 2% of the time, Pallas kernels for 0%

commit v1 on v0

v1 whole, which is shorter than its diff:
```python
import jax
import jax.numpy as jnp
from jax import lax
from jax.experimental import pallas as pl
from jax.experimental.pallas import tpu as pltpu
from jax.sharding import PartitionSpec as P

NX, NZ, NC = 4, 4, 2
FIRST = 384
GRID = ("row", "col")


def place(x, z, c):
    return ((x % NX) * NZ + z % NZ) * NC + c % NC


def shift(value, dx, dz, dc):
    perm = [
        (place(x, z, c), place(x + dx, z + dz, c + dc))
        for x in range(NX)
        for z in range(NZ)
        for c in range(NC)
    ]
    return lax.ppermute(value, GRID, perm)


def ring(value, dx, dz):
    half = value.shape[0] // 2
    fwd = shift(value, dx, dz, 0)
    bwd = shift(value, -dx, -dz, 0)
    far_low = shift(fwd[:half], dx, dz, 0)
    far_high = shift(bwd[half:], -dx, -dz, 0)
    return value, fwd, bwd, far_low, far_high


def gemm_body(order_ref, a_ref, l_ref, acc_ref, out_ref):
    @pl.when(pl.program_id(0) == 0)
    def _():
        out_ref[...] = acc_ref[...]

    block = a_ref.shape[2]
    for i in range(2):
        out_ref[i * block : (i + 1) * block, :] += lax.dot_general(
            a_ref[i], l_ref[...], (((0,), (0,)), ((), ())), preferred_element_type=jnp.float32
        )


def gemm(order, inverse, panel, acc):
    block = inverse.shape[2]
    cols = panel.shape[1]
    steps = panel.shape[0] // block
    return pl.pallas_call(
        gemm_body,
        grid_spec=pltpu.PrefetchScalarGridSpec(
            num_scalar_prefetch=1,
            grid=(steps,),
            in_specs=[
                pl.BlockSpec((2, block, block), lambda j, order: (0, order[j], 0)),
                pl.BlockSpec((block, cols), lambda j, order: (j, 0)),
                pl.BlockSpec((2 * block, cols), lambda j, order: (0, 0)),
            ],
            out_specs=pl.BlockSpec((2 * block, cols), lambda j, order: (0, 0)),
        ),
        out_shape=jax.ShapeDtypeStruct((2 * block, cols), jnp.float32),
        input_output_aliases={3: 0},
        compiler_params=pltpu.CompilerParams(vmem_limit_bytes=32 * 1024 * 1024),
    )(order, inverse, panel, acc)


def dot(left, right):
    return jnp.dot(left, right, preferred_element_type=jnp.float32)


def local(inverse, factor, diag_inverse, widths, pattern, owner, assign, pole_weights):
    device = lax.axis_index(GRID)
    here_x, here_z, here_c = device // (NZ * NC), device // NC % NZ, device % NC
    poles = lax.axis_size("pole")
    block = diag_inverse.shape[3]
    blocks_k = widths.shape[0]
    total = factor.shape[3]
    live = 2 * block
    inverse = inverse[0]

    full = jnp.argmax(widths).astype(jnp.int32)
    one = jnp.where(full == 0, 1, 0)
    two = jnp.where(full == 2, 1, 2)
    split = widths[one]
    slot = jnp.arange(live, dtype=jnp.int32)
    slot_k = jnp.where(slot < block, full, jnp.where(slot < block + split, one, two))
    slot_at = jnp.where(
        slot < block, slot, jnp.where(slot < block + split, slot - block, slot - block - split)
    )
    source = slot_k * block + slot_at
    spread = jnp.arange(total, dtype=jnp.int32)[:, None] == source[None, :]
    kept = lax.dynamic_index_in_dim(pattern, device, 0, False)
    kept_slot = sum(jnp.where(slot_k == k, kept[k], 0) for k in range(blocks_k))
    pick = jnp.where(spread, kept_slot[None, :], 0).astype(jnp.bfloat16)
    spread = spread.astype(jnp.bfloat16)
    own = [dot(factor[0, i], pick).astype(jnp.bfloat16) for i in range(2)]
    first = jnp.concatenate([own[0][:, :FIRST], own[1][:, :FIRST]], 1)
    second = jnp.concatenate([own[0][:, FIRST:], own[1][:, FIRST:]], 1)

    def order_of(offsets):
        return jnp.stack(
            [place(here_x + ox, here_z + oz, here_c + oc) for ox, oz, oc in offsets]
        ).astype(jnp.int32)

    wanted = lax.dynamic_index_in_dim(owner, device, 0, False)

    def pick_own(picked, panel, order):
        for_row = jnp.argmax(order == wanted)
        rows = lax.dynamic_slice_in_dim(panel, for_row * block, block, 0)
        return jnp.where(jnp.any(order == wanted), rows, picked)

    far = 2
    across = ring(second, 1, 0)
    across = jnp.concatenate(across, 0)
    x_order = (0, -1, 1, far)
    z_order = (0, -1, 1, far)
    z0, zf, zb, zl, zh = ring(first, 0, 1)
    groups = [(z0, (0,)), (jnp.concatenate([zf, zb], 0), (-1, 1)), (jnp.concatenate([zl, zh], 0), (far,))]

    sum_first = jnp.zeros((2 * block, 2 * FIRST), jnp.float32)
    sum_second = jnp.zeros((2 * block, 2 * (live - FIRST)), jnp.float32)
    own_first = jnp.zeros((block, 2 * FIRST), jnp.bfloat16)
    own_second = jnp.zeros((block, 2 * (live - FIRST)), jnp.bfloat16)

    for piece, offsets_z in groups:
        panel = jnp.concatenate(ring(piece, 1, 0), 0)
        for plane in range(NC):
            held = shift(panel, 0, 0, 1) if plane else panel
            order = order_of([(ox, oz, plane) for ox in x_order for oz in offsets_z])
            sum_first = gemm(order, inverse, held, sum_first)
            own_first = pick_own(own_first, held, order)

    panel = jnp.concatenate(ring(across, 0, 1), 0)
    for plane in range(NC):
        held = shift(panel, 0, 0, 1) if plane else panel
        order = order_of([(ox, oz, plane) for oz in z_order for ox in x_order])
        sum_second = gemm(order, inverse, held, sum_second)
        own_second = pick_own(own_second, held, order)

    def quadrants(sums):
        cols = sums.shape[1] // 2
        return sums[:block, :cols], sums[:block, cols:], sums[block:, :cols], sums[block:, cols:]

    rr, ri, ir, ii = [jnp.concatenate(q, 1) for q in zip(quadrants(sum_first), quadrants(sum_second))]
    x_real, x_imag = ii - rr, -(ri + ir)
    weight = lax.dynamic_index_in_dim(pole_weights, assign[0], 0, False)
    panel_part = weight[0] * x_imag + weight[1] * x_real
    own_real = jnp.concatenate([own_first[:, :FIRST], own_second[:, : live - FIRST]], 1)
    own_imag = jnp.concatenate([own_first[:, FIRST:], own_second[:, live - FIRST :]], 1)

    def expand(value):
        return dot(value.astype(jnp.bfloat16), spread.T).astype(jnp.bfloat16)

    own_both = expand(jnp.concatenate([own_real, own_imag], 0))
    x_both = expand(jnp.concatenate([x_real, x_imag], 0))
    corrections = []
    for k in range(blocks_k):
        cut = slice(k * block, (k + 1) * block)
        lr, li = own_both[:block, cut], own_both[block:, cut]
        xr, xi = x_both[:block, cut], x_both[block:, cut]
        product = lax.dot_general(
            jnp.concatenate([lr, li], 0),
            jnp.concatenate(
                [jnp.concatenate([xi, xr], 0), jnp.concatenate([xr, -xi], 0)], 1
            ),
            (((0,), (0,)), ((), ())),
            preferred_element_type=jnp.float32,
        )
        corrections.append(weight[0] * product[:, :block] + weight[1] * product[:, block:])
    correction = jnp.concatenate(corrections, 0)
    inverse_diag = diag_inverse[0].astype(jnp.float32)
    own_diag = weight[0] * inverse_diag[1] + weight[1] * inverse_diag[0]
    pieces = NX * NZ * NC
    depth = total // pieces
    is_own = (jnp.arange(pieces) == device)[:, None, None]
    diag_part = jnp.where(is_own, own_diag[None], 0) - correction.reshape(pieces, depth, block)

    share = depth // poles * block
    sent = jnp.concatenate(
        [
            panel_part.reshape(poles, block // poles, live),
            diag_part.reshape(pieces, poles, share).transpose(1, 0, 2),
        ],
        2,
    ).astype(jnp.bfloat16)
    got = lax.all_to_all(sent, "pole", 0, 0, tiled=True).astype(jnp.float32).sum(0)
    panel_share, diag_share = got[:, :live], got[:, live:]
    diag_share = lax.all_to_all(diag_share, GRID, 0, 0, tiled=True).sum(0)
    both = jnp.concatenate([panel_share.reshape(-1), diag_share.reshape(-1)]).reshape(1, -1, 128)
    both = lax.all_to_all(
        jnp.broadcast_to(both, (poles,) + both.shape[1:]), "pole", 0, 0, tiled=True
    ).reshape(poles, -1)
    cut = block // poles * live
    panel_total = both[:, :cut].reshape(block, live)
    diag_total = both[:, cut:].reshape(depth, block)
    panel_out = jnp.dot(
        panel_total, spread.T.astype(jnp.float32), precision=lax.Precision.HIGHEST
    )
    return panel_out, diag_total


def solution(mesh):
    placed = (
        P("pole", None, None, GRID),
        P("pole", None, GRID, None),
        P("pole", None, GRID, None),
        P(),
        P(),
        P(),
        P("pole"),
        P(),
    )
    return jax.shard_map(
        local,
        mesh=mesh,
        in_specs=placed,
        out_specs=(P(GRID, None), P(GRID, None)),
        check_vma=False,
    )
```

time: 437 us -> 270 us (0.62)
  waiting for transfers between devices: 339 us -> 37.3 us
  Pallas kernels: 0 us -> 48.9 us
  local copies, waits for them, and re-layouts: 5.93 us -> 51.5 us
  starting transfers between devices: 0.12 us -> 44.2 us
  other arithmetic: 6.54 us -> 38.1 us
  matrix products: 35.9 us -> 5.81 us
  between operations: 15.2 us -> 9.08 us
    all_gather x1 -> x0, waiting for transfers between devices: 172 us -> none  [local(): lax.all_gather(masked, ('row', 'col'), axis=1, tiled=True)]
    reduce_scatter x1 -> x0, waiting for transfers between devices: 90.9 us -> none  [local(): lax.psum_scatter(jnp.stack([part_real, part_imag]), ('row', 'col'), scatt...]
    psum x1 -> x0, waiting for transfers between devices: 76.1 us -> none  [local(): panel_total, diag_total = lax.psum((panel_local, diag_local), 'pole')]
    pallas_call x0 -> x8, Pallas kernels: none -> 48.9 us  [gemm(): pl.pallas_call(gemm_body, grid_spec=pltpu.PrefetchScalarGridSpec(num_scal...]
    ppermute x0 -> x28, starting transfers between devices: none -> 37.6 us  [shift(): return lax.ppermute(value, GRID, perm)]
    psum x1 -> x0, blocking collectives: 33.9 us -> none  [local(): panel_total, diag_total = lax.psum((panel_local, diag_local), 'pole')]
    all_to_all x0 -> x2, blocking collectives: none -> 31.7 us  [the longest x1 17.8 us: local(): lax.all_to_all(sent, 'pole', 0, 0, tiled=True).astype(jnp.float32).sum(0)]
    dot_general x10 -> x8, matrix products: 35.9 us -> 5.81 us  [the longest x4 3.03 us: dot(): return jnp.dot(left, right, preferred_element_type=jnp.float32)]
  transfers between devices with their start and end apart: 3 -> 29, of which waited for: 3 -> 8; matrix products, arithmetic and copies ran while one was open for 2% -> 21% of each run, Pallas kernels for 0% -> 17%
where the time goes in v1:
time: 270 us; the launch traced here: 267 us
  local copies, waits for them, and re-layouts  51.5 us (19%)
  Pallas kernels  48.9 us (18%)
  starting transfers between devices  44.2 us (16%)
  other arithmetic  38.1 us (14%)
  waiting for transfers between devices  37.3 us (14%)
  blocking collectives  31.7 us (12%)
  between operations  9.08 us (3%)
  matrix products  5.81 us (2%)
    pallas_call x8, Pallas kernels, gemm(): pl.pallas_call(gemm_body, grid_spec=pltpu.PrefetchScalarGridSpec(num_scal...  48.9 us
    ppermute x28, starting transfers between devices, shift(): return lax.ppermute(value, GRID, perm)  37.6 us
    unnamed x60, local copies, waits for them, and re-layouts  31.3 us
    ppermute x28, waiting for transfers between devices, shift(): return lax.ppermute(value, GRID, perm)  28.4 us
    all_to_all x1, blocking collectives, local(): lax.all_to_all(sent, 'pole', 0, 0, tiled=True).astype(jnp.float32).sum(0)  17.8 us
    all_to_all x1, blocking collectives, local(): lax.all_to_all(jnp.broadcast_to(both, (poles,) + both.shape[1:]), 'pole',...  13.9 us
    another operation x8, other arithmetic, pick_own(): for_row = jnp.argmax(order == wanted)  9.79 us
    all_to_all x1, waiting for transfers between devices, local(): diag_share = lax.all_to_all(diag_share, GRID, 0, 0, tiled=True).sum(0)  8.93 us
  transfers between devices with their start and end apart: 29, of which 8 were waited for; matrix products, arithmetic and copies ran while one was open for 21% of the time, Pallas kernels for 17%

profile of v1, /device:TPU:2, one launch (start us, length us, event | category | flops | bytes accessed | tf_op | source)
XLA Modules:
  0.0 266.6 jit_solution(3604353538080673648)
XLA Ops:
  0.7 1.4 iota_reduce_fusion
  5.9 3.2 %fusion.74 = (s32[512]{0:T(512)S(1)}, s32[512]{0:T(512)S(1)}) fusion(s32[]{:T(128)} %bitcast.7, s32[]{:T(128)S(6)} %select_n.622, s32[]{:T(128)S(6)} %select_n.621, s32[]{:T(128)S(6)} %add.702, s32[]{:T(128)} %get-tuple-element.11, s32[]{:T(128)} %bitcast.10, s32[]{:T(128)} %bitcast.9, s32[]{:T(128)} %bitcast.8), kind=kLoop, calls=%fused_computation.139 | loop fusion | flops 9216 | bytes 4128 | tf_op jit(solution)/shard_map/add | solution.py:93
  11.9 2.3 collective-permute-start.15
  14.2 4.6 %collective-permute-start.2 = (bf16[256,768]{1,0:T(8,128)(2,1)}, bf16[256,768]{1,0:T(8,128)(2,1)}, u32[]{:S(2)}, u32[]{:S(2)}) collective-permute-start(bf16[256,768]{1,0:T(8,128)(2,1)} %get-tuple-element.48), channel_id=1, source_target_pairs={{0,6},{1,7},{2,0},{3,1},{4,2},{5,3},{6,4},{7,5},{8,14},{9,15},{10,... | collective-permute-start | bytes 1179656 | tf_op jit(solution)/shard_map/ppermute | solution.py:24
  19.5 1.5 collective-permute-start.19
  31.2 2.0 collective-permute-start.21
  33.8 5.5 %collective-permute-done = bf16[256,768]{1,0:T(8,128)(2,1)S(1)} collective-permute-done((bf16[256,768]{1,0:T(8,128)(2,1)}, bf16[256,768]{1,0:T(8,128)(2,1)S(1)}, u32[]{:S(2)}, u32[]{:S(2)}) %collective-permute-start) | collective-permute-done | bytes 393248 | tf_op jit(solution)/shard_map/ppermute | solution.py:24
  40.1 2.8 %collective-permute-start.22 = (bf16[128,256]{1,0:T(8,128)(2,1)S(1)}, bf16[128,256]{1,0:T(8,128)(2,1)S(1)}, u32[]{:S(2)}, u32[]{:S(2)}) collective-permute-start(bf16[128,256]{1,0:T(8,128)(2,1)S(1)} %slice.250), channel_id=1, source_target_pairs={{0,24},{1,25},{2,26},{3,27},{4,28},{5,29},{6,30},{7,31},{8,0},{9,1... | collective-permute-start | bytes 196616 | tf_op jit(solution)/shard_map/ppermute | solution.py:24
  42.8 1.8 constant_dynamic-update-slice_fusion.9
  44.6 1.8 constant_dynamic-update-slice_fusion.8
  47.2 2.0 collective-permute-start.10
  50.5 2.8 %collective-permute-start.24 = (bf16[1024,256]{1,0:T(8,128)(2,1)}, bf16[1024,256]{1,0:T(8,128)(2,1)}, u32[]{:S(2)}, u32[]{:S(2)}) collective-permute-start(bf16[1024,256]{1,0:T(8,128)(2,1)} %get-tuple-element.66), channel_id=1, source_target_pairs={{0,6},{1,7},{2,0},{3,1},{4,2},{5,3},{6,4},{7,5},{8,14},{9,15},{10,... | collective-permute-start | bytes 1572872 | tf_op jit(solution)/shard_map/ppermute | solution.py:24
  57.0 3.2 %collective-permute-done.9 = bf16[512,768]{1,0:T(8,128)(2,1)} collective-permute-done((bf16[512,768]{1,0:T(8,128)(2,1)}, bf16[512,768]{1,0:T(8,128)(2,1)}, u32[]{:S(2)}, u32[]{:S(2)}) %collective-permute-start.9) | collective-permute-done | bytes 786464 | tf_op jit(solution)/shard_map/ppermute | solution.py:24
  60.2 3.9 %collective-permute-start.17 = (bf16[128,768]{1,0:T(8,128)(2,1)S(1)}, bf16[128,768]{1,0:T(8,128)(2,1)S(1)}, u32[]{:S(2)}, u32[]{:S(2)}) collective-permute-start(bf16[128,768]{1,0:T(8,128)(2,1)S(1)} %slice.245), channel_id=1, source_target_pairs={{0,24},{1,25},{2,26},{3,27},{4,28},{5,29},{6,30},{7,31},{8,0},{9,1... | collective-permute-start | bytes 589832 | tf_op jit(solution)/shard_map/ppermute | solution.py:24
  65.2 1.8 constant_dynamic-update-slice_fusion.19
  68.0 2.1 collective-permute-start.12
  70.1 1.8 constant_dynamic-update-slice_fusion.18
  75.9 2.0 collective-permute-start.26
  82.5 1.9 constant_dynamic-update-slice_fusion.29
  84.4 1.9 constant_dynamic-update-slice_fusion.28
  86.3 8.6 %collective-permute-done.25 = bf16[512,256]{1,0:T(8,128)(2,1)S(1)} collective-permute-done((bf16[512,256]{1,0:T(8,128)(2,1)S(1)}, bf16[512,256]{1,0:T(8,128)(2,1)S(1)}, u32[]{:S(2)}, u32[]{:S(2)}) %collective-permute-start.25) | collective-permute-done | bytes 262176 | tf_op jit(solution)/shard_map/ppermute | solution.py:24
  95.6 4.1 %collective-permute-start.3 = (bf16[128,768]{1,0:T(8,128)(2,1)S(1)}, bf16[128,768]{1,0:T(8,128)(2,1)S(1)}, u32[]{:S(2)}, u32[]{:S(2)}) collective-permute-start(bf16[128,768]{1,0:T(8,128)(2,1)S(1)} %slice.239), channel_id=1, source_target_pairs={{0,6},{1,7},{2,0},{3,1},{4,2},{5,3},{6,4},{7,5},{8,14},{9,15},{10,... | collective-permute-start | bytes 589832 | tf_op jit(solution)/shard_map/ppermute | solution.py:24
  100.5 3.3 %collective-permute-done.1 = bf16[128,768]{1,0:T(8,128)(2,1)S(1)} collective-permute-done((bf16[128,768]{1,0:T(8,128)(2,1)S(1)}, bf16[128,768]{1,0:T(8,128)(2,1)S(1)}, u32[]{:S(2)}, u32[]{:S(2)}) %collective-permute-start.1) | collective-permute-done | bytes 196640 | tf_op jit(solution)/shard_map/ppermute | solution.py:24
  105.3 2.0 collective-permute-start.5
  114.3 2.8 %collective-permute-done.5 = bf16[256,768]{1,0:T(8,128)(2,1)} collective-permute-done((bf16[256,768]{1,0:T(8,128)(2,1)}, bf16[256,768]{1,0:T(8,128)(2,1)}, u32[]{:S(2)}, u32[]{:S(2)}) %collective-permute-start.5) | collective-permute-done | bytes 393248 | tf_op jit(solution)/shard_map/ppermute | solution.py:24
  118.0 1.9 collective-permute-start.7
  121.2 1.8 constant_dynamic-update-slice_fusion.5
  122.9 1.8 constant_dynamic-update-slice_fusion.4
  124.7 4.0 %collective-permute-done.6 = bf16[128,768]{1,0:T(8,128)(2,1)S(1)} collective-permute-done((bf16[128,768]{1,0:T(8,128)(2,1)S(1)}, bf16[128,768]{1,0:T(8,128)(2,1)S(1)}, u32[]{:S(2)}, u32[]{:S(2)}) %collective-permute-start.6) | collective-permute-done | bytes 196640 | tf_op jit(solution)/shard_map/ppermute | solution.py:24
  137.8 3.4 %copy-done.1 = bf16[1,2,8192,256]{3,2,1,0:T(8,128)(2,1)S(1)} copy-done((bf16[1,2,8192,256]{3,2,1,0:T(8,128)(2,1)S(1)}, bf16[1,2,8192,256]{3,2,1,0:T(8,128)(2,1)}, u32[]{:S(2)}) %copy-start.1) | copy-done | bytes 8388632
  141.2 4.1 %shard_map.95.acc_ref = f32[512,768]{1,0:T(8,128)S(1)} custom-call(s32[4]{0:T(128)S(1)} %get-tuple-element.27.order_ref, bf16[2,8192,256]{2,1,0:T(8,128)(2,1)S(1)} %bitcast.76, bf16[1024,768]{1,0:T(8,128)(2,1)} %constant_dynamic-update-slice_fusion.16.l_ref, f32[512,768]{1,0:T(8,128)S(1)} %broadcast_in_dim.92.acc_ref), custom_call_target="tpu_custom_call", output_to_operand_aliasing={{}: (3, {})} | custom-call | tf_op jit(solution)/shard_map/pallas_call | solution.py:52
  145.3 3.4 %copy-done.2 = bf16[1,2,8192,256]{3,2,1,0:T(8,128)(2,1)S(1)} copy-done((bf16[1,2,8192,256]{3,2,1,0:T(8,128)(2,1)S(1)}, bf16[1,2,8192,256]{3,2,1,0:T(8,128)(2,1)}, u32[]{:S(2)}) %copy-start.2) | copy-done | bytes 8388632
  148.7 10.7 %shard_map.101.acc_ref = f32[512,256]{1,0:T(8,128)S(1)} custom-call(s32[16]{0:T(128)S(1)} %stack.191.order_ref, bf16[2,8192,256]{2,1,0:T(8,128)(2,1)S(1)} %bitcast.77, bf16[4096,256]{1,0:T(8,128)(2,1)} %constant_dynamic-update-slice_fusion.26.l_ref, f32[512,256]{1,0:T(8,128)S(1)} %broadcast_in_dim.93.acc_ref), custom_call_target="tpu_custom_call", output_to_operand_aliasing={{}: (3, {})} | custom-call | tf_op jit(solution)/shard_map/pallas_call | solution.py:52
  159.5 3.4 %copy-done.3 = bf16[1,2,8192,256]{3,2,1,0:T(8,128)(2,1)S(1)} copy-done((bf16[1,2,8192,256]{3,2,1,0:T(8,128)(2,1)S(1)}, bf16[1,2,8192,256]{3,2,1,0:T(8,128)(2,1)}, u32[]{:S(2)}) %copy-start.3) | copy-done | bytes 8388632
  162.8 4.1 %shard_map.96.acc_ref = f32[512,768]{1,0:T(8,128)S(1)} custom-call(s32[4]{0:T(128)S(1)} %get-tuple-element.76.order_ref, bf16[2,8192,256]{2,1,0:T(8,128)(2,1)S(1)} %bitcast.78, bf16[1024,768]{1,0:T(8,128)(2,1)} %collective-permute-done.18.l_ref, f32[512,768]{1,0:T(8,128)S(1)} %shard_map.95.acc_ref), custom_call_target="tpu_custom_call", output_to_operand_aliasing={{}: (3, {})} | custom-call | tf_op jit(solution)/shard_map/pallas_call | solution.py:52
  166.9 4.2 %shard_map.97.acc_ref = f32[512,768]{1,0:T(8,128)S(1)} custom-call(s32[8]{0:T(128)S(1)} %stack.179.order_ref, bf16[2,8192,256]{2,1,0:T(8,128)(2,1)S(1)} %bitcast.79, bf16[2048,768]{1,0:T(8,128)(2,1)S(1)} %constant_dynamic-update-slice_fusion.10.l_ref, f32[512,768]{1,0:T(8,128)S(1)} %shard_map.96.acc_ref), custom_call_target="tpu_custom_call", output_to_operand_aliasing={{}: (3, {})} | custom-call | tf_op jit(solution)/shard_map/pallas_call | solution.py:52
  171.2 10.7 %shard_map.102 = f32[512,256]{1,0:T(8,128)S(1)} custom-call(s32[16]{0:T(128)S(1)} %stack.190.order_ref, bf16[2,8192,256]{2,1,0:T(8,128)(2,1)S(1)} %bitcast.80, bf16[4096,256]{1,0:T(8,128)(2,1)} %collective-permute-done.27.l_ref, f32[512,256]{1,0:T(8,128)S(1)} %shard_map.101.acc_ref), custom_call_target="tpu_custom_call", output_to_operand_aliasing={{}: (3, {})} | custom-call | tf_op jit(solution)/shard_map/pallas_call | solution.py:52
  181.9 2.2 select_select_fusion.1
  184.2 7.0 %shard_map.98.acc_ref = f32[512,768]{1,0:T(8,128)S(1)} custom-call(s32[8]{0:T(128)S(1)} %stack.170.order_ref, bf16[2,8192,256]{2,1,0:T(8,128)(2,1)S(1)} %bitcast.81, bf16[2048,768]{1,0:T(8,128)(2,1)} %collective-permute-done.13.l_ref, f32[512,768]{1,0:T(8,128)S(1)} %shard_map.97.acc_ref), custom_call_target="tpu_custom_call", output_to_operand_aliasing={{}: (3, {})} | custom-call | tf_op jit(solution)/shard_map/pallas_call | solution.py:52
  191.2 4.1 %shard_map.99.acc_ref = f32[512,768]{1,0:T(8,128)S(1)} custom-call(s32[4]{0:T(128)S(1)} %get-tuple-element.23.order_ref, bf16[2,8192,256]{2,1,0:T(8,128)(2,1)S(1)} %bitcast.82, bf16[1024,768]{1,0:T(8,128)(2,1)} %constant_dynamic-update-slice_fusion.2.l_ref, f32[512,768]{1,0:T(8,128)S(1)} %shard_map.98.acc_ref), custom_call_target="tpu_custom_call", output_to_operand_aliasing={{}: (3, {})} | custom-call | tf_op jit(solution)/shard_map/pallas_call | solution.py:52
  195.3 4.1 %shard_map.100 = f32[512,768]{1,0:T(8,128)S(1)} custom-call(s32[4]{0:T(128)S(1)} %get-tuple-element.78.order_ref, bf16[2,8192,256]{2,1,0:T(8,128)(2,1)S(1)} %bitcast.83, bf16[1024,768]{1,0:T(8,128)(2,1)} %collective-permute-done.8.l_ref, f32[512,768]{1,0:T(8,128)S(1)} %shard_map.99.acc_ref), custom_call_target="tpu_custom_call", output_to_operand_aliasing={{}: (3, {})} | custom-call | tf_op jit(solution)/shard_map/pallas_call | solution.py:52
  199.5 5.3 %select_select_fusion = bf16[256,768]{1,0:T(8,128)(2,1)S(1)} fusion(bf16[1024,768]{1,0:T(8,128)(2,1)} %constant_dynamic-update-slice_fusion.16.l_ref, s32[]{:T(128)S(6)} %select_n.648, bf16[1024,768]{1,0:T(8,128)(2,1)} %collective-permute-done.18.l_ref, s32[]{:T(128)S(6)} %select_n.646, bf16[2048,768]{1,0:T(8,128)(2,1)S(1)} %constant_dynamic-update-slice_fusion.10.l_ref, ...), kind=kLoop, calls=%fused_computation.76 | loop fusion | flops 1179648 | bytes 2752542 | tf_op jit(solution)/shard_map/jit(_where)/select_n | solution.py:113
  213.0 2.6 fusion.20
  215.6 17.8 %all_to_all.19 = bf16[8,32,1280]{2,1,0:T(8,128)(2,1)S(1)} all-to-all(bf16[8,32,1280]{2,1,0:T(8,128)(2,1)S(1)} %pad_maximum_fusion.1), channel_id=1, replica_groups=mesh['pole'=8,'row'=4,'col'=8] {'pole'}, dimensions={0} | all-to-all | bytes 1310720 | tf_op jit(solution)/shard_map/all_to_all | solution.py:189
  234.2 6.6 %all-to-all-start.1 = ((f32[32,1,768]{2,1,0:T(1,128)}), f32[32,1,768]{2,1,0:T(1,128)S(1)}, u32[]{:S(2)}, u32[]{:S(2)}) async-start(f32[32,1,768]{2,1,0:T(1,128)} %all_to_all.13), calls=%async_computation.1 | async-start | bytes 196608 | tf_op jit(solution)/shard_map/all_to_all | solution.py:191
  240.9 8.9 %all-to-all-done.1 = f32[32,1,768]{2,1,0:T(1,128)S(1)} async-done(((f32[32,1,768]{2,1,0:T(1,128)}), f32[32,1,768]{2,1,0:T(1,128)S(1)}, u32[]{:S(2)}, u32[]{:S(2)}) %all-to-all-start.1) | async-done | bytes 98336 | tf_op jit(solution)/shard_map/all_to_all | solution.py:191
  249.9 13.9 %all_to_all.20 = f32[8,134,128]{2,1,0:T(8,128)S(1)} all-to-all(f32[8,134,128]{2,1,0:T(8,128)S(1)} %broadcast_in_dim.101), channel_id=1, replica_groups=mesh['pole'=8,'row'=4,'col'=8] {'pole'}, dimensions={0} | all-to-all | bytes 1097728 | tf_op jit(solution)/shard_map/all_to_all | solution.py:193
  264.8 1.8 fusion
  (170 shorter events, 59.1 us)
Async XLA Ops:
  0.6 4.0 %copy-start = (s32[32,3]{0,1:T(4,128)S(1)}, s32[32,3]{0,1:T(4,128)}, u32[]{:S(2)}) copy-start(s32[32,3]{0,1:T(4,128)} %param.12) | copy-start | bytes 1156
  0.6 9.8 %copy-start.18 = (bf16[1,2,256,768]{3,2,1,0:T(8,128)(2,1)S(1)}, bf16[1,2,256,768]{3,2,1,0:T(8,128)(2,1)}, u32[]{:S(2)}) copy-start(bf16[1,2,256,768]{3,2,1,0:T(8,128)(2,1)} %param.9) | copy-start | bytes 2359300
  10.9 11.4 %copy-start.19 = (s32[32]{0:T(128)S(1)}, s32[32]{0:T(128)}, u32[]{:S(2)}) copy-start(s32[32]{0:T(128)} %param.13) | copy-start | bytes 388
  11.9 41.4 %collective-permute-start.15 = (bf16[256,768]{1,0:T(8,128)(2,1)}, bf16[256,768]{1,0:T(8,128)(2,1)}, u32[]{:S(2)}, u32[]{:S(2)}) collective-permute-start(bf16[256,768]{1,0:T(8,128)(2,1)} %get-tuple-element.48), channel_id=1, source_target_pairs={{0,24},{1,25},{2,26},{3,27},{4,28},{5,29},{6,30},{7,31},{8,0},{9,1... | collective-permute-start | bytes 1179656 | tf_op jit(solution)/shard_map/ppermute | solution.py:24
  14.2 30.5 %collective-permute-start.2 = (bf16[256,768]{1,0:T(8,128)(2,1)}, bf16[256,768]{1,0:T(8,128)(2,1)}, u32[]{:S(2)}, u32[]{:S(2)}) collective-permute-start(bf16[256,768]{1,0:T(8,128)(2,1)} %get-tuple-element.48), channel_id=1, source_target_pairs={{0,6},{1,7},{2,0},{3,1},{4,2},{5,3},{6,4},{7,5},{8,14},{9,15},{10,... | collective-permute-start | bytes 1179656 | tf_op jit(solution)/shard_map/ppermute | solution.py:24
  18.7 20.6 %collective-permute-start = (bf16[256,768]{1,0:T(8,128)(2,1)}, bf16[256,768]{1,0:T(8,128)(2,1)S(1)}, u32[]{:S(2)}, u32[]{:S(2)}) collective-permute-start(bf16[256,768]{1,0:T(8,128)(2,1)} %get-tuple-element.48), channel_id=1, source_target_pairs={{0,2},{1,3},{2,4},{3,5},{4,6},{5,7},{6,0},{7,1},{8,10},{9,11},{10,... | collective-permute-start | bytes 1179656 | tf_op jit(solution)/shard_map/ppermute | solution.py:24
  19.5 10.9 %collective-permute-start.19 = (bf16[256,256]{1,0:T(8,128)(2,1)S(1)}, bf16[256,256]{1,0:T(8,128)(2,1)S(1)}, u32[]{:S(2)}, u32[]{:S(2)}) collective-permute-start(bf16[256,256]{1,0:T(8,128)(2,1)S(1)} %get-tuple-element.65), channel_id=1, source_target_pairs={{0,8},{1,9},{2,10},{3,11},{4,12},{5,13},{6,14},{7,15},{8,16},{9,17... | collective-permute-start | bytes 393224 | tf_op jit(solution)/shard_map/ppermute | solution.py:24
  21.0 10.2 %collective-permute-start.20 = (bf16[256,256]{1,0:T(8,128)(2,1)S(1)}, bf16[256,256]{1,0:T(8,128)(2,1)S(1)}, u32[]{:S(2)}, u32[]{:S(2)}) collective-permute-start(bf16[256,256]{1,0:T(8,128)(2,1)S(1)} %get-tuple-element.65), channel_id=1, source_target_pairs={{0,24},{1,25},{2,26},{3,27},{4,28},{5,29},{6,30},{7,31},{8,0},{9,1... | collective-permute-start | bytes 393224 | tf_op jit(solution)/shard_map/ppermute | solution.py:24
  30.4 34.7 %collective-permute-start.14 = (bf16[256,768]{1,0:T(8,128)(2,1)}, bf16[256,768]{1,0:T(8,128)(2,1)}, u32[]{:S(2)}, u32[]{:S(2)}) collective-permute-start(bf16[256,768]{1,0:T(8,128)(2,1)} %get-tuple-element.48), channel_id=1, source_target_pairs={{0,8},{1,9},{2,10},{3,11},{4,12},{5,13},{6,14},{7,15},{8,16},{9,17... | collective-permute-start | bytes 1179656 | tf_op jit(solution)/shard_map/ppermute | solution.py:24
  31.2 16.0 %collective-permute-start.21 = (bf16[128,256]{1,0:T(8,128)(2,1)S(1)}, bf16[128,256]{1,0:T(8,128)(2,1)S(1)}, u32[]{:S(2)}, u32[]{:S(2)}) collective-permute-start(bf16[128,256]{1,0:T(8,128)(2,1)S(1)} %slice.249), channel_id=1, source_target_pairs={{0,8},{1,9},{2,10},{3,11},{4,12},{5,13},{6,14},{7,15},{8,16},{9,17... | collective-permute-start | bytes 196616 | tf_op jit(solution)/shard_map/ppermute | solution.py:24
  40.1 9.8 %collective-permute-start.22 = (bf16[128,256]{1,0:T(8,128)(2,1)S(1)}, bf16[128,256]{1,0:T(8,128)(2,1)S(1)}, u32[]{:S(2)}, u32[]{:S(2)}) collective-permute-start(bf16[128,256]{1,0:T(8,128)(2,1)S(1)} %slice.250), channel_id=1, source_target_pairs={{0,24},{1,25},{2,26},{3,27},{4,28},{5,29},{6,30},{7,31},{8,0},{9,1... | collective-permute-start | bytes 196616 | tf_op jit(solution)/shard_map/ppermute | solution.py:24
  46.4 13.8 %collective-permute-start.9 = (bf16[512,768]{1,0:T(8,128)(2,1)}, bf16[512,768]{1,0:T(8,128)(2,1)}, u32[]{:S(2)}, u32[]{:S(2)}) collective-permute-start(bf16[512,768]{1,0:T(8,128)(2,1)} %get-tuple-element.49), channel_id=1, source_target_pairs={{0,8},{1,9},{2,10},{3,11},{4,12},{5,13},{6,14},{7,15},{8,16},{9,17... | collective-permute-start | bytes 2359304 | tf_op jit(solution)/shard_map/ppermute | solution.py:24
  47.2 19.8 %collective-permute-start.10 = (bf16[512,768]{1,0:T(8,128)(2,1)}, bf16[512,768]{1,0:T(8,128)(2,1)}, u32[]{:S(2)}, u32[]{:S(2)}) collective-permute-start(bf16[512,768]{1,0:T(8,128)(2,1)} %get-tuple-element.49), channel_id=1, source_target_pairs={{0,24},{1,25},{2,26},{3,27},{4,28},{5,29},{6,30},{7,31},{8,0},{9,1... | collective-permute-start | bytes 2359304 | tf_op jit(solution)/shard_map/ppermute | solution.py:24
  50.5 23.3 %collective-permute-start.24 = (bf16[1024,256]{1,0:T(8,128)(2,1)}, bf16[1024,256]{1,0:T(8,128)(2,1)}, u32[]{:S(2)}, u32[]{:S(2)}) collective-permute-start(bf16[1024,256]{1,0:T(8,128)(2,1)} %get-tuple-element.66), channel_id=1, source_target_pairs={{0,6},{1,7},{2,0},{3,1},{4,2},{5,3},{6,4},{7,5},{8,14},{9,15},{10,... | collective-permute-start | bytes 1572872 | tf_op jit(solution)/shard_map/ppermute | solution.py:24
  53.3 22.7 %collective-permute-start.23 = (bf16[1024,256]{1,0:T(8,128)(2,1)}, bf16[1024,256]{1,0:T(8,128)(2,1)}, u32[]{:S(2)}, u32[]{:S(2)}) collective-permute-start(bf16[1024,256]{1,0:T(8,128)(2,1)} %get-tuple-element.66), channel_id=1, source_target_pairs={{0,2},{1,3},{2,4},{3,5},{4,6},{5,7},{6,0},{7,1},{8,10},{9,11},{10,... | collective-permute-start | bytes 1572872 | tf_op jit(solution)/shard_map/ppermute | solution.py:24
  60.2 47.8 %collective-permute-start.17 = (bf16[128,768]{1,0:T(8,128)(2,1)S(1)}, bf16[128,768]{1,0:T(8,128)(2,1)S(1)}, u32[]{:S(2)}, u32[]{:S(2)}) collective-permute-start(bf16[128,768]{1,0:T(8,128)(2,1)S(1)} %slice.245), channel_id=1, source_target_pairs={{0,24},{1,25},{2,26},{3,27},{4,28},{5,29},{6,30},{7,31},{8,0},{9,1... | collective-permute-start | bytes 589832 | tf_op jit(solution)/shard_map/ppermute | solution.py:24
  65.1 16.2 %collective-permute-start.11 = (bf16[256,768]{1,0:T(8,128)(2,1)S(1)}, bf16[256,768]{1,0:T(8,128)(2,1)S(1)}, u32[]{:S(2)}, u32[]{:S(2)}) collective-permute-start(bf16[256,768]{1,0:T(8,128)(2,1)S(1)} %slice.242), channel_id=1, source_target_pairs={{0,8},{1,9},{2,10},{3,11},{4,12},{5,13},{6,14},{7,15},{8,16},{9,17... | collective-permute-start | bytes 1179656 | tf_op jit(solution)/shard_map/ppermute | solution.py:24
  65.2 8.6 %copy-start.15 = (bf16[256,768]{1,0:T(8,128)(2,1)S(1)}, bf16[256,768]{1,0:T(8,128)(2,1)}, u32[]{:S(2)}) copy-start(bf16[256,768]{1,0:T(8,128)(2,1)} %copy-done.14) | copy-start | bytes 1179652
  68.0 14.3 %collective-permute-start.12 = (bf16[256,768]{1,0:T(8,128)(2,1)S(1)}, bf16[256,768]{1,0:T(8,128)(2,1)S(1)}, u32[]{:S(2)}, u32[]{:S(2)}) collective-permute-start(bf16[256,768]{1,0:T(8,128)(2,1)S(1)} %slice.243), channel_id=1, source_target_pairs={{0,24},{1,25},{2,26},{3,27},{4,28},{5,29},{6,30},{7,31},{8,0},{9,1... | collective-permute-start | bytes 1179656 | tf_op jit(solution)/shard_map/ppermute | solution.py:24
  73.9 33.4 %collective-permute-start.16 = (bf16[128,768]{1,0:T(8,128)(2,1)S(1)}, bf16[128,768]{1,0:T(8,128)(2,1)S(1)}, u32[]{:S(2)}, u32[]{:S(2)}) collective-permute-start(bf16[128,768]{1,0:T(8,128)(2,1)S(1)} %slice.244), channel_id=1, source_target_pairs={{0,8},{1,9},{2,10},{3,11},{4,12},{5,13},{6,14},{7,15},{8,16},{9,17... | collective-permute-start | bytes 589832 | tf_op jit(solution)/shard_map/ppermute | solution.py:24
  75.9 19.6 %collective-permute-start.26 = (bf16[512,256]{1,0:T(8,128)(2,1)S(1)}, bf16[512,256]{1,0:T(8,128)(2,1)S(1)}, u32[]{:S(2)}, u32[]{:S(2)}) collective-permute-start(bf16[512,256]{1,0:T(8,128)(2,1)S(1)} %slice.252), channel_id=1, source_target_pairs={{0,6},{1,7},{2,0},{3,1},{4,2},{5,3},{6,4},{7,5},{8,14},{9,15},{10,... | collective-permute-start | bytes 786440 | tf_op jit(solution)/shard_map/ppermute | solution.py:24
  81.3 13.5 %collective-permute-start.25 = (bf16[512,256]{1,0:T(8,128)(2,1)S(1)}, bf16[512,256]{1,0:T(8,128)(2,1)S(1)}, u32[]{:S(2)}, u32[]{:S(2)}) collective-permute-start(bf16[512,256]{1,0:T(8,128)(2,1)S(1)} %slice.251), channel_id=1, source_target_pairs={{0,2},{1,3},{2,4},{3,5},{4,6},{5,7},{6,0},{7,1},{8,10},{9,11},{10,... | collective-permute-start | bytes 786440 | tf_op jit(solution)/shard_map/ppermute | solution.py:24
  82.4 101.8 %collective-permute-start.13 = (bf16[2048,768]{1,0:T(8,128)(2,1)S(1)}, bf16[2048,768]{1,0:T(8,128)(2,1)}, u32[]{:S(2)}, u32[]{:S(2)}) collective-permute-start(bf16[2048,768]{1,0:T(8,128)(2,1)S(1)} %constant_dynamic-update-slice_fusion.10.l_ref), channel_id=1, source_target_pairs={{0,1},{1,0},{2,3},{3,2},{4,5},{5,4},{6,7},{7,6},{8,9},{9,8},{10,11... | collective-permute-start | bytes 9437192 | tf_op jit(solution)/shard_map/ppermute | solution.py:24
  94.9 8.9 %collective-permute-start.1 = (bf16[128,768]{1,0:T(8,128)(2,1)S(1)}, bf16[128,768]{1,0:T(8,128)(2,1)S(1)}, u32[]{:S(2)}, u32[]{:S(2)}) collective-permute-start(bf16[128,768]{1,0:T(8,128)(2,1)S(1)} %slice.238), channel_id=1, source_target_pairs={{0,2},{1,3},{2,4},{3,5},{4,6},{5,7},{6,0},{7,1},{8,10},{9,11},{10,... | collective-permute-start | bytes 589832 | tf_op jit(solution)/shard_map/ppermute | solution.py:24
  95.6 8.9 %collective-permute-start.3 = (bf16[128,768]{1,0:T(8,128)(2,1)S(1)}, bf16[128,768]{1,0:T(8,128)(2,1)S(1)}, u32[]{:S(2)}, u32[]{:S(2)}) collective-permute-start(bf16[128,768]{1,0:T(8,128)(2,1)S(1)} %slice.239), channel_id=1, source_target_pairs={{0,6},{1,7},{2,0},{3,1},{4,2},{5,3},{6,4},{7,5},{8,14},{9,15},{10,... | collective-permute-start | bytes 589832 | tf_op jit(solution)/shard_map/ppermute | solution.py:24
  103.7 67.4 %collective-permute-start.27 = (bf16[4096,256]{1,0:T(8,128)(2,1)}, bf16[4096,256]{1,0:T(8,128)(2,1)}, u32[]{:S(2)}, u32[]{:S(2)}) collective-permute-start(bf16[4096,256]{1,0:T(8,128)(2,1)} %constant_dynamic-update-slice_fusion.26.l_ref), channel_id=1, source_target_pairs={{0,1},{1,0},{2,3},{3,2},{4,5},{5,4},{6,7},{7,6},{8,9},{9,8},{10,11... | collective-permute-start | bytes 6291464 | tf_op jit(solution)/shard_map/ppermute | solution.py:24
  105.3 11.8 %collective-permute-start.5 = (bf16[256,768]{1,0:T(8,128)(2,1)}, bf16[256,768]{1,0:T(8,128)(2,1)}, u32[]{:S(2)}, u32[]{:S(2)}) collective-permute-start(bf16[256,768]{1,0:T(8,128)(2,1)} %get-tuple-element.53), channel_id=1, source_target_pairs={{0,24},{1,25},{2,26},{3,27},{4,28},{5,29},{6,30},{7,31},{8,0},{9,1... | collective-permute-start | bytes 1179656 | tf_op jit(solution)/shard_map/ppermute | solution.py:24
  107.3 12.6 %collective-permute-start.4 = (bf16[256,768]{1,0:T(8,128)(2,1)}, bf16[256,768]{1,0:T(8,128)(2,1)}, u32[]{:S(2)}, u32[]{:S(2)}) collective-permute-start(bf16[256,768]{1,0:T(8,128)(2,1)} %get-tuple-element.53), channel_id=1, source_target_pairs={{0,8},{1,9},{2,10},{3,11},{4,12},{5,13},{6,14},{7,15},{8,16},{9,17... | collective-permute-start | bytes 1179656 | tf_op jit(solution)/shard_map/ppermute | solution.py:24
  108.7 50.8 %collective-permute-start.18 = (bf16[1024,768]{1,0:T(8,128)(2,1)}, bf16[1024,768]{1,0:T(8,128)(2,1)}, u32[]{:S(2)}, u32[]{:S(2)}) collective-permute-start(bf16[1024,768]{1,0:T(8,128)(2,1)} %constant_dynamic-update-slice_fusion.16.l_ref), channel_id=1, source_target_pairs={{0,1},{1,0},{2,3},{3,2},{4,5},{5,4},{6,7},{7,6},{8,9},{9,8},{10,11... | collective-permute-start | bytes 4718600 | tf_op jit(solution)/shard_map/ppermute | solution.py:24
  114.3 18.4 %copy-start.16 = (bf16[1,2,24,256]{3,2,1,0:T(8,128)(2,1)S(1)}, bf16[1,2,24,256]{3,2,1,0:T(8,128)(2,1)}, u32[]{:S(2)}) copy-start(bf16[1,2,24,256]{3,2,1,0:T(8,128)(2,1)} %param.10) | copy-start | bytes 73732
  114.3 18.4 %copy-start.17 = (f32[20,2]{0,1:T(2,128)S(1)}, f32[20,2]{0,1:T(2,128)}, u32[]{:S(2)}) copy-start(f32[20,2]{0,1:T(2,128)} %param.15) | copy-start | bytes 484
  118.0 11.4 %collective-permute-start.7 = (bf16[128,768]{1,0:T(8,128)(2,1)S(1)}, bf16[128,768]{1,0:T(8,128)(2,1)S(1)}, u32[]{:S(2)}, u32[]{:S(2)}) collective-permute-start(bf16[128,768]{1,0:T(8,128)(2,1)S(1)} %slice.241), channel_id=1, source_target_pairs={{0,24},{1,25},{2,26},{3,27},{4,28},{5,29},{6,30},{7,31},{8,0},{9,1... | collective-permute-start | bytes 589832 | tf_op jit(solution)/shard_map/ppermute | solution.py:24
  120.8 7.9 %collective-permute-start.6 = (bf16[128,768]{1,0:T(8,128)(2,1)S(1)}, bf16[128,768]{1,0:T(8,128)(2,1)S(1)}, u32[]{:S(2)}, u32[]{:S(2)}) collective-permute-start(bf16[128,768]{1,0:T(8,128)(2,1)S(1)} %slice.240), channel_id=1, source_target_pairs={{0,8},{1,9},{2,10},{3,11},{4,12},{5,13},{6,14},{7,15},{8,16},{9,17... | collective-permute-start | bytes 589832 | tf_op jit(solution)/shard_map/ppermute | solution.py:24
  130.2 65.1 %collective-permute-start.8 = (bf16[1024,768]{1,0:T(8,128)(2,1)}, bf16[1024,768]{1,0:T(8,128)(2,1)}, u32[]{:S(2)}, u32[]{:S(2)}) collective-permute-start(bf16[1024,768]{1,0:T(8,128)(2,1)} %constant_dynamic-update-slice_fusion.2.l_ref), channel_id=1, source_target_pairs={{0,1},{1,0},{2,3},{3,2},{4,5},{5,4},{6,7},{7,6},{8,9},{9,8},{10,11... | collective-permute-start | bytes 4718600 | tf_op jit(solution)/shard_map/ppermute | solution.py:24
  137.8 3.4 %copy-start.1 = (bf16[1,2,8192,256]{3,2,1,0:T(8,128)(2,1)S(1)}, bf16[1,2,8192,256]{3,2,1,0:T(8,128)(2,1)}, u32[]{:S(2)}) copy-start(bf16[1,2,8192,256]{3,2,1,0:T(8,128)(2,1)} %param.8) | copy-start | bytes 25165828
  145.3 3.4 %copy-start.2 = (bf16[1,2,8192,256]{3,2,1,0:T(8,128)(2,1)S(1)}, bf16[1,2,8192,256]{3,2,1,0:T(8,128)(2,1)}, u32[]{:S(2)}) copy-start(bf16[1,2,8192,256]{3,2,1,0:T(8,128)(2,1)} %param.8) | copy-start | bytes 25165828
  159.4 3.4 %copy-start.3 = (bf16[1,2,8192,256]{3,2,1,0:T(8,128)(2,1)S(1)}, bf16[1,2,8192,256]{3,2,1,0:T(8,128)(2,1)}, u32[]{:S(2)}) copy-start(bf16[1,2,8192,256]{3,2,1,0:T(8,128)(2,1)} %param.8) | copy-start | bytes 25165828
  184.2 20.7 %copy-start.10 = (f32[256,128]{1,0:T(8,128)}, f32[256,128]{1,0:T(8,128)S(1)}, u32[]{:S(2)}) copy-start(f32[256,128]{1,0:T(8,128)S(1)} %get-tuple-element.41) | copy-start | bytes 393220
  184.2 20.7 %copy-start.11 = (f32[256,128]{1,0:T(8,128)}, f32[256,128]{1,0:T(8,128)S(1)}, u32[]{:S(2)}) copy-start(f32[256,128]{1,0:T(8,128)S(1)} %get-tuple-element.42) | copy-start | bytes 393220
  184.2 20.8 %copy-start.12 = (f32[256,128]{1,0:T(8,128)}, f32[256,128]{1,0:T(8,128)S(1)}, u32[]{:S(2)}) copy-start(f32[256,128]{1,0:T(8,128)S(1)} %get-tuple-element.43) | copy-start | bytes 393220
  184.2 20.8 %copy-start.13 = (f32[256,128]{1,0:T(8,128)}, f32[256,128]{1,0:T(8,128)S(1)}, u32[]{:S(2)}) copy-start(f32[256,128]{1,0:T(8,128)S(1)} %get-tuple-element.44) | copy-start | bytes 393220
  199.5 5.4 %copy-start.4 = (f32[256,384]{1,0:T(8,128)}, f32[256,384]{1,0:T(8,128)S(1)}, u32[]{:S(2)}) copy-start(f32[256,384]{1,0:T(8,128)S(1)} %get-tuple-element.29) | copy-start | bytes 1179652
  199.5 5.6 %copy-start.6 = (f32[256,384]{1,0:T(8,128)}, f32[256,384]{1,0:T(8,128)S(1)}, u32[]{:S(2)}) copy-start(f32[256,384]{1,0:T(8,128)S(1)} %get-tuple-element.30) | copy-start | bytes 1179652
  199.5 5.6 %copy-start.8 = (f32[256,384]{1,0:T(8,128)}, f32[256,384]{1,0:T(8,128)S(1)}, u32[]{:S(2)}) copy-start(f32[256,384]{1,0:T(8,128)S(1)} %get-tuple-element.31) | copy-start | bytes 1179652
  211.6 1.4 copy-start.5
  211.6 1.4 copy-start.7
  211.6 1.4 copy-start.9
  234.2 15.6 %all-to-all-start.1 = ((f32[32,1,768]{2,1,0:T(1,128)}), f32[32,1,768]{2,1,0:T(1,128)S(1)}, u32[]{:S(2)}, u32[]{:S(2)}) async-start(f32[32,1,768]{2,1,0:T(1,128)} %all_to_all.13), calls=%async_computation.1 | async-start | bytes 196608 | tf_op jit(solution)/shard_map/all_to_all | solution.py:191
  (1 other events, 0.8 us)

commit v2 on v0

v2 whole, which is shorter than its diff:
```python
import functools

import jax
import jax.numpy as jnp
from jax import lax
from jax.experimental import pallas as pl
from jax.experimental.pallas import tpu as pltpu
from jax.sharding import PartitionSpec as P

NX, NZ, NC = 4, 4, 2
POLES = 8
B = 256
HALF = 128
GRID = ("row", "col")
MIB = 1024 * 1024
VMEM = pl.BlockSpec(memory_space=pltpu.VMEM)
SMEM = pl.BlockSpec(memory_space=pltpu.SMEM)
ANY = pl.BlockSpec(memory_space=pl.ANY)


def place(x, z, c):
    return ((x % NX) * NZ + z % NZ) * NC + c % NC


def shift(value, dx, dz, dc=0):
    perm = [
        (place(x, z, c), place(x + dx, z + dz, c + dc))
        for x in range(NX)
        for z in range(NZ)
        for c in range(NC)
    ]
    return lax.ppermute(value, GRID, perm)


def params(mib):
    return pltpu.CompilerParams(vmem_limit_bytes=mib * MIB)


def transposed_dot(left, right):
    return lax.dot_general(
        left, right, (((0,), (0,)), ((), ())), preferred_element_type=jnp.float32
    )


def layout(widths):
    full = jnp.where(widths[0] == B, 0, jnp.where(widths[1] == B, 1, 2))
    one = jnp.where(full == 0, 1, 0)
    two = jnp.where(full == 2, 1, 2)
    return full, one, two, widths[one]


def moved(split):
    at_row = lax.broadcasted_iota(jnp.int32, (B, B), 0)
    at_col = lax.broadcasted_iota(jnp.int32, (B, B), 1)
    return (at_row + split == at_col).astype(jnp.float32).astype(jnp.bfloat16)


def prepare_body(device, widths, pattern, factor, top, rest, give):
    dev = device[0]
    full, one, two, split = layout(widths)

    def cut(i, k):
        return factor[i, :, pl.ds(pl.multiple_of(k * B, B), B)]

    def kept(value, k):
        keep = (pattern[dev, k] > 0).astype(jnp.float32)
        return (value.astype(jnp.float32) * keep).astype(jnp.bfloat16)

    col = lax.broadcasted_iota(jnp.int32, (B, B), 1)
    move = moved(split)
    large, small = [], []
    for i in range(2):
        large.append(kept(cut(i, full), full))
        late = jnp.dot(cut(i, two), move, preferred_element_type=jnp.float32)
        keep_one = (pattern[dev, one] > 0).astype(jnp.float32)
        keep_two = (pattern[dev, two] > 0).astype(jnp.float32)
        both = jnp.where(col < split, cut(i, one).astype(jnp.float32) * keep_one, late * keep_two)
        small.append(both.astype(jnp.bfloat16))

    def store(mine, other):
        for i in range(2):
            at = slice(i * B, (i + 1) * B)
            top[:, at] = mine[i][:HALF]
            rest[:, at] = mine[i][HALF:]
            give[:, at] = other[i]

    @pl.when(dev % NC == 0)
    def _():
        store(large, small)

    @pl.when(dev % NC == 1)
    def _():
        store(small, large)


def prepare(device, widths, pattern, factor):
    half = jax.ShapeDtypeStruct((HALF, 2 * B), jnp.bfloat16)
    return pl.pallas_call(
        prepare_body,
        in_specs=[SMEM, SMEM, SMEM, VMEM],
        out_specs=[VMEM] * 3,
        out_shape=[half, half, jax.ShapeDtypeStruct((B, 2 * B), jnp.bfloat16)],
        compiler_params=params(16),
    )(device, widths, pattern, factor)


def gemm_body(segments, chunks, has_acc, *refs):
    device, own, sib = refs[:3]
    acc = refs[3] if has_acc else None
    dev = device[0]
    core, here_x, here_z = dev % NC, dev // (NZ * NC), dev // NC % NZ
    pieces = refs[3 + has_acc : 3 + has_acc + len(segments)]
    out, a_buf, l_buf, a_sem, l_sem = refs[3 + has_acc + len(segments) :]
    waits = []
    at, s = 0, 0
    for i, rows in enumerate(segments):
        total = sum(size for *_, size in rows)
        copy = pltpu.make_async_copy(pieces[i], l_buf.at[pl.ds(at, total)], l_sem.at[i])
        copy.start()
        mine = [copy]
        for ox, oz, same, low, n in rows:
            block = place(here_x + ox, here_z + oz, core if same else 1 - core)
            source = pl.ds(pl.multiple_of(block * B + low, HALF), n)
            for j, a in enumerate((own, sib)):
                copy = pltpu.make_async_copy(
                    a.at[:, source], a_buf.at[2 * j : 2 * j + 2, pl.ds(at, n)], a_sem.at[j, s]
                )
                copy.start()
                mine.append(copy)
            at, s = at + n, s + 1
        waits.append((mine, at))
    begin, done = 0, 0
    for chunk in chunks:
        for i in range(done, done + chunk):
            for copy in waits[i][0]:
                copy.wait()
        end = waits[done + chunk - 1][1]
        for q in range(4):
            part = transposed_dot(a_buf[q, begin:end], l_buf[begin:end])
            rows = slice(q * B, (q + 1) * B)
            if begin:
                out[rows] += part
            elif has_acc:
                out[rows] = acc[rows] + part
            else:
                out[rows] = part
        begin, done = end, done + chunk


def gemm(device, own, sib, acc, pieces, segments):
    depth = sum(size for rows in segments for *_, size in rows)
    count = sum(map(len, segments))
    has_acc = acc is not None
    return pl.pallas_call(
        functools.partial(gemm_body, segments, (2, 2), has_acc),
        in_specs=[SMEM, ANY, ANY] + [VMEM] * has_acc + [ANY] * len(pieces),
        out_specs=VMEM,
        out_shape=jax.ShapeDtypeStruct((4 * B, 2 * B), jnp.float32),
        scratch_shapes=[
            pltpu.VMEM((4, depth, B), jnp.bfloat16),
            pltpu.VMEM((depth, 2 * B), jnp.bfloat16),
            pltpu.SemaphoreType.DMA((2, count)),
            pltpu.SemaphoreType.DMA((len(pieces),)),
        ],
        compiler_params=params(32),
    )(device, own, sib, *([acc] if has_acc else []), *pieces)


def finish_body(sources, *refs):
    device, widths, owner, assign, weights, acc, dinv = refs[:7]
    pieces = refs[7 : 7 + len(sources)]
    sent, own, diag, sem = refs[7 + len(sources) :]
    dev = device[0]
    core = dev % NC
    here_x, here_z = dev // (NZ * NC), dev // NC % NZ
    full, one, two, split = layout(widths)

    waits = []
    for j in range(2):
        block = dev if j == 0 else dev + 1 - 2 * core
        want = owner[block]
        chip, same = want // NC, want % NC == core
        for h in range(2):
            target = own.at[pl.ds(j * B + h * HALF, HALF)]
            for piece, rows in zip(pieces, sources, strict=True):
                for at, is_same, part, (ox, oz) in rows:
                    if part != h:
                        continue
                    here = place(here_x + ox, here_z + oz, 0) // NC

                    @pl.when((here == chip) & (same == is_same))
                    def _(piece=piece, at=at, target=target, j=j, h=h):
                        pltpu.make_async_copy(
                            piece.at[pl.ds(at, HALF)], target, sem.at[j, h]
                        ).start()

            waits.append(
                pltpu.make_async_copy(pieces[0].at[pl.ds(0, HALF)], target, sem.at[j, h])
            )

    wr, wi = weights[assign[0], 0], weights[assign[0], 1]
    parts = []
    for j in range(2):
        top, low = acc[2 * j * B : (2 * j + 1) * B], acc[(2 * j + 1) * B : (2 * j + 2) * B]
        x_real = low[:, B:] - top[:, :B]
        x_imag = -(top[:, B:] + low[:, :B])
        density = (wr * x_imag + wi * x_real).astype(jnp.bfloat16)
        for p in range(POLES):
            rows = B // POLES
            sent[p, j * rows : (j + 1) * rows] = density[p * rows : (p + 1) * rows]
        parts.append((x_real.astype(jnp.bfloat16), x_imag.astype(jnp.bfloat16)))
    for copy in waits:
        copy.wait()
    real = imag = 0
    for j in range(2):
        l_real, l_imag = own[j * B : (j + 1) * B, :B], own[j * B : (j + 1) * B, B:]
        x_real, x_imag = parts[j]
        real += transposed_dot(l_real, x_real) - transposed_dot(l_imag, x_imag)
        imag += transposed_dot(l_real, x_imag) + transposed_dot(l_imag, x_real)
    both = wr * imag + wi * real

    cut = jnp.where(core == 0, B, split)
    at_row = lax.broadcasted_iota(jnp.int32, (B, B), 0)
    at_col = lax.broadcasted_iota(jnp.int32, (B, B), 1)
    before = jnp.where((at_row < cut) & (at_col < cut), both, 0)
    after = jnp.where((at_row >= cut) & (at_col >= cut), both, 0).astype(jnp.bfloat16)
    move = moved(cut)
    after = lax.dot_general(move, after, (((1,), (0,)), ((), ())), preferred_element_type=jnp.float32)
    after = lax.dot_general(
        after.astype(jnp.bfloat16), move, (((1,), (1,)), ((), ())), preferred_element_type=jnp.float32
    )
    diag[...] = jnp.zeros_like(diag)
    first = jnp.where(core == 0, full, one)
    second = jnp.where(core == 0, one, two)
    depth = dinv.shape[1]
    mine = pl.ds(pl.multiple_of(dev * depth, 8), depth)
    weighted = wr * dinv[1] + wi * dinv[0]
    for h in range(B // HALF):
        cols = slice(h * HALF, (h + 1) * HALF)
        diag[h, pl.ds(pl.multiple_of(first * B, B), B)] = -before[:, cols]
        diag[h, pl.ds(pl.multiple_of(second * B, B), B)] = -after[:, cols]
        diag[h, mine] += weighted[:, cols]
        for p in range(POLES):
            sent[p, 2 * B // POLES :, cols] = diag[
                h, pl.ds(p, diag.shape[1] // POLES, stride=POLES)
            ].astype(jnp.bfloat16)


def finish(device, widths, owner, assign, weights, acc, dinv, pieces, sources, total):
    return pl.pallas_call(
        functools.partial(finish_body, sources),
        in_specs=[SMEM] * 5 + [VMEM] * 2 + [ANY] * len(pieces),
        out_specs=VMEM,
        out_shape=jax.ShapeDtypeStruct((POLES, (2 * B + total) // POLES, B), jnp.bfloat16),
        scratch_shapes=[
            pltpu.VMEM((2 * B, 2 * B), jnp.bfloat16),
            pltpu.VMEM((B // HALF, total, HALF), jnp.float32),
            pltpu.SemaphoreType.DMA((2, 2)),
        ],
        compiler_params=params(32),
    )(device, widths, owner, assign, weights, acc, dinv, *pieces)


def spread_body(device, widths, got, panel, diag):
    core = device[0] % NC
    full, one, two, split = layout(widths)
    rows = B // POLES
    col = lax.broadcasted_iota(jnp.int32, (rows, B), 1)
    for p in range(POLES):
        out = slice(p * rows, (p + 1) * rows)
        mine, other = got[p, :rows], got[p, rows : 2 * rows]
        large = jnp.where(core == 0, mine, other)
        small = jnp.where(core == 0, other, mine)
        panel[out, pl.ds(pl.multiple_of(full * B, B), B)] = large
        panel[out, pl.ds(pl.multiple_of(one * B, B), B)] = jnp.where(col < split, small, 0)
        late = pltpu.roll(small, B - split, 1)
        panel[out, pl.ds(pl.multiple_of(two * B, B), B)] = jnp.where(col < B - split, late, 0)
        for t in range(diag.shape[0] // POLES):
            diag[t * POLES + p : t * POLES + p + 1] = got[p, 2 * rows + t : 2 * rows + t + 1]


def spread(device, widths, got, total, depth):
    return pl.pallas_call(
        spread_body,
        in_specs=[SMEM, SMEM, VMEM],
        out_specs=[VMEM, VMEM],
        out_shape=[
            jax.ShapeDtypeStruct((B, total), jnp.float32),
            jax.ShapeDtypeStruct((depth, B), jnp.float32),
        ],
        compiler_params=params(16),
    )(device, widths, got)


def local(inverse, factor, diag_inverse, widths, pattern, owner, assign, pole_weights):
    dev = lax.axis_index(GRID)
    device = dev[None].astype(jnp.int32)
    total = factor.shape[3]
    depth = diag_inverse.shape[2]
    own_inverse = inverse[0]
    top, rest, give = prepare(device, widths, pattern, factor[0])
    taken = shift(give, 0, 0, 1)
    sib_inverse = shift(own_inverse, 0, 0, 1)

    pieces, sources = [], []

    def multiply(acc, held, offsets, kind):
        parts = ((True, HALF, HALF),) if kind else ((True, 0, HALF), (False, 0, B))
        segments = []
        for piece, some in zip(held, offsets, strict=True):
            rows, listed, at = [], [], 0
            for ox, oz in some:
                for same, low, size in parts:
                    rows.append((ox, oz, same, low, size))
                    for k in range(0, size, HALF):
                        listed.append((at + k, same, (low + k) // HALF, (ox, oz)))
                    at += size
            pieces.append(piece)
            sources.append(tuple(listed))
            segments.append(tuple(rows))
        return gemm(device, own_inverse, sib_inverse, acc, held, tuple(segments))

    def after(values, *others):
        values, _ = lax.optimization_barrier((values, others))
        return values

    def along_x(oz):
        return [[(ox, oz)] for ox in (0, -1, 1, 2)]

    rest_f, rest_b = shift(rest, 1, 0), shift(rest, -1, 0)
    main = jnp.concatenate([top, taken], 0)
    zf, zb = shift(main, 0, 1), shift(main, 0, -1)
    rest_far = shift(rest_f, 1, 0)
    main_f, main_b = shift(main, 1, 0), shift(main, -1, 0)
    across = jnp.concatenate([rest, rest_f, rest_b, rest_far], 0)
    main_far = shift(main_b, -1, 0)
    z_far = shift(zf, 0, 1)
    zff, zbb = shift(zf, 1, 0), shift(zb, -1, 0)
    zfb, zbf = shift(zf, -1, 0), shift(zb, 1, 0)
    across = after(across, zf, zb)
    across_b = shift(across, 0, -1)
    acc = multiply(None, (main, main_f, main_b, main_far), along_x(0), 0)
    z_far, acc = after((z_far, acc), zff, zbb)
    far_f, far_b = shift(z_far, 1, 0), shift(z_far, -1, 0)
    zff, zbb, across, acc = after((zff, zbb, across, acc), z_far)
    zf_far, zb_far = shift(zff, 1, 0), shift(zbb, -1, 0)
    across_f = shift(across, 0, 1)
    across_b, acc = after((across_b, acc), zf_far)
    across_far = shift(across_b, 0, -1)
    acc = multiply(acc, (zf, zff, zfb, zf_far), along_x(-1), 0)
    far_f, acc = after((far_f, acc), zb_far)
    far_far = shift(far_f, 1, 0)
    acc = multiply(acc, (zb, zbf, zbb, zb_far), along_x(1), 0)
    across_far, acc = after((across_far, acc), across_f)
    acc = multiply(
        acc,
        (across, across_f, across_b, across_far),
        [[(ox, oz) for ox in (0, -1, 1, 2)] for oz in (0, -1, 1, 2)],
        1,
    )
    acc = multiply(acc, (z_far, far_f, far_b, far_far), along_x(2), 0)

    sent = finish(
        device, widths, owner, assign, pole_weights, acc,
        diag_inverse[0].astype(jnp.float32), pieces, tuple(sources), total,
    )

    got = lax.all_to_all(sent, "pole", 0, 0, tiled=True).astype(jnp.float32).sum(0)
    rows = B // POLES
    other = shift(got[rows : 2 * rows], 0, 0, 1)
    share = depth // POLES
    diag = got[2 * rows :].reshape(NX * NZ * NC, share * B)
    diag = lax.all_to_all(diag, GRID, 0, 0, tiled=True).sum(0).reshape(share, B)
    diag = jnp.pad(diag, ((0, 8 - share), (0, 0)))
    both = jnp.concatenate([got[:rows], other, diag], 0)
    both = lax.all_to_all(
        jnp.broadcast_to(both[None], (POLES,) + both.shape), "pole", 0, 0, tiled=True
    )
    return tuple(spread(device, widths, both, total, depth))


def solution(mesh):
    placed = (
        P("pole", None, None, GRID),
        P("pole", None, GRID, None),
        P("pole", None, GRID, None),
        P(),
        P(),
        P(),
        P("pole"),
        P(),
    )
    return jax.shard_map(
        local,
        mesh=mesh,
        in_specs=placed,
        out_specs=(P(GRID, None), P(GRID, None)),
        check_vma=False,
    )
```

time: 437 us -> 162 us (0.37)
  waiting for transfers between devices: 339 us -> 32.7 us
  starting transfers between devices: 0.12 us -> 55.2 us
  matrix products: 35.9 us -> 0 us
  Pallas kernels: 0 us -> 25.7 us
  between operations: 15.2 us -> 1.76 us
  local copies, waits for them, and re-layouts: 5.93 us -> 13.7 us
  other arithmetic: 6.54 us -> 0.95 us
    all_gather x1 -> x0, waiting for transfers between devices: 172 us -> none  [local(): lax.all_gather(masked, ('row', 'col'), axis=1, tiled=True)]
    reduce_scatter x1 -> x0, waiting for transfers between devices: 90.9 us -> none  [local(): lax.psum_scatter(jnp.stack([part_real, part_imag]), ('row', 'col'), scatt...]
    psum x1 -> x0, waiting for transfers between devices: 76.1 us -> none  [local(): panel_total, diag_total = lax.psum((panel_local, diag_local), 'pole')]
    ppermute x0 -> x24, starting transfers between devices: none -> 43.2 us  [shift(): return lax.ppermute(value, GRID, perm)]
    dot_general x10 -> x0, matrix products: 35.9 us -> none  [the longest x4 33.7 us: inner_dot(): lax.dot_general(left, right, (((0,), (0,)), ((), ())), preferred_element_...]
    psum x1 -> x0, blocking collectives: 33.9 us -> none  [local(): panel_total, diag_total = lax.psum((panel_local, diag_local), 'pole')]
    all_to_all x0 -> x2, blocking collectives: none -> 30.3 us  [the longest x1 16.1 us: local(): lax.all_to_all(sent, 'pole', 0, 0, tiled=True).astype(jnp.float32).sum(0)]
    pallas_call x0 -> x8, Pallas kernels: none -> 25.7 us  [the longest x5 19.8 us: gemm(): pl.pallas_call(functools.partial(gemm_body, segments, (2, 2), has_acc), i...]
  transfers between devices with their start and end apart: 3 -> 25, of which waited for: 3 -> 8; matrix products, arithmetic and copies ran while one was open for 2% -> 2% of each run, Pallas kernels for 0% -> 11%
where the time goes in v2:
time: 162 us; the launch traced here: 160 us
  starting transfers between devices  55.2 us (34%)
  waiting for transfers between devices  32.7 us (20%)
  blocking collectives  30.3 us (19%)
  Pallas kernels  25.7 us (16%)
  local copies, waits for them, and re-layouts  13.7 us (8%)
  between operations  1.76 us (1%)
    ppermute x24, starting transfers between devices, shift(): return lax.ppermute(value, GRID, perm)  43.2 us
    ppermute x24, waiting for transfers between devices, shift(): return lax.ppermute(value, GRID, perm)  24 us
    pallas_call x5, Pallas kernels, gemm(): pl.pallas_call(functools.partial(gemm_body, segments, (2, 2), has_acc), i...  19.8 us
    all_to_all x1, blocking collectives, local(): lax.all_to_all(sent, 'pole', 0, 0, tiled=True).astype(jnp.float32).sum(0)  16.1 us
    all_to_all x1, blocking collectives, local(): lax.all_to_all(jnp.broadcast_to(both[None], (POLES,) + both.shape), 'pole...  14.2 us
    unnamed x55, local copies, waits for them, and re-layouts  12.9 us
    all_to_all x1, starting transfers between devices, local(): diag = lax.all_to_all(diag, GRID, 0, 0, tiled=True).sum(0).reshape(share, B)  12 us
    all_to_all x1, waiting for transfers between devices, local(): diag = lax.all_to_all(diag, GRID, 0, 0, tiled=True).sum(0).reshape(share, B)  8.72 us
  transfers between devices with their start and end apart: 25, of which 8 were waited for; matrix products, arithmetic and copies ran while one was open for 2% of the time, Pallas kernels for 11%

profile of v2, /device:TPU:2, one launch (start us, length us, event | category | flops | bytes accessed | tf_op | source)
XLA Modules:
  0.0 160.3 jit_solution(1035184961210562151)
XLA Ops:
  0.7 0.8 copy.12.pattern
  1.5 1.1 copy-done.22
  3.3 1.1 shard_map.95
  5.0 1.5 collective-permute-start.1
  6.5 0.8 collective-permute-start.2
  7.3 3.7 %collective-permute-done.1 = bf16[128,512]{1,0:T(8,128)(2,1)S(1)} collective-permute-done((bf16[128,512]{1,0:T(8,128)(2,1)S(1)}, bf16[128,512]{1,0:T(8,128)(2,1)S(1)}, u32[]{:S(2)}, u32[]{:S(2)}) %collective-permute-start.1) | collective-permute-done | bytes 131104 | tf_op jit(solution)/shard_map/ppermute | solution.py:32
  11.0 1.0 collective-permute-start.3
  12.0 2.3 %collective-permute-done.4 = bf16[256,512]{1,0:T(8,128)(2,1)S(1)} collective-permute-done((bf16[256,512]{1,0:T(8,128)(2,1)S(1)}, bf16[256,512]{1,0:T(8,128)(2,1)S(1)}, u32[]{:S(2)}, u32[]{:S(2)}) %collective-permute-start.4) | collective-permute-done | bytes 262176 | tf_op jit(solution)/shard_map/ppermute | solution.py:32
  14.3 2.3 %collective-permute-start.12 = (bf16[384,512]{1,0:T(8,128)(2,1)S(1)}, bf16[384,512]{1,0:T(8,128)(2,1)S(1)}, u32[]{:S(2)}, u32[]{:S(2)}) collective-permute-start(bf16[384,512]{1,0:T(8,128)(2,1)S(1)} %constant_dynamic-update-slice_fusion.refs_3_.refs_7_), channel_id=1, source_target_pairs={{0,24},{1,25},{2,26},{3,27},{4,28},{5,29},{6,30},{7,31},{8,0},{9,1... | collective-permute-start | bytes 1179656 | tf_op jit(solution)/shard_map/ppermute | solution.py:32
  16.6 1.5 collective-permute-start.5
  18.2 1.5 collective-permute-start.11
  19.7 3.0 %collective-permute-start.6 = (bf16[384,512]{1,0:T(8,128)(2,1)S(1)}, bf16[384,512]{1,0:T(8,128)(2,1)}, u32[]{:S(2)}, u32[]{:S(2)}) collective-permute-start(bf16[384,512]{1,0:T(8,128)(2,1)S(1)} %constant_dynamic-update-slice_fusion.refs_3_.refs_7_), channel_id=1, source_target_pairs={{0,6},{1,7},{2,0},{3,1},{4,2},{5,3},{6,4},{7,5},{8,14},{9,15},{10,... | collective-permute-start | bytes 1179656 | tf_op jit(solution)/shard_map/ppermute | solution.py:32
  22.7 2.8 %collective-permute-done.12.refs_5_.refs_9_ = bf16[384,512]{1,0:T(8,128)(2,1)S(1)} collective-permute-done((bf16[384,512]{1,0:T(8,128)(2,1)S(1)}, bf16[384,512]{1,0:T(8,128)(2,1)S(1)}, u32[]{:S(2)}, u32[]{:S(2)}) %collective-permute-start.12) | collective-permute-done | bytes 393248 | tf_op jit(solution)/shard_map/ppermute | solution.py:32
  25.5 2.3 %collective-permute-start.13 = (bf16[384,512]{1,0:T(8,128)(2,1)S(1)}, bf16[384,512]{1,0:T(8,128)(2,1)S(1)}, u32[]{:S(2)}, u32[]{:S(2)}) collective-permute-start(bf16[384,512]{1,0:T(8,128)(2,1)S(1)} %collective-permute-done.12.refs_5_.refs_9_), channel_id=1, source_target_pairs={{0,24},{1,25},{2,26},{3,27},{4,28},{5,29},{6,30},{7,31},{8,0},{9,1... | collective-permute-start | bytes 1179656 | tf_op jit(solution)/shard_map/ppermute | solution.py:32
  27.8 5.5 %collective-permute-done.5.refs_4_.refs_11_ = bf16[384,512]{1,0:T(8,128)(2,1)S(1)} collective-permute-done((bf16[384,512]{1,0:T(8,128)(2,1)S(1)}, bf16[384,512]{1,0:T(8,128)(2,1)S(1)}, u32[]{:S(2)}, u32[]{:S(2)}) %collective-permute-start.5) | collective-permute-done | bytes 393248 | tf_op jit(solution)/shard_map/ppermute | solution.py:32
  33.3 1.5 collective-permute-start.8
  34.8 6.0 %collective-permute-start.10 = (bf16[384,512]{1,0:T(8,128)(2,1)S(1)}, bf16[384,512]{1,0:T(8,128)(2,1)}, u32[]{:S(2)}, u32[]{:S(2)}) collective-permute-start(bf16[384,512]{1,0:T(8,128)(2,1)S(1)} %collective-permute-done.5.refs_4_.refs_11_), channel_id=1, source_target_pairs={{0,2},{1,3},{2,4},{3,5},{4,6},{5,7},{6,0},{7,1},{8,10},{9,11},{10,... | collective-permute-start | bytes 1179656 | tf_op jit(solution)/shard_map/ppermute | solution.py:32
  41.2 1.6 %collective-permute-start.9 = (bf16[384,512]{1,0:T(8,128)(2,1)}, bf16[384,512]{1,0:T(8,128)(2,1)S(1)}, u32[]{:S(2)}, u32[]{:S(2)}) collective-permute-start(bf16[384,512]{1,0:T(8,128)(2,1)} %collective-permute-done.6.refs_4_.refs_15_), channel_id=1, source_target_pairs={{0,24},{1,25},{2,26},{3,27},{4,28},{5,29},{6,30},{7,31},{8,0},{9,1... | collective-permute-start | bytes 1179656 | tf_op jit(solution)/shard_map/ppermute | solution.py:32
  42.9 2.9 %collective-permute-start.7 = (bf16[512,512]{1,0:T(8,128)(2,1)S(1)}, bf16[512,512]{1,0:T(8,128)(2,1)S(1)}, u32[]{:S(2)}, u32[]{:S(2)}) collective-permute-start(bf16[512,512]{1,0:T(8,128)(2,1)S(1)} %pad_maximum_fusion.refs_4_.refs_19_), channel_id=1, source_target_pairs={{0,6},{1,7},{2,0},{3,1},{4,2},{5,3},{6,4},{7,5},{8,14},{9,15},{10,... | collective-permute-start | bytes 1572872 | tf_op jit(solution)/shard_map/ppermute | solution.py:32
  45.9 3.4 %copy-done = bf16[1,2,8192,256]{3,2,1,0:T(8,128)(2,1)S(1)} copy-done((bf16[1,2,8192,256]{3,2,1,0:T(8,128)(2,1)S(1)}, bf16[1,2,8192,256]{3,2,1,0:T(8,128)(2,1)}, u32[]{:S(2)}) %copy-start) | copy-done | bytes 8388632
  49.3 3.7 %shard_map.96.refs_3_ = f32[1024,512]{1,0:T(8,128)S(1)} custom-call(s32[1]{0:T(128)} %bitcast.device.refs_0_, bf16[2,8192,256]{2,1,0:T(8,128)(2,1)S(1)} %bitcast.7, bf16[2,8192,256]{2,1,0:T(8,128)(2,1)} %collective-permute-done.refs_2_, bf16[384,512]{1,0:T(8,128)(2,1)S(1)} %constant_dynamic-update-slice_fusion.refs_3_.refs_7_, ...), custom_call_target="tpu_custom_call" | custom-call | tf_op jit(solution)/shard_map/pallas_call | solution.py:154
  53.0 4.2 %collective-permute-done.10.refs_4_.refs_23_ = bf16[384,512]{1,0:T(8,128)(2,1)} collective-permute-done((bf16[384,512]{1,0:T(8,128)(2,1)S(1)}, bf16[384,512]{1,0:T(8,128)(2,1)}, u32[]{:S(2)}, u32[]{:S(2)}) %collective-permute-start.10) | collective-permute-done | bytes 393248 | tf_op jit(solution)/shard_map/ppermute | solution.py:32
  57.2 1.5 collective-permute-start.14
  58.7 1.2 collective-permute-start.17
  60.0 3.2 %collective-permute-start.18 = (bf16[384,512]{1,0:T(8,128)(2,1)S(1)}, bf16[384,512]{1,0:T(8,128)(2,1)S(1)}, u32[]{:S(2)}, u32[]{:S(2)}) collective-permute-start(bf16[384,512]{1,0:T(8,128)(2,1)S(1)} %collective-permute-done.9.refs_6_.refs_17_), channel_id=1, source_target_pairs={{0,24},{1,25},{2,26},{3,27},{4,28},{5,29},{6,30},{7,31},{8,0},{9,1... | collective-permute-start | bytes 1179656 | tf_op jit(solution)/shard_map/ppermute | solution.py:32
  63.1 5.0 %collective-permute-done.7.refs_6_.refs_21_ = bf16[512,512]{1,0:T(8,128)(2,1)S(1)} collective-permute-done((bf16[512,512]{1,0:T(8,128)(2,1)S(1)}, bf16[512,512]{1,0:T(8,128)(2,1)S(1)}, u32[]{:S(2)}, u32[]{:S(2)}) %collective-permute-start.7) | collective-permute-done | bytes 524320 | tf_op jit(solution)/shard_map/ppermute | solution.py:32
  68.1 3.9 %collective-permute-start.20 = (bf16[512,512]{1,0:T(8,128)(2,1)S(1)}, bf16[512,512]{1,0:T(8,128)(2,1)}, u32[]{:S(2)}, u32[]{:S(2)}) collective-permute-start(bf16[512,512]{1,0:T(8,128)(2,1)S(1)} %pad_maximum_fusion.refs_4_.refs_19_), channel_id=1, source_target_pairs={{0,2},{1,3},{2,4},{3,5},{4,6},{5,7},{6,0},{7,1},{8,10},{9,11},{10,... | collective-permute-start | bytes 1572872 | tf_op jit(solution)/shard_map/ppermute | solution.py:32
  72.1 2.5 %collective-permute-start.15 = (bf16[512,512]{1,0:T(8,128)(2,1)S(1)}, bf16[512,512]{1,0:T(8,128)(2,1)}, u32[]{:S(2)}, u32[]{:S(2)}) collective-permute-start(bf16[512,512]{1,0:T(8,128)(2,1)S(1)} %collective-permute-done.7.refs_6_.refs_21_), channel_id=1, source_target_pairs={{0,6},{1,7},{2,0},{3,1},{4,2},{5,3},{6,4},{7,5},{8,14},{9,15},{10,... | collective-permute-start | bytes 1572872 | tf_op jit(solution)/shard_map/ppermute | solution.py:32
  74.6 1.5 collective-permute-start.19
  76.1 3.9 %shard_map.97.refs_3_ = f32[1024,512]{1,0:T(8,128)S(1)} custom-call(s32[1]{0:T(128)} %bitcast.device.refs_0_, bf16[2,8192,256]{2,1,0:T(8,128)(2,1)S(1)} %bitcast.8, bf16[2,8192,256]{2,1,0:T(8,128)(2,1)} %collective-permute-done.refs_2_, f32[1024,512]{1,0:T(8,128)S(1)} %shard_map.96.refs_3_, bf16[384,512]{1,0:T(8,128)(2,1)S(1)} %collective-permute-done.5.refs_4_.refs_11_, ...), custom_call_target="tpu_custom_call" | custom-call | tf_op jit(solution)/shard_map/pallas_call | solution.py:154
  80.0 0.8 copy-done.19
  80.8 1.4 collective-permute-start.21
  82.2 1.0 collective-permute-start.22
  83.2 0.8 copy.13.refs_4_
  84.6 0.7 bitcast_convert_fusion.refs_6_
  85.4 3.4 %copy-done.1 = bf16[1,2,8192,256]{3,2,1,0:T(8,128)(2,1)S(1)} copy-done((bf16[1,2,8192,256]{3,2,1,0:T(8,128)(2,1)S(1)}, bf16[1,2,8192,256]{3,2,1,0:T(8,128)(2,1)}, u32[]{:S(2)}) %copy-start.1) | copy-done | bytes 8388632
  88.8 1.0 copy-done.13
  89.8 1.0 copy-done.20
  90.8 3.6 %shard_map.98.refs_3_ = f32[1024,512]{1,0:T(8,128)S(1)} custom-call(s32[1]{0:T(128)} %bitcast.device.refs_0_, bf16[2,8192,256]{2,1,0:T(8,128)(2,1)S(1)} %bitcast.9, bf16[2,8192,256]{2,1,0:T(8,128)(2,1)} %collective-permute-done.refs_2_, f32[1024,512]{1,0:T(8,128)S(1)} %shard_map.97.refs_3_, bf16[384,512]{1,0:T(8,128)(2,1)} %collective-permute-done.6.refs_4_.refs_15_, ...), custom_call_target="tpu_custom_call" | custom-call | tf_op jit(solution)/shard_map/pallas_call | solution.py:154
  94.4 4.7 %shard_map.99.refs_3_ = f32[1024,512]{1,0:T(8,128)S(1)} custom-call(s32[1]{0:T(128)} %bitcast.device.refs_0_, bf16[2,8192,256]{2,1,0:T(8,128)(2,1)S(1)} %bitcast.10, bf16[2,8192,256]{2,1,0:T(8,128)(2,1)} %collective-permute-done.refs_2_, f32[1024,512]{1,0:T(8,128)S(1)} %shard_map.98.refs_3_, bf16[512,512]{1,0:T(8,128)(2,1)S(1)} %pad_maximum_fusion.refs_4_.refs_19_, ...), custom_call_target="tpu_custom_call" | custom-call | tf_op jit(solution)/shard_map/pallas_call | solution.py:154
  99.3 3.8 %shard_map.100.refs_5_ = f32[1024,512]{1,0:T(8,128)S(1)} custom-call(s32[1]{0:T(128)} %bitcast.device.refs_0_, bf16[2,8192,256]{2,1,0:T(8,128)(2,1)S(1)} %bitcast.11, bf16[2,8192,256]{2,1,0:T(8,128)(2,1)} %collective-permute-done.refs_2_, f32[1024,512]{1,0:T(8,128)S(1)} %shard_map.99.refs_3_, bf16[384,512]{1,0:T(8,128)(2,1)} %collective-permute-done.10.refs_4_.refs_23_, ...), custom_call_target="tpu_custom_call" | custom-call | tf_op jit(solution)/shard_map/pallas_call | solution.py:154
  103.3 3.2 %shard_map.101 = bf16[8,160,256]{2,1,0:T(8,128)(2,1)S(1)} custom-call(s32[1]{0:T(128)} %bitcast.device.refs_0_, s32[3]{0:T(128)S(1)} %copy-done.24, s32[32]{0:T(128)S(1)} %copy-done.25, s32[1]{0:T(128)S(6)} %copy.15.refs_3_, f32[20,2]{1,0:T(8,128)S(1)} %copy.13.refs_4_, f32[1024,512]{1,0:T(8,128)S(1)} %shard_map.100.refs_5_, ...), custom_call_target="tpu_custom_call" | custom-call | tf_op jit(solution)/shard_map/pallas_call | solution.py:250
  106.5 16.1 %all_to_all.19 = bf16[8,160,256]{2,1,0:T(8,128)(2,1)S(1)} all-to-all(bf16[8,160,256]{2,1,0:T(8,128)(2,1)S(1)} %shard_map.101), channel_id=1, replica_groups=mesh['pole'=8,'row'=4,'col'=8] {'pole'}, dimensions={0} | all-to-all | bytes 1310720 | tf_op jit(solution)/shard_map/all_to_all | solution.py:368
  122.7 0.7 all_to_all.13
  123.4 12.0 %all-to-all-start.1 = ((f32[32,1,768]{2,1,0:T(1,128)}), f32[32,1,768]{2,1,0:T(1,128)S(1)}, u32[]{:S(2)}, u32[]{:S(2)}) async-start(f32[32,1,768]{2,1,0:T(1,128)} %all_to_all.13), calls=%async_computation.1 | async-start | bytes 196608 | tf_op jit(solution)/shard_map/all_to_all | solution.py:373
  135.7 8.7 %all-to-all-done.1 = f32[32,1,768]{2,1,0:T(1,128)S(1)} async-done(((f32[32,1,768]{2,1,0:T(1,128)}), f32[32,1,768]{2,1,0:T(1,128)S(1)}, u32[]{:S(2)}, u32[]{:S(2)}) %all-to-all-start.1) | async-done | bytes 98336 | tf_op jit(solution)/shard_map/all_to_all | solution.py:373
  144.6 14.2 %all_to_all.20.got = f32[8,72,256]{2,1,0:T(8,128)S(1)} all-to-all(f32[8,72,256]{2,1,0:T(8,128)S(1)} %broadcast_in_dim.10), channel_id=1, replica_groups=mesh['pole'=8,'row'=4,'col'=8] {'pole'}, dimensions={0} | all-to-all | bytes 1179648 | tf_op jit(solution)/shard_map/all_to_all | solution.py:376
  158.8 1.6 shard_map.102
  (78 shorter events, 2.4 us)
Async XLA Ops:
  0.6 45.3 %collective-permute-start = (bf16[2,8192,256]{2,1,0:T(8,128)(2,1)}, bf16[2,8192,256]{2,1,0:T(8,128)(2,1)}, u32[]{:S(2)}, u32[]{:S(2)}) collective-permute-start(bf16[2,8192,256]{2,1,0:T(8,128)(2,1)} %bitcast.6), channel_id=1, source_target_pairs={{0,1},{1,0},{2,3},{3,2},{4,5},{5,4},{6,7},{7,6},{8,9},{9,8},{10,11... | collective-permute-start | bytes 25165832 | tf_op jit(solution)/shard_map/ppermute | solution.py:32
  1.5 1.1 copy-start.22
  4.4 9.8 %collective-permute-start.4 = (bf16[256,512]{1,0:T(8,128)(2,1)S(1)}, bf16[256,512]{1,0:T(8,128)(2,1)S(1)}, u32[]{:S(2)}, u32[]{:S(2)}) collective-permute-start(bf16[256,512]{1,0:T(8,128)(2,1)S(1)} %get-tuple-element.20), channel_id=1, source_target_pairs={{0,1},{1,0},{2,3},{3,2},{4,5},{5,4},{6,7},{7,6},{8,9},{9,8},{10,11... | collective-permute-start | bytes 786440 | tf_op jit(solution)/shard_map/ppermute | solution.py:32
  5.0 6.0 %collective-permute-start.1 = (bf16[128,512]{1,0:T(8,128)(2,1)S(1)}, bf16[128,512]{1,0:T(8,128)(2,1)S(1)}, u32[]{:S(2)}, u32[]{:S(2)}) collective-permute-start(bf16[128,512]{1,0:T(8,128)(2,1)S(1)} %get-tuple-element.18), channel_id=1, source_target_pairs={{0,8},{1,9},{2,10},{3,11},{4,12},{5,13},{6,14},{7,15},{8,16},{9,17... | collective-permute-start | bytes 393224 | tf_op jit(solution)/shard_map/ppermute | solution.py:32
  6.5 11.7 %collective-permute-start.2 = (bf16[128,512]{1,0:T(8,128)(2,1)S(1)}, bf16[128,512]{1,0:T(8,128)(2,1)S(1)}, u32[]{:S(2)}, u32[]{:S(2)}) collective-permute-start(bf16[128,512]{1,0:T(8,128)(2,1)S(1)} %get-tuple-element.18), channel_id=1, source_target_pairs={{0,24},{1,25},{2,26},{3,27},{4,28},{5,29},{6,30},{7,31},{8,0},{9,1... | collective-permute-start | bytes 393224 | tf_op jit(solution)/shard_map/ppermute | solution.py:32
  11.0 8.6 %collective-permute-start.3 = (bf16[128,512]{1,0:T(8,128)(2,1)S(1)}, bf16[128,512]{1,0:T(8,128)(2,1)S(1)}, u32[]{:S(2)}, u32[]{:S(2)}) collective-permute-start(bf16[128,512]{1,0:T(8,128)(2,1)S(1)} %collective-permute-done.1), channel_id=1, source_target_pairs={{0,8},{1,9},{2,10},{3,11},{4,12},{5,13},{6,14},{7,15},{8,16},{9,17... | collective-permute-start | bytes 393224 | tf_op jit(solution)/shard_map/ppermute | solution.py:32
  14.3 11.2 %collective-permute-start.12 = (bf16[384,512]{1,0:T(8,128)(2,1)S(1)}, bf16[384,512]{1,0:T(8,128)(2,1)S(1)}, u32[]{:S(2)}, u32[]{:S(2)}) collective-permute-start(bf16[384,512]{1,0:T(8,128)(2,1)S(1)} %constant_dynamic-update-slice_fusion.refs_3_.refs_7_), channel_id=1, source_target_pairs={{0,24},{1,25},{2,26},{3,27},{4,28},{5,29},{6,30},{7,31},{8,0},{9,1... | collective-permute-start | bytes 1179656 | tf_op jit(solution)/shard_map/ppermute | solution.py:32
  16.6 16.7 %collective-permute-start.5 = (bf16[384,512]{1,0:T(8,128)(2,1)S(1)}, bf16[384,512]{1,0:T(8,128)(2,1)S(1)}, u32[]{:S(2)}, u32[]{:S(2)}) collective-permute-start(bf16[384,512]{1,0:T(8,128)(2,1)S(1)} %constant_dynamic-update-slice_fusion.refs_3_.refs_7_), channel_id=1, source_target_pairs={{0,2},{1,3},{2,4},{3,5},{4,6},{5,7},{6,0},{7,1},{8,10},{9,11},{10,... | collective-permute-start | bytes 1179656 | tf_op jit(solution)/shard_map/ppermute | solution.py:32
  18.2 16.7 %collective-permute-start.11 = (bf16[384,512]{1,0:T(8,128)(2,1)S(1)}, bf16[384,512]{1,0:T(8,128)(2,1)S(1)}, u32[]{:S(2)}, u32[]{:S(2)}) collective-permute-start(bf16[384,512]{1,0:T(8,128)(2,1)S(1)} %constant_dynamic-update-slice_fusion.refs_3_.refs_7_), channel_id=1, source_target_pairs={{0,8},{1,9},{2,10},{3,11},{4,12},{5,13},{6,14},{7,15},{8,16},{9,17... | collective-permute-start | bytes 1179656 | tf_op jit(solution)/shard_map/ppermute | solution.py:32
  19.7 21.6 %collective-permute-start.6 = (bf16[384,512]{1,0:T(8,128)(2,1)S(1)}, bf16[384,512]{1,0:T(8,128)(2,1)}, u32[]{:S(2)}, u32[]{:S(2)}) collective-permute-start(bf16[384,512]{1,0:T(8,128)(2,1)S(1)} %constant_dynamic-update-slice_fusion.refs_3_.refs_7_), channel_id=1, source_target_pairs={{0,6},{1,7},{2,0},{3,1},{4,2},{5,3},{6,4},{7,5},{8,14},{9,15},{10,... | collective-permute-start | bytes 1179656 | tf_op jit(solution)/shard_map/ppermute | solution.py:32
  25.5 27.5 %copy-start.2 = (bf16[384,512]{1,0:T(8,128)(2,1)}, bf16[384,512]{1,0:T(8,128)(2,1)S(1)}, u32[]{:S(2)}) copy-start(bf16[384,512]{1,0:T(8,128)(2,1)S(1)} %collective-permute-done.12.refs_5_.refs_9_) | copy-start | bytes 1179652
  25.5 17.4 %collective-permute-start.13 = (bf16[384,512]{1,0:T(8,128)(2,1)S(1)}, bf16[384,512]{1,0:T(8,128)(2,1)S(1)}, u32[]{:S(2)}, u32[]{:S(2)}) collective-permute-start(bf16[384,512]{1,0:T(8,128)(2,1)S(1)} %collective-permute-done.12.refs_5_.refs_9_), channel_id=1, source_target_pairs={{0,24},{1,25},{2,26},{3,27},{4,28},{5,29},{6,30},{7,31},{8,0},{9,1... | collective-permute-start | bytes 1179656 | tf_op jit(solution)/shard_map/ppermute | solution.py:32
  33.3 42.8 %copy-start.4 = (bf16[384,512]{1,0:T(8,128)(2,1)}, bf16[384,512]{1,0:T(8,128)(2,1)S(1)}, u32[]{:S(2)}) copy-start(bf16[384,512]{1,0:T(8,128)(2,1)S(1)} %collective-permute-done.5.refs_4_.refs_11_) | copy-start | bytes 1179652
  33.3 19.7 %collective-permute-start.8 = (bf16[384,512]{1,0:T(8,128)(2,1)S(1)}, bf16[384,512]{1,0:T(8,128)(2,1)S(1)}, u32[]{:S(2)}, u32[]{:S(2)}) collective-permute-start(bf16[384,512]{1,0:T(8,128)(2,1)S(1)} %collective-permute-done.5.refs_4_.refs_11_), channel_id=1, source_target_pairs={{0,8},{1,9},{2,10},{3,11},{4,12},{5,13},{6,14},{7,15},{8,16},{9,17... | collective-permute-start | bytes 1179656 | tf_op jit(solution)/shard_map/ppermute | solution.py:32
  34.8 18.2 %copy-start.6 = (bf16[384,512]{1,0:T(8,128)(2,1)}, bf16[384,512]{1,0:T(8,128)(2,1)S(1)}, u32[]{:S(2)}) copy-start(bf16[384,512]{1,0:T(8,128)(2,1)S(1)} %collective-permute-done.11.refs_4_.refs_8_) | copy-start | bytes 1179652
  34.8 22.4 %collective-permute-start.10 = (bf16[384,512]{1,0:T(8,128)(2,1)S(1)}, bf16[384,512]{1,0:T(8,128)(2,1)}, u32[]{:S(2)}, u32[]{:S(2)}) collective-permute-start(bf16[384,512]{1,0:T(8,128)(2,1)S(1)} %collective-permute-done.5.refs_4_.refs_11_), channel_id=1, source_target_pairs={{0,2},{1,3},{2,4},{3,5},{4,6},{5,7},{6,0},{7,1},{8,10},{9,11},{10,... | collective-permute-start | bytes 1179656 | tf_op jit(solution)/shard_map/ppermute | solution.py:32
  41.2 16.0 %collective-permute-start.9 = (bf16[384,512]{1,0:T(8,128)(2,1)}, bf16[384,512]{1,0:T(8,128)(2,1)S(1)}, u32[]{:S(2)}, u32[]{:S(2)}) collective-permute-start(bf16[384,512]{1,0:T(8,128)(2,1)} %collective-permute-done.6.refs_4_.refs_15_), channel_id=1, source_target_pairs={{0,24},{1,25},{2,26},{3,27},{4,28},{5,29},{6,30},{7,31},{8,0},{9,1... | collective-permute-start | bytes 1179656 | tf_op jit(solution)/shard_map/ppermute | solution.py:32
  42.9 10.1 %copy-start.8 = (bf16[384,512]{1,0:T(8,128)(2,1)}, bf16[384,512]{1,0:T(8,128)(2,1)S(1)}, u32[]{:S(2)}) copy-start(bf16[384,512]{1,0:T(8,128)(2,1)S(1)} %collective-permute-done.13.refs_6_.refs_10_) | copy-start | bytes 1179652
  42.9 25.2 %collective-permute-start.7 = (bf16[512,512]{1,0:T(8,128)(2,1)S(1)}, bf16[512,512]{1,0:T(8,128)(2,1)S(1)}, u32[]{:S(2)}, u32[]{:S(2)}) collective-permute-start(bf16[512,512]{1,0:T(8,128)(2,1)S(1)} %pad_maximum_fusion.refs_4_.refs_19_), channel_id=1, source_target_pairs={{0,6},{1,7},{2,0},{3,1},{4,2},{5,3},{6,4},{7,5},{8,14},{9,15},{10,... | collective-permute-start | bytes 1572872 | tf_op jit(solution)/shard_map/ppermute | solution.py:32
  45.9 3.4 %copy-start = (bf16[1,2,8192,256]{3,2,1,0:T(8,128)(2,1)S(1)}, bf16[1,2,8192,256]{3,2,1,0:T(8,128)(2,1)}, u32[]{:S(2)}) copy-start(bf16[1,2,8192,256]{3,2,1,0:T(8,128)(2,1)} %param.8) | copy-start | bytes 25165828
  53.0 26.9 %copy-start.10 = (bf16[384,512]{1,0:T(8,128)(2,1)}, bf16[384,512]{1,0:T(8,128)(2,1)S(1)}, u32[]{:S(2)}) copy-start(bf16[384,512]{1,0:T(8,128)(2,1)S(1)} %collective-permute-done.8.refs_5_.refs_12_) | copy-start | bytes 1179652
  57.2 22.8 %copy-start.12 = (bf16[384,512]{1,0:T(8,128)(2,1)}, bf16[384,512]{1,0:T(8,128)(2,1)S(1)}, u32[]{:S(2)}) copy-start(bf16[384,512]{1,0:T(8,128)(2,1)S(1)} %collective-permute-done.9.refs_6_.refs_17_) | copy-start | bytes 1179652
  57.2 14.9 %collective-permute-start.14 = (bf16[384,512]{1,0:T(8,128)(2,1)S(1)}, bf16[384,512]{1,0:T(8,128)(2,1)S(1)}, u32[]{:S(2)}, u32[]{:S(2)}) collective-permute-start(bf16[384,512]{1,0:T(8,128)(2,1)S(1)} %collective-permute-done.8.refs_5_.refs_12_), channel_id=1, source_target_pairs={{0,8},{1,9},{2,10},{3,11},{4,12},{5,13},{6,14},{7,15},{8,16},{9,17... | collective-permute-start | bytes 1179656 | tf_op jit(solution)/shard_map/ppermute | solution.py:32
  58.7 15.9 %collective-permute-start.17 = (bf16[384,512]{1,0:T(8,128)(2,1)S(1)}, bf16[384,512]{1,0:T(8,128)(2,1)S(1)}, u32[]{:S(2)}, u32[]{:S(2)}) collective-permute-start(bf16[384,512]{1,0:T(8,128)(2,1)S(1)} %collective-permute-done.5.refs_4_.refs_11_), channel_id=1, source_target_pairs={{0,24},{1,25},{2,26},{3,27},{4,28},{5,29},{6,30},{7,31},{8,0},{9,1... | collective-permute-start | bytes 1179656 | tf_op jit(solution)/shard_map/ppermute | solution.py:32
  60.0 20.1 %collective-permute-start.18 = (bf16[384,512]{1,0:T(8,128)(2,1)S(1)}, bf16[384,512]{1,0:T(8,128)(2,1)S(1)}, u32[]{:S(2)}, u32[]{:S(2)}) collective-permute-start(bf16[384,512]{1,0:T(8,128)(2,1)S(1)} %collective-permute-done.9.refs_6_.refs_17_), channel_id=1, source_target_pairs={{0,24},{1,25},{2,26},{3,27},{4,28},{5,29},{6,30},{7,31},{8,0},{9,1... | collective-permute-start | bytes 1179656 | tf_op jit(solution)/shard_map/ppermute | solution.py:32
  63.1 19.1 %collective-permute-start.16 = (bf16[384,512]{1,0:T(8,128)(2,1)}, bf16[384,512]{1,0:T(8,128)(2,1)}, u32[]{:S(2)}, u32[]{:S(2)}) collective-permute-start(bf16[384,512]{1,0:T(8,128)(2,1)} %collective-permute-done.10.refs_4_.refs_23_), channel_id=1, source_target_pairs={{0,8},{1,9},{2,10},{3,11},{4,12},{5,13},{6,14},{7,15},{8,16},{9,17... | collective-permute-start | bytes 1179656 | tf_op jit(solution)/shard_map/ppermute | solution.py:32
  68.1 26.3 %collective-permute-start.20 = (bf16[512,512]{1,0:T(8,128)(2,1)S(1)}, bf16[512,512]{1,0:T(8,128)(2,1)}, u32[]{:S(2)}, u32[]{:S(2)}) collective-permute-start(bf16[512,512]{1,0:T(8,128)(2,1)S(1)} %pad_maximum_fusion.refs_4_.refs_19_), channel_id=1, source_target_pairs={{0,2},{1,3},{2,4},{3,5},{4,6},{5,7},{6,0},{7,1},{8,10},{9,11},{10,... | collective-permute-start | bytes 1572872 | tf_op jit(solution)/shard_map/ppermute | solution.py:32
  72.1 7.9 %copy-start.15 = (bf16[384,512]{1,0:T(8,128)(2,1)}, bf16[384,512]{1,0:T(8,128)(2,1)S(1)}, u32[]{:S(2)}) copy-start(bf16[384,512]{1,0:T(8,128)(2,1)S(1)} %collective-permute-done.14.refs_7_.refs_14_) | copy-start | bytes 1179652
  72.1 22.3 %collective-permute-start.15 = (bf16[512,512]{1,0:T(8,128)(2,1)S(1)}, bf16[512,512]{1,0:T(8,128)(2,1)}, u32[]{:S(2)}, u32[]{:S(2)}) collective-permute-start(bf16[512,512]{1,0:T(8,128)(2,1)S(1)} %collective-permute-done.7.refs_6_.refs_21_), channel_id=1, source_target_pairs={{0,6},{1,7},{2,0},{3,1},{4,2},{5,3},{6,4},{7,5},{8,14},{9,15},{10,... | collective-permute-start | bytes 1572872 | tf_op jit(solution)/shard_map/ppermute | solution.py:32
  74.6 5.4 %copy-start.17 = (bf16[384,512]{1,0:T(8,128)(2,1)}, bf16[384,512]{1,0:T(8,128)(2,1)S(1)}, u32[]{:S(2)}) copy-start(bf16[384,512]{1,0:T(8,128)(2,1)S(1)} %collective-permute-done.17.refs_6_.refs_13_) | copy-start | bytes 1179652
  74.6 10.8 %collective-permute-start.19 = (bf16[384,512]{1,0:T(8,128)(2,1)}, bf16[384,512]{1,0:T(8,128)(2,1)}, u32[]{:S(2)}, u32[]{:S(2)}) collective-permute-start(bf16[384,512]{1,0:T(8,128)(2,1)} %collective-permute-done.6.refs_4_.refs_15_), channel_id=1, source_target_pairs={{0,8},{1,9},{2,10},{3,11},{4,12},{5,13},{6,14},{7,15},{8,16},{9,17... | collective-permute-start | bytes 1179656 | tf_op jit(solution)/shard_map/ppermute | solution.py:32
  80.8 18.5 %collective-permute-start.21 = (bf16[384,512]{1,0:T(8,128)(2,1)}, bf16[384,512]{1,0:T(8,128)(2,1)}, u32[]{:S(2)}, u32[]{:S(2)}) collective-permute-start(bf16[384,512]{1,0:T(8,128)(2,1)} %collective-permute-done.10.refs_4_.refs_23_), channel_id=1, source_target_pairs={{0,24},{1,25},{2,26},{3,27},{4,28},{5,29},{6,30},{7,31},{8,0},{9,1... | collective-permute-start | bytes 1179656 | tf_op jit(solution)/shard_map/ppermute | solution.py:32
  82.2 17.1 %collective-permute-start.22 = (bf16[384,512]{1,0:T(8,128)(2,1)}, bf16[384,512]{1,0:T(8,128)(2,1)}, u32[]{:S(2)}, u32[]{:S(2)}) collective-permute-start(bf16[384,512]{1,0:T(8,128)(2,1)} %collective-permute-done.16.refs_5_.refs_24_), channel_id=1, source_target_pairs={{0,8},{1,9},{2,10},{3,11},{4,12},{5,13},{6,14},{7,15},{8,16},{9,17... | collective-permute-start | bytes 1179656 | tf_op jit(solution)/shard_map/ppermute | solution.py:32
  85.4 3.4 %copy-start.1 = (bf16[1,2,8192,256]{3,2,1,0:T(8,128)(2,1)S(1)}, bf16[1,2,8192,256]{3,2,1,0:T(8,128)(2,1)}, u32[]{:S(2)}) copy-start(bf16[1,2,8192,256]{3,2,1,0:T(8,128)(2,1)} %param.8) | copy-start | bytes 25165828
  88.8 1.0 copy-start.13
  99.2 4.0 %copy-start.3 = (bf16[384,512]{1,0:T(8,128)(2,1)S(1)}, bf16[384,512]{1,0:T(8,128)(2,1)}, u32[]{:S(2)}) copy-start(bf16[384,512]{1,0:T(8,128)(2,1)} %copy-done.2) | copy-start | bytes 1179652
  99.2 4.0 %copy-start.5 = (bf16[384,512]{1,0:T(8,128)(2,1)S(1)}, bf16[384,512]{1,0:T(8,128)(2,1)}, u32[]{:S(2)}) copy-start(bf16[384,512]{1,0:T(8,128)(2,1)} %copy-done.4) | copy-start | bytes 1179652
  99.2 4.0 %copy-start.7 = (bf16[384,512]{1,0:T(8,128)(2,1)S(1)}, bf16[384,512]{1,0:T(8,128)(2,1)}, u32[]{:S(2)}) copy-start(bf16[384,512]{1,0:T(8,128)(2,1)} %copy-done.6) | copy-start | bytes 1179652
  99.2 4.0 %copy-start.9 = (bf16[384,512]{1,0:T(8,128)(2,1)S(1)}, bf16[384,512]{1,0:T(8,128)(2,1)}, u32[]{:S(2)}) copy-start(bf16[384,512]{1,0:T(8,128)(2,1)} %copy-done.8) | copy-start | bytes 1179652
  99.2 4.0 %copy-start.11 = (bf16[384,512]{1,0:T(8,128)(2,1)S(1)}, bf16[384,512]{1,0:T(8,128)(2,1)}, u32[]{:S(2)}) copy-start(bf16[384,512]{1,0:T(8,128)(2,1)} %copy-done.10) | copy-start | bytes 1179652
  99.2 4.0 %copy-start.14 = (bf16[384,512]{1,0:T(8,128)(2,1)S(1)}, bf16[384,512]{1,0:T(8,128)(2,1)}, u32[]{:S(2)}) copy-start(bf16[384,512]{1,0:T(8,128)(2,1)} %copy-done.12) | copy-start | bytes 1179652
  99.2 4.0 %copy-start.16 = (bf16[384,512]{1,0:T(8,128)(2,1)S(1)}, bf16[384,512]{1,0:T(8,128)(2,1)}, u32[]{:S(2)}) copy-start(bf16[384,512]{1,0:T(8,128)(2,1)} %copy-done.15) | copy-start | bytes 1179652
  99.2 4.0 %copy-start.18 = (bf16[384,512]{1,0:T(8,128)(2,1)S(1)}, bf16[384,512]{1,0:T(8,128)(2,1)}, u32[]{:S(2)}) copy-start(bf16[384,512]{1,0:T(8,128)(2,1)} %copy-done.17) | copy-start | bytes 1179652
  99.3 4.0 %copy-start.21 = (bf16[384,512]{1,0:T(8,128)(2,1)S(1)}, bf16[384,512]{1,0:T(8,128)(2,1)}, u32[]{:S(2)}) copy-start(bf16[384,512]{1,0:T(8,128)(2,1)} %copy-done.19) | copy-start | bytes 1179652
  99.3 4.0 %copy-start.24 = (s32[3]{0:T(128)S(1)}, s32[3]{0:T(128)}, u32[]{:S(2)}) copy-start(s32[3]{0:T(128)} %widths.3) | copy-start | bytes 40
  99.3 4.0 %copy-start.25 = (s32[32]{0:T(128)S(1)}, s32[32]{0:T(128)}, u32[]{:S(2)}) copy-start(s32[32]{0:T(128)} %refs_2_.1) | copy-start | bytes 388
  123.4 21.0 %all-to-all-start.1 = ((f32[32,1,768]{2,1,0:T(1,128)}), f32[32,1,768]{2,1,0:T(1,128)S(1)}, u32[]{:S(2)}, u32[]{:S(2)}) async-start(f32[32,1,768]{2,1,0:T(1,128)} %all_to_all.13), calls=%async_computation.1 | async-start | bytes 196608 | tf_op jit(solution)/shard_map/all_to_all | solution.py:373
  135.4 9.0 %collective-permute-start.23 = (f32[32,256]{1,0:T(8,128)S(1)}, f32[32,256]{1,0:T(8,128)S(1)}, u32[]{:S(2)}, u32[]{:S(2)}) collective-permute-start(f32[32,256]{1,0:T(8,128)S(1)} %get-tuple-element.35), channel_id=1, source_target_pairs={{0,1},{1,0},{2,3},{3,2},{4,5},{5,4},{6,7},{7,6},{8,9},{9,8},{10,11... | collective-permute-start | bytes 98312 | tf_op jit(solution)/shard_map/ppermute | solution.py:32
  (3 other events, 2.4 us)

commit v3 on v2

--- a/solution.py
+++ b/solution.py
@@ -13,9 +13,11 @@
 HALF = 128
 GRID = ("row", "col")
 MIB = 1024 * 1024
+LIMIT = 20
 VMEM = pl.BlockSpec(memory_space=pltpu.VMEM)
 SMEM = pl.BlockSpec(memory_space=pltpu.SMEM)
 ANY = pl.BlockSpec(memory_space=pl.ANY)
+HBM = pl.BlockSpec(memory_space=pltpu.HBM)
 
 
 def place(x, z, c):
@@ -153,7 +155,7 @@
     has_acc = acc is not None
     return pl.pallas_call(
         functools.partial(gemm_body, segments, (2, 2), has_acc),
-        in_specs=[SMEM, ANY, ANY] + [VMEM] * has_acc + [ANY] * len(pieces),
+        in_specs=[SMEM, HBM, HBM] + [VMEM] * has_acc + [ANY] * len(pieces),
         out_specs=VMEM,
         out_shape=jax.ShapeDtypeStruct((4 * B, 2 * B), jnp.float32),
         scratch_shapes=[
@@ -162,15 +164,15 @@
             pltpu.SemaphoreType.DMA((2, count)),
             pltpu.SemaphoreType.DMA((len(pieces),)),
         ],
-        compiler_params=params(32),
+        compiler_params=params(LIMIT),
     )(device, own, sib, *([acc] if has_acc else []), *pieces)
 
 
 def finish_body(sources, *refs):
     device, widths, owner, assign, weights, acc, dinv = refs[:7]
     pieces = refs[7 : 7 + len(sources)]
-    sent, own, diag, sem = refs[7 + len(sources) :]
-    dev = device[0]
+    shared, *parts_out, own, diag, weighted, sem = refs[7 + len(sources) :]
+    dev, pole = device[0], device[1]
     core = dev % NC
     here_x, here_z = dev // (NZ * NC), dev // NC % NZ
     full, one, two, split = layout(widths)
@@ -204,10 +206,10 @@
         top, low = acc[2 * j * B : (2 * j + 1) * B], acc[(2 * j + 1) * B : (2 * j + 2) * B]
         x_real = low[:, B:] - top[:, :B]
         x_imag = -(top[:, B:] + low[:, :B])
-        density = (wr * x_imag + wi * x_real).astype(jnp.bfloat16)
-        for p in range(POLES):
-            rows = B // POLES
-            sent[p, j * rows : (j + 1) * rows] = density[p * rows : (p + 1) * rows]
+        weighted[...] = (wr * x_imag + wi * x_real).astype(jnp.bfloat16)
+        for d in range(POLES):
+            rows = pl.ds(pl.multiple_of((pole ^ d) * (B // POLES), B // POLES), B // POLES)
+            parts_out[d][j * (B // POLES) : (j + 1) * (B // POLES)] = weighted[rows]
         parts.append((x_real.astype(jnp.bfloat16), x_imag.astype(jnp.bfloat16)))
     for copy in waits:
         copy.wait()
@@ -232,32 +234,30 @@
     diag[...] = jnp.zeros_like(diag)
     first = jnp.where(core == 0, full, one)
     second = jnp.where(core == 0, one, two)
+    diag[pl.ds(pl.multiple_of(first * B, B), B)] = -before
+    diag[pl.ds(pl.multiple_of(second * B, B), B)] = -after
     depth = dinv.shape[1]
     mine = pl.ds(pl.multiple_of(dev * depth, 8), depth)
-    weighted = wr * dinv[1] + wi * dinv[0]
-    for h in range(B // HALF):
-        cols = slice(h * HALF, (h + 1) * HALF)
-        diag[h, pl.ds(pl.multiple_of(first * B, B), B)] = -before[:, cols]
-        diag[h, pl.ds(pl.multiple_of(second * B, B), B)] = -after[:, cols]
-        diag[h, mine] += weighted[:, cols]
-        for p in range(POLES):
-            sent[p, 2 * B // POLES :, cols] = diag[
-                h, pl.ds(p, diag.shape[1] // POLES, stride=POLES)
-            ].astype(jnp.bfloat16)
+    diag[mine] += wr * dinv[1] + wi * dinv[0]
+    shared[...] = diag[...].astype(jnp.bfloat16)
 
 
 def finish(device, widths, owner, assign, weights, acc, dinv, pieces, sources, total):
     return pl.pallas_call(
         functools.partial(finish_body, sources),
         in_specs=[SMEM] * 5 + [VMEM] * 2 + [ANY] * len(pieces),
-        out_specs=VMEM,
-        out_shape=jax.ShapeDtypeStruct((POLES, (2 * B + total) // POLES, B), jnp.bfloat16),
+        out_specs=[VMEM] * (1 + POLES),
+        out_shape=[
+            jax.ShapeDtypeStruct((n, B), jnp.bfloat16)
+            for n in (total,) + (2 * B // POLES,) * POLES
+        ],
         scratch_shapes=[
             pltpu.VMEM((2 * B, 2 * B), jnp.bfloat16),
-            pltpu.VMEM((B // HALF, total, HALF), jnp.float32),
+            pltpu.VMEM((total, B), jnp.float32),
+            pltpu.VMEM((B, B), jnp.bfloat16),
             pltpu.SemaphoreType.DMA((2, 2)),
         ],
-        compiler_params=params(32),
+        compiler_params=params(LIMIT),
     )(device, widths, owner, assign, weights, acc, dinv, *pieces)
 
 
@@ -275,8 +275,7 @@
         panel[out, pl.ds(pl.multiple_of(one * B, B), B)] = jnp.where(col < split, small, 0)
         late = pltpu.roll(small, B - split, 1)
         panel[out, pl.ds(pl.multiple_of(two * B, B), B)] = jnp.where(col < B - split, late, 0)
-        for t in range(diag.shape[0] // POLES):
-            diag[t * POLES + p : t * POLES + p + 1] = got[p, 2 * rows + t : 2 * rows + t + 1]
+    diag[...] = sum(got[p, 2 * rows :] for p in range(POLES))
 
 
 def spread(device, widths, got, total, depth):
@@ -294,14 +293,12 @@
 
 def local(inverse, factor, diag_inverse, widths, pattern, owner, assign, pole_weights):
     dev = lax.axis_index(GRID)
-    device = dev[None].astype(jnp.int32)
+    device = jnp.stack([dev, lax.axis_index("pole")]).astype(jnp.int32)
     total = factor.shape[3]
     depth = diag_inverse.shape[2]
-    own_inverse = inverse[0]
+    own_inverse = pltpu.with_memory_space_constraint(inverse[0], pltpu.HBM)
     top, rest, give = prepare(device, widths, pattern, factor[0])
     taken = shift(give, 0, 0, 1)
-    sib_inverse = shift(own_inverse, 0, 0, 1)
-
     pieces, sources = [], []
 
     def multiply(acc, held, offsets, kind):
@@ -329,29 +326,30 @@
 
     rest_f, rest_b = shift(rest, 1, 0), shift(rest, -1, 0)
     main = jnp.concatenate([top, taken], 0)
+    rest_f, rest_b = after((rest_f, rest_b), main)
     zf, zb = shift(main, 0, 1), shift(main, 0, -1)
     rest_far = shift(rest_f, 1, 0)
-    main_f, main_b = shift(main, 1, 0), shift(main, -1, 0)
+    main_x = after(main, rest_f, rest_b)
+    main_f, main_b = shift(main_x, 1, 0), shift(main_x, -1, 0)
     across = jnp.concatenate([rest, rest_f, rest_b, rest_far], 0)
+    sib_inverse = shift(after(inverse[0], rest_far), 0, 0, 1)
+    sib_inverse = pltpu.with_memory_space_constraint(sib_inverse, pltpu.HBM)
     main_far = shift(main_b, -1, 0)
     z_far = shift(zf, 0, 1)
+    across_b = shift(after(across, zf, zb), 0, -1)
     zff, zbb = shift(zf, 1, 0), shift(zb, -1, 0)
-    zfb, zbf = shift(zf, -1, 0), shift(zb, 1, 0)
-    across = after(across, zf, zb)
-    across_b = shift(across, 0, -1)
+    zf_late, zb_late = after((zf, zb), main_far)
+    zfb, zbf = shift(zf_late, -1, 0), shift(zb_late, 1, 0)
     acc = multiply(None, (main, main_f, main_b, main_far), along_x(0), 0)
     z_far, acc = after((z_far, acc), zff, zbb)
     far_f, far_b = shift(z_far, 1, 0), shift(z_far, -1, 0)
-    zff, zbb, across, acc = after((zff, zbb, across, acc), z_far)
+    across_f = shift(after(across, z_far), 0, 1)
     zf_far, zb_far = shift(zff, 1, 0), shift(zbb, -1, 0)
-    across_f = shift(across, 0, 1)
-    across_b, acc = after((across_b, acc), zf_far)
     across_far = shift(across_b, 0, -1)
     acc = multiply(acc, (zf, zff, zfb, zf_far), along_x(-1), 0)
-    far_f, acc = after((far_f, acc), zb_far)
+    acc = multiply(acc, (zb, zbf, zbb, zb_far), along_x(1), 0)
+    far_f, acc = after((far_f, acc))
     far_far = shift(far_f, 1, 0)
-    acc = multiply(acc, (zb, zbf, zbb, zb_far), along_x(1), 0)
-    across_far, acc = after((across_far, acc), across_f)
     acc = multiply(
         acc,
         (across, across_f, across_b, across_far),
@@ -360,18 +358,21 @@
     )
     acc = multiply(acc, (z_far, far_f, far_b, far_far), along_x(2), 0)
 
-    sent = finish(
+    shared, *parts = finish(
         device, widths, owner, assign, pole_weights, acc,
         diag_inverse[0].astype(jnp.float32), pieces, tuple(sources), total,
     )
 
-    got = lax.all_to_all(sent, "pole", 0, 0, tiled=True).astype(jnp.float32).sum(0)
+    shared = shared.reshape(NX * NZ * NC, depth, B)
+    shared = lax.all_to_all(shared, GRID, 0, 0, tiled=True)
+    got = [
+        lax.ppermute(part, "pole", [(p, p ^ d) for p in range(POLES)]) if d else part
+        for d, part in enumerate(parts)
+    ]
+    got = sum(part.astype(jnp.float32) for part in got)
     rows = B // POLES
-    other = shift(got[rows : 2 * rows], 0, 0, 1)
-    share = depth // POLES
-    diag = got[2 * rows :].reshape(NX * NZ * NC, share * B)
-    diag = lax.all_to_all(diag, GRID, 0, 0, tiled=True).sum(0).reshape(share, B)
-    diag = jnp.pad(diag, ((0, 8 - share), (0, 0)))
+    other = shift(got[rows:], 0, 0, 1)
+    diag = shared.astype(jnp.float32).sum(0)
     both = jnp.concatenate([got[:rows], other, diag], 0)
     both = lax.all_to_all(
         jnp.broadcast_to(both[None], (POLES,) + both.shape), "pole", 0, 0, tiled=True

time: 162 us -> 155 us (0.957)
  waiting for transfers between devices: 32.7 us -> 48.5 us
  blocking collectives: 30.3 us -> 15.2 us
  local copies, waits for them, and re-layouts: 13.7 us -> 6.26 us
  Pallas kernels: 25.7 us -> 30.7 us
  starting transfers between devices: 55.2 us -> 51.1 us
    ppermute x24, waiting for transfers between devices: 24 us -> 42.5 us  [shift(): return lax.ppermute(value, GRID, perm)]
    all_to_all x1 -> x0, blocking collectives: 16.1 us -> none  [local(): lax.all_to_all(sent, 'pole', 0, 0, tiled=True).astype(jnp.float32).sum(0)]
    ppermute x0 -> x7, starting transfers between devices: none -> 12.4 us  [local(): lax.ppermute(part, 'pole', [(p, p ^ d) for p in range(POLES)])]
    ppermute x24, starting transfers between devices: 43.2 us -> 32.6 us  [shift(): return lax.ppermute(value, GRID, perm)]
    all_to_all x1, waiting for transfers between devices: 8.72 us -> 0.01 us  [local(): shared = lax.all_to_all(shared, GRID, 0, 0, tiled=True)]
    unnamed x55 -> x60, local copies, waits for them, and re-layouts: 12.9 us -> 6.17 us
    ppermute x0 -> x7, waiting for transfers between devices: none -> 6.01 us  [local(): lax.ppermute(part, 'pole', [(p, p ^ d) for p in range(POLES)])]
    all_to_all x1, starting transfers between devices: 12 us -> 6.16 us  [local(): shared = lax.all_to_all(shared, GRID, 0, 0, tiled=True)]
  transfers between devices with their start and end apart: 25 -> 32, of which waited for: 8 -> 15; matrix products, arithmetic and copies ran while one was open for 2% -> 1% of each run, Pallas kernels for 11% -> 12%
where the time goes in v3:
time: 155 us
  starting transfers between devices  51.1 us (33%)
  waiting for transfers between devices  48.5 us (31%)
  Pallas kernels  30.7 us (20%)
  blocking collectives  15.2 us (10%)
  local copies, waits for them, and re-layouts  6.26 us (4%)
  between operations  1.81 us (1%)
    ppermute x24, waiting for transfers between devices, shift(): return lax.ppermute(value, GRID, perm)  42.5 us
    ppermute x24, starting transfers between devices, shift(): return lax.ppermute(value, GRID, perm)  32.6 us
    pallas_call x5, Pallas kernels, gemm(): pl.pallas_call(functools.partial(gemm_body, segments, (2, 2), has_acc), i...  23.6 us
    all_to_all x1, blocking collectives, local(): lax.all_to_all(jnp.broadcast_to(both[None], (POLES,) + both.shape), 'pole...  15.2 us
    ppermute x7, starting transfers between devices, local(): lax.ppermute(part, 'pole', [(p, p ^ d) for p in range(POLES)])  12.4 us
    unnamed x60, local copies, waits for them, and re-layouts  6.17 us
    all_to_all x1, starting transfers between devices, local(): shared = lax.all_to_all(shared, GRID, 0, 0, tiled=True)  6.16 us
    ppermute x7, waiting for transfers between devices, local(): lax.ppermute(part, 'pole', [(p, p ^ d) for p in range(POLES)])  6.01 us
  transfers between devices with their start and end apart: 32, of which 15 were waited for; matrix products, arithmetic and copies ran while one was open for 1% of the time, Pallas kernels for 12%

profile of v3, /device:TPU:2, one launch (start us, length us, event | category | flops | bytes accessed | tf_op | source)
XLA Modules:
  0.0 154.6 jit_solution(14554454706262177350)
XLA Ops:
  0.6 0.8 copy.10.pattern
  1.5 1.1 copy-done.22
  3.3 1.1 shard_map.95
  4.5 1.6 %collective-permute-start = (bf16[128,512]{1,0:T(8,128)(2,1)S(1)}, bf16[128,512]{1,0:T(8,128)(2,1)S(1)}, u32[]{:S(2)}, u32[]{:S(2)}) collective-permute-start(bf16[128,512]{1,0:T(8,128)(2,1)S(1)} %get-tuple-element.26), channel_id=1, source_target_pairs={{0,8},{1,9},{2,10},{3,11},{4,12},{5,13},{6,14},{7,15},{8,16},{9,17... | collective-permute-start | bytes 393224 | tf_op jit(solution)/shard_map/ppermute | solution.py:34
  6.1 0.9 collective-permute-start.1
  7.0 3.9 %collective-permute-done = bf16[128,512]{1,0:T(8,128)(2,1)S(1)} collective-permute-done((bf16[128,512]{1,0:T(8,128)(2,1)S(1)}, bf16[128,512]{1,0:T(8,128)(2,1)S(1)}, u32[]{:S(2)}, u32[]{:S(2)}) %collective-permute-start) | collective-permute-done | bytes 131104 | tf_op jit(solution)/shard_map/ppermute | solution.py:34
  10.9 0.7 collective-permute-done.1
  11.6 1.7 %collective-permute-start.3 = (bf16[128,512]{1,0:T(8,128)(2,1)S(1)}, bf16[128,512]{1,0:T(8,128)(2,1)S(1)}, u32[]{:S(2)}, u32[]{:S(2)}) collective-permute-start(bf16[128,512]{1,0:T(8,128)(2,1)S(1)} %collective-permute-done), channel_id=1, source_target_pairs={{0,8},{1,9},{2,10},{3,11},{4,12},{5,13},{6,14},{7,15},{8,16},{9,17... | collective-permute-start | bytes 393224 | tf_op jit(solution)/shard_map/ppermute | solution.py:34
  13.3 3.9 %collective-permute-done.3 = bf16[128,512]{1,0:T(8,128)(2,1)S(1)} collective-permute-done((bf16[128,512]{1,0:T(8,128)(2,1)S(1)}, bf16[128,512]{1,0:T(8,128)(2,1)S(1)}, u32[]{:S(2)}, u32[]{:S(2)}) %collective-permute-start.3) | collective-permute-done | bytes 131104 | tf_op jit(solution)/shard_map/ppermute | solution.py:34
  17.2 3.0 %collective-permute-start.8 = (bf16[384,512]{1,0:T(8,128)(2,1)S(1)}, bf16[384,512]{1,0:T(8,128)(2,1)S(1)}, u32[]{:S(2)}, u32[]{:S(2)}) collective-permute-start(bf16[384,512]{1,0:T(8,128)(2,1)S(1)} %constant_dynamic-update-slice_fusion.refs_3_.refs_7_), channel_id=1, source_target_pairs={{0,24},{1,25},{2,26},{3,27},{4,28},{5,29},{6,30},{7,31},{8,0},{9,1... | collective-permute-start | bytes 1179656 | tf_op jit(solution)/shard_map/ppermute | solution.py:34
  20.2 1.5 collective-permute-start.5
  21.7 3.0 %collective-permute-start.11 = (bf16[384,512]{1,0:T(8,128)(2,1)S(1)}, bf16[384,512]{1,0:T(8,128)(2,1)S(1)}, u32[]{:S(2)}, u32[]{:S(2)}) collective-permute-start(bf16[384,512]{1,0:T(8,128)(2,1)S(1)} %constant_dynamic-update-slice_fusion.refs_3_.refs_7_), channel_id=1, source_target_pairs={{0,6},{1,7},{2,0},{3,1},{4,2},{5,3},{6,4},{7,5},{8,14},{9,15},{10,... | collective-permute-start | bytes 1179656 | tf_op jit(solution)/shard_map/ppermute | solution.py:34
  25.0 4.2 %collective-permute-done.8.refs_5_.refs_9_ = bf16[384,512]{1,0:T(8,128)(2,1)S(1)} collective-permute-done((bf16[384,512]{1,0:T(8,128)(2,1)S(1)}, bf16[384,512]{1,0:T(8,128)(2,1)S(1)}, u32[]{:S(2)}, u32[]{:S(2)}) %collective-permute-start.8) | collective-permute-done | bytes 393248 | tf_op jit(solution)/shard_map/ppermute | solution.py:34
  29.2 2.5 %collective-permute-start.9 = (bf16[384,512]{1,0:T(8,128)(2,1)S(1)}, bf16[384,512]{1,0:T(8,128)(2,1)S(1)}, u32[]{:S(2)}, u32[]{:S(2)}) collective-permute-start(bf16[384,512]{1,0:T(8,128)(2,1)S(1)} %collective-permute-done.8.refs_5_.refs_9_), channel_id=1, source_target_pairs={{0,24},{1,25},{2,26},{3,27},{4,28},{5,29},{6,30},{7,31},{8,0},{9,1... | collective-permute-start | bytes 1179656 | tf_op jit(solution)/shard_map/ppermute | solution.py:34
  31.7 5.5 %collective-permute-done.5.refs_4_.refs_11_ = bf16[384,512]{1,0:T(8,128)(2,1)S(1)} collective-permute-done((bf16[384,512]{1,0:T(8,128)(2,1)S(1)}, bf16[384,512]{1,0:T(8,128)(2,1)S(1)}, u32[]{:S(2)}, u32[]{:S(2)}) %collective-permute-start.5) | collective-permute-done | bytes 393248 | tf_op jit(solution)/shard_map/ppermute | solution.py:34
  37.4 6.5 %collective-permute-done.11.refs_4_.refs_15_ = bf16[384,512]{1,0:T(8,128)(2,1)S(1)} collective-permute-done((bf16[384,512]{1,0:T(8,128)(2,1)S(1)}, bf16[384,512]{1,0:T(8,128)(2,1)S(1)}, u32[]{:S(2)}, u32[]{:S(2)}) %collective-permute-start.11) | collective-permute-done | bytes 393248 | tf_op jit(solution)/shard_map/ppermute | solution.py:34
  43.8 2.7 %collective-permute-start.19 = (bf16[512,512]{1,0:T(8,128)(2,1)S(1)}, bf16[512,512]{1,0:T(8,128)(2,1)S(1)}, u32[]{:S(2)}, u32[]{:S(2)}) collective-permute-start(bf16[512,512]{1,0:T(8,128)(2,1)S(1)} %constant_dynamic-update-slice_fusion.2.refs_4_.refs_19_), channel_id=1, source_target_pairs={{0,6},{1,7},{2,0},{3,1},{4,2},{5,3},{6,4},{7,5},{8,14},{9,15},{10,... | collective-permute-start | bytes 1572872 | tf_op jit(solution)/shard_map/ppermute | solution.py:34
  46.5 1.7 %collective-permute-start.12 = (bf16[384,512]{1,0:T(8,128)(2,1)S(1)}, bf16[384,512]{1,0:T(8,128)(2,1)S(1)}, u32[]{:S(2)}, u32[]{:S(2)}) collective-permute-start(bf16[384,512]{1,0:T(8,128)(2,1)S(1)} %collective-permute-done.11.refs_4_.refs_15_), channel_id=1, source_target_pairs={{0,24},{1,25},{2,26},{3,27},{4,28},{5,29},{6,30},{7,31},{8,0},{9,1... | collective-permute-start | bytes 1179656 | tf_op jit(solution)/shard_map/ppermute | solution.py:34
  48.2 1.3 collective-permute-start.6
  49.5 1.4 collective-permute-start.14
  51.5 2.7 %copy-done.26 = bf16[2,8192,256]{2,1,0:T(8,128)(2,1)} copy-done((bf16[2,8192,256]{2,1,0:T(8,128)(2,1)}, bf16[2,8192,256]{2,1,0:T(8,128)(2,1)S(1)}, u32[]{:S(2)}) %copy-start.26) | copy-done | bytes 8388632
  54.2 4.3 %shard_map.96.refs_3_ = f32[1024,512]{1,0:T(8,128)S(1)} custom-call(s32[2]{0:T(128)S(1)} %pad_add_fusion.device.refs_0_, bf16[2,8192,256]{2,1,0:T(8,128)(2,1)} %bitcast.10, bf16[2,8192,256]{2,1,0:T(8,128)(2,1)} %copy-done.26, bf16[384,512]{1,0:T(8,128)(2,1)S(1)} %constant_dynamic-update-slice_fusion.refs_3_.refs_7_, ...), custom_call_target="tpu_custom_call" | custom-call | tf_op jit(solution)/shard_map/pallas_call | solution.py:156
  58.6 1.1 collective-permute-start.16
  59.7 6.7 %collective-permute-done.6.refs_4_.refs_23_ = bf16[384,512]{1,0:T(8,128)(2,1)} collective-permute-done((bf16[384,512]{1,0:T(8,128)(2,1)S(1)}, bf16[384,512]{1,0:T(8,128)(2,1)}, u32[]{:S(2)}, u32[]{:S(2)}) %collective-permute-start.6) | collective-permute-done | bytes 393248 | tf_op jit(solution)/shard_map/ppermute | solution.py:34
  66.4 2.8 %collective-permute-start.17 = (bf16[384,512]{1,0:T(8,128)(2,1)S(1)}, bf16[384,512]{1,0:T(8,128)(2,1)S(1)}, u32[]{:S(2)}, u32[]{:S(2)}) collective-permute-start(bf16[384,512]{1,0:T(8,128)(2,1)S(1)} %collective-permute-done.12.refs_6_.refs_17_), channel_id=1, source_target_pairs={{0,24},{1,25},{2,26},{3,27},{4,28},{5,29},{6,30},{7,31},{8,0},{9,1... | collective-permute-start | bytes 1179656 | tf_op jit(solution)/shard_map/ppermute | solution.py:34
  70.0 3.4 %collective-permute-start.20 = (bf16[512,512]{1,0:T(8,128)(2,1)S(1)}, bf16[512,512]{1,0:T(8,128)(2,1)}, u32[]{:S(2)}, u32[]{:S(2)}) collective-permute-start(bf16[512,512]{1,0:T(8,128)(2,1)S(1)} %collective-permute-done.19.refs_6_.refs_21_), channel_id=1, source_target_pairs={{0,6},{1,7},{2,0},{3,1},{4,2},{5,3},{6,4},{7,5},{8,14},{9,15},{10,... | collective-permute-start | bytes 1572872 | tf_op jit(solution)/shard_map/ppermute | solution.py:34
  73.5 4.5 %shard_map.97.refs_3_ = f32[1024,512]{1,0:T(8,128)S(1)} custom-call(s32[2]{0:T(128)S(1)} %pad_add_fusion.device.refs_0_, bf16[2,8192,256]{2,1,0:T(8,128)(2,1)} %bitcast.11, bf16[2,8192,256]{2,1,0:T(8,128)(2,1)} %copy-done.26, f32[1024,512]{1,0:T(8,128)S(1)} %shard_map.96.refs_3_, bf16[384,512]{1,0:T(8,128)(2,1)S(1)} %collective-permute-done.5.refs_4_.refs_11_, ...), custom_call_target="tpu_custom_call" | custom-call | tf_op jit(solution)/shard_map/pallas_call | solution.py:156
  78.0 1.1 collective-permute-start.21
  79.1 4.4 %shard_map.98.refs_3_ = f32[1024,512]{1,0:T(8,128)S(1)} custom-call(s32[2]{0:T(128)S(1)} %pad_add_fusion.device.refs_0_, bf16[2,8192,256]{2,1,0:T(8,128)(2,1)} %bitcast.12, bf16[2,8192,256]{2,1,0:T(8,128)(2,1)} %copy-done.26, f32[1024,512]{1,0:T(8,128)S(1)} %shard_map.97.refs_3_, bf16[384,512]{1,0:T(8,128)(2,1)S(1)} %collective-permute-done.11.refs_4_.refs_15_, ...), custom_call_target="tpu_custom_call" | custom-call | tf_op jit(solution)/shard_map/pallas_call | solution.py:156
  83.6 1.3 collective-permute-start.22
  84.9 0.8 copy.11.refs_4_
  86.3 0.7 bitcast_convert_fusion.refs_6_
  87.0 6.6 %collective-permute-done.20.refs_7_.refs_22_ = bf16[512,512]{1,0:T(8,128)(2,1)} collective-permute-done((bf16[512,512]{1,0:T(8,128)(2,1)S(1)}, bf16[512,512]{1,0:T(8,128)(2,1)}, u32[]{:S(2)}, u32[]{:S(2)}) %collective-permute-start.20) | collective-permute-done | bytes 524320 | tf_op jit(solution)/shard_map/ppermute | solution.py:34
  93.6 3.0 %collective-permute-done.18.refs_5_.refs_20_ = bf16[512,512]{1,0:T(8,128)(2,1)} collective-permute-done((bf16[512,512]{1,0:T(8,128)(2,1)S(1)}, bf16[512,512]{1,0:T(8,128)(2,1)}, u32[]{:S(2)}, u32[]{:S(2)}) %collective-permute-start.18) | collective-permute-done | bytes 524320 | tf_op jit(solution)/shard_map/ppermute | solution.py:34
  96.6 5.4 %shard_map.99.refs_3_ = f32[1024,512]{1,0:T(8,128)S(1)} custom-call(s32[2]{0:T(128)S(1)} %pad_add_fusion.device.refs_0_, bf16[2,8192,256]{2,1,0:T(8,128)(2,1)} %bitcast.13, bf16[2,8192,256]{2,1,0:T(8,128)(2,1)} %copy-done.26, f32[1024,512]{1,0:T(8,128)S(1)} %shard_map.98.refs_3_, bf16[512,512]{1,0:T(8,128)(2,1)S(1)} %constant_dynamic-update-slice_fusion.2.refs_4_.refs_19_, ...), custom_call_target="tpu_custom_call" | custom-call | tf_op jit(solution)/shard_map/pallas_call | solution.py:156
  102.2 5.0 %shard_map.100.refs_5_ = f32[1024,512]{1,0:T(8,128)S(1)} custom-call(s32[2]{0:T(128)S(1)} %pad_add_fusion.device.refs_0_, bf16[2,8192,256]{2,1,0:T(8,128)(2,1)} %bitcast.14, bf16[2,8192,256]{2,1,0:T(8,128)(2,1)} %copy-done.26, f32[1024,512]{1,0:T(8,128)S(1)} %shard_map.99.refs_3_, bf16[384,512]{1,0:T(8,128)(2,1)} %collective-permute-done.6.refs_4_.refs_23_, ...), custom_call_target="tpu_custom_call" | custom-call | tf_op jit(solution)/shard_map/pallas_call | solution.py:156
  107.3 4.5 %shard_map.101 = (bf16[768,256]{1,0:T(8,128)(2,1)}, bf16[64,256]{1,0:T(8,128)(2,1)S(1)}, bf16[64,256]{1,0:T(8,128)(2,1)S(1)}, bf16[64,256]{1,0:T(8,128)(2,1)S(1)...) custom-call(s32[2]{0:T(128)S(1)} %pad_add_fusion.device.refs_0_, ...), custom_call_target="tpu_custom_call" | custom-call | tf_op jit(solution)/shard_map/pallas_call | solution.py:246
  111.8 6.2 %all-to-all-start = ((bf16[32,24,256]{2,1,0:T(8,128)(2,1)}), bf16[32,24,256]{2,1,0:T(8,128)(2,1)S(1)}, u32[]{:S(2)}, u32[]{:S(2)}) async-start(bf16[32,24,256]{2,1,0:T(8,128)(2,1)} %bitcast.5), calls=%async_computation | async-start | bytes 786432 | tf_op jit(solution)/shard_map/all_to_all | solution.py:367
  118.0 1.6 %collective-permute-start.23 = (bf16[64,256]{1,0:T(8,128)(2,1)S(1)}, bf16[64,256]{1,0:T(8,128)(2,1)S(1)}, u32[]{:S(2)}, u32[]{:S(2)}) collective-permute-start(bf16[64,256]{1,0:T(8,128)(2,1)S(1)} %get-tuple-element.42), channel_id=1, source_target_pairs={{0,32},{32,0},{64,96},{96,64},{128,160},{160,128},{192,224},{224,1... | collective-permute-start | bytes 98312 | tf_op jit(solution)/shard_map/ppermute | solution.py:369
  119.6 2.9 %collective-permute-start.24 = (bf16[64,256]{1,0:T(8,128)(2,1)S(1)}, bf16[64,256]{1,0:T(8,128)(2,1)S(1)}, u32[]{:S(2)}, u32[]{:S(2)}) collective-permute-start(bf16[64,256]{1,0:T(8,128)(2,1)S(1)} %get-tuple-element.43), channel_id=1, source_target_pairs={{0,64},{32,96},{64,0},{96,32},{128,192},{160,224},{192,128},{224,1... | collective-permute-start | bytes 98312 | tf_op jit(solution)/shard_map/ppermute | solution.py:369
  122.8 2.3 %collective-permute-start.26 = (bf16[64,256]{1,0:T(8,128)(2,1)S(1)}, bf16[64,256]{1,0:T(8,128)(2,1)S(1)}, u32[]{:S(2)}, u32[]{:S(2)}) collective-permute-start(bf16[64,256]{1,0:T(8,128)(2,1)S(1)} %get-tuple-element.45), channel_id=1, source_target_pairs={{0,128},{32,160},{64,192},{96,224},{128,0},{160,32},{192,64},{224,... | collective-permute-start | bytes 98312 | tf_op jit(solution)/shard_map/ppermute | solution.py:369
  125.0 5.3 %collective-permute-start.28 = (bf16[64,256]{1,0:T(8,128)(2,1)S(1)}, bf16[64,256]{1,0:T(8,128)(2,1)S(1)}, u32[]{:S(2)}, u32[]{:S(2)}) collective-permute-start(bf16[64,256]{1,0:T(8,128)(2,1)S(1)} %get-tuple-element.47), channel_id=1, source_target_pairs={{0,192},{32,224},{64,128},{96,160},{128,64},{160,96},{192,0},{224,... | collective-permute-start | bytes 98312 | tf_op jit(solution)/shard_map/ppermute | solution.py:369
  130.4 1.8 %collective-permute-done.27 = bf16[64,256]{1,0:T(8,128)(2,1)S(1)} collective-permute-done((bf16[64,256]{1,0:T(8,128)(2,1)S(1)}, bf16[64,256]{1,0:T(8,128)(2,1)S(1)}, u32[]{:S(2)}, u32[]{:S(2)}) %collective-permute-start.27) | collective-permute-done | bytes 32800 | tf_op jit(solution)/shard_map/ppermute | solution.py:369
  132.2 2.6 %collective-permute-done.28 = bf16[64,256]{1,0:T(8,128)(2,1)S(1)} collective-permute-done((bf16[64,256]{1,0:T(8,128)(2,1)S(1)}, bf16[64,256]{1,0:T(8,128)(2,1)S(1)}, u32[]{:S(2)}, u32[]{:S(2)}) %collective-permute-start.28) | collective-permute-done | bytes 32800 | tf_op jit(solution)/shard_map/ppermute | solution.py:369
  134.8 1.6 %collective-permute-done.29 = bf16[64,256]{1,0:T(8,128)(2,1)S(1)} collective-permute-done((bf16[64,256]{1,0:T(8,128)(2,1)S(1)}, bf16[64,256]{1,0:T(8,128)(2,1)S(1)}, u32[]{:S(2)}, u32[]{:S(2)}) %collective-permute-start.29) | collective-permute-done | bytes 32800 | tf_op jit(solution)/shard_map/ppermute | solution.py:369
  136.6 1.1 collective-permute-done.30
  137.8 15.2 %all_to_all.10.got = f32[8,88,256]{2,1,0:T(8,128)S(1)} all-to-all(f32[8,88,256]{2,1,0:T(8,128)S(1)} %broadcast_in_dim.2), channel_id=1, replica_groups=mesh['pole'=8,'row'=4,'col'=8] {'pole'}, dimensions={0} | all-to-all | bytes 1441792 | tf_op jit(solution)/shard_map/all_to_all | solution.py:377
  153.0 1.6 %shard_map.102 = (f32[256,768]{1,0:T(8,128)}, f32[24,256]{1,0:T(8,128)}) custom-call(s32[2]{0:T(128)S(1)} %pad_add_fusion.device.refs_0_, s32[3]{0:T(128)S(1)} %copy-done.24, f32[8,88,256]{2,1,0:T(8,128)S(1)} %all_to_all.10.got), custom_call_target="tpu_custom_call" | custom-call | tf_op jit(solution)/shard_map/pallas_call | solution.py:282
  (94 shorter events, 3.4 us)
Async XLA Ops:
  4.4 2.6 %collective-permute-start.2 = (bf16[256,512]{1,0:T(8,128)(2,1)S(1)}, bf16[256,512]{1,0:T(8,128)(2,1)S(1)}, u32[]{:S(2)}, u32[]{:S(2)}) collective-permute-start(bf16[256,512]{1,0:T(8,128)(2,1)S(1)} %get-tuple-element.28), channel_id=1, source_target_pairs={{0,1},{1,0},{2,3},{3,2},{4,5},{5,4},{6,7},{7,6},{8,9},{9,8},{10,11... | collective-permute-start | bytes 786440 | tf_op jit(solution)/shard_map/ppermute | solution.py:34
  4.5 6.4 %collective-permute-start = (bf16[128,512]{1,0:T(8,128)(2,1)S(1)}, bf16[128,512]{1,0:T(8,128)(2,1)S(1)}, u32[]{:S(2)}, u32[]{:S(2)}) collective-permute-start(bf16[128,512]{1,0:T(8,128)(2,1)S(1)} %get-tuple-element.26), channel_id=1, source_target_pairs={{0,8},{1,9},{2,10},{3,11},{4,12},{5,13},{6,14},{7,15},{8,16},{9,17... | collective-permute-start | bytes 393224 | tf_op jit(solution)/shard_map/ppermute | solution.py:34
  6.1 5.6 %collective-permute-start.1 = (bf16[128,512]{1,0:T(8,128)(2,1)S(1)}, bf16[128,512]{1,0:T(8,128)(2,1)S(1)}, u32[]{:S(2)}, u32[]{:S(2)}) collective-permute-start(bf16[128,512]{1,0:T(8,128)(2,1)S(1)} %get-tuple-element.26), channel_id=1, source_target_pairs={{0,24},{1,25},{2,26},{3,27},{4,28},{5,29},{6,30},{7,31},{8,0},{9,1... | collective-permute-start | bytes 393224 | tf_op jit(solution)/shard_map/ppermute | solution.py:34
  11.6 5.6 %collective-permute-start.3 = (bf16[128,512]{1,0:T(8,128)(2,1)S(1)}, bf16[128,512]{1,0:T(8,128)(2,1)S(1)}, u32[]{:S(2)}, u32[]{:S(2)}) collective-permute-start(bf16[128,512]{1,0:T(8,128)(2,1)S(1)} %collective-permute-done), channel_id=1, source_target_pairs={{0,8},{1,9},{2,10},{3,11},{4,12},{5,13},{6,14},{7,15},{8,16},{9,17... | collective-permute-start | bytes 393224 | tf_op jit(solution)/shard_map/ppermute | solution.py:34
  17.2 33.7 %collective-permute-start.4 = (bf16[2,8192,256]{2,1,0:T(8,128)(2,1)}, bf16[2,8192,256]{2,1,0:T(8,128)(2,1)S(1)}, u32[]{:S(2)}, u32[]{:S(2)}) collective-permute-start(bf16[2,8192,256]{2,1,0:T(8,128)(2,1)} %bitcast.9), channel_id=1, source_target_pairs={{0,1},{1,0},{2,3},{3,2},{4,5},{5,4},{6,7},{7,6},{8,9},{9,8},{10,11... | collective-permute-start | bytes 25165832 | tf_op jit(solution)/shard_map/ppermute | solution.py:34
  17.2 12.0 %collective-permute-start.8 = (bf16[384,512]{1,0:T(8,128)(2,1)S(1)}, bf16[384,512]{1,0:T(8,128)(2,1)S(1)}, u32[]{:S(2)}, u32[]{:S(2)}) collective-permute-start(bf16[384,512]{1,0:T(8,128)(2,1)S(1)} %constant_dynamic-update-slice_fusion.refs_3_.refs_7_), channel_id=1, source_target_pairs={{0,24},{1,25},{2,26},{3,27},{4,28},{5,29},{6,30},{7,31},{8,0},{9,1... | collective-permute-start | bytes 1179656 | tf_op jit(solution)/shard_map/ppermute | solution.py:34
  20.2 17.1 %collective-permute-start.5 = (bf16[384,512]{1,0:T(8,128)(2,1)S(1)}, bf16[384,512]{1,0:T(8,128)(2,1)S(1)}, u32[]{:S(2)}, u32[]{:S(2)}) collective-permute-start(bf16[384,512]{1,0:T(8,128)(2,1)S(1)} %constant_dynamic-update-slice_fusion.refs_3_.refs_7_), channel_id=1, source_target_pairs={{0,2},{1,3},{2,4},{3,5},{4,6},{5,7},{6,0},{7,1},{8,10},{9,11},{10,... | collective-permute-start | bytes 1179656 | tf_op jit(solution)/shard_map/ppermute | solution.py:34
  21.7 22.1 %collective-permute-start.11 = (bf16[384,512]{1,0:T(8,128)(2,1)S(1)}, bf16[384,512]{1,0:T(8,128)(2,1)S(1)}, u32[]{:S(2)}, u32[]{:S(2)}) collective-permute-start(bf16[384,512]{1,0:T(8,128)(2,1)S(1)} %constant_dynamic-update-slice_fusion.refs_3_.refs_7_), channel_id=1, source_target_pairs={{0,6},{1,7},{2,0},{3,1},{4,2},{5,3},{6,4},{7,5},{8,14},{9,15},{10,... | collective-permute-start | bytes 1179656 | tf_op jit(solution)/shard_map/ppermute | solution.py:34
  24.8 21.8 %collective-permute-start.7 = (bf16[384,512]{1,0:T(8,128)(2,1)S(1)}, bf16[384,512]{1,0:T(8,128)(2,1)S(1)}, u32[]{:S(2)}, u32[]{:S(2)}) collective-permute-start(bf16[384,512]{1,0:T(8,128)(2,1)S(1)} %constant_dynamic-update-slice_fusion.refs_3_.refs_7_), channel_id=1, source_target_pairs={{0,8},{1,9},{2,10},{3,11},{4,12},{5,13},{6,14},{7,15},{8,16},{9,17... | collective-permute-start | bytes 1179656 | tf_op jit(solution)/shard_map/ppermute | solution.py:34
  29.2 29.3 %copy-start = (bf16[384,512]{1,0:T(8,128)(2,1)}, bf16[384,512]{1,0:T(8,128)(2,1)S(1)}, u32[]{:S(2)}) copy-start(bf16[384,512]{1,0:T(8,128)(2,1)S(1)} %collective-permute-done.8.refs_5_.refs_9_) | copy-start | bytes 1179652
  29.2 19.0 %collective-permute-start.9 = (bf16[384,512]{1,0:T(8,128)(2,1)S(1)}, bf16[384,512]{1,0:T(8,128)(2,1)S(1)}, u32[]{:S(2)}, u32[]{:S(2)}) collective-permute-start(bf16[384,512]{1,0:T(8,128)(2,1)S(1)} %collective-permute-done.8.refs_5_.refs_9_), channel_id=1, source_target_pairs={{0,24},{1,25},{2,26},{3,27},{4,28},{5,29},{6,30},{7,31},{8,0},{9,1... | collective-permute-start | bytes 1179656 | tf_op jit(solution)/shard_map/ppermute | solution.py:34
  37.3 36.2 %copy-start.2 = (bf16[384,512]{1,0:T(8,128)(2,1)}, bf16[384,512]{1,0:T(8,128)(2,1)S(1)}, u32[]{:S(2)}) copy-start(bf16[384,512]{1,0:T(8,128)(2,1)S(1)} %collective-permute-done.5.refs_4_.refs_11_) | copy-start | bytes 1179652
  37.3 12.2 %collective-permute-start.10 = (bf16[384,512]{1,0:T(8,128)(2,1)S(1)}, bf16[384,512]{1,0:T(8,128)(2,1)S(1)}, u32[]{:S(2)}, u32[]{:S(2)}) collective-permute-start(bf16[384,512]{1,0:T(8,128)(2,1)S(1)} %collective-permute-done.5.refs_4_.refs_11_), channel_id=1, source_target_pairs={{0,8},{1,9},{2,10},{3,11},{4,12},{5,13},{6,14},{7,15},{8,16},{9,17... | collective-permute-start | bytes 1179656 | tf_op jit(solution)/shard_map/ppermute | solution.py:34
  43.8 35.2 %copy-start.4 = (bf16[384,512]{1,0:T(8,128)(2,1)}, bf16[384,512]{1,0:T(8,128)(2,1)S(1)}, u32[]{:S(2)}) copy-start(bf16[384,512]{1,0:T(8,128)(2,1)S(1)} %collective-permute-done.11.refs_4_.refs_15_) | copy-start | bytes 1179652
  43.8 25.7 %collective-permute-start.19 = (bf16[512,512]{1,0:T(8,128)(2,1)S(1)}, bf16[512,512]{1,0:T(8,128)(2,1)S(1)}, u32[]{:S(2)}, u32[]{:S(2)}) collective-permute-start(bf16[512,512]{1,0:T(8,128)(2,1)S(1)} %constant_dynamic-update-slice_fusion.2.refs_4_.refs_19_), channel_id=1, source_target_pairs={{0,6},{1,7},{2,0},{3,1},{4,2},{5,3},{6,4},{7,5},{8,14},{9,15},{10,... | collective-permute-start | bytes 1572872 | tf_op jit(solution)/shard_map/ppermute | solution.py:34
  46.5 12.0 %copy-start.6 = (bf16[384,512]{1,0:T(8,128)(2,1)}, bf16[384,512]{1,0:T(8,128)(2,1)S(1)}, u32[]{:S(2)}) copy-start(bf16[384,512]{1,0:T(8,128)(2,1)S(1)} %collective-permute-done.7.refs_4_.refs_8_) | copy-start | bytes 1179652
  46.5 12.1 %collective-permute-start.12 = (bf16[384,512]{1,0:T(8,128)(2,1)S(1)}, bf16[384,512]{1,0:T(8,128)(2,1)S(1)}, u32[]{:S(2)}, u32[]{:S(2)}) collective-permute-start(bf16[384,512]{1,0:T(8,128)(2,1)S(1)} %collective-permute-done.11.refs_4_.refs_15_), channel_id=1, source_target_pairs={{0,24},{1,25},{2,26},{3,27},{4,28},{5,29},{6,30},{7,31},{8,0},{9,1... | collective-permute-start | bytes 1179656 | tf_op jit(solution)/shard_map/ppermute | solution.py:34
  48.2 10.3 %copy-start.8 = (bf16[384,512]{1,0:T(8,128)(2,1)}, bf16[384,512]{1,0:T(8,128)(2,1)S(1)}, u32[]{:S(2)}) copy-start(bf16[384,512]{1,0:T(8,128)(2,1)S(1)} %collective-permute-done.9.refs_6_.refs_10_) | copy-start | bytes 1179652
  48.2 18.2 %collective-permute-start.6 = (bf16[384,512]{1,0:T(8,128)(2,1)S(1)}, bf16[384,512]{1,0:T(8,128)(2,1)}, u32[]{:S(2)}, u32[]{:S(2)}) collective-permute-start(bf16[384,512]{1,0:T(8,128)(2,1)S(1)} %collective-permute-done.5.refs_4_.refs_11_), channel_id=1, source_target_pairs={{0,2},{1,3},{2,4},{3,5},{4,6},{5,7},{6,0},{7,1},{8,10},{9,11},{10,... | collective-permute-start | bytes 1179656 | tf_op jit(solution)/shard_map/ppermute | solution.py:34
  49.5 24.0 %copy-start.10 = (bf16[384,512]{1,0:T(8,128)(2,1)}, bf16[384,512]{1,0:T(8,128)(2,1)S(1)}, u32[]{:S(2)}) copy-start(bf16[384,512]{1,0:T(8,128)(2,1)S(1)} %collective-permute-done.10.refs_5_.refs_12_) | copy-start | bytes 1179652
  49.5 20.6 %collective-permute-start.14 = (bf16[384,512]{1,0:T(8,128)(2,1)S(1)}, bf16[384,512]{1,0:T(8,128)(2,1)S(1)}, u32[]{:S(2)}, u32[]{:S(2)}) collective-permute-start(bf16[384,512]{1,0:T(8,128)(2,1)S(1)} %collective-permute-done.5.refs_4_.refs_11_), channel_id=1, source_target_pairs={{0,24},{1,25},{2,26},{3,27},{4,28},{5,29},{6,30},{7,31},{8,0},{9,1... | collective-permute-start | bytes 1179656 | tf_op jit(solution)/shard_map/ppermute | solution.py:34
  50.9 22.5 %collective-permute-start.15 = (bf16[384,512]{1,0:T(8,128)(2,1)S(1)}, bf16[384,512]{1,0:T(8,128)(2,1)S(1)}, u32[]{:S(2)}, u32[]{:S(2)}) collective-permute-start(bf16[384,512]{1,0:T(8,128)(2,1)S(1)} %collective-permute-done.10.refs_5_.refs_12_), channel_id=1, source_target_pairs={{0,8},{1,9},{2,10},{3,11},{4,12},{5,13},{6,14},{7,15},{8,16},{9,17... | collective-permute-start | bytes 1179656 | tf_op jit(solution)/shard_map/ppermute | solution.py:34
  58.6 20.5 %copy-start.12 = (bf16[384,512]{1,0:T(8,128)(2,1)}, bf16[384,512]{1,0:T(8,128)(2,1)S(1)}, u32[]{:S(2)}) copy-start(bf16[384,512]{1,0:T(8,128)(2,1)S(1)} %collective-permute-done.12.refs_6_.refs_17_) | copy-start | bytes 1179652
  58.6 19.4 %collective-permute-start.16 = (bf16[384,512]{1,0:T(8,128)(2,1)S(1)}, bf16[384,512]{1,0:T(8,128)(2,1)S(1)}, u32[]{:S(2)}, u32[]{:S(2)}) collective-permute-start(bf16[384,512]{1,0:T(8,128)(2,1)S(1)} %collective-permute-done.11.refs_4_.refs_15_), channel_id=1, source_target_pairs={{0,8},{1,9},{2,10},{3,11},{4,12},{5,13},{6,14},{7,15},{8,16},{9,17... | collective-permute-start | bytes 1179656 | tf_op jit(solution)/shard_map/ppermute | solution.py:34
  66.4 12.7 %collective-permute-start.17 = (bf16[384,512]{1,0:T(8,128)(2,1)S(1)}, bf16[384,512]{1,0:T(8,128)(2,1)S(1)}, u32[]{:S(2)}, u32[]{:S(2)}) collective-permute-start(bf16[384,512]{1,0:T(8,128)(2,1)S(1)} %collective-permute-done.12.refs_6_.refs_17_), channel_id=1, source_target_pairs={{0,24},{1,25},{2,26},{3,27},{4,28},{5,29},{6,30},{7,31},{8,0},{9,1... | collective-permute-start | bytes 1179656 | tf_op jit(solution)/shard_map/ppermute | solution.py:34
  69.5 14.0 %collective-permute-start.13 = (bf16[384,512]{1,0:T(8,128)(2,1)}, bf16[384,512]{1,0:T(8,128)(2,1)}, u32[]{:S(2)}, u32[]{:S(2)}) collective-permute-start(bf16[384,512]{1,0:T(8,128)(2,1)} %collective-permute-done.6.refs_4_.refs_23_), channel_id=1, source_target_pairs={{0,8},{1,9},{2,10},{3,11},{4,12},{5,13},{6,14},{7,15},{8,16},{9,17... | collective-permute-start | bytes 1179656 | tf_op jit(solution)/shard_map/ppermute | solution.py:34
  70.0 7.9 %copy-start.14 = (bf16[384,512]{1,0:T(8,128)(2,1)}, bf16[384,512]{1,0:T(8,128)(2,1)S(1)}, u32[]{:S(2)}) copy-start(bf16[384,512]{1,0:T(8,128)(2,1)S(1)} %collective-permute-done.14.refs_6_.refs_13_) | copy-start | bytes 1179652
  70.0 23.6 %collective-permute-start.20 = (bf16[512,512]{1,0:T(8,128)(2,1)S(1)}, bf16[512,512]{1,0:T(8,128)(2,1)}, u32[]{:S(2)}, u32[]{:S(2)}) collective-permute-start(bf16[512,512]{1,0:T(8,128)(2,1)S(1)} %collective-permute-done.19.refs_6_.refs_21_), channel_id=1, source_target_pairs={{0,6},{1,7},{2,0},{3,1},{4,2},{5,3},{6,4},{7,5},{8,14},{9,15},{10,... | collective-permute-start | bytes 1572872 | tf_op jit(solution)/shard_map/ppermute | solution.py:34
  73.5 23.2 %collective-permute-start.18 = (bf16[512,512]{1,0:T(8,128)(2,1)S(1)}, bf16[512,512]{1,0:T(8,128)(2,1)}, u32[]{:S(2)}, u32[]{:S(2)}) collective-permute-start(bf16[512,512]{1,0:T(8,128)(2,1)S(1)} %constant_dynamic-update-slice_fusion.2.refs_4_.refs_19_), channel_id=1, source_target_pairs={{0,2},{1,3},{2,4},{3,5},{4,6},{5,7},{6,0},{7,1},{8,10},{9,11},{10,... | collective-permute-start | bytes 1572872 | tf_op jit(solution)/shard_map/ppermute | solution.py:34
  78.0 5.5 %copy-start.18 = (bf16[384,512]{1,0:T(8,128)(2,1)}, bf16[384,512]{1,0:T(8,128)(2,1)S(1)}, u32[]{:S(2)}) copy-start(bf16[384,512]{1,0:T(8,128)(2,1)S(1)} %collective-permute-done.16.refs_5_.refs_16_) | copy-start | bytes 1179652
  78.0 24.2 %collective-permute-start.21 = (bf16[384,512]{1,0:T(8,128)(2,1)}, bf16[384,512]{1,0:T(8,128)(2,1)}, u32[]{:S(2)}, u32[]{:S(2)}) collective-permute-start(bf16[384,512]{1,0:T(8,128)(2,1)} %collective-permute-done.6.refs_4_.refs_23_), channel_id=1, source_target_pairs={{0,24},{1,25},{2,26},{3,27},{4,28},{5,29},{6,30},{7,31},{8,0},{9,1... | collective-permute-start | bytes 1179656 | tf_op jit(solution)/shard_map/ppermute | solution.py:34
  83.6 18.6 %collective-permute-start.22 = (bf16[384,512]{1,0:T(8,128)(2,1)}, bf16[384,512]{1,0:T(8,128)(2,1)}, u32[]{:S(2)}, u32[]{:S(2)}) collective-permute-start(bf16[384,512]{1,0:T(8,128)(2,1)} %collective-permute-done.13.refs_5_.refs_24_), channel_id=1, source_target_pairs={{0,8},{1,9},{2,10},{3,11},{4,12},{5,13},{6,14},{7,15},{8,16},{9,17... | collective-permute-start | bytes 1179656 | tf_op jit(solution)/shard_map/ppermute | solution.py:34
  102.0 5.2 %copy-start.1 = (bf16[384,512]{1,0:T(8,128)(2,1)S(1)}, bf16[384,512]{1,0:T(8,128)(2,1)}, u32[]{:S(2)}) copy-start(bf16[384,512]{1,0:T(8,128)(2,1)} %copy-done) | copy-start | bytes 1179652
  102.0 5.2 %copy-start.3 = (bf16[384,512]{1,0:T(8,128)(2,1)S(1)}, bf16[384,512]{1,0:T(8,128)(2,1)}, u32[]{:S(2)}) copy-start(bf16[384,512]{1,0:T(8,128)(2,1)} %copy-done.2) | copy-start | bytes 1179652
  102.0 5.2 %copy-start.5 = (bf16[384,512]{1,0:T(8,128)(2,1)S(1)}, bf16[384,512]{1,0:T(8,128)(2,1)}, u32[]{:S(2)}) copy-start(bf16[384,512]{1,0:T(8,128)(2,1)} %copy-done.4) | copy-start | bytes 1179652
  102.0 5.2 %copy-start.7 = (bf16[384,512]{1,0:T(8,128)(2,1)S(1)}, bf16[384,512]{1,0:T(8,128)(2,1)}, u32[]{:S(2)}) copy-start(bf16[384,512]{1,0:T(8,128)(2,1)} %copy-done.6) | copy-start | bytes 1179652
  102.0 5.2 %copy-start.9 = (bf16[384,512]{1,0:T(8,128)(2,1)S(1)}, bf16[384,512]{1,0:T(8,128)(2,1)}, u32[]{:S(2)}) copy-start(bf16[384,512]{1,0:T(8,128)(2,1)} %copy-done.8) | copy-start | bytes 1179652
  102.1 5.2 %copy-start.11 = (bf16[384,512]{1,0:T(8,128)(2,1)S(1)}, bf16[384,512]{1,0:T(8,128)(2,1)}, u32[]{:S(2)}) copy-start(bf16[384,512]{1,0:T(8,128)(2,1)} %copy-done.10) | copy-start | bytes 1179652
  102.1 5.2 %copy-start.13 = (bf16[384,512]{1,0:T(8,128)(2,1)S(1)}, bf16[384,512]{1,0:T(8,128)(2,1)}, u32[]{:S(2)}) copy-start(bf16[384,512]{1,0:T(8,128)(2,1)} %copy-done.12) | copy-start | bytes 1179652
  111.8 24.8 %all-to-all-start = ((bf16[32,24,256]{2,1,0:T(8,128)(2,1)}), bf16[32,24,256]{2,1,0:T(8,128)(2,1)S(1)}, u32[]{:S(2)}, u32[]{:S(2)}) async-start(bf16[32,24,256]{2,1,0:T(8,128)(2,1)} %bitcast.5), calls=%async_computation | async-start | bytes 786432 | tf_op jit(solution)/shard_map/all_to_all | solution.py:367
  118.0 7.1 %collective-permute-start.23 = (bf16[64,256]{1,0:T(8,128)(2,1)S(1)}, bf16[64,256]{1,0:T(8,128)(2,1)S(1)}, u32[]{:S(2)}, u32[]{:S(2)}) collective-permute-start(bf16[64,256]{1,0:T(8,128)(2,1)S(1)} %get-tuple-element.42), channel_id=1, source_target_pairs={{0,32},{32,0},{64,96},{96,64},{128,160},{160,128},{192,224},{224,1... | collective-permute-start | bytes 98312 | tf_op jit(solution)/shard_map/ppermute | solution.py:369
  119.6 10.8 %collective-permute-start.24 = (bf16[64,256]{1,0:T(8,128)(2,1)S(1)}, bf16[64,256]{1,0:T(8,128)(2,1)S(1)}, u32[]{:S(2)}, u32[]{:S(2)}) collective-permute-start(bf16[64,256]{1,0:T(8,128)(2,1)S(1)} %get-tuple-element.43), channel_id=1, source_target_pairs={{0,64},{32,96},{64,0},{96,32},{128,192},{160,224},{192,128},{224,1... | collective-permute-start | bytes 98312 | tf_op jit(solution)/shard_map/ppermute | solution.py:369
  122.5 7.9 %collective-permute-start.25 = (bf16[64,256]{1,0:T(8,128)(2,1)S(1)}, bf16[64,256]{1,0:T(8,128)(2,1)S(1)}, u32[]{:S(2)}, u32[]{:S(2)}) collective-permute-start(bf16[64,256]{1,0:T(8,128)(2,1)S(1)} %get-tuple-element.44), channel_id=1, source_target_pairs={{0,96},{32,64},{64,32},{96,0},{128,224},{160,192},{192,160},{224,1... | collective-permute-start | bytes 98312 | tf_op jit(solution)/shard_map/ppermute | solution.py:369
  122.8 7.6 %collective-permute-start.26 = (bf16[64,256]{1,0:T(8,128)(2,1)S(1)}, bf16[64,256]{1,0:T(8,128)(2,1)S(1)}, u32[]{:S(2)}, u32[]{:S(2)}) collective-permute-start(bf16[64,256]{1,0:T(8,128)(2,1)S(1)} %get-tuple-element.45), channel_id=1, source_target_pairs={{0,128},{32,160},{64,192},{96,224},{128,0},{160,32},{192,64},{224,... | collective-permute-start | bytes 98312 | tf_op jit(solution)/shard_map/ppermute | solution.py:369
  125.0 7.2 %collective-permute-start.27 = (bf16[64,256]{1,0:T(8,128)(2,1)S(1)}, bf16[64,256]{1,0:T(8,128)(2,1)S(1)}, u32[]{:S(2)}, u32[]{:S(2)}) collective-permute-start(bf16[64,256]{1,0:T(8,128)(2,1)S(1)} %get-tuple-element.46), channel_id=1, source_target_pairs={{0,160},{32,128},{64,224},{96,192},{128,32},{160,0},{192,96},{224,... | collective-permute-start | bytes 98312 | tf_op jit(solution)/shard_map/ppermute | solution.py:369
  125.0 9.7 %collective-permute-start.28 = (bf16[64,256]{1,0:T(8,128)(2,1)S(1)}, bf16[64,256]{1,0:T(8,128)(2,1)S(1)}, u32[]{:S(2)}, u32[]{:S(2)}) collective-permute-start(bf16[64,256]{1,0:T(8,128)(2,1)S(1)} %get-tuple-element.47), channel_id=1, source_target_pairs={{0,192},{32,224},{64,128},{96,160},{128,64},{160,96},{192,0},{224,... | collective-permute-start | bytes 98312 | tf_op jit(solution)/shard_map/ppermute | solution.py:369
  130.4 6.0 %collective-permute-start.29 = (bf16[64,256]{1,0:T(8,128)(2,1)S(1)}, bf16[64,256]{1,0:T(8,128)(2,1)S(1)}, u32[]{:S(2)}, u32[]{:S(2)}) collective-permute-start(bf16[64,256]{1,0:T(8,128)(2,1)S(1)} %get-tuple-element.48), channel_id=1, source_target_pairs={{0,224},{32,192},{64,160},{96,128},{128,96},{160,64},{192,32},{224... | collective-permute-start | bytes 98312 | tf_op jit(solution)/shard_map/ppermute | solution.py:369
  136.4 1.3 collective-permute-start.30
  (11 other events, 45.3 us)

commit v4 on v3

--- a/solution.py
+++ b/solution.py
@@ -10,7 +10,8 @@
 NX, NZ, NC = 4, 4, 2
 POLES = 8
 B = 256
-HALF = 128
+TOP = 128
+SIZES = (TOP, B - TOP)
 GRID = ("row", "col")
 MIB = 1024 * 1024
 LIMIT = 20
@@ -27,6 +28,30 @@
 def shift(value, dx, dz, dc=0):
     perm = [
         (place(x, z, c), place(x + dx, z + dz, c + dc))
+        for x in range(NX)
+        for z in range(NZ)
+        for c in range(NC)
+    ]
+    return lax.ppermute(value, GRID, perm)
+
+
+def alternate(fwd, bwd, core, dx, dz):
+    perm = [
+        (place(x, z, c), place(x + (dx if c == 0 else -dx), z + (dz if c == 0 else -dz), c))
+        for x in range(NX)
+        for z in range(NZ)
+        for c in range(NC)
+    ]
+    return lax.ppermute(jnp.where(core == 0, fwd, bwd), GRID, perm)
+
+
+def side(z, core):
+    return 1 - 2 * ((z + core) % 2)
+
+
+def pair(value, turn):
+    perm = [
+        (place(x, z, c), place(x, z + turn * side(z, c), c))
         for x in range(NX)
         for z in range(NZ)
         for c in range(NC)
@@ -82,8 +107,8 @@
     def store(mine, other):
         for i in range(2):
             at = slice(i * B, (i + 1) * B)
-            top[:, at] = mine[i][:HALF]
-            rest[:, at] = mine[i][HALF:]
+            top[:, at] = mine[i][:TOP]
+            rest[:, at] = mine[i][TOP:]
             give[:, at] = other[i]
 
     @pl.when(dev % NC == 0)
@@ -96,23 +121,27 @@
 
 
 def prepare(device, widths, pattern, factor):
-    half = jax.ShapeDtypeStruct((HALF, 2 * B), jnp.bfloat16)
+    shapes = [jax.ShapeDtypeStruct((n, 2 * B), jnp.bfloat16) for n in SIZES + (B,)]
     return pl.pallas_call(
         prepare_body,
         in_specs=[SMEM, SMEM, SMEM, VMEM],
         out_specs=[VMEM] * 3,
-        out_shape=[half, half, jax.ShapeDtypeStruct((B, 2 * B), jnp.bfloat16)],
+        out_shape=shapes,
         compiler_params=params(16),
     )(device, widths, pattern, factor)
 
 
-def gemm_body(segments, chunks, has_acc, *refs):
+def gemm_body(segments, has_acc, *refs):
     device, own, sib = refs[:3]
     acc = refs[3] if has_acc else None
-    dev = device[0]
+    pieces = refs[3 + has_acc : 3 + has_acc + len(segments)]
+    out, *scratch = refs[3 + has_acc + len(segments) :]
+    waits = gemm_fetch(segments, device[0], own, sib, pieces, *scratch)
+    gemm_sum(waits, acc, out, *scratch[:2])
+
+
+def gemm_fetch(segments, dev, own, sib, pieces, a_buf, l_buf, a_sem, l_sem):
     core, here_x, here_z = dev % NC, dev // (NZ * NC), dev // NC % NZ
-    pieces = refs[3 + has_acc : 3 + has_acc + len(segments)]
-    out, a_buf, l_buf, a_sem, l_sem = refs[3 + has_acc + len(segments) :]
     waits = []
     at, s = 0, 0
     for i, rows in enumerate(segments):
@@ -120,9 +149,10 @@
         copy = pltpu.make_async_copy(pieces[i], l_buf.at[pl.ds(at, total)], l_sem.at[i])
         copy.start()
         mine = [copy]
-        for ox, oz, same, low, n in rows:
-            block = place(here_x + ox, here_z + oz, core if same else 1 - core)
-            source = pl.ds(pl.multiple_of(block * B + low, HALF), n)
+        for ox, oz, sided, same, low, n in rows:
+            go = oz * side(here_z, core) if sided else oz
+            block = place(here_x + ox, here_z + go, core if same else 1 - core)
+            source = pl.ds(pl.multiple_of(block * B + low, 32), n)
             for j, a in enumerate((own, sib)):
                 copy = pltpu.make_async_copy(
                     a.at[:, source], a_buf.at[2 * j : 2 * j + 2, pl.ds(at, n)], a_sem.at[j, s]
@@ -131,8 +161,12 @@
                 mine.append(copy)
             at, s = at + n, s + 1
         waits.append((mine, at))
-    begin, done = 0, 0
-    for chunk in chunks:
+    return waits
+
+
+def gemm_sum(waits, acc, out, a_buf, l_buf):
+    begin, done, chunk = 0, 0, 2
+    while done < len(waits):
         for i in range(done, done + chunk):
             for copy in waits[i][0]:
                 copy.wait()
@@ -142,36 +176,43 @@
             rows = slice(q * B, (q + 1) * B)
             if begin:
                 out[rows] += part
-            elif has_acc:
+            elif acc is not None:
                 out[rows] = acc[rows] + part
             else:
                 out[rows] = part
         begin, done = end, done + chunk
 
 
+def gemm_scratch(segments):
+    depth = sum(size for rows in segments for *_, size in rows)
+    return [
+        pltpu.VMEM((4, depth, B), jnp.bfloat16),
+        pltpu.VMEM((depth, 2 * B), jnp.bfloat16),
+        pltpu.SemaphoreType.DMA((2, sum(map(len, segments)))),
+        pltpu.SemaphoreType.DMA((len(segments),)),
+    ]
+
+
 def gemm(device, own, sib, acc, pieces, segments):
-    depth = sum(size for rows in segments for *_, size in rows)
-    count = sum(map(len, segments))
     has_acc = acc is not None
     return pl.pallas_call(
-        functools.partial(gemm_body, segments, (2, 2), has_acc),
+        functools.partial(gemm_body, segments, has_acc),
         in_specs=[SMEM, HBM, HBM] + [VMEM] * has_acc + [ANY] * len(pieces),
         out_specs=VMEM,
         out_shape=jax.ShapeDtypeStruct((4 * B, 2 * B), jnp.float32),
-        scratch_shapes=[
-            pltpu.VMEM((4, depth, B), jnp.bfloat16),
-            pltpu.VMEM((depth, 2 * B), jnp.bfloat16),
-            pltpu.SemaphoreType.DMA((2, count)),
-            pltpu.SemaphoreType.DMA((len(pieces),)),
-        ],
+        scratch_shapes=gemm_scratch(segments),
         compiler_params=params(LIMIT),
     )(device, own, sib, *([acc] if has_acc else []), *pieces)
 
 
-def finish_body(sources, *refs):
-    device, widths, owner, assign, weights, acc, dinv = refs[:7]
-    pieces = refs[7 : 7 + len(sources)]
-    shared, *parts_out, own, diag, weighted, sem = refs[7 + len(sources) :]
+def finish_body(sources, segments, *refs):
+    device, widths, owner, assign, weights, acc, dinv, own_inverse, sib_inverse = refs[:9]
+    pieces = refs[9 : 9 + len(sources)]
+    shared = refs[9 + len(sources)]
+    parts_out = refs[10 + len(sources) : 10 + len(sources) + POLES]
+    total, own, diag, weighted, sem, *scratch = refs[10 + len(sources) + POLES :]
+    last = pieces[len(sources) - len(segments) :]
+    fetched = gemm_fetch(segments, device[0], own_inverse, sib_inverse, last, *scratch)
     dev, pole = device[0], device[1]
     core = dev % NC
     here_x, here_z = dev // (NZ * NC), dev // NC % NZ
@@ -183,23 +224,27 @@
         want = owner[block]
         chip, same = want // NC, want % NC == core
         for h in range(2):
-            target = own.at[pl.ds(j * B + h * HALF, HALF)]
+            size = SIZES[h]
+            target = own.at[pl.ds(j * B + h * TOP, size)]
             for piece, rows in zip(pieces, sources, strict=True):
-                for at, is_same, part, (ox, oz) in rows:
+                for at, is_same, part, (ox, oz, sided) in rows:
                     if part != h:
                         continue
-                    here = place(here_x + ox, here_z + oz, 0) // NC
+                    go = oz * side(here_z, core) if sided else oz
+                    here = place(here_x + ox, here_z + go, 0) // NC
 
                     @pl.when((here == chip) & (same == is_same))
-                    def _(piece=piece, at=at, target=target, j=j, h=h):
+                    def _(piece=piece, at=at, size=size, target=target, j=j, h=h):
                         pltpu.make_async_copy(
-                            piece.at[pl.ds(at, HALF)], target, sem.at[j, h]
+                            piece.at[pl.ds(at, size)], target, sem.at[j, h]
                         ).start()
 
             waits.append(
-                pltpu.make_async_copy(pieces[0].at[pl.ds(0, HALF)], target, sem.at[j, h])
+                pltpu.make_async_copy(pieces[0].at[pl.ds(0, size)], target, sem.at[j, h])
             )
 
+    gemm_sum(fetched, acc, total, *scratch[:2])
+    acc = total
     wr, wi = weights[assign[0], 0], weights[assign[0], 1]
     parts = []
     for j in range(2):
@@ -242,23 +287,27 @@
     shared[...] = diag[...].astype(jnp.bfloat16)
 
 
-def finish(device, widths, owner, assign, weights, acc, dinv, pieces, sources, total):
+def finish(
+    device, widths, owner, assign, weights, acc, dinv, own, sib, pieces, sources, segments, total
+):
     return pl.pallas_call(
-        functools.partial(finish_body, sources),
-        in_specs=[SMEM] * 5 + [VMEM] * 2 + [ANY] * len(pieces),
+        functools.partial(finish_body, sources, segments),
+        in_specs=[SMEM] * 5 + [VMEM] * 2 + [HBM] * 2 + [ANY] * len(pieces),
         out_specs=[VMEM] * (1 + POLES),
         out_shape=[
             jax.ShapeDtypeStruct((n, B), jnp.bfloat16)
             for n in (total,) + (2 * B // POLES,) * POLES
         ],
         scratch_shapes=[
+            pltpu.VMEM((4 * B, 2 * B), jnp.float32),
             pltpu.VMEM((2 * B, 2 * B), jnp.bfloat16),
             pltpu.VMEM((total, B), jnp.float32),
             pltpu.VMEM((B, B), jnp.bfloat16),
             pltpu.SemaphoreType.DMA((2, 2)),
+            *gemm_scratch(segments),
         ],
         compiler_params=params(LIMIT),
-    )(device, widths, owner, assign, weights, acc, dinv, *pieces)
+    )(device, widths, owner, assign, weights, acc, dinv, own, sib, *pieces)
 
 
 def spread_body(device, widths, got, panel, diag):
@@ -301,29 +350,29 @@
     taken = shift(give, 0, 0, 1)
     pieces, sources = [], []
 
-    def multiply(acc, held, offsets, kind):
-        parts = ((True, HALF, HALF),) if kind else ((True, 0, HALF), (False, 0, B))
+    def listing(held, offsets, kind):
+        parts = ((True, TOP, B - TOP),) if kind else ((True, 0, TOP), (False, 0, B))
         segments = []
         for piece, some in zip(held, offsets, strict=True):
             rows, listed, at = [], [], 0
-            for ox, oz in some:
+            for ox, oz, sided in some:
                 for same, low, size in parts:
-                    rows.append((ox, oz, same, low, size))
-                    for k in range(0, size, HALF):
-                        listed.append((at + k, same, (low + k) // HALF, (ox, oz)))
+                    rows.append((ox, oz, sided, same, low, size))
+                    for h, begin in enumerate((0, TOP)):
+                        if low <= begin < low + size:
+                            listed.append((at + begin - low, same, h, (ox, oz, sided)))
                     at += size
-            pieces.append(piece)
+            pieces.append(pltpu.with_memory_space_constraint(piece, pltpu.HBM))
             sources.append(tuple(listed))
             segments.append(tuple(rows))
-        return gemm(device, own_inverse, sib_inverse, acc, held, tuple(segments))
+        return tuple(segments)
 
     def after(values, *others):
         values, _ = lax.optimization_barrier((values, others))
         return values
 
-    def along_x(oz):
-        return [[(ox, oz)] for ox in (0, -1, 1, 2)]
-
+    orders = (0, -1, 1, 2)
+    core = dev % NC
     rest_f, rest_b = shift(rest, 1, 0), shift(rest, -1, 0)
     main = jnp.concatenate([top, taken], 0)
     rest_f, rest_b = after((rest_f, rest_b), main)
@@ -332,7 +381,7 @@
     main_x = after(main, rest_f, rest_b)
     main_f, main_b = shift(main_x, 1, 0), shift(main_x, -1, 0)
     across = jnp.concatenate([rest, rest_f, rest_b, rest_far], 0)
-    sib_inverse = shift(after(inverse[0], rest_far), 0, 0, 1)
+    sib_inverse = shift(after(inverse[0], main), 0, 0, 1)
     sib_inverse = pltpu.with_memory_space_constraint(sib_inverse, pltpu.HBM)
     main_far = shift(main_b, -1, 0)
     z_far = shift(zf, 0, 1)
@@ -340,27 +389,31 @@
     zff, zbb = shift(zf, 1, 0), shift(zb, -1, 0)
     zf_late, zb_late = after((zf, zb), main_far)
     zfb, zbf = shift(zf_late, -1, 0), shift(zb_late, 1, 0)
-    acc = multiply(None, (main, main_f, main_b, main_far), along_x(0), 0)
+    held = (main, main_f, main_b, main_far)
+    segments = listing(held, [[(ox, 0, False)] for ox in orders], 0)
+    acc = gemm(device, own_inverse, sib_inverse, None, held, segments)
     z_far, acc = after((z_far, acc), zff, zbb)
     far_f, far_b = shift(z_far, 1, 0), shift(z_far, -1, 0)
     across_f = shift(after(across, z_far), 0, 1)
     zf_far, zb_far = shift(zff, 1, 0), shift(zbb, -1, 0)
     across_far = shift(across_b, 0, -1)
-    acc = multiply(acc, (zf, zff, zfb, zf_far), along_x(-1), 0)
-    acc = multiply(acc, (zb, zbf, zbb, zb_far), along_x(1), 0)
+    held = (zf, zff, zfb, zf_far)
+    segments = listing(held, [[(ox, -1, False)] for ox in orders], 0)
+    acc = gemm(device, own_inverse, sib_inverse, acc, held, segments)
+    held = (zb, zbf, zbb, zb_far)
+    segments = listing(held, [[(ox, 1, False)] for ox in orders], 0)
+    acc = gemm(device, own_inverse, sib_inverse, acc, held, segments)
     far_f, acc = after((far_f, acc))
     far_far = shift(far_f, 1, 0)
-    acc = multiply(
-        acc,
-        (across, across_f, across_b, across_far),
-        [[(ox, oz) for ox in (0, -1, 1, 2)] for oz in (0, -1, 1, 2)],
-        1,
-    )
-    acc = multiply(acc, (z_far, far_f, far_b, far_far), along_x(2), 0)
+    held = (across, across_f, across_b, across_far)
+    segments = listing(held, [[(ox, oz, False) for ox in orders] for oz in orders], 1)
+    held = (z_far, far_f, far_b, far_far)
+    segments += listing(held, [[(ox, 2, False)] for ox in orders], 0)
 
     shared, *parts = finish(
         device, widths, owner, assign, pole_weights, acc,
-        diag_inverse[0].astype(jnp.float32), pieces, tuple(sources), total,
+        diag_inverse[0].astype(jnp.float32), own_inverse, sib_inverse,
+        pieces, tuple(sources), segments, total,
     )
 
     shared = shared.reshape(NX * NZ * NC, depth, B)

time: 155 us -> 146 us (0.942)
  Pallas kernels: 30.7 us -> 26.8 us
  starting transfers between devices: 51.1 us -> 48.6 us
    pallas_call x6 -> x4, Pallas kernels: 28 us -> 24.1 us  [the longest x3 13.2 us: gemm(): pl.pallas_call(functools.partial(gemm_body, segments, has_acc), in_specs=...]
    ppermute x24, starting transfers between devices: 32.6 us -> 29.5 us  [shift(): return lax.ppermute(value, GRID, perm)]
    unnamed x60 -> x48, local copies, waits for them, and re-layouts: 6.17 us -> 6.06 us
  transfers between devices with their start and end apart: 32 -> 32, of which waited for: 15 -> 16; matrix products, arithmetic and copies ran while one was open for 1% -> 0% of each run, Pallas kernels for 12% -> 9%
where the time goes in v4:
time: 146 us
  starting transfers between devices  48.6 us (33%)
  waiting for transfers between devices  47.4 us (32%)
  Pallas kernels  26.8 us (18%)
  blocking collectives  15.2 us (10%)
  local copies, waits for them, and re-layouts  6.15 us (4%)
  between operations  1.66 us (1%)
    ppermute x24, waiting for transfers between devices, shift(): return lax.ppermute(value, GRID, perm)  41.3 us
    ppermute x24, starting transfers between devices, shift(): return lax.ppermute(value, GRID, perm)  29.5 us
    all_to_all x1, blocking collectives, local(): lax.all_to_all(jnp.broadcast_to(both[None], (POLES,) + both.shape), 'pole...  15.2 us
    pallas_call x3, Pallas kernels, gemm(): pl.pallas_call(functools.partial(gemm_body, segments, has_acc), in_specs=...  13.2 us
    ppermute x7, starting transfers between devices, local(): lax.ppermute(part, 'pole', [(p, p ^ d) for p in range(POLES)])  12.3 us
    pallas_call x1, Pallas kernels, finish(): pl.pallas_call(functools.partial(finish_body, sources, segments), in_spec...  10.9 us
    all_to_all x1, starting transfers between devices, local(): shared = lax.all_to_all(shared, GRID, 0, 0, tiled=True)  6.71 us
    unnamed x48, local copies, waits for them, and re-layouts  6.06 us
  transfers between devices with their start and end apart: 32, of which 16 were waited for; matrix products, arithmetic and copies ran while one was open for 0% of the time, Pallas kernels for 9%

profile of v4, /device:TPU:2, one launch (start us, length us, event | category | flops | bytes accessed | tf_op | source)
XLA Modules:
  0.0 145.9 jit_solution(1773372066570497505)
XLA Ops:
  0.6 0.8 copy.10.pattern
  1.5 1.1 copy-done.12
  2.6 0.7 copy-done.13
  3.3 1.1 shard_map.95
  4.5 1.5 %collective-permute-done = bf16[256,512]{1,0:T(8,128)(2,1)S(1)} collective-permute-done((bf16[256,512]{1,0:T(8,128)(2,1)S(1)}, bf16[256,512]{1,0:T(8,128)(2,1)S(1)}, u32[]{:S(2)}, u32[]{:S(2)}) %collective-permute-start) | collective-permute-done | bytes 262176 | tf_op jit(solution)/shard_map/ppermute | solution.py:35
  6.1 0.2 collective-permute-start.3
  6.3 2.3 %collective-permute-start.5 = (bf16[128,512]{1,0:T(8,128)(2,1)S(1)}, bf16[128,512]{1,0:T(8,128)(2,1)S(1)}, u32[]{:S(2)}, u32[]{:S(2)}) collective-permute-start(bf16[128,512]{1,0:T(8,128)(2,1)S(1)} %get-tuple-element.29), channel_id=1, source_target_pairs={{0,24},{1,25},{2,26},{3,27},{4,28},{5,29},{6,30},{7,31},{8,0},{9,1... | collective-permute-start | bytes 393224 | tf_op jit(solution)/shard_map/ppermute | solution.py:35
  8.6 3.5 %collective-permute-done.5 = bf16[128,512]{1,0:T(8,128)(2,1)S(1)} collective-permute-done((bf16[128,512]{1,0:T(8,128)(2,1)S(1)}, bf16[128,512]{1,0:T(8,128)(2,1)S(1)}, u32[]{:S(2)}, u32[]{:S(2)}) %collective-permute-start.5) | collective-permute-done | bytes 131104 | tf_op jit(solution)/shard_map/ppermute | solution.py:35
  12.1 2.0 %collective-permute-done.4 = bf16[128,512]{1,0:T(8,128)(2,1)S(1)} collective-permute-done((bf16[128,512]{1,0:T(8,128)(2,1)S(1)}, bf16[128,512]{1,0:T(8,128)(2,1)S(1)}, u32[]{:S(2)}, u32[]{:S(2)}) %collective-permute-start.4) | collective-permute-done | bytes 131104 | tf_op jit(solution)/shard_map/ppermute | solution.py:35
  14.0 2.2 %collective-permute-start.7 = (bf16[384,512]{1,0:T(8,128)(2,1)S(1)}, bf16[384,512]{1,0:T(8,128)(2,1)S(1)}, u32[]{:S(2)}, u32[]{:S(2)}) collective-permute-start(bf16[384,512]{1,0:T(8,128)(2,1)S(1)} %constant_dynamic-update-slice_fusion.refs_3_.refs_9_), channel_id=1, source_target_pairs={{0,24},{1,25},{2,26},{3,27},{4,28},{5,29},{6,30},{7,31},{8,0},{9,1... | collective-permute-start | bytes 1179656 | tf_op jit(solution)/shard_map/ppermute | solution.py:35
  16.3 6.3 %collective-permute-start.10 = (bf16[384,512]{1,0:T(8,128)(2,1)S(1)}, bf16[384,512]{1,0:T(8,128)(2,1)S(1)}, u32[]{:S(2)}, u32[]{:S(2)}) collective-permute-start(bf16[384,512]{1,0:T(8,128)(2,1)S(1)} %constant_dynamic-update-slice_fusion.refs_3_.refs_9_), channel_id=1, source_target_pairs={{0,6},{1,7},{2,0},{3,1},{4,2},{5,3},{6,4},{7,5},{8,14},{9,15},{10,... | collective-permute-start | bytes 1179656 | tf_op jit(solution)/shard_map/ppermute | solution.py:35
  22.7 1.6 %collective-permute-done.7.refs_5_.refs_11_ = bf16[384,512]{1,0:T(8,128)(2,1)S(1)} collective-permute-done((bf16[384,512]{1,0:T(8,128)(2,1)S(1)}, bf16[384,512]{1,0:T(8,128)(2,1)S(1)}, u32[]{:S(2)}, u32[]{:S(2)}) %collective-permute-start.7) | collective-permute-done | bytes 393248 | tf_op jit(solution)/shard_map/ppermute | solution.py:35
  24.3 2.2 %collective-permute-start.8 = (bf16[384,512]{1,0:T(8,128)(2,1)S(1)}, bf16[384,512]{1,0:T(8,128)(2,1)S(1)}, u32[]{:S(2)}, u32[]{:S(2)}) collective-permute-start(bf16[384,512]{1,0:T(8,128)(2,1)S(1)} %collective-permute-done.7.refs_5_.refs_11_), channel_id=1, source_target_pairs={{0,24},{1,25},{2,26},{3,27},{4,28},{5,29},{6,30},{7,31},{8,0},{9,1... | collective-permute-start | bytes 1179656 | tf_op jit(solution)/shard_map/ppermute | solution.py:35
  26.6 11.9 %collective-permute-done.10.refs_4_.refs_17_ = bf16[384,512]{1,0:T(8,128)(2,1)S(1)} collective-permute-done((bf16[384,512]{1,0:T(8,128)(2,1)S(1)}, bf16[384,512]{1,0:T(8,128)(2,1)S(1)}, u32[]{:S(2)}, u32[]{:S(2)}) %collective-permute-start.10) | collective-permute-done | bytes 393248 | tf_op jit(solution)/shard_map/ppermute | solution.py:35
  38.6 3.8 %collective-permute-done.1.refs_4_.refs_13_ = bf16[384,512]{1,0:T(8,128)(2,1)S(1)} collective-permute-done((bf16[384,512]{1,0:T(8,128)(2,1)S(1)}, bf16[384,512]{1,0:T(8,128)(2,1)S(1)}, u32[]{:S(2)}, u32[]{:S(2)}) %collective-permute-start.1) | collective-permute-done | bytes 393248 | tf_op jit(solution)/shard_map/ppermute | solution.py:35
  42.4 0.9 collective-permute-start.19
  43.3 1.9 %collective-permute-start.11 = (bf16[384,512]{1,0:T(8,128)(2,1)S(1)}, bf16[384,512]{1,0:T(8,128)(2,1)S(1)}, u32[]{:S(2)}, u32[]{:S(2)}) collective-permute-start(bf16[384,512]{1,0:T(8,128)(2,1)S(1)} %collective-permute-done.10.refs_4_.refs_17_), channel_id=1, source_target_pairs={{0,24},{1,25},{2,26},{3,27},{4,28},{5,29},{6,30},{7,31},{8,0},{9,1... | collective-permute-start | bytes 1179656 | tf_op jit(solution)/shard_map/ppermute | solution.py:35
  45.2 2.1 %collective-permute-start.2 = (bf16[384,512]{1,0:T(8,128)(2,1)S(1)}, bf16[384,512]{1,0:T(8,128)(2,1)}, u32[]{:S(2)}, u32[]{:S(2)}) collective-permute-start(bf16[384,512]{1,0:T(8,128)(2,1)S(1)} %collective-permute-done.1.refs_4_.refs_13_), channel_id=1, source_target_pairs={{0,2},{1,3},{2,4},{3,5},{4,6},{5,7},{6,0},{7,1},{8,10},{9,11},{10,... | collective-permute-start | bytes 1179656 | tf_op jit(solution)/shard_map/ppermute | solution.py:35
  47.3 6.0 %collective-permute-done.9.refs_5_.refs_14_ = bf16[384,512]{1,0:T(8,128)(2,1)S(1)} collective-permute-done((bf16[384,512]{1,0:T(8,128)(2,1)S(1)}, bf16[384,512]{1,0:T(8,128)(2,1)S(1)}, u32[]{:S(2)}, u32[]{:S(2)}) %collective-permute-start.9) | collective-permute-done | bytes 393248 | tf_op jit(solution)/shard_map/ppermute | solution.py:35
  53.3 3.8 %collective-permute-start.13 = (bf16[384,512]{1,0:T(8,128)(2,1)S(1)}, bf16[384,512]{1,0:T(8,128)(2,1)S(1)}, u32[]{:S(2)}, u32[]{:S(2)}) collective-permute-start(bf16[384,512]{1,0:T(8,128)(2,1)S(1)} %collective-permute-done.1.refs_4_.refs_13_), channel_id=1, source_target_pairs={{0,24},{1,25},{2,26},{3,27},{4,28},{5,29},{6,30},{7,31},{8,0},{9,1... | collective-permute-start | bytes 1179656 | tf_op jit(solution)/shard_map/ppermute | solution.py:35
  57.2 3.3 %copy-done.16 = bf16[2,8192,256]{2,1,0:T(8,128)(2,1)} copy-done((bf16[2,8192,256]{2,1,0:T(8,128)(2,1)}, bf16[2,8192,256]{2,1,0:T(8,128)(2,1)S(1)}, u32[]{:S(2)}) %copy-start.16) | copy-done | bytes 8388632
  60.5 4.3 %shard_map.96.refs_3_ = f32[1024,512]{1,0:T(8,128)S(1)} custom-call(s32[2]{0:T(128)S(1)} %pad_add_fusion.device.refs_0_, bf16[2,8192,256]{2,1,0:T(8,128)(2,1)} %bitcast.10, bf16[2,8192,256]{2,1,0:T(8,128)(2,1)} %copy-done.16, bf16[384,512]{1,0:T(8,128)(2,1)S(1)} %constant_dynamic-update-slice_fusion.refs_3_.refs_9_, ...), custom_call_target="tpu_custom_call" | custom-call | tf_op jit(solution)/shard_map/pallas_call | solution.py:198
  64.9 2.0 %collective-permute-start.16 = (bf16[384,512]{1,0:T(8,128)(2,1)S(1)}, bf16[384,512]{1,0:T(8,128)(2,1)S(1)}, u32[]{:S(2)}, u32[]{:S(2)}) collective-permute-start(bf16[384,512]{1,0:T(8,128)(2,1)S(1)} %collective-permute-done.11.refs_6_.refs_19_), channel_id=1, source_target_pairs={{0,24},{1,25},{2,26},{3,27},{4,28},{5,29},{6,30},{7,31},{8,0},{9,1... | collective-permute-start | bytes 1179656 | tf_op jit(solution)/shard_map/ppermute | solution.py:35
  66.9 0.1 collective-permute-start.12
  67.0 0.3 collective-permute-done.14.refs_7_.refs_16_
  67.3 2.7 %collective-permute-start.18 = (bf16[512,512]{1,0:T(8,128)(2,1)S(1)}, bf16[512,512]{1,0:T(8,128)(2,1)}, u32[]{:S(2)}, u32[]{:S(2)}) collective-permute-start(bf16[512,512]{1,0:T(8,128)(2,1)S(1)} %constant_dynamic-update-slice_fusion.2.refs_21_), channel_id=1, source_target_pairs={{0,2},{1,3},{2,4},{3,5},{4,6},{5,7},{6,0},{7,1},{8,10},{9,11},{10,... | collective-permute-start | bytes 1572872 | tf_op jit(solution)/shard_map/ppermute | solution.py:35
  70.0 4.5 %shard_map.97.refs_3_ = f32[1024,512]{1,0:T(8,128)S(1)} custom-call(s32[2]{0:T(128)S(1)} %pad_add_fusion.device.refs_0_, bf16[2,8192,256]{2,1,0:T(8,128)(2,1)} %bitcast.11, bf16[2,8192,256]{2,1,0:T(8,128)(2,1)} %copy-done.16, f32[1024,512]{1,0:T(8,128)S(1)} %shard_map.96.refs_3_, bf16[384,512]{1,0:T(8,128)(2,1)S(1)} %collective-permute-done.1.refs_4_.refs_13_, ...), custom_call_target="tpu_custom_call" | custom-call | tf_op jit(solution)/shard_map/pallas_call | solution.py:198
  74.6 2.3 %collective-permute-done.16.refs_7_.refs_20_ = bf16[384,512]{1,0:T(8,128)(2,1)S(1)} collective-permute-done((bf16[384,512]{1,0:T(8,128)(2,1)S(1)}, bf16[384,512]{1,0:T(8,128)(2,1)S(1)}, u32[]{:S(2)}, u32[]{:S(2)}) %collective-permute-start.16) | collective-permute-done | bytes 393248 | tf_op jit(solution)/shard_map/ppermute | solution.py:35
  76.9 2.0 %collective-permute-start.21 = (bf16[384,512]{1,0:T(8,128)(2,1)}, bf16[384,512]{1,0:T(8,128)(2,1)}, u32[]{:S(2)}, u32[]{:S(2)}) collective-permute-start(bf16[384,512]{1,0:T(8,128)(2,1)} %collective-permute-done.2.refs_25_), channel_id=1, source_target_pairs={{0,24},{1,25},{2,26},{3,27},{4,28},{5,29},{6,30},{7,31},{8,0},{9,1... | collective-permute-start | bytes 1179656 | tf_op jit(solution)/shard_map/ppermute | solution.py:35
  78.9 4.5 %shard_map.98.refs_5_ = f32[1024,512]{1,0:T(8,128)S(1)} custom-call(s32[2]{0:T(128)S(1)} %pad_add_fusion.device.refs_0_, bf16[2,8192,256]{2,1,0:T(8,128)(2,1)} %bitcast.12, bf16[2,8192,256]{2,1,0:T(8,128)(2,1)} %copy-done.16, f32[1024,512]{1,0:T(8,128)S(1)} %shard_map.97.refs_3_, bf16[384,512]{1,0:T(8,128)(2,1)S(1)} %collective-permute-done.10.refs_4_.refs_17_, ...), custom_call_target="tpu_custom_call" | custom-call | tf_op jit(solution)/shard_map/pallas_call | solution.py:198
  83.4 0.3 collective-permute-start.22
  84.4 0.1 copy.11.refs_4_
  84.5 0.5 collective-permute-done.21.refs_27_
  85.0 6.8 %collective-permute-done.22.refs_28_ = bf16[384,512]{1,0:T(8,128)(2,1)} collective-permute-done((bf16[384,512]{1,0:T(8,128)(2,1)}, bf16[384,512]{1,0:T(8,128)(2,1)}, u32[]{:S(2)}, u32[]{:S(2)}) %collective-permute-start.22) | collective-permute-done | bytes 393248 | tf_op jit(solution)/shard_map/ppermute | solution.py:35
  91.8 10.9 %shard_map.99 = (bf16[768,256]{1,0:T(8,128)(2,1)}, bf16[64,256]{1,0:T(8,128)(2,1)S(1)}, bf16[64,256]{1,0:T(8,128)(2,1)S(1)}, bf16[64,256]{1,0:T(8,128)(2,1)S(1)}...) custom-call(s32[2]{0:T(128)S(1)} %pad_add_fusion.device.refs_0_, ...), custom_call_target="tpu_custom_call" | custom-call | tf_op jit(solution)/shard_map/pallas_call | solution.py:293
  102.7 6.7 %all-to-all-start = ((bf16[32,24,256]{2,1,0:T(8,128)(2,1)}), bf16[32,24,256]{2,1,0:T(8,128)(2,1)S(1)}, u32[]{:S(2)}, u32[]{:S(2)}) async-start(bf16[32,24,256]{2,1,0:T(8,128)(2,1)} %bitcast.5), calls=%async_computation | async-start | bytes 786432 | tf_op jit(solution)/shard_map/all_to_all | solution.py:420
  109.4 1.7 %collective-permute-start.23 = (bf16[64,256]{1,0:T(8,128)(2,1)S(1)}, bf16[64,256]{1,0:T(8,128)(2,1)S(1)}, u32[]{:S(2)}, u32[]{:S(2)}) collective-permute-start(bf16[64,256]{1,0:T(8,128)(2,1)S(1)} %get-tuple-element.42), channel_id=1, source_target_pairs={{0,32},{32,0},{64,96},{96,64},{128,160},{160,128},{192,224},{224,1... | collective-permute-start | bytes 98312 | tf_op jit(solution)/shard_map/ppermute | solution.py:422
  111.1 2.9 %collective-permute-start.24 = (bf16[64,256]{1,0:T(8,128)(2,1)S(1)}, bf16[64,256]{1,0:T(8,128)(2,1)S(1)}, u32[]{:S(2)}, u32[]{:S(2)}) collective-permute-start(bf16[64,256]{1,0:T(8,128)(2,1)S(1)} %get-tuple-element.43), channel_id=1, source_target_pairs={{0,64},{32,96},{64,0},{96,32},{128,192},{160,224},{192,128},{224,1... | collective-permute-start | bytes 98312 | tf_op jit(solution)/shard_map/ppermute | solution.py:422
  113.9 0.2 collective-permute-start.25
  114.2 2.2 %collective-permute-start.26 = (bf16[64,256]{1,0:T(8,128)(2,1)S(1)}, bf16[64,256]{1,0:T(8,128)(2,1)S(1)}, u32[]{:S(2)}, u32[]{:S(2)}) collective-permute-start(bf16[64,256]{1,0:T(8,128)(2,1)S(1)} %get-tuple-element.45), channel_id=1, source_target_pairs={{0,128},{32,160},{64,192},{96,224},{128,0},{160,32},{192,64},{224,... | collective-permute-start | bytes 98312 | tf_op jit(solution)/shard_map/ppermute | solution.py:422
  116.4 5.3 %collective-permute-start.28 = (bf16[64,256]{1,0:T(8,128)(2,1)S(1)}, bf16[64,256]{1,0:T(8,128)(2,1)S(1)}, u32[]{:S(2)}, u32[]{:S(2)}) collective-permute-start(bf16[64,256]{1,0:T(8,128)(2,1)S(1)} %get-tuple-element.47), channel_id=1, source_target_pairs={{0,192},{32,224},{64,128},{96,160},{128,64},{160,96},{192,0},{224,... | collective-permute-start | bytes 98312 | tf_op jit(solution)/shard_map/ppermute | solution.py:422
  121.7 0.1 collective-permute-done.26
  121.8 1.9 %collective-permute-done.27 = bf16[64,256]{1,0:T(8,128)(2,1)S(1)} collective-permute-done((bf16[64,256]{1,0:T(8,128)(2,1)S(1)}, bf16[64,256]{1,0:T(8,128)(2,1)S(1)}, u32[]{:S(2)}, u32[]{:S(2)}) %collective-permute-start.27) | collective-permute-done | bytes 32800 | tf_op jit(solution)/shard_map/ppermute | solution.py:422
  123.8 2.3 %collective-permute-done.28 = bf16[64,256]{1,0:T(8,128)(2,1)S(1)} collective-permute-done((bf16[64,256]{1,0:T(8,128)(2,1)S(1)}, bf16[64,256]{1,0:T(8,128)(2,1)S(1)}, u32[]{:S(2)}, u32[]{:S(2)}) %collective-permute-start.28) | collective-permute-done | bytes 32800 | tf_op jit(solution)/shard_map/ppermute | solution.py:422
  126.1 1.6 %collective-permute-done.29 = bf16[64,256]{1,0:T(8,128)(2,1)S(1)} collective-permute-done((bf16[64,256]{1,0:T(8,128)(2,1)S(1)}, bf16[64,256]{1,0:T(8,128)(2,1)S(1)}, u32[]{:S(2)}, u32[]{:S(2)}) %collective-permute-start.29) | collective-permute-done | bytes 32800 | tf_op jit(solution)/shard_map/ppermute | solution.py:422
  128.0 1.1 collective-permute-done.30
  129.2 15.2 %all_to_all.10.got = f32[8,88,256]{2,1,0:T(8,128)S(1)} all-to-all(f32[8,88,256]{2,1,0:T(8,128)S(1)} %broadcast_in_dim.2), channel_id=1, replica_groups=mesh['pole'=8,'row'=4,'col'=8] {'pole'}, dimensions={0} | all-to-all | bytes 1441792 | tf_op jit(solution)/shard_map/all_to_all | solution.py:430
  144.4 1.6 %shard_map.100 = (f32[256,768]{1,0:T(8,128)}, f32[24,256]{1,0:T(8,128)}) custom-call(s32[2]{0:T(128)S(1)} %pad_add_fusion.device.refs_0_, s32[3]{0:T(128)S(1)} %copy-done.14, f32[8,88,256]{2,1,0:T(8,128)S(1)} %all_to_all.10.got), custom_call_target="tpu_custom_call" | custom-call | tf_op jit(solution)/shard_map/pallas_call | solution.py:331
  (80 shorter events, 0.8 us)
Async XLA Ops:
  4.4 1.6 %collective-permute-start = (bf16[256,512]{1,0:T(8,128)(2,1)S(1)}, bf16[256,512]{1,0:T(8,128)(2,1)S(1)}, u32[]{:S(2)}, u32[]{:S(2)}) collective-permute-start(bf16[256,512]{1,0:T(8,128)(2,1)S(1)} %get-tuple-element.27), channel_id=1, source_target_pairs={{0,1},{1,0},{2,3},{3,2},{4,5},{5,4},{6,7},{7,6},{8,9},{9,8},{10,11... | collective-permute-start | bytes 786440 | tf_op jit(solution)/shard_map/ppermute | solution.py:35
  6.1 58.7 %copy-start = (bf16[384,512]{1,0:T(8,128)(2,1)}, bf16[384,512]{1,0:T(8,128)(2,1)S(1)}, u32[]{:S(2)}) copy-start(bf16[384,512]{1,0:T(8,128)(2,1)S(1)} %constant_dynamic-update-slice_fusion.refs_3_.refs_9_) | copy-start | bytes 1179652
  6.1 51.1 %collective-permute-start.3 = (bf16[2,8192,256]{2,1,0:T(8,128)(2,1)}, bf16[2,8192,256]{2,1,0:T(8,128)(2,1)S(1)}, u32[]{:S(2)}, u32[]{:S(2)}) collective-permute-start(bf16[2,8192,256]{2,1,0:T(8,128)(2,1)} %bitcast.9), channel_id=1, source_target_pairs={{0,1},{1,0},{2,3},{3,2},{4,5},{5,4},{6,7},{7,6},{8,9},{9,8},{10,11... | collective-permute-start | bytes 25165832 | tf_op jit(solution)/shard_map/ppermute | solution.py:35
  6.3 5.8 %collective-permute-start.5 = (bf16[128,512]{1,0:T(8,128)(2,1)S(1)}, bf16[128,512]{1,0:T(8,128)(2,1)S(1)}, u32[]{:S(2)}, u32[]{:S(2)}) collective-permute-start(bf16[128,512]{1,0:T(8,128)(2,1)S(1)} %get-tuple-element.29), channel_id=1, source_target_pairs={{0,24},{1,25},{2,26},{3,27},{4,28},{5,29},{6,30},{7,31},{8,0},{9,1... | collective-permute-start | bytes 393224 | tf_op jit(solution)/shard_map/ppermute | solution.py:35
  8.6 5.5 %collective-permute-start.4 = (bf16[128,512]{1,0:T(8,128)(2,1)S(1)}, bf16[128,512]{1,0:T(8,128)(2,1)S(1)}, u32[]{:S(2)}, u32[]{:S(2)}) collective-permute-start(bf16[128,512]{1,0:T(8,128)(2,1)S(1)} %get-tuple-element.29), channel_id=1, source_target_pairs={{0,8},{1,9},{2,10},{3,11},{4,12},{5,13},{6,14},{7,15},{8,16},{9,17... | collective-permute-start | bytes 393224 | tf_op jit(solution)/shard_map/ppermute | solution.py:35
  14.0 10.3 %collective-permute-start.7 = (bf16[384,512]{1,0:T(8,128)(2,1)S(1)}, bf16[384,512]{1,0:T(8,128)(2,1)S(1)}, u32[]{:S(2)}, u32[]{:S(2)}) collective-permute-start(bf16[384,512]{1,0:T(8,128)(2,1)S(1)} %constant_dynamic-update-slice_fusion.refs_3_.refs_9_), channel_id=1, source_target_pairs={{0,24},{1,25},{2,26},{3,27},{4,28},{5,29},{6,30},{7,31},{8,0},{9,1... | collective-permute-start | bytes 1179656 | tf_op jit(solution)/shard_map/ppermute | solution.py:35
  16.3 6.3 %collective-permute-start.17 = (bf16[128,512]{1,0:T(8,128)(2,1)S(1)}, bf16[128,512]{1,0:T(8,128)(2,1)S(1)}, u32[]{:S(2)}, u32[]{:S(2)}) collective-permute-start(bf16[128,512]{1,0:T(8,128)(2,1)S(1)} %collective-permute-done.4), channel_id=1, source_target_pairs={{0,8},{1,9},{2,10},{3,11},{4,12},{5,13},{6,14},{7,15},{8,16},{9,17... | collective-permute-start | bytes 393224 | tf_op jit(solution)/shard_map/ppermute | solution.py:35
  16.3 22.3 %collective-permute-start.10 = (bf16[384,512]{1,0:T(8,128)(2,1)S(1)}, bf16[384,512]{1,0:T(8,128)(2,1)S(1)}, u32[]{:S(2)}, u32[]{:S(2)}) collective-permute-start(bf16[384,512]{1,0:T(8,128)(2,1)S(1)} %constant_dynamic-update-slice_fusion.refs_3_.refs_9_), channel_id=1, source_target_pairs={{0,6},{1,7},{2,0},{3,1},{4,2},{5,3},{6,4},{7,5},{8,14},{9,15},{10,... | collective-permute-start | bytes 1179656 | tf_op jit(solution)/shard_map/ppermute | solution.py:35
  22.6 19.8 %collective-permute-start.1 = (bf16[384,512]{1,0:T(8,128)(2,1)S(1)}, bf16[384,512]{1,0:T(8,128)(2,1)S(1)}, u32[]{:S(2)}, u32[]{:S(2)}) collective-permute-start(bf16[384,512]{1,0:T(8,128)(2,1)S(1)} %constant_dynamic-update-slice_fusion.refs_3_.refs_9_), channel_id=1, source_target_pairs={{0,2},{1,3},{2,4},{3,5},{4,6},{5,7},{6,0},{7,1},{8,10},{9,11},{10,... | collective-permute-start | bytes 1179656 | tf_op jit(solution)/shard_map/ppermute | solution.py:35
  22.6 20.7 %collective-permute-start.6 = (bf16[384,512]{1,0:T(8,128)(2,1)S(1)}, bf16[384,512]{1,0:T(8,128)(2,1)S(1)}, u32[]{:S(2)}, u32[]{:S(2)}) collective-permute-start(bf16[384,512]{1,0:T(8,128)(2,1)S(1)} %constant_dynamic-update-slice_fusion.refs_3_.refs_9_), channel_id=1, source_target_pairs={{0,8},{1,9},{2,10},{3,11},{4,12},{5,13},{6,14},{7,15},{8,16},{9,17... | collective-permute-start | bytes 1179656 | tf_op jit(solution)/shard_map/ppermute | solution.py:35
  24.3 40.5 %copy-start.1 = (bf16[384,512]{1,0:T(8,128)(2,1)}, bf16[384,512]{1,0:T(8,128)(2,1)S(1)}, u32[]{:S(2)}) copy-start(bf16[384,512]{1,0:T(8,128)(2,1)S(1)} %collective-permute-done.7.refs_5_.refs_11_) | copy-start | bytes 1179652
  24.3 20.9 %collective-permute-start.8 = (bf16[384,512]{1,0:T(8,128)(2,1)S(1)}, bf16[384,512]{1,0:T(8,128)(2,1)S(1)}, u32[]{:S(2)}, u32[]{:S(2)}) collective-permute-start(bf16[384,512]{1,0:T(8,128)(2,1)S(1)} %collective-permute-done.7.refs_5_.refs_11_), channel_id=1, source_target_pairs={{0,24},{1,25},{2,26},{3,27},{4,28},{5,29},{6,30},{7,31},{8,0},{9,1... | collective-permute-start | bytes 1179656 | tf_op jit(solution)/shard_map/ppermute | solution.py:35
  26.6 40.7 %copy-start.17 = (bf16[512,512]{1,0:T(8,128)(2,1)}, bf16[512,512]{1,0:T(8,128)(2,1)S(1)}, u32[]{:S(2)}) copy-start(bf16[512,512]{1,0:T(8,128)(2,1)S(1)} %constant_dynamic-update-slice_fusion.2.refs_21_) | copy-start | bytes 1572868
  38.6 40.3 %copy-start.2 = (bf16[384,512]{1,0:T(8,128)(2,1)}, bf16[384,512]{1,0:T(8,128)(2,1)S(1)}, u32[]{:S(2)}) copy-start(bf16[384,512]{1,0:T(8,128)(2,1)S(1)} %collective-permute-done.10.refs_4_.refs_17_) | copy-start | bytes 1179652
  42.4 27.7 %copy-start.3 = (bf16[384,512]{1,0:T(8,128)(2,1)}, bf16[384,512]{1,0:T(8,128)(2,1)S(1)}, u32[]{:S(2)}) copy-start(bf16[384,512]{1,0:T(8,128)(2,1)S(1)} %collective-permute-done.1.refs_4_.refs_13_) | copy-start | bytes 1179652
  42.4 11.0 %collective-permute-start.9 = (bf16[384,512]{1,0:T(8,128)(2,1)S(1)}, bf16[384,512]{1,0:T(8,128)(2,1)S(1)}, u32[]{:S(2)}, u32[]{:S(2)}) collective-permute-start(bf16[384,512]{1,0:T(8,128)(2,1)S(1)} %collective-permute-done.1.refs_4_.refs_13_), channel_id=1, source_target_pairs={{0,8},{1,9},{2,10},{3,11},{4,12},{5,13},{6,14},{7,15},{8,16},{9,17... | collective-permute-start | bytes 1179656 | tf_op jit(solution)/shard_map/ppermute | solution.py:35
  42.4 24.5 %collective-permute-start.19 = (bf16[512,512]{1,0:T(8,128)(2,1)S(1)}, bf16[512,512]{1,0:T(8,128)(2,1)S(1)}, u32[]{:S(2)}, u32[]{:S(2)}) collective-permute-start(bf16[512,512]{1,0:T(8,128)(2,1)S(1)} %constant_dynamic-update-slice_fusion.2.refs_21_), channel_id=1, source_target_pairs={{0,6},{1,7},{2,0},{3,1},{4,2},{5,3},{6,4},{7,5},{8,14},{9,15},{10,... | collective-permute-start | bytes 1572872 | tf_op jit(solution)/shard_map/ppermute | solution.py:35
  43.3 21.5 %copy-start.4 = (bf16[384,512]{1,0:T(8,128)(2,1)}, bf16[384,512]{1,0:T(8,128)(2,1)S(1)}, u32[]{:S(2)}) copy-start(bf16[384,512]{1,0:T(8,128)(2,1)S(1)} %collective-permute-done.6.refs_4_.refs_10_) | copy-start | bytes 1179652
  43.3 21.5 %collective-permute-start.11 = (bf16[384,512]{1,0:T(8,128)(2,1)S(1)}, bf16[384,512]{1,0:T(8,128)(2,1)S(1)}, u32[]{:S(2)}, u32[]{:S(2)}) collective-permute-start(bf16[384,512]{1,0:T(8,128)(2,1)S(1)} %collective-permute-done.10.refs_4_.refs_17_), channel_id=1, source_target_pairs={{0,24},{1,25},{2,26},{3,27},{4,28},{5,29},{6,30},{7,31},{8,0},{9,1... | collective-permute-start | bytes 1179656 | tf_op jit(solution)/shard_map/ppermute | solution.py:35
  45.2 19.6 %copy-start.5 = (bf16[384,512]{1,0:T(8,128)(2,1)}, bf16[384,512]{1,0:T(8,128)(2,1)S(1)}, u32[]{:S(2)}) copy-start(bf16[384,512]{1,0:T(8,128)(2,1)S(1)} %collective-permute-done.8.refs_6_.refs_12_) | copy-start | bytes 1179652
  45.2 19.7 %collective-permute-start.2 = (bf16[384,512]{1,0:T(8,128)(2,1)S(1)}, bf16[384,512]{1,0:T(8,128)(2,1)}, u32[]{:S(2)}, u32[]{:S(2)}) collective-permute-start(bf16[384,512]{1,0:T(8,128)(2,1)S(1)} %collective-permute-done.1.refs_4_.refs_13_), channel_id=1, source_target_pairs={{0,2},{1,3},{2,4},{3,5},{4,6},{5,7},{6,0},{7,1},{8,10},{9,11},{10,... | collective-permute-start | bytes 1179656 | tf_op jit(solution)/shard_map/ppermute | solution.py:35
  53.3 16.7 %copy-start.6 = (bf16[384,512]{1,0:T(8,128)(2,1)}, bf16[384,512]{1,0:T(8,128)(2,1)S(1)}, u32[]{:S(2)}) copy-start(bf16[384,512]{1,0:T(8,128)(2,1)S(1)} %collective-permute-done.9.refs_5_.refs_14_) | copy-start | bytes 1179652
  53.3 13.7 %collective-permute-start.13 = (bf16[384,512]{1,0:T(8,128)(2,1)S(1)}, bf16[384,512]{1,0:T(8,128)(2,1)S(1)}, u32[]{:S(2)}, u32[]{:S(2)}) collective-permute-start(bf16[384,512]{1,0:T(8,128)(2,1)S(1)} %collective-permute-done.1.refs_4_.refs_13_), channel_id=1, source_target_pairs={{0,24},{1,25},{2,26},{3,27},{4,28},{5,29},{6,30},{7,31},{8,0},{9,1... | collective-permute-start | bytes 1179656 | tf_op jit(solution)/shard_map/ppermute | solution.py:35
  57.1 10.2 %collective-permute-start.14 = (bf16[384,512]{1,0:T(8,128)(2,1)S(1)}, bf16[384,512]{1,0:T(8,128)(2,1)S(1)}, u32[]{:S(2)}, u32[]{:S(2)}) collective-permute-start(bf16[384,512]{1,0:T(8,128)(2,1)S(1)} %collective-permute-done.9.refs_5_.refs_14_), channel_id=1, source_target_pairs={{0,8},{1,9},{2,10},{3,11},{4,12},{5,13},{6,14},{7,15},{8,16},{9,17... | collective-permute-start | bytes 1179656 | tf_op jit(solution)/shard_map/ppermute | solution.py:35
  64.8 14.1 %copy-start.7 = (bf16[384,512]{1,0:T(8,128)(2,1)}, bf16[384,512]{1,0:T(8,128)(2,1)S(1)}, u32[]{:S(2)}) copy-start(bf16[384,512]{1,0:T(8,128)(2,1)S(1)} %collective-permute-done.11.refs_6_.refs_19_) | copy-start | bytes 1179652
  64.8 14.1 %collective-permute-start.15 = (bf16[384,512]{1,0:T(8,128)(2,1)S(1)}, bf16[384,512]{1,0:T(8,128)(2,1)S(1)}, u32[]{:S(2)}, u32[]{:S(2)}) collective-permute-start(bf16[384,512]{1,0:T(8,128)(2,1)S(1)} %collective-permute-done.10.refs_4_.refs_17_), channel_id=1, source_target_pairs={{0,8},{1,9},{2,10},{3,11},{4,12},{5,13},{6,14},{7,15},{8,16},{9,17... | collective-permute-start | bytes 1179656 | tf_op jit(solution)/shard_map/ppermute | solution.py:35
  64.9 12.0 %collective-permute-start.16 = (bf16[384,512]{1,0:T(8,128)(2,1)S(1)}, bf16[384,512]{1,0:T(8,128)(2,1)S(1)}, u32[]{:S(2)}, u32[]{:S(2)}) collective-permute-start(bf16[384,512]{1,0:T(8,128)(2,1)S(1)} %collective-permute-done.11.refs_6_.refs_19_), channel_id=1, source_target_pairs={{0,24},{1,25},{2,26},{3,27},{4,28},{5,29},{6,30},{7,31},{8,0},{9,1... | collective-permute-start | bytes 1179656 | tf_op jit(solution)/shard_map/ppermute | solution.py:35
  66.9 7.6 %copy-start.18 = (bf16[512,512]{1,0:T(8,128)(2,1)}, bf16[512,512]{1,0:T(8,128)(2,1)S(1)}, u32[]{:S(2)}) copy-start(bf16[512,512]{1,0:T(8,128)(2,1)S(1)} %collective-permute-done.19.refs_23_) | copy-start | bytes 1572868
  66.9 16.5 %collective-permute-start.12 = (bf16[384,512]{1,0:T(8,128)(2,1)}, bf16[384,512]{1,0:T(8,128)(2,1)}, u32[]{:S(2)}, u32[]{:S(2)}) collective-permute-start(bf16[384,512]{1,0:T(8,128)(2,1)} %collective-permute-done.2.refs_25_), channel_id=1, source_target_pairs={{0,8},{1,9},{2,10},{3,11},{4,12},{5,13},{6,14},{7,15},{8,16},{9,17... | collective-permute-start | bytes 1179656 | tf_op jit(solution)/shard_map/ppermute | solution.py:35
  67.0 7.5 %copy-start.8 = (bf16[384,512]{1,0:T(8,128)(2,1)}, bf16[384,512]{1,0:T(8,128)(2,1)S(1)}, u32[]{:S(2)}) copy-start(bf16[384,512]{1,0:T(8,128)(2,1)S(1)} %collective-permute-done.13.refs_6_.refs_15_) | copy-start | bytes 1179652
  67.0 17.5 %collective-permute-start.20 = (bf16[512,512]{1,0:T(8,128)(2,1)S(1)}, bf16[512,512]{1,0:T(8,128)(2,1)}, u32[]{:S(2)}, u32[]{:S(2)}) collective-permute-start(bf16[512,512]{1,0:T(8,128)(2,1)S(1)} %collective-permute-done.19.refs_23_), channel_id=1, source_target_pairs={{0,6},{1,7},{2,0},{3,1},{4,2},{5,3},{6,4},{7,5},{8,14},{9,15},{10,... | collective-permute-start | bytes 1572872 | tf_op jit(solution)/shard_map/ppermute | solution.py:35
  67.3 7.2 %copy-start.9 = (bf16[384,512]{1,0:T(8,128)(2,1)}, bf16[384,512]{1,0:T(8,128)(2,1)S(1)}, u32[]{:S(2)}) copy-start(bf16[384,512]{1,0:T(8,128)(2,1)S(1)} %collective-permute-done.14.refs_7_.refs_16_) | copy-start | bytes 1179652
  67.3 17.6 %collective-permute-start.18 = (bf16[512,512]{1,0:T(8,128)(2,1)S(1)}, bf16[512,512]{1,0:T(8,128)(2,1)}, u32[]{:S(2)}, u32[]{:S(2)}) collective-permute-start(bf16[512,512]{1,0:T(8,128)(2,1)S(1)} %constant_dynamic-update-slice_fusion.2.refs_21_), channel_id=1, source_target_pairs={{0,2},{1,3},{2,4},{3,5},{4,6},{5,7},{6,0},{7,1},{8,10},{9,11},{10,... | collective-permute-start | bytes 1572872 | tf_op jit(solution)/shard_map/ppermute | solution.py:35
  74.5 9.8 %copy-start.20 = (f32[20,2]{0,1:T(2,128)S(1)}, f32[20,2]{0,1:T(2,128)}, u32[]{:S(2)}) copy-start(f32[20,2]{0,1:T(2,128)} %param.15) | copy-start | bytes 484
  74.6 9.9 %copy-start.19 = (bf16[1,2,24,256]{3,2,1,0:T(8,128)(2,1)S(1)}, bf16[1,2,24,256]{3,2,1,0:T(8,128)(2,1)}, u32[]{:S(2)}) copy-start(bf16[1,2,24,256]{3,2,1,0:T(8,128)(2,1)} %param.10) | copy-start | bytes 73732
  74.6 17.2 %copy-start.14 = (s32[3]{0:T(128)S(1)}, s32[3]{0:T(128)}, u32[]{:S(2)}) copy-start(s32[3]{0:T(128)} %widths.3) | copy-start | bytes 40
  74.6 17.2 %copy-start.15 = (s32[32]{0:T(128)S(1)}, s32[32]{0:T(128)}, u32[]{:S(2)}) copy-start(s32[32]{0:T(128)} %refs_2_.1) | copy-start | bytes 388
  76.9 8.1 %collective-permute-start.21 = (bf16[384,512]{1,0:T(8,128)(2,1)}, bf16[384,512]{1,0:T(8,128)(2,1)}, u32[]{:S(2)}, u32[]{:S(2)}) collective-permute-start(bf16[384,512]{1,0:T(8,128)(2,1)} %collective-permute-done.2.refs_25_), channel_id=1, source_target_pairs={{0,24},{1,25},{2,26},{3,27},{4,28},{5,29},{6,30},{7,31},{8,0},{9,1... | collective-permute-start | bytes 1179656 | tf_op jit(solution)/shard_map/ppermute | solution.py:35
  83.4 8.4 %collective-permute-start.22 = (bf16[384,512]{1,0:T(8,128)(2,1)}, bf16[384,512]{1,0:T(8,128)(2,1)}, u32[]{:S(2)}, u32[]{:S(2)}) collective-permute-start(bf16[384,512]{1,0:T(8,128)(2,1)} %collective-permute-done.12.refs_26_), channel_id=1, source_target_pairs={{0,8},{1,9},{2,10},{3,11},{4,12},{5,13},{6,14},{7,15},{8,16},{9,17... | collective-permute-start | bytes 1179656 | tf_op jit(solution)/shard_map/ppermute | solution.py:35
  102.7 25.2 %all-to-all-start = ((bf16[32,24,256]{2,1,0:T(8,128)(2,1)}), bf16[32,24,256]{2,1,0:T(8,128)(2,1)S(1)}, u32[]{:S(2)}, u32[]{:S(2)}) async-start(bf16[32,24,256]{2,1,0:T(8,128)(2,1)} %bitcast.5), calls=%async_computation | async-start | bytes 786432 | tf_op jit(solution)/shard_map/all_to_all | solution.py:420
  109.4 7.0 %collective-permute-start.23 = (bf16[64,256]{1,0:T(8,128)(2,1)S(1)}, bf16[64,256]{1,0:T(8,128)(2,1)S(1)}, u32[]{:S(2)}, u32[]{:S(2)}) collective-permute-start(bf16[64,256]{1,0:T(8,128)(2,1)S(1)} %get-tuple-element.42), channel_id=1, source_target_pairs={{0,32},{32,0},{64,96},{96,64},{128,160},{160,128},{192,224},{224,1... | collective-permute-start | bytes 98312 | tf_op jit(solution)/shard_map/ppermute | solution.py:422
  111.1 10.7 %collective-permute-start.24 = (bf16[64,256]{1,0:T(8,128)(2,1)S(1)}, bf16[64,256]{1,0:T(8,128)(2,1)S(1)}, u32[]{:S(2)}, u32[]{:S(2)}) collective-permute-start(bf16[64,256]{1,0:T(8,128)(2,1)S(1)} %get-tuple-element.43), channel_id=1, source_target_pairs={{0,64},{32,96},{64,0},{96,32},{128,192},{160,224},{192,128},{224,1... | collective-permute-start | bytes 98312 | tf_op jit(solution)/shard_map/ppermute | solution.py:422
  113.9 7.8 %collective-permute-start.25 = (bf16[64,256]{1,0:T(8,128)(2,1)S(1)}, bf16[64,256]{1,0:T(8,128)(2,1)S(1)}, u32[]{:S(2)}, u32[]{:S(2)}) collective-permute-start(bf16[64,256]{1,0:T(8,128)(2,1)S(1)} %get-tuple-element.44), channel_id=1, source_target_pairs={{0,96},{32,64},{64,32},{96,0},{128,224},{160,192},{192,160},{224,1... | collective-permute-start | bytes 98312 | tf_op jit(solution)/shard_map/ppermute | solution.py:422
  114.2 7.7 %collective-permute-start.26 = (bf16[64,256]{1,0:T(8,128)(2,1)S(1)}, bf16[64,256]{1,0:T(8,128)(2,1)S(1)}, u32[]{:S(2)}, u32[]{:S(2)}) collective-permute-start(bf16[64,256]{1,0:T(8,128)(2,1)S(1)} %get-tuple-element.45), channel_id=1, source_target_pairs={{0,128},{32,160},{64,192},{96,224},{128,0},{160,32},{192,64},{224,... | collective-permute-start | bytes 98312 | tf_op jit(solution)/shard_map/ppermute | solution.py:422
  116.4 7.4 %collective-permute-start.27 = (bf16[64,256]{1,0:T(8,128)(2,1)S(1)}, bf16[64,256]{1,0:T(8,128)(2,1)S(1)}, u32[]{:S(2)}, u32[]{:S(2)}) collective-permute-start(bf16[64,256]{1,0:T(8,128)(2,1)S(1)} %get-tuple-element.46), channel_id=1, source_target_pairs={{0,160},{32,128},{64,224},{96,192},{128,32},{160,0},{192,96},{224,... | collective-permute-start | bytes 98312 | tf_op jit(solution)/shard_map/ppermute | solution.py:422
  116.4 9.7 %collective-permute-start.28 = (bf16[64,256]{1,0:T(8,128)(2,1)S(1)}, bf16[64,256]{1,0:T(8,128)(2,1)S(1)}, u32[]{:S(2)}, u32[]{:S(2)}) collective-permute-start(bf16[64,256]{1,0:T(8,128)(2,1)S(1)} %get-tuple-element.47), channel_id=1, source_target_pairs={{0,192},{32,224},{64,128},{96,160},{128,64},{160,96},{192,0},{224,... | collective-permute-start | bytes 98312 | tf_op jit(solution)/shard_map/ppermute | solution.py:422
  121.7 6.0 %collective-permute-start.29 = (bf16[64,256]{1,0:T(8,128)(2,1)S(1)}, bf16[64,256]{1,0:T(8,128)(2,1)S(1)}, u32[]{:S(2)}, u32[]{:S(2)}) collective-permute-start(bf16[64,256]{1,0:T(8,128)(2,1)S(1)} %get-tuple-element.48), channel_id=1, source_target_pairs={{0,224},{32,192},{64,160},{96,128},{128,96},{160,64},{192,32},{224... | collective-permute-start | bytes 98312 | tf_op jit(solution)/shard_map/ppermute | solution.py:422
  127.8 1.3 collective-permute-start.30
  (5 other events, 16.1 us)

commit v5 on v4

--- a/solution.py
+++ b/solution.py
@@ -8,7 +8,7 @@
 from jax.sharding import PartitionSpec as P
 
 NX, NZ, NC = 4, 4, 2
-POLES = 8
+POLES, NY = 8, 4
 B = 256
 TOP = 128
 SIZES = (TOP, B - TOP)
@@ -80,6 +80,18 @@
     at_row = lax.broadcasted_iota(jnp.int32, (B, B), 0)
     at_col = lax.broadcasted_iota(jnp.int32, (B, B), 1)
     return (at_row + split == at_col).astype(jnp.float32).astype(jnp.bfloat16)
+
+
+def pass_on(*values, flops):
+    n = len(values)
+    return pl.pallas_call(
+        lambda *refs: None,
+        in_specs=[ANY] * n,
+        out_specs=[ANY] * n,
+        out_shape=[jax.ShapeDtypeStruct(v.shape, v.dtype) for v in values],
+        input_output_aliases={i: i for i in range(n)},
+        cost_estimate=pl.CostEstimate(flops=flops, transcendentals=0, bytes_accessed=0),
+    )(*values)
 
 
 def prepare_body(device, widths, pattern, factor, top, rest, give):
@@ -208,9 +220,8 @@
 def finish_body(sources, segments, *refs):
     device, widths, owner, assign, weights, acc, dinv, own_inverse, sib_inverse = refs[:9]
     pieces = refs[9 : 9 + len(sources)]
-    shared = refs[9 + len(sources)]
-    parts_out = refs[10 + len(sources) : 10 + len(sources) + POLES]
-    total, own, diag, weighted, sem, *scratch = refs[10 + len(sources) + POLES :]
+    mine_out, other_out, over_out, *parts_out = refs[9 + len(sources) : 12 + len(sources) + NY]
+    total, own, diag, weighted, sem, *scratch = refs[12 + len(sources) + NY :]
     last = pieces[len(sources) - len(segments) :]
     fetched = gemm_fetch(segments, device[0], own_inverse, sib_inverse, last, *scratch)
     dev, pole = device[0], device[1]
@@ -251,10 +262,14 @@
         top, low = acc[2 * j * B : (2 * j + 1) * B], acc[(2 * j + 1) * B : (2 * j + 2) * B]
         x_real = low[:, B:] - top[:, :B]
         x_imag = -(top[:, B:] + low[:, :B])
-        weighted[...] = (wr * x_imag + wi * x_real).astype(jnp.bfloat16)
+        weighted[...] = wr * x_imag + wi * x_real
+        size = B // POLES
         for d in range(POLES):
-            rows = pl.ds(pl.multiple_of((pole ^ d) * (B // POLES), B // POLES), B // POLES)
-            parts_out[d][j * (B // POLES) : (j + 1) * (B // POLES)] = weighted[rows]
+            value = weighted[pl.ds(pl.multiple_of((pole ^ d) * size, size), size)]
+            if d < NY:
+                parts_out[d][j * size : (j + 1) * size] = value
+            else:
+                over_out[d - NY, j * size : (j + 1) * size] = value
         parts.append((x_real.astype(jnp.bfloat16), x_imag.astype(jnp.bfloat16)))
     for copy in waits:
         copy.wait()
@@ -284,7 +299,11 @@
     depth = dinv.shape[1]
     mine = pl.ds(pl.multiple_of(dev * depth, 8), depth)
     diag[mine] += wr * dinv[1] + wi * dinv[0]
-    shared[...] = diag[...].astype(jnp.bfloat16)
+    for i in range(NX * NZ):
+        rows = slice(i * depth, (i + 1) * depth)
+        mine_out[rows] = diag[pl.ds(pl.multiple_of((NC * i + core) * depth, 8), depth)]
+        total[rows, :B] = diag[pl.ds(pl.multiple_of((NC * i + 1 - core) * depth, 8), depth)]
+    other_out[...] = total[: NX * NZ * depth, :B].astype(jnp.bfloat16)
 
 
 def finish(
@@ -293,16 +312,18 @@
     return pl.pallas_call(
         functools.partial(finish_body, sources, segments),
         in_specs=[SMEM] * 5 + [VMEM] * 2 + [HBM] * 2 + [ANY] * len(pieces),
-        out_specs=[VMEM] * (1 + POLES),
+        out_specs=[VMEM] * (3 + NY),
         out_shape=[
-            jax.ShapeDtypeStruct((n, B), jnp.bfloat16)
-            for n in (total,) + (2 * B // POLES,) * POLES
-        ],
+            jax.ShapeDtypeStruct((total // NC, B), jnp.float32),
+            jax.ShapeDtypeStruct((total // NC, B), jnp.bfloat16),
+            jax.ShapeDtypeStruct((NY, 2 * B // POLES, B), jnp.float32),
+        ]
+        + [jax.ShapeDtypeStruct((2 * B // POLES, B), jnp.float32)] * NY,
         scratch_shapes=[
             pltpu.VMEM((4 * B, 2 * B), jnp.float32),
             pltpu.VMEM((2 * B, 2 * B), jnp.bfloat16),
             pltpu.VMEM((total, B), jnp.float32),
-            pltpu.VMEM((B, B), jnp.bfloat16),
+            pltpu.VMEM((B, B), jnp.float32),
             pltpu.SemaphoreType.DMA((2, 2)),
             *gemm_scratch(segments),
         ],
@@ -315,16 +336,19 @@
     full, one, two, split = layout(widths)
     rows = B // POLES
     col = lax.broadcasted_iota(jnp.int32, (rows, B), 1)
+    shares = []
     for p in range(POLES):
         out = slice(p * rows, (p + 1) * rows)
-        mine, other = got[p, :rows], got[p, rows : 2 * rows]
+        part = got[p].astype(jnp.float32)
+        mine, other = part[:rows], part[rows : 2 * rows]
         large = jnp.where(core == 0, mine, other)
         small = jnp.where(core == 0, other, mine)
         panel[out, pl.ds(pl.multiple_of(full * B, B), B)] = large
         panel[out, pl.ds(pl.multiple_of(one * B, B), B)] = jnp.where(col < split, small, 0)
         late = pltpu.roll(small, B - split, 1)
         panel[out, pl.ds(pl.multiple_of(two * B, B), B)] = jnp.where(col < B - split, late, 0)
-    diag[...] = sum(got[p, 2 * rows :] for p in range(POLES))
+        shares.append((part[2 * rows : 3 * rows] + part[3 * rows :])[: diag.shape[0]])
+    diag[...] = sum(shares)
 
 
 def spread(device, widths, got, total, depth):
@@ -377,6 +401,7 @@
     main = jnp.concatenate([top, taken], 0)
     rest_f, rest_b = after((rest_f, rest_b), main)
     zf, zb = shift(main, 0, 1), shift(main, 0, -1)
+    zf, zb = pass_on(zf, zb, flops=60_000_000_000)
     rest_far = shift(rest_f, 1, 0)
     main_x = after(main, rest_f, rest_b)
     main_f, main_b = shift(main_x, 1, 0), shift(main_x, -1, 0)
@@ -410,23 +435,30 @@
     held = (z_far, far_f, far_b, far_far)
     segments += listing(held, [[(ox, 2, False)] for ox in orders], 0)
 
-    shared, *parts = finish(
+    mine, given, over, *parts = finish(
         device, widths, owner, assign, pole_weights, acc,
         diag_inverse[0].astype(jnp.float32), own_inverse, sib_inverse,
         pieces, tuple(sources), segments, total,
     )
 
-    shared = shared.reshape(NX * NZ * NC, depth, B)
-    shared = lax.all_to_all(shared, GRID, 0, 0, tiled=True)
+    mine = mine + shift(given, 0, 0, 1).astype(jnp.float32)
+    mine = mine.reshape(NX * NZ, depth, B)
+    groups = [[NC * i + c for i in range(NX * NZ)] for c in range(NC)]
+    shared = lax.all_to_all(mine, GRID, 0, 0, axis_index_groups=groups, tiled=True)
+    over = lax.ppermute(over, "pole", [(p, p ^ NY) for p in range(POLES)])
+    got = [part + over[d] for d, part in enumerate(parts)]
     got = [
         lax.ppermute(part, "pole", [(p, p ^ d) for p in range(POLES)]) if d else part
-        for d, part in enumerate(parts)
+        for d, part in enumerate(got)
     ]
-    got = sum(part.astype(jnp.float32) for part in got)
+    got = sum(got).astype(jnp.bfloat16)
     rows = B // POLES
     other = shift(got[rows:], 0, 0, 1)
     diag = shared.astype(jnp.float32).sum(0)
-    both = jnp.concatenate([got[:rows], other, diag], 0)
+    high = diag.astype(jnp.bfloat16)
+    low = (diag - high.astype(jnp.float32)).astype(jnp.bfloat16)
+    pad = ((0, rows - depth), (0, 0))
+    both = jnp.concatenate([got[:rows], other, jnp.pad(high, pad), jnp.pad(low, pad)], 0)
     both = lax.all_to_all(
         jnp.broadcast_to(both[None], (POLES,) + both.shape), "pole", 0, 0, tiled=True
     )

time: 146 us -> 139 us (0.952)
  starting transfers between devices: 48.6 us -> 45.4 us
  local copies, waits for them, and re-layouts: 6.15 us -> 3.59 us
  blocking collectives: 15.2 us -> 13.6 us
    ppermute x7 -> x3, starting transfers between devices: 12.3 us -> 4.64 us  [local(): lax.ppermute(part, 'pole', [(p, p ^ d) for p in range(POLES)])]
    ppermute x24 -> x25, starting transfers between devices: 29.5 us -> 34.6 us  [shift(): return lax.ppermute(value, GRID, perm)]
    all_to_all x1, waiting for transfers between devices: 0.01 us -> 3.59 us  [local(): lax.all_to_all(mine, GRID, 0, 0, axis_index_groups=groups, tiled=True)]
    ppermute x24 -> x25, waiting for transfers between devices: 41.3 us -> 38.7 us  [shift(): return lax.ppermute(value, GRID, perm)]
    unnamed x48, local copies, waits for them, and re-layouts: 6.06 us -> 3.52 us
    all_to_all x1, blocking collectives: 15.2 us -> 13.6 us  [local(): lax.all_to_all(jnp.broadcast_to(both[None], (POLES,) + both.shape), 'pole...]
    ppermute x7 -> x3, waiting for transfers between devices: 6.02 us -> 5.05 us  [local(): lax.ppermute(part, 'pole', [(p, p ^ d) for p in range(POLES)])]
  transfers between devices with their start and end apart: 32 -> 30, of which waited for: 16 -> 14; matrix products, arithmetic and copies ran while one was open for 0% -> 1% of each run, Pallas kernels for 9% -> 10%
where the time goes in v5:
time: 139 us
  waiting for transfers between devices  47.8 us (34%)
  starting transfers between devices  45.4 us (33%)
  Pallas kernels  26.1 us (19%)
  blocking collectives  13.6 us (10%)
  local copies, waits for them, and re-layouts  3.59 us (3%)
  between operations  1.65 us (1%)
    ppermute x25, waiting for transfers between devices, shift(): return lax.ppermute(value, GRID, perm)  38.7 us
    ppermute x25, starting transfers between devices, shift(): return lax.ppermute(value, GRID, perm)  34.6 us
    all_to_all x1, blocking collectives, local(): lax.all_to_all(jnp.broadcast_to(both[None], (POLES,) + both.shape), 'pole...  13.6 us
    pallas_call x3, Pallas kernels, gemm(): pl.pallas_call(functools.partial(gemm_body, segments, has_acc), in_specs=...  13.2 us
    pallas_call x1, Pallas kernels, finish(): pl.pallas_call(functools.partial(finish_body, sources, segments), in_spec...  10.2 us
    all_to_all x1, starting transfers between devices, local(): lax.all_to_all(mine, GRID, 0, 0, axis_index_groups=groups, tiled=True)  6.07 us
    ppermute x3, waiting for transfers between devices, local(): lax.ppermute(part, 'pole', [(p, p ^ d) for p in range(POLES)])  5.05 us
    ppermute x3, starting transfers between devices, local(): lax.ppermute(part, 'pole', [(p, p ^ d) for p in range(POLES)])  4.64 us
  transfers between devices with their start and end apart: 30, of which 14 were waited for; matrix products, arithmetic and copies ran while one was open for 1% of the time, Pallas kernels for 10%

profile of v5, /device:TPU:2, one launch (start us, length us, event | category | flops | bytes accessed | tf_op | source)
XLA Modules:
  0.0 139.0 jit_solution(3215660831683175307)
XLA Ops:
  0.6 0.8 copy.12.pattern
  1.5 1.1 copy-done.14
  2.6 0.7 copy-done.15
  3.3 1.1 shard_map.95
  4.5 1.5 %collective-permute-done = bf16[256,512]{1,0:T(8,128)(2,1)S(1)} collective-permute-done((bf16[256,512]{1,0:T(8,128)(2,1)S(1)}, bf16[256,512]{1,0:T(8,128)(2,1)S(1)}, u32[]{:S(2)}, u32[]{:S(2)}) %collective-permute-start) | collective-permute-done | bytes 262176 | tf_op jit(solution)/shard_map/ppermute | solution.py:35
  6.1 0.2 collective-permute-start.4
  6.3 2.3 %collective-permute-start.6 = (bf16[128,512]{1,0:T(8,128)(2,1)S(1)}, bf16[128,512]{1,0:T(8,128)(2,1)S(1)}, u32[]{:S(2)}, u32[]{:S(2)}) collective-permute-start(bf16[128,512]{1,0:T(8,128)(2,1)S(1)} %get-tuple-element.30), channel_id=1, source_target_pairs={{0,24},{1,25},{2,26},{3,27},{4,28},{5,29},{6,30},{7,31},{8,0},{9,1... | collective-permute-start | bytes 393224 | tf_op jit(solution)/shard_map/ppermute | solution.py:35
  8.6 6.1 %collective-permute-start.2 = (bf16[384,512]{1,0:T(8,128)(2,1)S(1)}, bf16[384,512]{1,0:T(8,128)(2,1)S(1)}, u32[]{:S(2)}, u32[]{:S(2)}) collective-permute-start(bf16[384,512]{1,0:T(8,128)(2,1)S(1)} %constant_dynamic-update-slice_fusion.refs_3_.refs_9_), channel_id=1, source_target_pairs={{0,6},{1,7},{2,0},{3,1},{4,2},{5,3},{6,4},{7,5},{8,14},{9,15},{10,... | collective-permute-start | bytes 1179656 | tf_op jit(solution)/shard_map/ppermute | solution.py:35
  14.6 1.6 %collective-permute-start.8 = (bf16[384,512]{1,0:T(8,128)(2,1)S(1)}, bf16[384,512]{1,0:T(8,128)(2,1)S(1)}, u32[]{:S(2)}, u32[]{:S(2)}) collective-permute-start(bf16[384,512]{1,0:T(8,128)(2,1)S(1)} %constant_dynamic-update-slice_fusion.refs_3_.refs_9_), channel_id=1, source_target_pairs={{0,24},{1,25},{2,26},{3,27},{4,28},{5,29},{6,30},{7,31},{8,0},{9,1... | collective-permute-start | bytes 1179656 | tf_op jit(solution)/shard_map/ppermute | solution.py:35
  16.3 0.5 collective-permute-start.17
  16.9 5.4 %collective-permute-done.17 = bf16[128,512]{1,0:T(8,128)(2,1)S(1)} collective-permute-done((bf16[128,512]{1,0:T(8,128)(2,1)S(1)}, bf16[128,512]{1,0:T(8,128)(2,1)S(1)}, u32[]{:S(2)}, u32[]{:S(2)}) %collective-permute-start.17) | collective-permute-done | bytes 131104 | tf_op jit(solution)/shard_map/ppermute | solution.py:35
  22.3 3.0 %collective-permute-done.8.refs_5_.refs_11_ = bf16[384,512]{1,0:T(8,128)(2,1)S(1)} collective-permute-done((bf16[384,512]{1,0:T(8,128)(2,1)S(1)}, bf16[384,512]{1,0:T(8,128)(2,1)S(1)}, u32[]{:S(2)}, u32[]{:S(2)}) %collective-permute-start.8) | collective-permute-done | bytes 393248 | tf_op jit(solution)/shard_map/ppermute | solution.py:35
  25.3 2.0 %collective-permute-start.9 = (bf16[384,512]{1,0:T(8,128)(2,1)S(1)}, bf16[384,512]{1,0:T(8,128)(2,1)S(1)}, u32[]{:S(2)}, u32[]{:S(2)}) collective-permute-start(bf16[384,512]{1,0:T(8,128)(2,1)S(1)} %collective-permute-done.8.refs_5_.refs_11_), channel_id=1, source_target_pairs={{0,24},{1,25},{2,26},{3,27},{4,28},{5,29},{6,30},{7,31},{8,0},{9,1... | collective-permute-start | bytes 1179656 | tf_op jit(solution)/shard_map/ppermute | solution.py:35
  27.3 4.1 %collective-permute-done.2.refs_1_ = bf16[384,512]{1,0:T(8,128)(2,1)S(1)} collective-permute-done((bf16[384,512]{1,0:T(8,128)(2,1)S(1)}, bf16[384,512]{1,0:T(8,128)(2,1)S(1)}, u32[]{:S(2)}, u32[]{:S(2)}) %collective-permute-start.2) | collective-permute-done | bytes 393248 | tf_op jit(solution)/shard_map/ppermute | solution.py:35
  31.4 3.8 %collective-permute-done.1.refs_0_ = bf16[384,512]{1,0:T(8,128)(2,1)S(1)} collective-permute-done((bf16[384,512]{1,0:T(8,128)(2,1)S(1)}, bf16[384,512]{1,0:T(8,128)(2,1)S(1)}, u32[]{:S(2)}, u32[]{:S(2)}) %collective-permute-start.1) | collective-permute-done | bytes 393248 | tf_op jit(solution)/shard_map/ppermute | solution.py:35
  35.3 0.8 copy-done.12
  36.0 1.5 %collective-permute-start.10 = (bf16[384,512]{1,0:T(8,128)(2,1)}, bf16[384,512]{1,0:T(8,128)(2,1)S(1)}, u32[]{:S(2)}, u32[]{:S(2)}) collective-permute-start(bf16[384,512]{1,0:T(8,128)(2,1)} %get-tuple-element.37.refs_4_.refs_13_), channel_id=1, source_target_pairs={{0,8},{1,9},{2,10},{3,11},{4,12},{5,13},{6,14},{7,15},{8,16},{9,17... | collective-permute-start | bytes 1179656 | tf_op jit(solution)/shard_map/ppermute | solution.py:35
  37.5 1.5 %collective-permute-start.19 = (bf16[512,512]{1,0:T(8,128)(2,1)S(1)}, bf16[512,512]{1,0:T(8,128)(2,1)}, u32[]{:S(2)}, u32[]{:S(2)}) collective-permute-start(bf16[512,512]{1,0:T(8,128)(2,1)S(1)} %constant_dynamic-update-slice_fusion.2.refs_21_), channel_id=1, source_target_pairs={{0,6},{1,7},{2,0},{3,1},{4,2},{5,3},{6,4},{7,5},{8,14},{9,15},{10,... | collective-permute-start | bytes 1572872 | tf_op jit(solution)/shard_map/ppermute | solution.py:35
  39.0 0.5 collective-permute-start.11
  39.5 1.5 %collective-permute-start.3 = (bf16[384,512]{1,0:T(8,128)(2,1)}, bf16[384,512]{1,0:T(8,128)(2,1)}, u32[]{:S(2)}, u32[]{:S(2)}) collective-permute-start(bf16[384,512]{1,0:T(8,128)(2,1)} %get-tuple-element.37.refs_4_.refs_13_), channel_id=1, source_target_pairs={{0,2},{1,3},{2,4},{3,5},{4,6},{5,7},{6,0},{7,1},{8,10},{9,11},{10,... | collective-permute-start | bytes 1179656 | tf_op jit(solution)/shard_map/ppermute | solution.py:35
  41.0 3.8 %collective-permute-done.10.refs_5_.refs_14_ = bf16[384,512]{1,0:T(8,128)(2,1)S(1)} collective-permute-done((bf16[384,512]{1,0:T(8,128)(2,1)}, bf16[384,512]{1,0:T(8,128)(2,1)S(1)}, u32[]{:S(2)}, u32[]{:S(2)}) %collective-permute-start.10) | collective-permute-done | bytes 393248 | tf_op jit(solution)/shard_map/ppermute | solution.py:35
  44.8 2.5 %collective-permute-start.13 = (bf16[384,512]{1,0:T(8,128)(2,1)}, bf16[384,512]{1,0:T(8,128)(2,1)S(1)}, u32[]{:S(2)}, u32[]{:S(2)}) collective-permute-start(bf16[384,512]{1,0:T(8,128)(2,1)} %get-tuple-element.37.refs_4_.refs_13_), channel_id=1, source_target_pairs={{0,24},{1,25},{2,26},{3,27},{4,28},{5,29},{6,30},{7,31},{8,0},{9,1... | collective-permute-start | bytes 1179656 | tf_op jit(solution)/shard_map/ppermute | solution.py:35
  47.3 1.5 %collective-permute-start.14 = (bf16[384,512]{1,0:T(8,128)(2,1)S(1)}, bf16[384,512]{1,0:T(8,128)(2,1)S(1)}, u32[]{:S(2)}, u32[]{:S(2)}) collective-permute-start(bf16[384,512]{1,0:T(8,128)(2,1)S(1)} %collective-permute-done.10.refs_5_.refs_14_), channel_id=1, source_target_pairs={{0,8},{1,9},{2,10},{3,11},{4,12},{5,13},{6,14},{7,15},{8,16},{9,17... | collective-permute-start | bytes 1179656 | tf_op jit(solution)/shard_map/ppermute | solution.py:35
  48.8 4.3 %shard_map.97.refs_3_ = f32[1024,512]{1,0:T(8,128)S(1)} custom-call(s32[2]{0:T(128)S(1)} %pad_add_fusion.device.refs_0_, bf16[2,8192,256]{2,1,0:T(8,128)(2,1)} %bitcast.34, bf16[2,8192,256]{2,1,0:T(8,128)(2,1)} %collective-permute-done.4.refs_2_.refs_8_, bf16[384,512]{1,0:T(8,128)(2,1)S(1)} %constant_dynamic-update-slice_fusion.refs_3_.refs_9_, ...), custom_call_target="tpu_custom_call" | custom-call | tf_op jit(solution)/shard_map/pallas_call | solution.py:210
  53.1 2.5 %collective-permute-start.15 = (bf16[384,512]{1,0:T(8,128)(2,1)S(1)}, bf16[384,512]{1,0:T(8,128)(2,1)S(1)}, u32[]{:S(2)}, u32[]{:S(2)}) collective-permute-start(bf16[384,512]{1,0:T(8,128)(2,1)S(1)} %copy-done.11), channel_id=1, source_target_pairs={{0,8},{1,9},{2,10},{3,11},{4,12},{5,13},{6,14},{7,15},{8,16},{9,17... | collective-permute-start | bytes 1179656 | tf_op jit(solution)/shard_map/ppermute | solution.py:35
  55.6 4.4 %collective-permute-done.3.refs_25_ = bf16[384,512]{1,0:T(8,128)(2,1)} collective-permute-done((bf16[384,512]{1,0:T(8,128)(2,1)}, bf16[384,512]{1,0:T(8,128)(2,1)}, u32[]{:S(2)}, u32[]{:S(2)}) %collective-permute-start.3) | collective-permute-done | bytes 393248 | tf_op jit(solution)/shard_map/ppermute | solution.py:35
  60.0 2.9 %collective-permute-start.16 = (bf16[384,512]{1,0:T(8,128)(2,1)S(1)}, bf16[384,512]{1,0:T(8,128)(2,1)S(1)}, u32[]{:S(2)}, u32[]{:S(2)}) collective-permute-start(bf16[384,512]{1,0:T(8,128)(2,1)S(1)} %collective-permute-done.11.refs_6_.refs_19_), channel_id=1, source_target_pairs={{0,24},{1,25},{2,26},{3,27},{4,28},{5,29},{6,30},{7,31},{8,0},{9,1... | collective-permute-start | bytes 1179656 | tf_op jit(solution)/shard_map/ppermute | solution.py:35
  62.9 0.2 collective-permute-start.12
  63.0 4.7 %collective-permute-start.20 = (bf16[512,512]{1,0:T(8,128)(2,1)}, bf16[512,512]{1,0:T(8,128)(2,1)}, u32[]{:S(2)}, u32[]{:S(2)}) collective-permute-start(bf16[512,512]{1,0:T(8,128)(2,1)} %collective-permute-done.19.refs_23_), channel_id=1, source_target_pairs={{0,6},{1,7},{2,0},{3,1},{4,2},{5,3},{6,4},{7,5},{8,14},{9,15},{10,... | collective-permute-start | bytes 1572872 | tf_op jit(solution)/shard_map/ppermute | solution.py:35
  67.8 4.5 %shard_map.98.refs_3_ = f32[1024,512]{1,0:T(8,128)S(1)} custom-call(s32[2]{0:T(128)S(1)} %pad_add_fusion.device.refs_0_, bf16[2,8192,256]{2,1,0:T(8,128)(2,1)} %bitcast.35, bf16[2,8192,256]{2,1,0:T(8,128)(2,1)} %collective-permute-done.4.refs_2_.refs_8_, f32[1024,512]{1,0:T(8,128)S(1)} %shard_map.97.refs_3_, bf16[384,512]{1,0:T(8,128)(2,1)S(1)} %copy-done.13, ...), custom_call_target="tpu_custom_call" | custom-call | tf_op jit(solution)/shard_map/pallas_call | solution.py:210
  72.4 0.1 collective-permute-start.21
  72.6 4.5 %shard_map.99.refs_5_ = f32[1024,512]{1,0:T(8,128)S(1)} custom-call(s32[2]{0:T(128)S(1)} %pad_add_fusion.device.refs_0_, bf16[2,8192,256]{2,1,0:T(8,128)(2,1)} %bitcast.36, bf16[2,8192,256]{2,1,0:T(8,128)(2,1)} %collective-permute-done.4.refs_2_.refs_8_, f32[1024,512]{1,0:T(8,128)S(1)} %shard_map.98.refs_3_, bf16[384,512]{1,0:T(8,128)(2,1)S(1)} %copy-done.11, ...), custom_call_target="tpu_custom_call" | custom-call | tf_op jit(solution)/shard_map/pallas_call | solution.py:210
  77.1 2.3 %collective-permute-start.22 = (bf16[384,512]{1,0:T(8,128)(2,1)}, bf16[384,512]{1,0:T(8,128)(2,1)}, u32[]{:S(2)}, u32[]{:S(2)}) collective-permute-start(bf16[384,512]{1,0:T(8,128)(2,1)} %collective-permute-done.12.refs_26_), channel_id=1, source_target_pairs={{0,8},{1,9},{2,10},{3,11},{4,12},{5,13},{6,14},{7,15},{8,16},{9,17... | collective-permute-start | bytes 1179656 | tf_op jit(solution)/shard_map/ppermute | solution.py:35
  80.1 8.4 %collective-permute-done.20.refs_24_ = bf16[512,512]{1,0:T(8,128)(2,1)} collective-permute-done((bf16[512,512]{1,0:T(8,128)(2,1)}, bf16[512,512]{1,0:T(8,128)(2,1)}, u32[]{:S(2)}, u32[]{:S(2)}) %collective-permute-start.20) | collective-permute-done | bytes 524320 | tf_op jit(solution)/shard_map/ppermute | solution.py:35
  88.5 2.9 %collective-permute-done.18.refs_22_ = bf16[512,512]{1,0:T(8,128)(2,1)} collective-permute-done((bf16[512,512]{1,0:T(8,128)(2,1)S(1)}, bf16[512,512]{1,0:T(8,128)(2,1)}, u32[]{:S(2)}, u32[]{:S(2)}) %collective-permute-start.18) | collective-permute-done | bytes 524320 | tf_op jit(solution)/shard_map/ppermute | solution.py:35
  91.4 10.2 %shard_map.100 = (f32[384,256]{1,0:T(8,128)S(1)}, bf16[384,256]{1,0:T(8,128)(2,1)S(1)}, f32[4,64,256]{2,1,0:T(8,128)S(1)}, f32[64,256]{1,0:T(8,128)S(1)}, f32[64...) custom-call(s32[2]{0:T(128)S(1)} %pad_add_fusion.device.refs_0_, s32[3]{0:T(128)S(1)} %copy-done.16, ...), custom_call_target="tpu_custom_call" | custom-call | tf_op jit(solution)/shard_map/pallas_call | solution.py:312
  101.7 1.3 collective-permute-done.28
  103.1 0.8 convert_add_fusion
  103.9 6.1 %all-to-all-start = ((f32[16,24,256]{2,1,0:T(8,128)}), f32[16,24,256]{2,1,0:T(8,128)S(1)}, u32[]{:S(2)}, u32[]{:S(2)}) async-start(f32[16,24,256]{2,1,0:T(8,128)} %bitcast.9), calls=%async_computation | async-start | bytes 786432 | tf_op jit(solution)/shard_map/all_to_all | solution.py:447
  109.9 0.4 collective-permute-done.23
  110.4 1.7 %collective-permute-start.24 = (f32[64,256]{1,0:T(8,128)S(1)}, f32[64,256]{1,0:T(8,128)S(1)}, u32[]{:S(2)}, u32[]{:S(2)}) collective-permute-start(f32[64,256]{1,0:T(8,128)S(1)} %get-tuple-element.52), channel_id=1, source_target_pairs={{0,32},{32,0},{64,96},{96,64},{128,160},{160,128},{192,224},{224,1... | collective-permute-start | bytes 196616 | tf_op jit(solution)/shard_map/ppermute | solution.py:451
  112.1 2.3 %collective-permute-start.26 = (f32[64,256]{1,0:T(8,128)S(1)}, f32[64,256]{1,0:T(8,128)S(1)}, u32[]{:S(2)}, u32[]{:S(2)}) collective-permute-start(f32[64,256]{1,0:T(8,128)S(1)} %get-tuple-element.53), channel_id=1, source_target_pairs={{0,96},{32,64},{64,32},{96,0},{128,224},{160,192},{192,160},{224,1... | collective-permute-start | bytes 196616 | tf_op jit(solution)/shard_map/ppermute | solution.py:451
  114.3 0.7 collective-permute-start.25
  115.0 2.5 %collective-permute-done.26 = f32[64,256]{1,0:T(8,128)S(1)} collective-permute-done((f32[64,256]{1,0:T(8,128)S(1)}, f32[64,256]{1,0:T(8,128)S(1)}, u32[]{:S(2)}, u32[]{:S(2)}) %collective-permute-start.26) | collective-permute-done | bytes 65568 | tf_op jit(solution)/shard_map/ppermute | solution.py:451
  117.5 2.5 %collective-permute-done.25 = f32[64,256]{1,0:T(8,128)S(1)} collective-permute-done((f32[64,256]{1,0:T(8,128)S(1)}, f32[64,256]{1,0:T(8,128)S(1)}, u32[]{:S(2)}, u32[]{:S(2)}) %collective-permute-start.25) | collective-permute-done | bytes 65568 | tf_op jit(solution)/shard_map/ppermute | solution.py:451
  120.2 3.6 %all-to-all-done = f32[16,24,256]{2,1,0:T(8,128)S(1)} async-done(((f32[16,24,256]{2,1,0:T(8,128)}), f32[16,24,256]{2,1,0:T(8,128)S(1)}, u32[]{:S(2)}, u32[]{:S(2)}) %all-to-all-start) | async-done | bytes 393248 | tf_op jit(solution)/shard_map/all_to_all | solution.py:447
  123.9 13.6 %all_to_all.10.got = bf16[8,128,256]{2,1,0:T(8,128)(2,1)S(1)} all-to-all(bf16[8,128,256]{2,1,0:T(8,128)(2,1)S(1)} %broadcast_in_dim.2), channel_id=1, replica_groups=mesh['pole'=8,'row'=4,'col'=8] {'pole'}, dimensions={0} | all-to-all | bytes 1048576 | tf_op jit(solution)/shard_map/all_to_all | solution.py:462
  137.5 1.6 %shard_map.101 = (f32[256,768]{1,0:T(8,128)}, f32[24,256]{1,0:T(8,128)}) custom-call(s32[2]{0:T(128)S(1)} %pad_add_fusion.device.refs_0_, s32[3]{0:T(128)S(1)} %copy-done.16, bf16[8,128,256]{2,1,0:T(8,128)(2,1)S(1)} %all_to_all.10.got), custom_call_target="tpu_custom_call" | custom-call | tf_op jit(solution)/shard_map/pallas_call | solution.py:355
  (80 shorter events, 1.0 us)
Async XLA Ops:
  4.4 1.6 %collective-permute-start = (bf16[256,512]{1,0:T(8,128)(2,1)S(1)}, bf16[256,512]{1,0:T(8,128)(2,1)S(1)}, u32[]{:S(2)}, u32[]{:S(2)}) collective-permute-start(bf16[256,512]{1,0:T(8,128)(2,1)S(1)} %get-tuple-element.27), channel_id=1, source_target_pairs={{0,1},{1,0},{2,3},{3,2},{4,5},{5,4},{6,7},{7,6},{8,9},{9,8},{10,11... | collective-permute-start | bytes 786440 | tf_op jit(solution)/shard_map/ppermute | solution.py:35
  6.1 42.7 %copy-start = (bf16[384,512]{1,0:T(8,128)(2,1)}, bf16[384,512]{1,0:T(8,128)(2,1)S(1)}, u32[]{:S(2)}) copy-start(bf16[384,512]{1,0:T(8,128)(2,1)S(1)} %constant_dynamic-update-slice_fusion.refs_3_.refs_9_) | copy-start | bytes 1179652
  6.1 41.2 %collective-permute-start.4 = (bf16[2,8192,256]{2,1,0:T(8,128)(2,1)}, bf16[2,8192,256]{2,1,0:T(8,128)(2,1)}, u32[]{:S(2)}, u32[]{:S(2)}) collective-permute-start(bf16[2,8192,256]{2,1,0:T(8,128)(2,1)} %bitcast.33), channel_id=1, source_target_pairs={{0,1},{1,0},{2,3},{3,2},{4,5},{5,4},{6,7},{7,6},{8,9},{9,8},{10,11... | collective-permute-start | bytes 25165832 | tf_op jit(solution)/shard_map/ppermute | solution.py:35
  6.3 8.3 %collective-permute-start.6 = (bf16[128,512]{1,0:T(8,128)(2,1)S(1)}, bf16[128,512]{1,0:T(8,128)(2,1)S(1)}, u32[]{:S(2)}, u32[]{:S(2)}) collective-permute-start(bf16[128,512]{1,0:T(8,128)(2,1)S(1)} %get-tuple-element.30), channel_id=1, source_target_pairs={{0,24},{1,25},{2,26},{3,27},{4,28},{5,29},{6,30},{7,31},{8,0},{9,1... | collective-permute-start | bytes 393224 | tf_op jit(solution)/shard_map/ppermute | solution.py:35
  8.6 6.1 %collective-permute-start.5 = (bf16[128,512]{1,0:T(8,128)(2,1)S(1)}, bf16[128,512]{1,0:T(8,128)(2,1)S(1)}, u32[]{:S(2)}, u32[]{:S(2)}) collective-permute-start(bf16[128,512]{1,0:T(8,128)(2,1)S(1)} %get-tuple-element.30), channel_id=1, source_target_pairs={{0,8},{1,9},{2,10},{3,11},{4,12},{5,13},{6,14},{7,15},{8,16},{9,17... | collective-permute-start | bytes 393224 | tf_op jit(solution)/shard_map/ppermute | solution.py:35
  8.6 22.9 %collective-permute-start.2 = (bf16[384,512]{1,0:T(8,128)(2,1)S(1)}, bf16[384,512]{1,0:T(8,128)(2,1)S(1)}, u32[]{:S(2)}, u32[]{:S(2)}) collective-permute-start(bf16[384,512]{1,0:T(8,128)(2,1)S(1)} %constant_dynamic-update-slice_fusion.refs_3_.refs_9_), channel_id=1, source_target_pairs={{0,6},{1,7},{2,0},{3,1},{4,2},{5,3},{6,4},{7,5},{8,14},{9,15},{10,... | collective-permute-start | bytes 1179656 | tf_op jit(solution)/shard_map/ppermute | solution.py:35
  14.6 20.6 %collective-permute-start.1 = (bf16[384,512]{1,0:T(8,128)(2,1)S(1)}, bf16[384,512]{1,0:T(8,128)(2,1)S(1)}, u32[]{:S(2)}, u32[]{:S(2)}) collective-permute-start(bf16[384,512]{1,0:T(8,128)(2,1)S(1)} %constant_dynamic-update-slice_fusion.refs_3_.refs_9_), channel_id=1, source_target_pairs={{0,2},{1,3},{2,4},{3,5},{4,6},{5,7},{6,0},{7,1},{8,10},{9,11},{10,... | collective-permute-start | bytes 1179656 | tf_op jit(solution)/shard_map/ppermute | solution.py:35
  14.6 10.6 %collective-permute-start.8 = (bf16[384,512]{1,0:T(8,128)(2,1)S(1)}, bf16[384,512]{1,0:T(8,128)(2,1)S(1)}, u32[]{:S(2)}, u32[]{:S(2)}) collective-permute-start(bf16[384,512]{1,0:T(8,128)(2,1)S(1)} %constant_dynamic-update-slice_fusion.refs_3_.refs_9_), channel_id=1, source_target_pairs={{0,24},{1,25},{2,26},{3,27},{4,28},{5,29},{6,30},{7,31},{8,0},{9,1... | collective-permute-start | bytes 1179656 | tf_op jit(solution)/shard_map/ppermute | solution.py:35
  16.3 6.0 %collective-permute-start.17 = (bf16[128,512]{1,0:T(8,128)(2,1)S(1)}, bf16[128,512]{1,0:T(8,128)(2,1)S(1)}, u32[]{:S(2)}, u32[]{:S(2)}) collective-permute-start(bf16[128,512]{1,0:T(8,128)(2,1)S(1)} %collective-permute-done.5), channel_id=1, source_target_pairs={{0,8},{1,9},{2,10},{3,11},{4,12},{5,13},{6,14},{7,15},{8,16},{9,17... | collective-permute-start | bytes 393224 | tf_op jit(solution)/shard_map/ppermute | solution.py:35
  22.3 16.7 %collective-permute-start.7 = (bf16[384,512]{1,0:T(8,128)(2,1)S(1)}, bf16[384,512]{1,0:T(8,128)(2,1)S(1)}, u32[]{:S(2)}, u32[]{:S(2)}) collective-permute-start(bf16[384,512]{1,0:T(8,128)(2,1)S(1)} %constant_dynamic-update-slice_fusion.refs_3_.refs_9_), channel_id=1, source_target_pairs={{0,8},{1,9},{2,10},{3,11},{4,12},{5,13},{6,14},{7,15},{8,16},{9,17... | collective-permute-start | bytes 1179656 | tf_op jit(solution)/shard_map/ppermute | solution.py:35
  22.3 45.4 %copy-start.18 = (bf16[512,512]{1,0:T(8,128)(2,1)}, bf16[512,512]{1,0:T(8,128)(2,1)S(1)}, u32[]{:S(2)}) copy-start(bf16[512,512]{1,0:T(8,128)(2,1)S(1)} %constant_dynamic-update-slice_fusion.2.refs_21_) | copy-start | bytes 1572868
  25.3 23.5 %copy-start.1 = (bf16[384,512]{1,0:T(8,128)(2,1)}, bf16[384,512]{1,0:T(8,128)(2,1)S(1)}, u32[]{:S(2)}) copy-start(bf16[384,512]{1,0:T(8,128)(2,1)S(1)} %collective-permute-done.8.refs_5_.refs_11_) | copy-start | bytes 1179652
  25.3 14.3 %collective-permute-start.9 = (bf16[384,512]{1,0:T(8,128)(2,1)S(1)}, bf16[384,512]{1,0:T(8,128)(2,1)S(1)}, u32[]{:S(2)}, u32[]{:S(2)}) collective-permute-start(bf16[384,512]{1,0:T(8,128)(2,1)S(1)} %collective-permute-done.8.refs_5_.refs_11_), channel_id=1, source_target_pairs={{0,24},{1,25},{2,26},{3,27},{4,28},{5,29},{6,30},{7,31},{8,0},{9,1... | collective-permute-start | bytes 1179656 | tf_op jit(solution)/shard_map/ppermute | solution.py:35
  31.4 3.8 %copy-start.10 = (bf16[384,512]{1,0:T(8,128)(2,1)}, bf16[384,512]{1,0:T(8,128)(2,1)S(1)}, u32[]{:S(2)}) copy-start(bf16[384,512]{1,0:T(8,128)(2,1)S(1)} %collective-permute-done.2.refs_1_) | copy-start | bytes 1179652
  36.0 8.8 %collective-permute-start.10 = (bf16[384,512]{1,0:T(8,128)(2,1)}, bf16[384,512]{1,0:T(8,128)(2,1)S(1)}, u32[]{:S(2)}, u32[]{:S(2)}) collective-permute-start(bf16[384,512]{1,0:T(8,128)(2,1)} %get-tuple-element.37.refs_4_.refs_13_), channel_id=1, source_target_pairs={{0,8},{1,9},{2,10},{3,11},{4,12},{5,13},{6,14},{7,15},{8,16},{9,17... | collective-permute-start | bytes 1179656 | tf_op jit(solution)/shard_map/ppermute | solution.py:35
  37.5 15.6 %copy-start.11 = (bf16[384,512]{1,0:T(8,128)(2,1)S(1)}, bf16[384,512]{1,0:T(8,128)(2,1)}, u32[]{:S(2)}) copy-start(bf16[384,512]{1,0:T(8,128)(2,1)} %get-tuple-element.38.refs_4_.refs_17_) | copy-start | bytes 1179652
  37.5 30.3 %copy-start.13 = (bf16[384,512]{1,0:T(8,128)(2,1)S(1)}, bf16[384,512]{1,0:T(8,128)(2,1)}, u32[]{:S(2)}) copy-start(bf16[384,512]{1,0:T(8,128)(2,1)} %get-tuple-element.37.refs_4_.refs_13_) | copy-start | bytes 1179652
  37.5 25.3 %collective-permute-start.19 = (bf16[512,512]{1,0:T(8,128)(2,1)S(1)}, bf16[512,512]{1,0:T(8,128)(2,1)}, u32[]{:S(2)}, u32[]{:S(2)}) collective-permute-start(bf16[512,512]{1,0:T(8,128)(2,1)S(1)} %constant_dynamic-update-slice_fusion.2.refs_21_), channel_id=1, source_target_pairs={{0,6},{1,7},{2,0},{3,1},{4,2},{5,3},{6,4},{7,5},{8,14},{9,15},{10,... | collective-permute-start | bytes 1572872 | tf_op jit(solution)/shard_map/ppermute | solution.py:35
  39.0 14.1 %copy-start.2 = (bf16[384,512]{1,0:T(8,128)(2,1)}, bf16[384,512]{1,0:T(8,128)(2,1)S(1)}, u32[]{:S(2)}) copy-start(bf16[384,512]{1,0:T(8,128)(2,1)S(1)} %collective-permute-done.7.refs_4_.refs_10_) | copy-start | bytes 1179652
  39.0 14.1 %collective-permute-start.11 = (bf16[384,512]{1,0:T(8,128)(2,1)}, bf16[384,512]{1,0:T(8,128)(2,1)S(1)}, u32[]{:S(2)}, u32[]{:S(2)}) collective-permute-start(bf16[384,512]{1,0:T(8,128)(2,1)} %get-tuple-element.38.refs_4_.refs_17_), channel_id=1, source_target_pairs={{0,24},{1,25},{2,26},{3,27},{4,28},{5,29},{6,30},{7,31},{8,0},{9,1... | collective-permute-start | bytes 1179656 | tf_op jit(solution)/shard_map/ppermute | solution.py:35
  39.5 13.5 %copy-start.3 = (bf16[384,512]{1,0:T(8,128)(2,1)}, bf16[384,512]{1,0:T(8,128)(2,1)S(1)}, u32[]{:S(2)}) copy-start(bf16[384,512]{1,0:T(8,128)(2,1)S(1)} %collective-permute-done.9.refs_6_.refs_12_) | copy-start | bytes 1179652
  39.5 20.5 %collective-permute-start.3 = (bf16[384,512]{1,0:T(8,128)(2,1)}, bf16[384,512]{1,0:T(8,128)(2,1)}, u32[]{:S(2)}, u32[]{:S(2)}) collective-permute-start(bf16[384,512]{1,0:T(8,128)(2,1)} %get-tuple-element.37.refs_4_.refs_13_), channel_id=1, source_target_pairs={{0,2},{1,3},{2,4},{3,5},{4,6},{5,7},{6,0},{7,1},{8,10},{9,11},{10,... | collective-permute-start | bytes 1179656 | tf_op jit(solution)/shard_map/ppermute | solution.py:35
  44.8 23.0 %copy-start.4 = (bf16[384,512]{1,0:T(8,128)(2,1)}, bf16[384,512]{1,0:T(8,128)(2,1)S(1)}, u32[]{:S(2)}) copy-start(bf16[384,512]{1,0:T(8,128)(2,1)S(1)} %collective-permute-done.10.refs_5_.refs_14_) | copy-start | bytes 1179652
  44.8 18.2 %collective-permute-start.13 = (bf16[384,512]{1,0:T(8,128)(2,1)}, bf16[384,512]{1,0:T(8,128)(2,1)S(1)}, u32[]{:S(2)}, u32[]{:S(2)}) collective-permute-start(bf16[384,512]{1,0:T(8,128)(2,1)} %get-tuple-element.37.refs_4_.refs_13_), channel_id=1, source_target_pairs={{0,24},{1,25},{2,26},{3,27},{4,28},{5,29},{6,30},{7,31},{8,0},{9,1... | collective-permute-start | bytes 1179656 | tf_op jit(solution)/shard_map/ppermute | solution.py:35
  47.3 20.4 %collective-permute-start.14 = (bf16[384,512]{1,0:T(8,128)(2,1)S(1)}, bf16[384,512]{1,0:T(8,128)(2,1)S(1)}, u32[]{:S(2)}, u32[]{:S(2)}) collective-permute-start(bf16[384,512]{1,0:T(8,128)(2,1)S(1)} %collective-permute-done.10.refs_5_.refs_14_), channel_id=1, source_target_pairs={{0,8},{1,9},{2,10},{3,11},{4,12},{5,13},{6,14},{7,15},{8,16},{9,17... | collective-permute-start | bytes 1179656 | tf_op jit(solution)/shard_map/ppermute | solution.py:35
  53.1 19.5 %copy-start.5 = (bf16[384,512]{1,0:T(8,128)(2,1)}, bf16[384,512]{1,0:T(8,128)(2,1)S(1)}, u32[]{:S(2)}) copy-start(bf16[384,512]{1,0:T(8,128)(2,1)S(1)} %collective-permute-done.11.refs_6_.refs_19_) | copy-start | bytes 1179652
  53.1 19.3 %collective-permute-start.15 = (bf16[384,512]{1,0:T(8,128)(2,1)S(1)}, bf16[384,512]{1,0:T(8,128)(2,1)S(1)}, u32[]{:S(2)}, u32[]{:S(2)}) collective-permute-start(bf16[384,512]{1,0:T(8,128)(2,1)S(1)} %copy-done.11), channel_id=1, source_target_pairs={{0,8},{1,9},{2,10},{3,11},{4,12},{5,13},{6,14},{7,15},{8,16},{9,17... | collective-permute-start | bytes 1179656 | tf_op jit(solution)/shard_map/ppermute | solution.py:35
  60.0 12.6 %collective-permute-start.16 = (bf16[384,512]{1,0:T(8,128)(2,1)S(1)}, bf16[384,512]{1,0:T(8,128)(2,1)S(1)}, u32[]{:S(2)}, u32[]{:S(2)}) collective-permute-start(bf16[384,512]{1,0:T(8,128)(2,1)S(1)} %collective-permute-done.11.refs_6_.refs_19_), channel_id=1, source_target_pairs={{0,24},{1,25},{2,26},{3,27},{4,28},{5,29},{6,30},{7,31},{8,0},{9,1... | collective-permute-start | bytes 1179656 | tf_op jit(solution)/shard_map/ppermute | solution.py:35
  62.9 14.2 %collective-permute-start.12 = (bf16[384,512]{1,0:T(8,128)(2,1)}, bf16[384,512]{1,0:T(8,128)(2,1)}, u32[]{:S(2)}, u32[]{:S(2)}) collective-permute-start(bf16[384,512]{1,0:T(8,128)(2,1)} %collective-permute-done.3.refs_25_), channel_id=1, source_target_pairs={{0,8},{1,9},{2,10},{3,11},{4,12},{5,13},{6,14},{7,15},{8,16},{9,17... | collective-permute-start | bytes 1179656 | tf_op jit(solution)/shard_map/ppermute | solution.py:35
  63.0 9.3 %copy-start.6 = (bf16[384,512]{1,0:T(8,128)(2,1)}, bf16[384,512]{1,0:T(8,128)(2,1)S(1)}, u32[]{:S(2)}) copy-start(bf16[384,512]{1,0:T(8,128)(2,1)S(1)} %collective-permute-done.13.refs_6_.refs_15_) | copy-start | bytes 1179652
  63.0 25.4 %collective-permute-start.20 = (bf16[512,512]{1,0:T(8,128)(2,1)}, bf16[512,512]{1,0:T(8,128)(2,1)}, u32[]{:S(2)}, u32[]{:S(2)}) collective-permute-start(bf16[512,512]{1,0:T(8,128)(2,1)} %collective-permute-done.19.refs_23_), channel_id=1, source_target_pairs={{0,6},{1,7},{2,0},{3,1},{4,2},{5,3},{6,4},{7,5},{8,14},{9,15},{10,... | collective-permute-start | bytes 1572872 | tf_op jit(solution)/shard_map/ppermute | solution.py:35
  67.7 4.6 %copy-start.7 = (bf16[384,512]{1,0:T(8,128)(2,1)}, bf16[384,512]{1,0:T(8,128)(2,1)S(1)}, u32[]{:S(2)}) copy-start(bf16[384,512]{1,0:T(8,128)(2,1)S(1)} %collective-permute-done.14.refs_7_.refs_16_) | copy-start | bytes 1179652
  67.7 23.6 %collective-permute-start.18 = (bf16[512,512]{1,0:T(8,128)(2,1)S(1)}, bf16[512,512]{1,0:T(8,128)(2,1)}, u32[]{:S(2)}, u32[]{:S(2)}) collective-permute-start(bf16[512,512]{1,0:T(8,128)(2,1)S(1)} %constant_dynamic-update-slice_fusion.2.refs_21_), channel_id=1, source_target_pairs={{0,2},{1,3},{2,4},{3,5},{4,6},{5,7},{6,0},{7,1},{8,10},{9,11},{10,... | collective-permute-start | bytes 1572872 | tf_op jit(solution)/shard_map/ppermute | solution.py:35
  72.3 7.6 %copy-start.20 = (f32[20,2]{0,1:T(2,128)S(1)}, f32[20,2]{0,1:T(2,128)}, u32[]{:S(2)}) copy-start(f32[20,2]{0,1:T(2,128)} %param.15) | copy-start | bytes 484
  72.3 7.7 %copy-start.19 = (bf16[1,2,24,256]{3,2,1,0:T(8,128)(2,1)S(1)}, bf16[1,2,24,256]{3,2,1,0:T(8,128)(2,1)}, u32[]{:S(2)}) copy-start(bf16[1,2,24,256]{3,2,1,0:T(8,128)(2,1)} %param.10) | copy-start | bytes 73732
  72.4 19.0 %copy-start.16 = (s32[3]{0:T(128)S(1)}, s32[3]{0:T(128)}, u32[]{:S(2)}) copy-start(s32[3]{0:T(128)} %widths.3) | copy-start | bytes 40
  72.4 19.0 %copy-start.17 = (s32[32]{0:T(128)S(1)}, s32[32]{0:T(128)}, u32[]{:S(2)}) copy-start(s32[32]{0:T(128)} %refs_2_.1) | copy-start | bytes 388
  72.4 4.6 %copy-start.8 = (bf16[384,512]{1,0:T(8,128)(2,1)}, bf16[384,512]{1,0:T(8,128)(2,1)S(1)}, u32[]{:S(2)}) copy-start(bf16[384,512]{1,0:T(8,128)(2,1)S(1)} %collective-permute-done.15.refs_5_.refs_18_) | copy-start | bytes 1179652
  72.4 16.1 %collective-permute-start.21 = (bf16[384,512]{1,0:T(8,128)(2,1)}, bf16[384,512]{1,0:T(8,128)(2,1)}, u32[]{:S(2)}, u32[]{:S(2)}) collective-permute-start(bf16[384,512]{1,0:T(8,128)(2,1)} %collective-permute-done.3.refs_25_), channel_id=1, source_target_pairs={{0,24},{1,25},{2,26},{3,27},{4,28},{5,29},{6,30},{7,31},{8,0},{9,1... | collective-permute-start | bytes 1179656 | tf_op jit(solution)/shard_map/ppermute | solution.py:35
  72.6 4.5 %copy-start.9 = (bf16[384,512]{1,0:T(8,128)(2,1)}, bf16[384,512]{1,0:T(8,128)(2,1)S(1)}, u32[]{:S(2)}) copy-start(bf16[384,512]{1,0:T(8,128)(2,1)S(1)} %collective-permute-done.16.refs_7_.refs_20_) | copy-start | bytes 1179652
  77.1 14.3 %collective-permute-start.22 = (bf16[384,512]{1,0:T(8,128)(2,1)}, bf16[384,512]{1,0:T(8,128)(2,1)}, u32[]{:S(2)}, u32[]{:S(2)}) collective-permute-start(bf16[384,512]{1,0:T(8,128)(2,1)} %collective-permute-done.12.refs_26_), channel_id=1, source_target_pairs={{0,8},{1,9},{2,10},{3,11},{4,12},{5,13},{6,14},{7,15},{8,16},{9,17... | collective-permute-start | bytes 1179656 | tf_op jit(solution)/shard_map/ppermute | solution.py:35
  101.5 1.5 %collective-permute-start.28 = (bf16[384,256]{1,0:T(8,128)(2,1)S(1)}, bf16[384,256]{1,0:T(8,128)(2,1)S(1)}, u32[]{:S(2)}, u32[]{:S(2)}) collective-permute-start(bf16[384,256]{1,0:T(8,128)(2,1)S(1)} %get-tuple-element.49), channel_id=1, source_target_pairs={{0,1},{1,0},{2,3},{3,2},{4,5},{5,4},{6,7},{7,6},{8,9},{9,8},{10,11... | collective-permute-start | bytes 589832 | tf_op jit(solution)/shard_map/ppermute | solution.py:35
  101.6 8.7 %collective-permute-start.23 = (f32[4,64,256]{2,1,0:T(8,128)S(1)}, f32[4,64,256]{2,1,0:T(8,128)S(1)}, u32[]{:S(2)}, u32[]{:S(2)}) collective-permute-start(f32[4,64,256]{2,1,0:T(8,128)S(1)} %get-tuple-element.44), channel_id=1, source_target_pairs={{0,128},{32,160},{64,192},{96,224},{128,0},{160,32},{192,64},{224,... | collective-permute-start | bytes 786440 | tf_op jit(solution)/shard_map/ppermute | solution.py:448
  103.9 19.9 %all-to-all-start = ((f32[16,24,256]{2,1,0:T(8,128)}), f32[16,24,256]{2,1,0:T(8,128)S(1)}, u32[]{:S(2)}, u32[]{:S(2)}) async-start(f32[16,24,256]{2,1,0:T(8,128)} %bitcast.9), calls=%async_computation | async-start | bytes 786432 | tf_op jit(solution)/shard_map/all_to_all | solution.py:447
  110.4 4.6 %collective-permute-start.24 = (f32[64,256]{1,0:T(8,128)S(1)}, f32[64,256]{1,0:T(8,128)S(1)}, u32[]{:S(2)}, u32[]{:S(2)}) collective-permute-start(f32[64,256]{1,0:T(8,128)S(1)} %get-tuple-element.52), channel_id=1, source_target_pairs={{0,32},{32,0},{64,96},{96,64},{128,160},{160,128},{192,224},{224,1... | collective-permute-start | bytes 196616 | tf_op jit(solution)/shard_map/ppermute | solution.py:451
  112.1 5.5 %collective-permute-start.26 = (f32[64,256]{1,0:T(8,128)S(1)}, f32[64,256]{1,0:T(8,128)S(1)}, u32[]{:S(2)}, u32[]{:S(2)}) collective-permute-start(f32[64,256]{1,0:T(8,128)S(1)} %get-tuple-element.53), channel_id=1, source_target_pairs={{0,96},{32,64},{64,32},{96,0},{128,224},{160,192},{192,160},{224,1... | collective-permute-start | bytes 196616 | tf_op jit(solution)/shard_map/ppermute | solution.py:451
  114.3 5.8 %collective-permute-start.25 = (f32[64,256]{1,0:T(8,128)S(1)}, f32[64,256]{1,0:T(8,128)S(1)}, u32[]{:S(2)}, u32[]{:S(2)}) collective-permute-start(f32[64,256]{1,0:T(8,128)S(1)} %get-tuple-element.54), channel_id=1, source_target_pairs={{0,64},{32,96},{64,0},{96,32},{128,192},{160,224},{192,128},{224,1... | collective-permute-start | bytes 196616 | tf_op jit(solution)/shard_map/ppermute | solution.py:451
  120.1 3.7 %collective-permute-start.27 = (bf16[32,256]{1,0:T(8,128)(2,1)S(1)}, bf16[32,256]{1,0:T(8,128)(2,1)S(1)}, u32[]{:S(2)}, u32[]{:S(2)}) collective-permute-start(bf16[32,256]{1,0:T(8,128)(2,1)S(1)} %get-tuple-element.56), channel_id=1, source_target_pairs={{0,1},{1,0},{2,3},{3,2},{4,5},{5,4},{6,7},{7,6},{8,9},{9,8},{10,11... | collective-permute-start | bytes 49160 | tf_op jit(solution)/shard_map/ppermute | solution.py:35
  (3 other events, 2.5 us)

commit v6 on v5

--- a/solution.py
+++ b/solution.py
@@ -59,6 +59,10 @@
     return lax.ppermute(value, GRID, perm)
 
 
+def in_hbm(value):
+    return pltpu.with_memory_space_constraint(value, pltpu.HBM)
+
+
 def params(mib):
     return pltpu.CompilerParams(vmem_limit_bytes=mib * MIB)
 
@@ -102,7 +106,7 @@
         return factor[i, :, pl.ds(pl.multiple_of(k * B, B), B)]
 
     def kept(value, k):
-        keep = (pattern[dev, k] > 0).astype(jnp.float32)
+        keep = (pattern[k, dev] > 0).astype(jnp.float32)
         return (value.astype(jnp.float32) * keep).astype(jnp.bfloat16)
 
     col = lax.broadcasted_iota(jnp.int32, (B, B), 1)
@@ -111,8 +115,8 @@
     for i in range(2):
         large.append(kept(cut(i, full), full))
         late = jnp.dot(cut(i, two), move, preferred_element_type=jnp.float32)
-        keep_one = (pattern[dev, one] > 0).astype(jnp.float32)
-        keep_two = (pattern[dev, two] > 0).astype(jnp.float32)
+        keep_one = (pattern[one, dev] > 0).astype(jnp.float32)
+        keep_two = (pattern[two, dev] > 0).astype(jnp.float32)
         both = jnp.where(col < split, cut(i, one).astype(jnp.float32) * keep_one, late * keep_two)
         small.append(both.astype(jnp.bfloat16))
 
@@ -256,7 +260,7 @@
 
     gemm_sum(fetched, acc, total, *scratch[:2])
     acc = total
-    wr, wi = weights[assign[0], 0], weights[assign[0], 1]
+    wr, wi = weights[0, assign[0]], weights[1, assign[0]]
     parts = []
     for j in range(2):
         top, low = acc[2 * j * B : (2 * j + 1) * B], acc[(2 * j + 1) * B : (2 * j + 2) * B]
@@ -336,7 +340,7 @@
     full, one, two, split = layout(widths)
     rows = B // POLES
     col = lax.broadcasted_iota(jnp.int32, (rows, B), 1)
-    shares = []
+    shares, depth = [], diag.shape[0]
     for p in range(POLES):
         out = slice(p * rows, (p + 1) * rows)
         part = got[p].astype(jnp.float32)
@@ -347,7 +351,7 @@
         panel[out, pl.ds(pl.multiple_of(one * B, B), B)] = jnp.where(col < split, small, 0)
         late = pltpu.roll(small, B - split, 1)
         panel[out, pl.ds(pl.multiple_of(two * B, B), B)] = jnp.where(col < B - split, late, 0)
-        shares.append((part[2 * rows : 3 * rows] + part[3 * rows :])[: diag.shape[0]])
+        shares.append(part[2 * rows : 2 * rows + depth] + part[2 * rows + depth :])
     diag[...] = sum(shares)
 
 
@@ -370,7 +374,7 @@
     total = factor.shape[3]
     depth = diag_inverse.shape[2]
     own_inverse = pltpu.with_memory_space_constraint(inverse[0], pltpu.HBM)
-    top, rest, give = prepare(device, widths, pattern, factor[0])
+    top, rest, give = prepare(device, in_hbm(widths), in_hbm(pattern.T), in_hbm(factor[0]))
     taken = shift(give, 0, 0, 1)
     pieces, sources = [], []
 
@@ -430,13 +434,16 @@
     acc = gemm(device, own_inverse, sib_inverse, acc, held, segments)
     far_f, acc = after((far_f, acc))
     far_far = shift(far_f, 1, 0)
-    held = (across, across_f, across_b, across_far)
-    segments = listing(held, [[(ox, oz, False) for ox in orders] for oz in orders], 1)
-    held = (z_far, far_f, far_b, far_far)
-    segments += listing(held, [[(ox, 2, False)] for ox in orders], 0)
+    held, along = (z_far, far_f), (across, across_b)
+    segments = listing(held, [[(0, 2, False)], [(-1, 2, False)]], 0)
+    segments += listing(along, [[(ox, oz, False) for ox in orders] for oz in (0, 1)], 1)
+    acc = gemm(device, own_inverse, sib_inverse, acc, held + along, segments)
+    segments = listing((far_b, far_far), [[(1, 2, False)], [(2, 2, False)]], 0)
+    along = (across_f, across_far)
+    segments += listing(along, [[(ox, oz, False) for ox in orders] for oz in (-1, 2)], 1)
 
     mine, given, over, *parts = finish(
-        device, widths, owner, assign, pole_weights, acc,
+        device, widths, owner, assign, pole_weights.T, acc,
         diag_inverse[0].astype(jnp.float32), own_inverse, sib_inverse,
         pieces, tuple(sources), segments, total,
     )
@@ -457,8 +464,7 @@
     diag = shared.astype(jnp.float32).sum(0)
     high = diag.astype(jnp.bfloat16)
     low = (diag - high.astype(jnp.float32)).astype(jnp.bfloat16)
-    pad = ((0, rows - depth), (0, 0))
-    both = jnp.concatenate([got[:rows], other, jnp.pad(high, pad), jnp.pad(low, pad)], 0)
+    both = jnp.concatenate([got[:rows], other, high, low], 0)
     both = lax.all_to_all(
         jnp.broadcast_to(both[None], (POLES,) + both.shape), "pole", 0, 0, tiled=True
     )

time: 139 us -> 135 us (0.971)
  waiting for transfers between devices: 47.8 us -> 39.1 us
  starting transfers between devices: 45.4 us -> 50.6 us
  local copies, waits for them, and re-layouts: 3.59 us -> 1.72 us
  Pallas kernels: 26.1 us -> 27.9 us
    ppermute x25, waiting for transfers between devices: 38.7 us -> 30.2 us  [shift(): return lax.ppermute(value, GRID, perm)]
    all_to_all x1, starting transfers between devices: 6.07 us -> 12.5 us  [local(): lax.all_to_all(mine, GRID, 0, 0, axis_index_groups=groups, tiled=True)]
    pallas_call x3 -> x4, Pallas kernels: 13.2 us -> 18.1 us  [gemm(): pl.pallas_call(functools.partial(gemm_body, segments, has_acc), in_specs=...]
    pallas_call x1, Pallas kernels: 10.2 us -> 6.82 us  [finish(): pl.pallas_call(functools.partial(finish_body, sources, segments), in_spec...]
    unnamed x48 -> x56, local copies, waits for them, and re-layouts: 3.52 us -> 1.66 us
    ppermute x25, starting transfers between devices: 34.6 us -> 33.2 us  [shift(): return lax.ppermute(value, GRID, perm)]
  transfers between devices with their start and end apart: 30 -> 30, of which waited for: 14 -> 13; matrix products, arithmetic and copies ran while one was open for 1% -> 1% of each run, Pallas kernels for 10% -> 13%
where the time goes in v6:
time: 135 us
  starting transfers between devices  50.6 us (37%)
  waiting for transfers between devices  39.1 us (29%)
  Pallas kernels  27.9 us (21%)
  blocking collectives  13.2 us (10%)
  local copies, waits for them, and re-layouts  1.72 us (1%)
  between operations  1.71 us (1%)
    ppermute x25, starting transfers between devices, shift(): return lax.ppermute(value, GRID, perm)  33.2 us
    ppermute x25, waiting for transfers between devices, shift(): return lax.ppermute(value, GRID, perm)  30.2 us
    pallas_call x4, Pallas kernels, gemm(): pl.pallas_call(functools.partial(gemm_body, segments, has_acc), in_specs=...  18.1 us
    all_to_all x1, blocking collectives, local(): lax.all_to_all(jnp.broadcast_to(both[None], (POLES,) + both.shape), 'pole...  13.2 us
    all_to_all x1, starting transfers between devices, local(): lax.all_to_all(mine, GRID, 0, 0, axis_index_groups=groups, tiled=True)  12.5 us
    pallas_call x1, Pallas kernels, finish(): pl.pallas_call(functools.partial(finish_body, sources, segments), in_spec...  6.82 us
    ppermute x3, waiting for transfers between devices, local(): lax.ppermute(part, 'pole', [(p, p ^ d) for p in range(POLES)])  5.16 us
    ppermute x3, starting transfers between devices, local(): lax.ppermute(part, 'pole', [(p, p ^ d) for p in range(POLES)])  4.79 us
  transfers between devices with their start and end apart: 30, of which 13 were waited for; matrix products, arithmetic and copies ran while one was open for 1% of the time, Pallas kernels for 13%

profile of v6, /device:TPU:2, one launch (start us, length us, event | category | flops | bytes accessed | tf_op | source)
XLA Modules:
  0.0 135.2 jit_solution(10043072011621549355)
XLA Ops:
  0.7 1.5 %shard_map.95 = (bf16[128,512]{1,0:T(8,128)(2,1)S(1)}, bf16[128,512]{1,0:T(8,128)(2,1)S(1)}, bf16[256,512]{1,0:T(8,128)(2,1)S(1)}) custom-call(s32[2]{0:T(128)S(1)} %pad_add_fusion.device.refs_0_, s32[3]{0:T(128)} %widths.3, s32[3,32]{1,0:T(4,128)} %bitcast.42, bf16[2,256,768]{2,1,0:T(8,128)(2,1)} %bitcast.41), custom_call_target="tpu_custom_call" | custom-call | tf_op jit(solution)/shard_map/pallas_call | solution.py:141
  2.3 1.5 %collective-permute-done = bf16[256,512]{1,0:T(8,128)(2,1)S(1)} collective-permute-done((bf16[256,512]{1,0:T(8,128)(2,1)S(1)}, bf16[256,512]{1,0:T(8,128)(2,1)S(1)}, u32[]{:S(2)}, u32[]{:S(2)}) %collective-permute-start) | collective-permute-done | bytes 262176 | tf_op jit(solution)/shard_map/ppermute | solution.py:35
  3.8 0.2 collective-permute-start.1
  4.1 1.5 %collective-permute-start.5 = (bf16[128,512]{1,0:T(8,128)(2,1)S(1)}, bf16[128,512]{1,0:T(8,128)(2,1)S(1)}, u32[]{:S(2)}, u32[]{:S(2)}) collective-permute-start(bf16[128,512]{1,0:T(8,128)(2,1)S(1)} %get-tuple-element.30), channel_id=1, source_target_pairs={{0,8},{1,9},{2,10},{3,11},{4,12},{5,13},{6,14},{7,15},{8,16},{9,17... | collective-permute-start | bytes 393224 | tf_op jit(solution)/shard_map/ppermute | solution.py:35
  5.6 0.8 collective-permute-start.6
  6.4 3.0 %collective-permute-start.2 = (bf16[384,512]{1,0:T(8,128)(2,1)S(1)}, bf16[384,512]{1,0:T(8,128)(2,1)S(1)}, u32[]{:S(2)}, u32[]{:S(2)}) collective-permute-start(bf16[384,512]{1,0:T(8,128)(2,1)S(1)} %constant_dynamic-update-slice_fusion.refs_3_.refs_9_), channel_id=1, source_target_pairs={{0,2},{1,3},{2,4},{3,5},{4,6},{5,7},{6,0},{7,1},{8,10},{9,11},{10,... | collective-permute-start | bytes 1179656 | tf_op jit(solution)/shard_map/ppermute | solution.py:35
  9.4 3.0 %collective-permute-start.3 = (bf16[384,512]{1,0:T(8,128)(2,1)S(1)}, bf16[384,512]{1,0:T(8,128)(2,1)S(1)}, u32[]{:S(2)}, u32[]{:S(2)}) collective-permute-start(bf16[384,512]{1,0:T(8,128)(2,1)S(1)} %constant_dynamic-update-slice_fusion.refs_3_.refs_9_), channel_id=1, source_target_pairs={{0,6},{1,7},{2,0},{3,1},{4,2},{5,3},{6,4},{7,5},{8,14},{9,15},{10,... | collective-permute-start | bytes 1179656 | tf_op jit(solution)/shard_map/ppermute | solution.py:35
  12.4 1.7 %collective-permute-start.8 = (bf16[384,512]{1,0:T(8,128)(2,1)S(1)}, bf16[384,512]{1,0:T(8,128)(2,1)S(1)}, u32[]{:S(2)}, u32[]{:S(2)}) collective-permute-start(bf16[384,512]{1,0:T(8,128)(2,1)S(1)} %constant_dynamic-update-slice_fusion.refs_3_.refs_9_), channel_id=1, source_target_pairs={{0,24},{1,25},{2,26},{3,27},{4,28},{5,29},{6,30},{7,31},{8,0},{9,1... | collective-permute-start | bytes 1179656 | tf_op jit(solution)/shard_map/ppermute | solution.py:35
  14.2 0.4 collective-permute-start.17
  14.6 4.8 %collective-permute-done.17 = bf16[128,512]{1,0:T(8,128)(2,1)S(1)} collective-permute-done((bf16[128,512]{1,0:T(8,128)(2,1)S(1)}, bf16[128,512]{1,0:T(8,128)(2,1)S(1)}, u32[]{:S(2)}, u32[]{:S(2)}) %collective-permute-start.17) | collective-permute-done | bytes 131104 | tf_op jit(solution)/shard_map/ppermute | solution.py:35
  19.5 3.4 %collective-permute-done.8.refs_5_.refs_11_ = bf16[384,512]{1,0:T(8,128)(2,1)S(1)} collective-permute-done((bf16[384,512]{1,0:T(8,128)(2,1)S(1)}, bf16[384,512]{1,0:T(8,128)(2,1)S(1)}, u32[]{:S(2)}, u32[]{:S(2)}) %collective-permute-start.8) | collective-permute-done | bytes 393248 | tf_op jit(solution)/shard_map/ppermute | solution.py:35
  23.0 1.7 %collective-permute-start.9 = (bf16[384,512]{1,0:T(8,128)(2,1)S(1)}, bf16[384,512]{1,0:T(8,128)(2,1)S(1)}, u32[]{:S(2)}, u32[]{:S(2)}) collective-permute-start(bf16[384,512]{1,0:T(8,128)(2,1)S(1)} %collective-permute-done.8.refs_5_.refs_11_), channel_id=1, source_target_pairs={{0,24},{1,25},{2,26},{3,27},{4,28},{5,29},{6,30},{7,31},{8,0},{9,1... | collective-permute-start | bytes 1179656 | tf_op jit(solution)/shard_map/ppermute | solution.py:35
  24.7 6.4 %collective-permute-done.3.refs_1_ = bf16[384,512]{1,0:T(8,128)(2,1)S(1)} collective-permute-done((bf16[384,512]{1,0:T(8,128)(2,1)S(1)}, bf16[384,512]{1,0:T(8,128)(2,1)S(1)}, u32[]{:S(2)}, u32[]{:S(2)}) %collective-permute-start.3) | collective-permute-done | bytes 393248 | tf_op jit(solution)/shard_map/ppermute | solution.py:35
  31.1 0.7 copy-done.16
  31.8 1.5 %collective-permute-start.10 = (bf16[384,512]{1,0:T(8,128)(2,1)}, bf16[384,512]{1,0:T(8,128)(2,1)S(1)}, u32[]{:S(2)}, u32[]{:S(2)}) collective-permute-start(bf16[384,512]{1,0:T(8,128)(2,1)} %get-tuple-element.37.refs_4_.refs_13_), channel_id=1, source_target_pairs={{0,8},{1,9},{2,10},{3,11},{4,12},{5,13},{6,14},{7,15},{8,16},{9,17... | collective-permute-start | bytes 1179656 | tf_op jit(solution)/shard_map/ppermute | solution.py:35
  33.3 2.7 %collective-permute-start.18 = (bf16[512,512]{1,0:T(8,128)(2,1)S(1)}, bf16[512,512]{1,0:T(8,128)(2,1)S(1)}, u32[]{:S(2)}, u32[]{:S(2)}) collective-permute-start(bf16[512,512]{1,0:T(8,128)(2,1)S(1)} %constant_dynamic-update-slice_fusion.2.refs_6_.refs_23_), channel_id=1, source_target_pairs={{0,6},{1,7},{2,0},{3,1},{4,2},{5,3},{6,4},{7,5},{8,14},{9,15},{10,... | collective-permute-start | bytes 1572872 | tf_op jit(solution)/shard_map/ppermute | solution.py:35
  36.0 0.5 collective-permute-start.11
  36.6 1.1 collective-permute-start.4
  37.6 5.0 %collective-permute-done.10.refs_5_.refs_14_ = bf16[384,512]{1,0:T(8,128)(2,1)S(1)} collective-permute-done((bf16[384,512]{1,0:T(8,128)(2,1)}, bf16[384,512]{1,0:T(8,128)(2,1)S(1)}, u32[]{:S(2)}, u32[]{:S(2)}) %collective-permute-start.10) | collective-permute-done | bytes 393248 | tf_op jit(solution)/shard_map/ppermute | solution.py:35
  42.6 3.0 %collective-permute-start.13 = (bf16[384,512]{1,0:T(8,128)(2,1)}, bf16[384,512]{1,0:T(8,128)(2,1)S(1)}, u32[]{:S(2)}, u32[]{:S(2)}) collective-permute-start(bf16[384,512]{1,0:T(8,128)(2,1)} %get-tuple-element.37.refs_4_.refs_13_), channel_id=1, source_target_pairs={{0,24},{1,25},{2,26},{3,27},{4,28},{5,29},{6,30},{7,31},{8,0},{9,1... | collective-permute-start | bytes 1179656 | tf_op jit(solution)/shard_map/ppermute | solution.py:35
  45.6 4.3 %shard_map.97.refs_3_ = f32[1024,512]{1,0:T(8,128)S(1)} custom-call(s32[2]{0:T(128)S(1)} %pad_add_fusion.device.refs_0_, bf16[2,8192,256]{2,1,0:T(8,128)(2,1)} %bitcast.36, bf16[2,8192,256]{2,1,0:T(8,128)(2,1)} %collective-permute-done.1.refs_2_.refs_8_, bf16[384,512]{1,0:T(8,128)(2,1)S(1)} %constant_dynamic-update-slice_fusion.refs_3_.refs_9_, ...), custom_call_target="tpu_custom_call" | custom-call | tf_op jit(solution)/shard_map/pallas_call | solution.py:214
  49.9 0.6 collective-permute-start.15
  50.6 4.6 %collective-permute-done.4.refs_4_.refs_21_ = bf16[384,512]{1,0:T(8,128)(2,1)S(1)} collective-permute-done((bf16[384,512]{1,0:T(8,128)(2,1)}, bf16[384,512]{1,0:T(8,128)(2,1)S(1)}, u32[]{:S(2)}, u32[]{:S(2)}) %collective-permute-start.4) | collective-permute-done | bytes 393248 | tf_op jit(solution)/shard_map/ppermute | solution.py:35
  55.1 2.9 %collective-permute-start.16 = (bf16[384,512]{1,0:T(8,128)(2,1)S(1)}, bf16[384,512]{1,0:T(8,128)(2,1)S(1)}, u32[]{:S(2)}, u32[]{:S(2)}) collective-permute-start(bf16[384,512]{1,0:T(8,128)(2,1)S(1)} %collective-permute-done.11.refs_6_.refs_19_), channel_id=1, source_target_pairs={{0,24},{1,25},{2,26},{3,27},{4,28},{5,29},{6,30},{7,31},{8,0},{9,1... | collective-permute-start | bytes 1179656 | tf_op jit(solution)/shard_map/ppermute | solution.py:35
  58.0 0.8 collective-permute-done.18.refs_7_.refs_24_
  58.8 1.2 collective-permute-start.12
  60.0 3.5 %collective-permute-start.22 = (bf16[512,512]{1,0:T(8,128)(2,1)S(1)}, bf16[512,512]{1,0:T(8,128)(2,1)S(1)}, u32[]{:S(2)}, u32[]{:S(2)}) collective-permute-start(bf16[512,512]{1,0:T(8,128)(2,1)S(1)} %collective-permute-done.18.refs_7_.refs_24_), channel_id=1, source_target_pairs={{0,6},{1,7},{2,0},{3,1},{4,2},{5,3},{6,4},{7,5},{8,14},{9,15},{10,... | collective-permute-start | bytes 1572872 | tf_op jit(solution)/shard_map/ppermute | solution.py:35
  63.5 1.0 collective-permute-start.21
  64.5 4.5 %shard_map.98.refs_3_ = f32[1024,512]{1,0:T(8,128)S(1)} custom-call(s32[2]{0:T(128)S(1)} %pad_add_fusion.device.refs_0_, bf16[2,8192,256]{2,1,0:T(8,128)(2,1)} %bitcast.37, bf16[2,8192,256]{2,1,0:T(8,128)(2,1)} %collective-permute-done.1.refs_2_.refs_8_, f32[1024,512]{1,0:T(8,128)S(1)} %shard_map.97.refs_3_, bf16[384,512]{1,0:T(8,128)(2,1)S(1)} %copy-done.15, ...), custom_call_target="tpu_custom_call" | custom-call | tf_op jit(solution)/shard_map/pallas_call | solution.py:214
  69.0 2.0 %collective-permute-start.19 = (bf16[384,512]{1,0:T(8,128)(2,1)S(1)}, bf16[384,512]{1,0:T(8,128)(2,1)S(1)}, u32[]{:S(2)}, u32[]{:S(2)}) collective-permute-start(bf16[384,512]{1,0:T(8,128)(2,1)S(1)} %collective-permute-done.4.refs_4_.refs_21_), channel_id=1, source_target_pairs={{0,24},{1,25},{2,26},{3,27},{4,28},{5,29},{6,30},{7,31},{8,0},{9,1... | collective-permute-start | bytes 1179656 | tf_op jit(solution)/shard_map/ppermute | solution.py:35
  71.0 4.5 %shard_map.99.refs_3_ = f32[1024,512]{1,0:T(8,128)S(1)} custom-call(s32[2]{0:T(128)S(1)} %pad_add_fusion.device.refs_0_, bf16[2,8192,256]{2,1,0:T(8,128)(2,1)} %bitcast.38, bf16[2,8192,256]{2,1,0:T(8,128)(2,1)} %collective-permute-done.1.refs_2_.refs_8_, f32[1024,512]{1,0:T(8,128)S(1)} %shard_map.98.refs_3_, bf16[384,512]{1,0:T(8,128)(2,1)S(1)} %copy-done.17, ...), custom_call_target="tpu_custom_call" | custom-call | tf_op jit(solution)/shard_map/pallas_call | solution.py:214
  75.6 0.4 collective-permute-start.20
  76.7 4.8 %shard_map.100.refs_5_ = f32[1024,512]{1,0:T(8,128)S(1)} custom-call(s32[2]{0:T(128)S(1)} %pad_add_fusion.device.refs_0_, bf16[2,8192,256]{2,1,0:T(8,128)(2,1)} %bitcast.39, bf16[2,8192,256]{2,1,0:T(8,128)(2,1)} %collective-permute-done.1.refs_2_.refs_8_, f32[1024,512]{1,0:T(8,128)S(1)} %shard_map.99.refs_3_, ...), custom_call_target="tpu_custom_call" | custom-call | tf_op jit(solution)/shard_map/pallas_call | solution.py:214
  81.6 0.8 collective-permute-done.22.refs_28_
  82.4 1.7 %collective-permute-done.20.refs_26_ = bf16[384,512]{1,0:T(8,128)(2,1)S(1)} collective-permute-done((bf16[384,512]{1,0:T(8,128)(2,1)S(1)}, bf16[384,512]{1,0:T(8,128)(2,1)S(1)}, u32[]{:S(2)}, u32[]{:S(2)}) %collective-permute-start.20) | collective-permute-done | bytes 393248 | tf_op jit(solution)/shard_map/ppermute | solution.py:35
  84.1 0.8 copy-done.24
  84.8 6.8 %shard_map.101 = (f32[384,256]{1,0:T(8,128)S(1)}, bf16[384,256]{1,0:T(8,128)(2,1)S(1)}, f32[4,64,256]{2,1,0:T(8,128)S(1)}, f32[64,256]{1,0:T(8,128)S(1)}, f32[64...) custom-call(s32[2]{0:T(128)S(1)} %pad_add_fusion.device.refs_0_, s32[3]{0:T(128)S(1)} %copy-done.18, ...), custom_call_target="tpu_custom_call" | custom-call | tf_op jit(solution)/shard_map/pallas_call | solution.py:316
  91.9 1.3 collective-permute-done.28
  93.2 0.8 convert_add_fusion
  94.0 12.5 %all-to-all-start = ((f32[16,24,256]{2,1,0:T(8,128)}), f32[16,24,256]{2,1,0:T(8,128)S(1)}, u32[]{:S(2)}, u32[]{:S(2)}) async-start(f32[16,24,256]{2,1,0:T(8,128)} %bitcast.11), calls=%async_computation | async-start | bytes 786432 | tf_op jit(solution)/shard_map/all_to_all | solution.py:454
  106.5 1.5 %collective-permute-start.24 = (f32[64,256]{1,0:T(8,128)S(1)}, f32[64,256]{1,0:T(8,128)S(1)}, u32[]{:S(2)}, u32[]{:S(2)}) collective-permute-start(f32[64,256]{1,0:T(8,128)S(1)} %get-tuple-element.52), channel_id=1, source_target_pairs={{0,32},{32,0},{64,96},{96,64},{128,160},{160,128},{192,224},{224,1... | collective-permute-start | bytes 196616 | tf_op jit(solution)/shard_map/ppermute | solution.py:458
  108.0 3.0 %collective-permute-start.25 = (f32[64,256]{1,0:T(8,128)S(1)}, f32[64,256]{1,0:T(8,128)S(1)}, u32[]{:S(2)}, u32[]{:S(2)}) collective-permute-start(f32[64,256]{1,0:T(8,128)S(1)} %get-tuple-element.54), channel_id=1, source_target_pairs={{0,64},{32,96},{64,0},{96,32},{128,192},{160,224},{192,128},{224,1... | collective-permute-start | bytes 196616 | tf_op jit(solution)/shard_map/ppermute | solution.py:458
  111.0 0.3 collective-permute-start.26
  111.3 2.6 %collective-permute-done.25 = f32[64,256]{1,0:T(8,128)S(1)} collective-permute-done((f32[64,256]{1,0:T(8,128)S(1)}, f32[64,256]{1,0:T(8,128)S(1)}, u32[]{:S(2)}, u32[]{:S(2)}) %collective-permute-start.25) | collective-permute-done | bytes 65568 | tf_op jit(solution)/shard_map/ppermute | solution.py:458
  113.9 2.5 %collective-permute-done.26 = f32[64,256]{1,0:T(8,128)S(1)} collective-permute-done((f32[64,256]{1,0:T(8,128)S(1)}, f32[64,256]{1,0:T(8,128)S(1)}, u32[]{:S(2)}, u32[]{:S(2)}) %collective-permute-start.26) | collective-permute-done | bytes 65568 | tf_op jit(solution)/shard_map/ppermute | solution.py:458
  116.6 3.7 %all-to-all-done = f32[16,24,256]{2,1,0:T(8,128)S(1)} async-done(((f32[16,24,256]{2,1,0:T(8,128)}), f32[16,24,256]{2,1,0:T(8,128)S(1)}, u32[]{:S(2)}, u32[]{:S(2)}) %all-to-all-start) | async-done | bytes 393248 | tf_op jit(solution)/shard_map/all_to_all | solution.py:454
  120.4 13.2 %all_to_all.10.got = bf16[8,112,256]{2,1,0:T(8,128)(2,1)S(1)} all-to-all(bf16[8,112,256]{2,1,0:T(8,128)(2,1)S(1)} %broadcast_in_dim.2), channel_id=1, replica_groups=mesh['pole'=8,'row'=4,'col'=8] {'pole'}, dimensions={0} | all-to-all | bytes 917504 | tf_op jit(solution)/shard_map/all_to_all | solution.py:468
  133.6 1.6 %shard_map.102 = (f32[256,768]{1,0:T(8,128)}, f32[24,256]{1,0:T(8,128)}) custom-call(s32[2]{0:T(128)S(1)} %pad_add_fusion.device.refs_0_, s32[3]{0:T(128)S(1)} %copy-done.18, bf16[8,112,256]{2,1,0:T(8,128)(2,1)S(1)} %all_to_all.10.got), custom_call_target="tpu_custom_call" | custom-call | tf_op jit(solution)/shard_map/pallas_call | solution.py:359
  (89 shorter events, 1.0 us)
Async XLA Ops:
  2.2 1.6 %collective-permute-start = (bf16[256,512]{1,0:T(8,128)(2,1)S(1)}, bf16[256,512]{1,0:T(8,128)(2,1)S(1)}, u32[]{:S(2)}, u32[]{:S(2)}) collective-permute-start(bf16[256,512]{1,0:T(8,128)(2,1)S(1)} %get-tuple-element.27), channel_id=1, source_target_pairs={{0,1},{1,0},{2,3},{3,2},{4,5},{5,4},{6,7},{7,6},{8,9},{9,8},{10,11... | collective-permute-start | bytes 786440 | tf_op jit(solution)/shard_map/ppermute | solution.py:35
  3.8 41.7 %copy-start.1 = (bf16[384,512]{1,0:T(8,128)(2,1)}, bf16[384,512]{1,0:T(8,128)(2,1)S(1)}, u32[]{:S(2)}) copy-start(bf16[384,512]{1,0:T(8,128)(2,1)S(1)} %constant_dynamic-update-slice_fusion.refs_3_.refs_9_) | copy-start | bytes 1179652
  3.8 41.7 %collective-permute-start.1 = (bf16[2,8192,256]{2,1,0:T(8,128)(2,1)}, bf16[2,8192,256]{2,1,0:T(8,128)(2,1)}, u32[]{:S(2)}, u32[]{:S(2)}) collective-permute-start(bf16[2,8192,256]{2,1,0:T(8,128)(2,1)} %bitcast.35), channel_id=1, source_target_pairs={{0,1},{1,0},{2,3},{3,2},{4,5},{5,4},{6,7},{7,6},{8,9},{9,8},{10,11... | collective-permute-start | bytes 25165832 | tf_op jit(solution)/shard_map/ppermute | solution.py:35
  4.1 8.3 %collective-permute-start.5 = (bf16[128,512]{1,0:T(8,128)(2,1)S(1)}, bf16[128,512]{1,0:T(8,128)(2,1)S(1)}, u32[]{:S(2)}, u32[]{:S(2)}) collective-permute-start(bf16[128,512]{1,0:T(8,128)(2,1)S(1)} %get-tuple-element.30), channel_id=1, source_target_pairs={{0,8},{1,9},{2,10},{3,11},{4,12},{5,13},{6,14},{7,15},{8,16},{9,17... | collective-permute-start | bytes 393224 | tf_op jit(solution)/shard_map/ppermute | solution.py:35
  5.6 6.8 %collective-permute-start.6 = (bf16[128,512]{1,0:T(8,128)(2,1)S(1)}, bf16[128,512]{1,0:T(8,128)(2,1)S(1)}, u32[]{:S(2)}, u32[]{:S(2)}) collective-permute-start(bf16[128,512]{1,0:T(8,128)(2,1)S(1)} %get-tuple-element.30), channel_id=1, source_target_pairs={{0,24},{1,25},{2,26},{3,27},{4,28},{5,29},{6,30},{7,31},{8,0},{9,1... | collective-permute-start | bytes 393224 | tf_op jit(solution)/shard_map/ppermute | solution.py:35
  6.4 18.3 %collective-permute-start.2 = (bf16[384,512]{1,0:T(8,128)(2,1)S(1)}, bf16[384,512]{1,0:T(8,128)(2,1)S(1)}, u32[]{:S(2)}, u32[]{:S(2)}) collective-permute-start(bf16[384,512]{1,0:T(8,128)(2,1)S(1)} %constant_dynamic-update-slice_fusion.refs_3_.refs_9_), channel_id=1, source_target_pairs={{0,2},{1,3},{2,4},{3,5},{4,6},{5,7},{6,0},{7,1},{8,10},{9,11},{10,... | collective-permute-start | bytes 1179656 | tf_op jit(solution)/shard_map/ppermute | solution.py:35
  9.4 21.7 %collective-permute-start.3 = (bf16[384,512]{1,0:T(8,128)(2,1)S(1)}, bf16[384,512]{1,0:T(8,128)(2,1)S(1)}, u32[]{:S(2)}, u32[]{:S(2)}) collective-permute-start(bf16[384,512]{1,0:T(8,128)(2,1)S(1)} %constant_dynamic-update-slice_fusion.refs_3_.refs_9_), channel_id=1, source_target_pairs={{0,6},{1,7},{2,0},{3,1},{4,2},{5,3},{6,4},{7,5},{8,14},{9,15},{10,... | collective-permute-start | bytes 1179656 | tf_op jit(solution)/shard_map/ppermute | solution.py:35
  12.4 10.5 %collective-permute-start.8 = (bf16[384,512]{1,0:T(8,128)(2,1)S(1)}, bf16[384,512]{1,0:T(8,128)(2,1)S(1)}, u32[]{:S(2)}, u32[]{:S(2)}) collective-permute-start(bf16[384,512]{1,0:T(8,128)(2,1)S(1)} %constant_dynamic-update-slice_fusion.refs_3_.refs_9_), channel_id=1, source_target_pairs={{0,24},{1,25},{2,26},{3,27},{4,28},{5,29},{6,30},{7,31},{8,0},{9,1... | collective-permute-start | bytes 1179656 | tf_op jit(solution)/shard_map/ppermute | solution.py:35
  14.2 5.2 %collective-permute-start.17 = (bf16[128,512]{1,0:T(8,128)(2,1)S(1)}, bf16[128,512]{1,0:T(8,128)(2,1)S(1)}, u32[]{:S(2)}, u32[]{:S(2)}) collective-permute-start(bf16[128,512]{1,0:T(8,128)(2,1)S(1)} %collective-permute-done.5), channel_id=1, source_target_pairs={{0,8},{1,9},{2,10},{3,11},{4,12},{5,13},{6,14},{7,15},{8,16},{9,17... | collective-permute-start | bytes 393224 | tf_op jit(solution)/shard_map/ppermute | solution.py:35
  19.3 16.7 %collective-permute-start.7 = (bf16[384,512]{1,0:T(8,128)(2,1)S(1)}, bf16[384,512]{1,0:T(8,128)(2,1)S(1)}, u32[]{:S(2)}, u32[]{:S(2)}) collective-permute-start(bf16[384,512]{1,0:T(8,128)(2,1)S(1)} %constant_dynamic-update-slice_fusion.refs_3_.refs_9_), channel_id=1, source_target_pairs={{0,8},{1,9},{2,10},{3,11},{4,12},{5,13},{6,14},{7,15},{8,16},{9,17... | collective-permute-start | bytes 1179656 | tf_op jit(solution)/shard_map/ppermute | solution.py:35
  19.5 57.1 %copy-start = (bf16[512,512]{1,0:T(8,128)(2,1)}, bf16[512,512]{1,0:T(8,128)(2,1)S(1)}, u32[]{:S(2)}) copy-start(bf16[512,512]{1,0:T(8,128)(2,1)S(1)} %constant_dynamic-update-slice_fusion.2.refs_6_.refs_23_) | copy-start | bytes 1572868
  23.0 22.6 %copy-start.3 = (bf16[384,512]{1,0:T(8,128)(2,1)}, bf16[384,512]{1,0:T(8,128)(2,1)S(1)}, u32[]{:S(2)}) copy-start(bf16[384,512]{1,0:T(8,128)(2,1)S(1)} %collective-permute-done.8.refs_5_.refs_11_) | copy-start | bytes 1179652
  23.0 13.6 %collective-permute-start.9 = (bf16[384,512]{1,0:T(8,128)(2,1)S(1)}, bf16[384,512]{1,0:T(8,128)(2,1)S(1)}, u32[]{:S(2)}, u32[]{:S(2)}) collective-permute-start(bf16[384,512]{1,0:T(8,128)(2,1)S(1)} %collective-permute-done.8.refs_5_.refs_11_), channel_id=1, source_target_pairs={{0,24},{1,25},{2,26},{3,27},{4,28},{5,29},{6,30},{7,31},{8,0},{9,1... | collective-permute-start | bytes 1179656 | tf_op jit(solution)/shard_map/ppermute | solution.py:35
  24.7 6.4 %copy-start.14 = (bf16[384,512]{1,0:T(8,128)(2,1)}, bf16[384,512]{1,0:T(8,128)(2,1)S(1)}, u32[]{:S(2)}) copy-start(bf16[384,512]{1,0:T(8,128)(2,1)S(1)} %collective-permute-done.2.refs_0_) | copy-start | bytes 1179652
  31.8 10.8 %collective-permute-start.10 = (bf16[384,512]{1,0:T(8,128)(2,1)}, bf16[384,512]{1,0:T(8,128)(2,1)S(1)}, u32[]{:S(2)}, u32[]{:S(2)}) collective-permute-start(bf16[384,512]{1,0:T(8,128)(2,1)} %get-tuple-element.37.refs_4_.refs_13_), channel_id=1, source_target_pairs={{0,8},{1,9},{2,10},{3,11},{4,12},{5,13},{6,14},{7,15},{8,16},{9,17... | collective-permute-start | bytes 1179656 | tf_op jit(solution)/shard_map/ppermute | solution.py:35
  33.3 16.6 %copy-start.17 = (bf16[384,512]{1,0:T(8,128)(2,1)S(1)}, bf16[384,512]{1,0:T(8,128)(2,1)}, u32[]{:S(2)}) copy-start(bf16[384,512]{1,0:T(8,128)(2,1)} %get-tuple-element.38.refs_4_.refs_17_) | copy-start | bytes 1179652
  33.3 31.2 %copy-start.15 = (bf16[384,512]{1,0:T(8,128)(2,1)S(1)}, bf16[384,512]{1,0:T(8,128)(2,1)}, u32[]{:S(2)}) copy-start(bf16[384,512]{1,0:T(8,128)(2,1)} %get-tuple-element.37.refs_4_.refs_13_) | copy-start | bytes 1179652
  33.3 25.4 %collective-permute-start.18 = (bf16[512,512]{1,0:T(8,128)(2,1)S(1)}, bf16[512,512]{1,0:T(8,128)(2,1)S(1)}, u32[]{:S(2)}, u32[]{:S(2)}) collective-permute-start(bf16[512,512]{1,0:T(8,128)(2,1)S(1)} %constant_dynamic-update-slice_fusion.2.refs_6_.refs_23_), channel_id=1, source_target_pairs={{0,6},{1,7},{2,0},{3,1},{4,2},{5,3},{6,4},{7,5},{8,14},{9,15},{10,... | collective-permute-start | bytes 1572872 | tf_op jit(solution)/shard_map/ppermute | solution.py:35
  36.0 13.9 %copy-start.4 = (bf16[384,512]{1,0:T(8,128)(2,1)}, bf16[384,512]{1,0:T(8,128)(2,1)S(1)}, u32[]{:S(2)}) copy-start(bf16[384,512]{1,0:T(8,128)(2,1)S(1)} %collective-permute-done.7.refs_4_.refs_10_) | copy-start | bytes 1179652
  36.0 13.9 %collective-permute-start.11 = (bf16[384,512]{1,0:T(8,128)(2,1)}, bf16[384,512]{1,0:T(8,128)(2,1)S(1)}, u32[]{:S(2)}, u32[]{:S(2)}) collective-permute-start(bf16[384,512]{1,0:T(8,128)(2,1)} %get-tuple-element.38.refs_4_.refs_17_), channel_id=1, source_target_pairs={{0,24},{1,25},{2,26},{3,27},{4,28},{5,29},{6,30},{7,31},{8,0},{9,1... | collective-permute-start | bytes 1179656 | tf_op jit(solution)/shard_map/ppermute | solution.py:35
  36.6 13.3 %copy-start.5 = (bf16[384,512]{1,0:T(8,128)(2,1)}, bf16[384,512]{1,0:T(8,128)(2,1)S(1)}, u32[]{:S(2)}) copy-start(bf16[384,512]{1,0:T(8,128)(2,1)S(1)} %collective-permute-done.9.refs_6_.refs_12_) | copy-start | bytes 1179652
  36.6 18.6 %collective-permute-start.4 = (bf16[384,512]{1,0:T(8,128)(2,1)}, bf16[384,512]{1,0:T(8,128)(2,1)S(1)}, u32[]{:S(2)}, u32[]{:S(2)}) collective-permute-start(bf16[384,512]{1,0:T(8,128)(2,1)} %get-tuple-element.37.refs_4_.refs_13_), channel_id=1, source_target_pairs={{0,2},{1,3},{2,4},{3,5},{4,6},{5,7},{6,0},{7,1},{8,10},{9,11},{10,... | collective-permute-start | bytes 1179656 | tf_op jit(solution)/shard_map/ppermute | solution.py:35
  42.6 21.9 %copy-start.6 = (bf16[384,512]{1,0:T(8,128)(2,1)}, bf16[384,512]{1,0:T(8,128)(2,1)S(1)}, u32[]{:S(2)}) copy-start(bf16[384,512]{1,0:T(8,128)(2,1)S(1)} %collective-permute-done.10.refs_5_.refs_14_) | copy-start | bytes 1179652
  42.6 17.4 %collective-permute-start.13 = (bf16[384,512]{1,0:T(8,128)(2,1)}, bf16[384,512]{1,0:T(8,128)(2,1)S(1)}, u32[]{:S(2)}, u32[]{:S(2)}) collective-permute-start(bf16[384,512]{1,0:T(8,128)(2,1)} %get-tuple-element.37.refs_4_.refs_13_), channel_id=1, source_target_pairs={{0,24},{1,25},{2,26},{3,27},{4,28},{5,29},{6,30},{7,31},{8,0},{9,1... | collective-permute-start | bytes 1179656 | tf_op jit(solution)/shard_map/ppermute | solution.py:35
  45.6 17.9 %collective-permute-start.14 = (bf16[384,512]{1,0:T(8,128)(2,1)S(1)}, bf16[384,512]{1,0:T(8,128)(2,1)S(1)}, u32[]{:S(2)}, u32[]{:S(2)}) collective-permute-start(bf16[384,512]{1,0:T(8,128)(2,1)S(1)} %collective-permute-done.10.refs_5_.refs_14_), channel_id=1, source_target_pairs={{0,8},{1,9},{2,10},{3,11},{4,12},{5,13},{6,14},{7,15},{8,16},{9,17... | collective-permute-start | bytes 1179656 | tf_op jit(solution)/shard_map/ppermute | solution.py:35
  49.9 21.1 %copy-start.7 = (bf16[384,512]{1,0:T(8,128)(2,1)}, bf16[384,512]{1,0:T(8,128)(2,1)S(1)}, u32[]{:S(2)}) copy-start(bf16[384,512]{1,0:T(8,128)(2,1)S(1)} %collective-permute-done.11.refs_6_.refs_19_) | copy-start | bytes 1179652
  49.9 19.1 %collective-permute-start.15 = (bf16[384,512]{1,0:T(8,128)(2,1)S(1)}, bf16[384,512]{1,0:T(8,128)(2,1)S(1)}, u32[]{:S(2)}, u32[]{:S(2)}) collective-permute-start(bf16[384,512]{1,0:T(8,128)(2,1)S(1)} %copy-done.17), channel_id=1, source_target_pairs={{0,8},{1,9},{2,10},{3,11},{4,12},{5,13},{6,14},{7,15},{8,16},{9,17... | collective-permute-start | bytes 1179656 | tf_op jit(solution)/shard_map/ppermute | solution.py:35
  55.1 21.5 %copy-start.8 = (bf16[384,512]{1,0:T(8,128)(2,1)}, bf16[384,512]{1,0:T(8,128)(2,1)S(1)}, u32[]{:S(2)}) copy-start(bf16[384,512]{1,0:T(8,128)(2,1)S(1)} %collective-permute-done.4.refs_4_.refs_21_) | copy-start | bytes 1179652
  55.1 15.9 %collective-permute-start.16 = (bf16[384,512]{1,0:T(8,128)(2,1)S(1)}, bf16[384,512]{1,0:T(8,128)(2,1)S(1)}, u32[]{:S(2)}, u32[]{:S(2)}) collective-permute-start(bf16[384,512]{1,0:T(8,128)(2,1)S(1)} %collective-permute-done.11.refs_6_.refs_19_), channel_id=1, source_target_pairs={{0,24},{1,25},{2,26},{3,27},{4,28},{5,29},{6,30},{7,31},{8,0},{9,1... | collective-permute-start | bytes 1179656 | tf_op jit(solution)/shard_map/ppermute | solution.py:35
  58.8 17.9 %copy-start.2 = (bf16[512,512]{1,0:T(8,128)(2,1)}, bf16[512,512]{1,0:T(8,128)(2,1)S(1)}, u32[]{:S(2)}) copy-start(bf16[512,512]{1,0:T(8,128)(2,1)S(1)} %collective-permute-done.18.refs_7_.refs_24_) | copy-start | bytes 1572868
  58.8 16.8 %collective-permute-start.12 = (bf16[384,512]{1,0:T(8,128)(2,1)S(1)}, bf16[384,512]{1,0:T(8,128)(2,1)S(1)}, u32[]{:S(2)}, u32[]{:S(2)}) collective-permute-start(bf16[384,512]{1,0:T(8,128)(2,1)S(1)} %collective-permute-done.4.refs_4_.refs_21_), channel_id=1, source_target_pairs={{0,8},{1,9},{2,10},{3,11},{4,12},{5,13},{6,14},{7,15},{8,16},{9,17... | collective-permute-start | bytes 1179656 | tf_op jit(solution)/shard_map/ppermute | solution.py:35
  60.0 9.0 %copy-start.9 = (bf16[384,512]{1,0:T(8,128)(2,1)}, bf16[384,512]{1,0:T(8,128)(2,1)S(1)}, u32[]{:S(2)}) copy-start(bf16[384,512]{1,0:T(8,128)(2,1)S(1)} %collective-permute-done.13.refs_6_.refs_15_) | copy-start | bytes 1179652
  60.0 22.3 %collective-permute-start.22 = (bf16[512,512]{1,0:T(8,128)(2,1)S(1)}, bf16[512,512]{1,0:T(8,128)(2,1)S(1)}, u32[]{:S(2)}, u32[]{:S(2)}) collective-permute-start(bf16[512,512]{1,0:T(8,128)(2,1)S(1)} %collective-permute-done.18.refs_7_.refs_24_), channel_id=1, source_target_pairs={{0,6},{1,7},{2,0},{3,1},{4,2},{5,3},{6,4},{7,5},{8,14},{9,15},{10,... | collective-permute-start | bytes 1572872 | tf_op jit(solution)/shard_map/ppermute | solution.py:35
  63.5 18.8 %collective-permute-start.21 = (bf16[512,512]{1,0:T(8,128)(2,1)S(1)}, bf16[512,512]{1,0:T(8,128)(2,1)S(1)}, u32[]{:S(2)}, u32[]{:S(2)}) collective-permute-start(bf16[512,512]{1,0:T(8,128)(2,1)S(1)} %constant_dynamic-update-slice_fusion.2.refs_6_.refs_23_), channel_id=1, source_target_pairs={{0,2},{1,3},{2,4},{3,5},{4,6},{5,7},{6,0},{7,1},{8,10},{9,11},{10,... | collective-permute-start | bytes 1572872 | tf_op jit(solution)/shard_map/ppermute | solution.py:35
  69.0 7.6 %copy-start.25 = (bf16[1,2,24,256]{3,2,1,0:T(8,128)(2,1)S(1)}, bf16[1,2,24,256]{3,2,1,0:T(8,128)(2,1)}, u32[]{:S(2)}) copy-start(bf16[1,2,24,256]{3,2,1,0:T(8,128)(2,1)} %param.10) | copy-start | bytes 73732
  69.0 6.5 %copy-start.11 = (bf16[384,512]{1,0:T(8,128)(2,1)}, bf16[384,512]{1,0:T(8,128)(2,1)S(1)}, u32[]{:S(2)}) copy-start(bf16[384,512]{1,0:T(8,128)(2,1)S(1)} %collective-permute-done.15.refs_5_.refs_18_) | copy-start | bytes 1179652
  69.0 13.3 %collective-permute-start.19 = (bf16[384,512]{1,0:T(8,128)(2,1)S(1)}, bf16[384,512]{1,0:T(8,128)(2,1)S(1)}, u32[]{:S(2)}, u32[]{:S(2)}) collective-permute-start(bf16[384,512]{1,0:T(8,128)(2,1)S(1)} %collective-permute-done.4.refs_4_.refs_21_), channel_id=1, source_target_pairs={{0,24},{1,25},{2,26},{3,27},{4,28},{5,29},{6,30},{7,31},{8,0},{9,1... | collective-permute-start | bytes 1179656 | tf_op jit(solution)/shard_map/ppermute | solution.py:35
  75.6 8.5 %collective-permute-start.20 = (bf16[384,512]{1,0:T(8,128)(2,1)S(1)}, bf16[384,512]{1,0:T(8,128)(2,1)S(1)}, u32[]{:S(2)}, u32[]{:S(2)}) collective-permute-start(bf16[384,512]{1,0:T(8,128)(2,1)S(1)} %collective-permute-done.12.refs_5_.refs_22_), channel_id=1, source_target_pairs={{0,8},{1,9},{2,10},{3,11},{4,12},{5,13},{6,14},{7,15},{8,16},{9,17... | collective-permute-start | bytes 1179656 | tf_op jit(solution)/shard_map/ppermute | solution.py:35
  76.7 8.2 %copy-start.18 = (s32[3]{0:T(128)S(1)}, s32[3]{0:T(128)}, u32[]{:S(2)}) copy-start(s32[3]{0:T(128)} %widths.3) | copy-start | bytes 40
  76.7 8.2 %copy-start.19 = (f32[20,2]{0,1:T(2,128)S(1)}, f32[20,2]{0,1:T(2,128)}, u32[]{:S(2)}) copy-start(f32[20,2]{0,1:T(2,128)} %param.15) | copy-start | bytes 484
  76.7 8.1 %copy-start.20 = (s32[32]{0:T(128)S(1)}, s32[32]{0:T(128)}, u32[]{:S(2)}) copy-start(s32[32]{0:T(128)} %refs_2_.1) | copy-start | bytes 388
  91.7 1.5 %collective-permute-start.28 = (bf16[384,256]{1,0:T(8,128)(2,1)S(1)}, bf16[384,256]{1,0:T(8,128)(2,1)S(1)}, u32[]{:S(2)}, u32[]{:S(2)}) collective-permute-start(bf16[384,256]{1,0:T(8,128)(2,1)S(1)} %get-tuple-element.49), channel_id=1, source_target_pairs={{0,1},{1,0},{2,3},{3,2},{4,5},{5,4},{6,7},{7,6},{8,9},{9,8},{10,11... | collective-permute-start | bytes 589832 | tf_op jit(solution)/shard_map/ppermute | solution.py:35
  91.8 14.7 %collective-permute-start.23 = (f32[4,64,256]{2,1,0:T(8,128)S(1)}, f32[4,64,256]{2,1,0:T(8,128)S(1)}, u32[]{:S(2)}, u32[]{:S(2)}) collective-permute-start(f32[4,64,256]{2,1,0:T(8,128)S(1)} %get-tuple-element.44), channel_id=1, source_target_pairs={{0,128},{32,160},{64,192},{96,224},{128,0},{160,32},{192,64},{224,... | collective-permute-start | bytes 786440 | tf_op jit(solution)/shard_map/ppermute | solution.py:455
  94.0 26.3 %all-to-all-start = ((f32[16,24,256]{2,1,0:T(8,128)}), f32[16,24,256]{2,1,0:T(8,128)S(1)}, u32[]{:S(2)}, u32[]{:S(2)}) async-start(f32[16,24,256]{2,1,0:T(8,128)} %bitcast.11), calls=%async_computation | async-start | bytes 786432 | tf_op jit(solution)/shard_map/all_to_all | solution.py:454
  106.5 4.8 %collective-permute-start.24 = (f32[64,256]{1,0:T(8,128)S(1)}, f32[64,256]{1,0:T(8,128)S(1)}, u32[]{:S(2)}, u32[]{:S(2)}) collective-permute-start(f32[64,256]{1,0:T(8,128)S(1)} %get-tuple-element.52), channel_id=1, source_target_pairs={{0,32},{32,0},{64,96},{96,64},{128,160},{160,128},{192,224},{224,1... | collective-permute-start | bytes 196616 | tf_op jit(solution)/shard_map/ppermute | solution.py:458
  108.0 5.9 %collective-permute-start.25 = (f32[64,256]{1,0:T(8,128)S(1)}, f32[64,256]{1,0:T(8,128)S(1)}, u32[]{:S(2)}, u32[]{:S(2)}) collective-permute-start(f32[64,256]{1,0:T(8,128)S(1)} %get-tuple-element.54), channel_id=1, source_target_pairs={{0,64},{32,96},{64,0},{96,32},{128,192},{160,224},{192,128},{224,1... | collective-permute-start | bytes 196616 | tf_op jit(solution)/shard_map/ppermute | solution.py:458
  111.0 5.5 %collective-permute-start.26 = (f32[64,256]{1,0:T(8,128)S(1)}, f32[64,256]{1,0:T(8,128)S(1)}, u32[]{:S(2)}, u32[]{:S(2)}) collective-permute-start(f32[64,256]{1,0:T(8,128)S(1)} %get-tuple-element.53), channel_id=1, source_target_pairs={{0,96},{32,64},{64,32},{96,0},{128,224},{160,192},{192,160},{224,1... | collective-permute-start | bytes 196616 | tf_op jit(solution)/shard_map/ppermute | solution.py:458
  116.5 3.9 %collective-permute-start.27 = (bf16[32,256]{1,0:T(8,128)(2,1)S(1)}, bf16[32,256]{1,0:T(8,128)(2,1)S(1)}, u32[]{:S(2)}, u32[]{:S(2)}) collective-permute-start(bf16[32,256]{1,0:T(8,128)(2,1)S(1)} %get-tuple-element.56), channel_id=1, source_target_pairs={{0,1},{1,0},{2,3},{3,2},{4,5},{5,4},{6,7},{7,6},{8,9},{9,8},{10,11... | collective-permute-start | bytes 49160 | tf_op jit(solution)/shard_map/ppermute | solution.py:35
  (8 other events, 22.7 us)

commit v7 on v6

--- a/solution.py
+++ b/solution.py
@@ -443,7 +443,7 @@
     segments += listing(along, [[(ox, oz, False) for ox in orders] for oz in (-1, 2)], 1)
 
     mine, given, over, *parts = finish(
-        device, widths, owner, assign, pole_weights.T, acc,
+        device, in_hbm(widths), in_hbm(owner), assign, in_hbm(pole_weights.T), acc,
         diag_inverse[0].astype(jnp.float32), own_inverse, sib_inverse,
         pieces, tuple(sources), segments, total,
     )

time: 135 us -> 136 us (level)
  no operation moved by 1% of the time
where the time goes in v7:
time: 136 us; the launch traced here: 135 us
  starting transfers between devices  50.5 us (37%)
  waiting for transfers between devices  39.2 us (29%)
  Pallas kernels  28 us (21%)
  blocking collectives  13.2 us (10%)
  local copies, waits for them, and re-layouts  1.72 us (1%)
  between operations  1.69 us (1%)
    ppermute x25, starting transfers between devices, shift(): return lax.ppermute(value, GRID, perm)  33.2 us
    ppermute x25, waiting for transfers between devices, shift(): return lax.ppermute(value, GRID, perm)  30.2 us
    pallas_call x4, Pallas kernels, gemm(): pl.pallas_call(functools.partial(gemm_body, segments, has_acc), in_specs=...  18.1 us
    all_to_all x1, blocking collectives, local(): lax.all_to_all(jnp.broadcast_to(both[None], (POLES,) + both.shape), 'pole...  13.2 us
    all_to_all x1, starting transfers between devices, local(): lax.all_to_all(mine, GRID, 0, 0, axis_index_groups=groups, tiled=True)  12.4 us
    pallas_call x1, Pallas kernels, finish(): pl.pallas_call(functools.partial(finish_body, sources, segments), in_spec...  6.89 us
    ppermute x3, waiting for transfers between devices, local(): lax.ppermute(part, 'pole', [(p, p ^ d) for p in range(POLES)])  5.16 us
    ppermute x3, starting transfers between devices, local(): lax.ppermute(part, 'pole', [(p, p ^ d) for p in range(POLES)])  4.79 us
  transfers between devices with their start and end apart: 30, of which 13 were waited for; matrix products, arithmetic and copies ran while one was open for 1% of the time, Pallas kernels for 13%

profile of v7, /device:TPU:2, one launch (start us, length us, event | category | flops | bytes accessed | tf_op | source)
XLA Modules:
  0.0 135.2 jit_solution(14695683076058433958)
XLA Ops:
  0.7 1.5 %shard_map.95 = (bf16[128,512]{1,0:T(8,128)(2,1)S(1)}, bf16[128,512]{1,0:T(8,128)(2,1)S(1)}, bf16[256,512]{1,0:T(8,128)(2,1)S(1)}) custom-call(s32[2]{0:T(128)S(1)} %pad_add_fusion.device.refs_0_, s32[3]{0:T(128)} %widths.3, s32[3,32]{1,0:T(4,128)} %bitcast.41, bf16[2,256,768]{2,1,0:T(8,128)(2,1)} %bitcast.40), custom_call_target="tpu_custom_call" | custom-call | tf_op jit(solution)/shard_map/pallas_call | solution.py:141
  2.3 1.5 %collective-permute-done = bf16[256,512]{1,0:T(8,128)(2,1)S(1)} collective-permute-done((bf16[256,512]{1,0:T(8,128)(2,1)S(1)}, bf16[256,512]{1,0:T(8,128)(2,1)S(1)}, u32[]{:S(2)}, u32[]{:S(2)}) %collective-permute-start) | collective-permute-done | bytes 262176 | tf_op jit(solution)/shard_map/ppermute | solution.py:35
  3.8 0.2 collective-permute-start.1
  4.1 1.5 %collective-permute-start.5 = (bf16[128,512]{1,0:T(8,128)(2,1)S(1)}, bf16[128,512]{1,0:T(8,128)(2,1)S(1)}, u32[]{:S(2)}, u32[]{:S(2)}) collective-permute-start(bf16[128,512]{1,0:T(8,128)(2,1)S(1)} %get-tuple-element.30), channel_id=1, source_target_pairs={{0,8},{1,9},{2,10},{3,11},{4,12},{5,13},{6,14},{7,15},{8,16},{9,17... | collective-permute-start | bytes 393224 | tf_op jit(solution)/shard_map/ppermute | solution.py:35
  5.6 0.8 collective-permute-start.6
  6.4 3.0 %collective-permute-start.2 = (bf16[384,512]{1,0:T(8,128)(2,1)S(1)}, bf16[384,512]{1,0:T(8,128)(2,1)S(1)}, u32[]{:S(2)}, u32[]{:S(2)}) collective-permute-start(bf16[384,512]{1,0:T(8,128)(2,1)S(1)} %constant_dynamic-update-slice_fusion.refs_3_.refs_9_), channel_id=1, source_target_pairs={{0,2},{1,3},{2,4},{3,5},{4,6},{5,7},{6,0},{7,1},{8,10},{9,11},{10,... | collective-permute-start | bytes 1179656 | tf_op jit(solution)/shard_map/ppermute | solution.py:35
  9.4 3.0 %collective-permute-start.3 = (bf16[384,512]{1,0:T(8,128)(2,1)S(1)}, bf16[384,512]{1,0:T(8,128)(2,1)S(1)}, u32[]{:S(2)}, u32[]{:S(2)}) collective-permute-start(bf16[384,512]{1,0:T(8,128)(2,1)S(1)} %constant_dynamic-update-slice_fusion.refs_3_.refs_9_), channel_id=1, source_target_pairs={{0,6},{1,7},{2,0},{3,1},{4,2},{5,3},{6,4},{7,5},{8,14},{9,15},{10,... | collective-permute-start | bytes 1179656 | tf_op jit(solution)/shard_map/ppermute | solution.py:35
  12.4 1.7 %collective-permute-start.8 = (bf16[384,512]{1,0:T(8,128)(2,1)S(1)}, bf16[384,512]{1,0:T(8,128)(2,1)S(1)}, u32[]{:S(2)}, u32[]{:S(2)}) collective-permute-start(bf16[384,512]{1,0:T(8,128)(2,1)S(1)} %constant_dynamic-update-slice_fusion.refs_3_.refs_9_), channel_id=1, source_target_pairs={{0,24},{1,25},{2,26},{3,27},{4,28},{5,29},{6,30},{7,31},{8,0},{9,1... | collective-permute-start | bytes 1179656 | tf_op jit(solution)/shard_map/ppermute | solution.py:35
  14.2 0.4 collective-permute-start.17
  14.6 4.8 %collective-permute-done.17 = bf16[128,512]{1,0:T(8,128)(2,1)S(1)} collective-permute-done((bf16[128,512]{1,0:T(8,128)(2,1)S(1)}, bf16[128,512]{1,0:T(8,128)(2,1)S(1)}, u32[]{:S(2)}, u32[]{:S(2)}) %collective-permute-start.17) | collective-permute-done | bytes 131104 | tf_op jit(solution)/shard_map/ppermute | solution.py:35
  19.5 3.4 %collective-permute-done.8.refs_5_.refs_11_ = bf16[384,512]{1,0:T(8,128)(2,1)S(1)} collective-permute-done((bf16[384,512]{1,0:T(8,128)(2,1)S(1)}, bf16[384,512]{1,0:T(8,128)(2,1)S(1)}, u32[]{:S(2)}, u32[]{:S(2)}) %collective-permute-start.8) | collective-permute-done | bytes 393248 | tf_op jit(solution)/shard_map/ppermute | solution.py:35
  23.0 1.7 %collective-permute-start.9 = (bf16[384,512]{1,0:T(8,128)(2,1)S(1)}, bf16[384,512]{1,0:T(8,128)(2,1)S(1)}, u32[]{:S(2)}, u32[]{:S(2)}) collective-permute-start(bf16[384,512]{1,0:T(8,128)(2,1)S(1)} %collective-permute-done.8.refs_5_.refs_11_), channel_id=1, source_target_pairs={{0,24},{1,25},{2,26},{3,27},{4,28},{5,29},{6,30},{7,31},{8,0},{9,1... | collective-permute-start | bytes 1179656 | tf_op jit(solution)/shard_map/ppermute | solution.py:35
  24.7 6.4 %collective-permute-done.3.refs_1_ = bf16[384,512]{1,0:T(8,128)(2,1)S(1)} collective-permute-done((bf16[384,512]{1,0:T(8,128)(2,1)S(1)}, bf16[384,512]{1,0:T(8,128)(2,1)S(1)}, u32[]{:S(2)}, u32[]{:S(2)}) %collective-permute-start.3) | collective-permute-done | bytes 393248 | tf_op jit(solution)/shard_map/ppermute | solution.py:35
  31.1 0.8 copy-done.16
  31.8 1.5 %collective-permute-start.10 = (bf16[384,512]{1,0:T(8,128)(2,1)}, bf16[384,512]{1,0:T(8,128)(2,1)S(1)}, u32[]{:S(2)}, u32[]{:S(2)}) collective-permute-start(bf16[384,512]{1,0:T(8,128)(2,1)} %get-tuple-element.37.refs_4_.refs_13_), channel_id=1, source_target_pairs={{0,8},{1,9},{2,10},{3,11},{4,12},{5,13},{6,14},{7,15},{8,16},{9,17... | collective-permute-start | bytes 1179656 | tf_op jit(solution)/shard_map/ppermute | solution.py:35
  33.3 2.7 %collective-permute-start.18 = (bf16[512,512]{1,0:T(8,128)(2,1)S(1)}, bf16[512,512]{1,0:T(8,128)(2,1)S(1)}, u32[]{:S(2)}, u32[]{:S(2)}) collective-permute-start(bf16[512,512]{1,0:T(8,128)(2,1)S(1)} %constant_dynamic-update-slice_fusion.2.refs_6_.refs_23_), channel_id=1, source_target_pairs={{0,6},{1,7},{2,0},{3,1},{4,2},{5,3},{6,4},{7,5},{8,14},{9,15},{10,... | collective-permute-start | bytes 1572872 | tf_op jit(solution)/shard_map/ppermute | solution.py:35
  36.0 0.5 collective-permute-start.11
  36.6 1.1 collective-permute-start.4
  37.7 5.0 %collective-permute-done.10.refs_5_.refs_14_ = bf16[384,512]{1,0:T(8,128)(2,1)S(1)} collective-permute-done((bf16[384,512]{1,0:T(8,128)(2,1)}, bf16[384,512]{1,0:T(8,128)(2,1)S(1)}, u32[]{:S(2)}, u32[]{:S(2)}) %collective-permute-start.10) | collective-permute-done | bytes 393248 | tf_op jit(solution)/shard_map/ppermute | solution.py:35
  42.6 3.0 %collective-permute-start.13 = (bf16[384,512]{1,0:T(8,128)(2,1)}, bf16[384,512]{1,0:T(8,128)(2,1)S(1)}, u32[]{:S(2)}, u32[]{:S(2)}) collective-permute-start(bf16[384,512]{1,0:T(8,128)(2,1)} %get-tuple-element.37.refs_4_.refs_13_), channel_id=1, source_target_pairs={{0,24},{1,25},{2,26},{3,27},{4,28},{5,29},{6,30},{7,31},{8,0},{9,1... | collective-permute-start | bytes 1179656 | tf_op jit(solution)/shard_map/ppermute | solution.py:35
  45.6 4.3 %shard_map.97.refs_3_ = f32[1024,512]{1,0:T(8,128)S(1)} custom-call(s32[2]{0:T(128)S(1)} %pad_add_fusion.device.refs_0_, bf16[2,8192,256]{2,1,0:T(8,128)(2,1)} %bitcast.35, bf16[2,8192,256]{2,1,0:T(8,128)(2,1)} %collective-permute-done.1.refs_2_.refs_8_, bf16[384,512]{1,0:T(8,128)(2,1)S(1)} %constant_dynamic-update-slice_fusion.refs_3_.refs_9_, ...), custom_call_target="tpu_custom_call" | custom-call | tf_op jit(solution)/shard_map/pallas_call | solution.py:214
  49.9 0.6 collective-permute-start.15
  50.6 4.6 %collective-permute-done.4.refs_4_.refs_21_ = bf16[384,512]{1,0:T(8,128)(2,1)S(1)} collective-permute-done((bf16[384,512]{1,0:T(8,128)(2,1)}, bf16[384,512]{1,0:T(8,128)(2,1)S(1)}, u32[]{:S(2)}, u32[]{:S(2)}) %collective-permute-start.4) | collective-permute-done | bytes 393248 | tf_op jit(solution)/shard_map/ppermute | solution.py:35
  55.1 2.9 %collective-permute-start.16 = (bf16[384,512]{1,0:T(8,128)(2,1)S(1)}, bf16[384,512]{1,0:T(8,128)(2,1)S(1)}, u32[]{:S(2)}, u32[]{:S(2)}) collective-permute-start(bf16[384,512]{1,0:T(8,128)(2,1)S(1)} %collective-permute-done.11.refs_6_.refs_19_), channel_id=1, source_target_pairs={{0,24},{1,25},{2,26},{3,27},{4,28},{5,29},{6,30},{7,31},{8,0},{9,1... | collective-permute-start | bytes 1179656 | tf_op jit(solution)/shard_map/ppermute | solution.py:35
  58.0 0.8 collective-permute-done.18.refs_7_.refs_24_
  58.8 1.2 collective-permute-start.12
  60.0 3.5 %collective-permute-start.22 = (bf16[512,512]{1,0:T(8,128)(2,1)S(1)}, bf16[512,512]{1,0:T(8,128)(2,1)S(1)}, u32[]{:S(2)}, u32[]{:S(2)}) collective-permute-start(bf16[512,512]{1,0:T(8,128)(2,1)S(1)} %collective-permute-done.18.refs_7_.refs_24_), channel_id=1, source_target_pairs={{0,6},{1,7},{2,0},{3,1},{4,2},{5,3},{6,4},{7,5},{8,14},{9,15},{10,... | collective-permute-start | bytes 1572872 | tf_op jit(solution)/shard_map/ppermute | solution.py:35
  63.5 1.0 collective-permute-start.21
  64.5 4.5 %shard_map.98.refs_3_ = f32[1024,512]{1,0:T(8,128)S(1)} custom-call(s32[2]{0:T(128)S(1)} %pad_add_fusion.device.refs_0_, bf16[2,8192,256]{2,1,0:T(8,128)(2,1)} %bitcast.36, bf16[2,8192,256]{2,1,0:T(8,128)(2,1)} %collective-permute-done.1.refs_2_.refs_8_, f32[1024,512]{1,0:T(8,128)S(1)} %shard_map.97.refs_3_, bf16[384,512]{1,0:T(8,128)(2,1)S(1)} %copy-done.15, ...), custom_call_target="tpu_custom_call" | custom-call | tf_op jit(solution)/shard_map/pallas_call | solution.py:214
  69.0 2.0 %collective-permute-start.19 = (bf16[384,512]{1,0:T(8,128)(2,1)S(1)}, bf16[384,512]{1,0:T(8,128)(2,1)S(1)}, u32[]{:S(2)}, u32[]{:S(2)}) collective-permute-start(bf16[384,512]{1,0:T(8,128)(2,1)S(1)} %collective-permute-done.4.refs_4_.refs_21_), channel_id=1, source_target_pairs={{0,24},{1,25},{2,26},{3,27},{4,28},{5,29},{6,30},{7,31},{8,0},{9,1... | collective-permute-start | bytes 1179656 | tf_op jit(solution)/shard_map/ppermute | solution.py:35
  71.1 4.5 %shard_map.99.refs_3_ = f32[1024,512]{1,0:T(8,128)S(1)} custom-call(s32[2]{0:T(128)S(1)} %pad_add_fusion.device.refs_0_, bf16[2,8192,256]{2,1,0:T(8,128)(2,1)} %bitcast.37, bf16[2,8192,256]{2,1,0:T(8,128)(2,1)} %collective-permute-done.1.refs_2_.refs_8_, f32[1024,512]{1,0:T(8,128)S(1)} %shard_map.98.refs_3_, bf16[384,512]{1,0:T(8,128)(2,1)S(1)} %copy-done.17, ...), custom_call_target="tpu_custom_call" | custom-call | tf_op jit(solution)/shard_map/pallas_call | solution.py:214
  75.6 0.4 collective-permute-start.20
  76.7 4.8 %shard_map.100.refs_5_ = f32[1024,512]{1,0:T(8,128)S(1)} custom-call(s32[2]{0:T(128)S(1)} %pad_add_fusion.device.refs_0_, bf16[2,8192,256]{2,1,0:T(8,128)(2,1)} %bitcast.38, bf16[2,8192,256]{2,1,0:T(8,128)(2,1)} %collective-permute-done.1.refs_2_.refs_8_, f32[1024,512]{1,0:T(8,128)S(1)} %shard_map.99.refs_3_, ...), custom_call_target="tpu_custom_call" | custom-call | tf_op jit(solution)/shard_map/pallas_call | solution.py:214
  81.5 0.8 collective-permute-done.22.refs_28_
  82.4 1.7 %collective-permute-done.20.refs_26_ = bf16[384,512]{1,0:T(8,128)(2,1)S(1)} collective-permute-done((bf16[384,512]{1,0:T(8,128)(2,1)S(1)}, bf16[384,512]{1,0:T(8,128)(2,1)S(1)}, u32[]{:S(2)}, u32[]{:S(2)}) %collective-permute-start.20) | collective-permute-done | bytes 393248 | tf_op jit(solution)/shard_map/ppermute | solution.py:35
  84.1 0.8 copy-done.22
  84.9 6.9 %shard_map.101 = (f32[384,256]{1,0:T(8,128)S(1)}, bf16[384,256]{1,0:T(8,128)(2,1)S(1)}, f32[4,64,256]{2,1,0:T(8,128)S(1)}, f32[64,256]{1,0:T(8,128)S(1)}, f32[64...) custom-call(s32[2]{0:T(128)S(1)} %pad_add_fusion.device.refs_0_, s32[3]{0:T(128)} %widths.3, ...), custom_call_target="tpu_custom_call" | custom-call | tf_op jit(solution)/shard_map/pallas_call | solution.py:316
  92.0 1.3 collective-permute-done.28
  93.3 0.8 convert_add_fusion
  94.1 12.4 %all-to-all-start = ((f32[16,24,256]{2,1,0:T(8,128)}), f32[16,24,256]{2,1,0:T(8,128)S(1)}, u32[]{:S(2)}, u32[]{:S(2)}) async-start(f32[16,24,256]{2,1,0:T(8,128)} %bitcast.11), calls=%async_computation | async-start | bytes 786432 | tf_op jit(solution)/shard_map/all_to_all | solution.py:454
  106.5 1.4 %collective-permute-start.24 = (f32[64,256]{1,0:T(8,128)S(1)}, f32[64,256]{1,0:T(8,128)S(1)}, u32[]{:S(2)}, u32[]{:S(2)}) collective-permute-start(f32[64,256]{1,0:T(8,128)S(1)} %get-tuple-element.52), channel_id=1, source_target_pairs={{0,32},{32,0},{64,96},{96,64},{128,160},{160,128},{192,224},{224,1... | collective-permute-start | bytes 196616 | tf_op jit(solution)/shard_map/ppermute | solution.py:458
  107.9 3.1 %collective-permute-start.25 = (f32[64,256]{1,0:T(8,128)S(1)}, f32[64,256]{1,0:T(8,128)S(1)}, u32[]{:S(2)}, u32[]{:S(2)}) collective-permute-start(f32[64,256]{1,0:T(8,128)S(1)} %get-tuple-element.54), channel_id=1, source_target_pairs={{0,64},{32,96},{64,0},{96,32},{128,192},{160,224},{192,128},{224,1... | collective-permute-start | bytes 196616 | tf_op jit(solution)/shard_map/ppermute | solution.py:458
  111.0 0.3 collective-permute-start.26
  111.3 2.6 %collective-permute-done.25 = f32[64,256]{1,0:T(8,128)S(1)} collective-permute-done((f32[64,256]{1,0:T(8,128)S(1)}, f32[64,256]{1,0:T(8,128)S(1)}, u32[]{:S(2)}, u32[]{:S(2)}) %collective-permute-start.25) | collective-permute-done | bytes 65568 | tf_op jit(solution)/shard_map/ppermute | solution.py:458
  113.9 2.5 %collective-permute-done.26 = f32[64,256]{1,0:T(8,128)S(1)} collective-permute-done((f32[64,256]{1,0:T(8,128)S(1)}, f32[64,256]{1,0:T(8,128)S(1)}, u32[]{:S(2)}, u32[]{:S(2)}) %collective-permute-start.26) | collective-permute-done | bytes 65568 | tf_op jit(solution)/shard_map/ppermute | solution.py:458
  116.6 3.8 %all-to-all-done = f32[16,24,256]{2,1,0:T(8,128)S(1)} async-done(((f32[16,24,256]{2,1,0:T(8,128)}), f32[16,24,256]{2,1,0:T(8,128)S(1)}, u32[]{:S(2)}, u32[]{:S(2)}) %all-to-all-start) | async-done | bytes 393248 | tf_op jit(solution)/shard_map/all_to_all | solution.py:454
  120.5 13.2 %all_to_all.10.got = bf16[8,112,256]{2,1,0:T(8,128)(2,1)S(1)} all-to-all(bf16[8,112,256]{2,1,0:T(8,128)(2,1)S(1)} %broadcast_in_dim.2), channel_id=1, replica_groups=mesh['pole'=8,'row'=4,'col'=8] {'pole'}, dimensions={0} | all-to-all | bytes 917504 | tf_op jit(solution)/shard_map/all_to_all | solution.py:468
  133.6 1.6 %shard_map.102 = (f32[256,768]{1,0:T(8,128)}, f32[24,256]{1,0:T(8,128)}) custom-call(s32[2]{0:T(128)S(1)} %pad_add_fusion.device.refs_0_, s32[3]{0:T(128)S(1)} %copy-done.18, bf16[8,112,256]{2,1,0:T(8,128)(2,1)S(1)} %all_to_all.10.got), custom_call_target="tpu_custom_call" | custom-call | tf_op jit(solution)/shard_map/pallas_call | solution.py:359
  (85 shorter events, 1.0 us)
Async XLA Ops:
  2.2 1.6 %collective-permute-start = (bf16[256,512]{1,0:T(8,128)(2,1)S(1)}, bf16[256,512]{1,0:T(8,128)(2,1)S(1)}, u32[]{:S(2)}, u32[]{:S(2)}) collective-permute-start(bf16[256,512]{1,0:T(8,128)(2,1)S(1)} %get-tuple-element.27), channel_id=1, source_target_pairs={{0,1},{1,0},{2,3},{3,2},{4,5},{5,4},{6,7},{7,6},{8,9},{9,8},{10,11... | collective-permute-start | bytes 786440 | tf_op jit(solution)/shard_map/ppermute | solution.py:35
  3.8 41.7 %copy-start.1 = (bf16[384,512]{1,0:T(8,128)(2,1)}, bf16[384,512]{1,0:T(8,128)(2,1)S(1)}, u32[]{:S(2)}) copy-start(bf16[384,512]{1,0:T(8,128)(2,1)S(1)} %constant_dynamic-update-slice_fusion.refs_3_.refs_9_) | copy-start | bytes 1179652
  3.8 41.7 %collective-permute-start.1 = (bf16[2,8192,256]{2,1,0:T(8,128)(2,1)}, bf16[2,8192,256]{2,1,0:T(8,128)(2,1)}, u32[]{:S(2)}, u32[]{:S(2)}) collective-permute-start(bf16[2,8192,256]{2,1,0:T(8,128)(2,1)} %bitcast.34), channel_id=1, source_target_pairs={{0,1},{1,0},{2,3},{3,2},{4,5},{5,4},{6,7},{7,6},{8,9},{9,8},{10,11... | collective-permute-start | bytes 25165832 | tf_op jit(solution)/shard_map/ppermute | solution.py:35
  4.1 8.3 %collective-permute-start.5 = (bf16[128,512]{1,0:T(8,128)(2,1)S(1)}, bf16[128,512]{1,0:T(8,128)(2,1)S(1)}, u32[]{:S(2)}, u32[]{:S(2)}) collective-permute-start(bf16[128,512]{1,0:T(8,128)(2,1)S(1)} %get-tuple-element.30), channel_id=1, source_target_pairs={{0,8},{1,9},{2,10},{3,11},{4,12},{5,13},{6,14},{7,15},{8,16},{9,17... | collective-permute-start | bytes 393224 | tf_op jit(solution)/shard_map/ppermute | solution.py:35
  5.6 6.8 %collective-permute-start.6 = (bf16[128,512]{1,0:T(8,128)(2,1)S(1)}, bf16[128,512]{1,0:T(8,128)(2,1)S(1)}, u32[]{:S(2)}, u32[]{:S(2)}) collective-permute-start(bf16[128,512]{1,0:T(8,128)(2,1)S(1)} %get-tuple-element.30), channel_id=1, source_target_pairs={{0,24},{1,25},{2,26},{3,27},{4,28},{5,29},{6,30},{7,31},{8,0},{9,1... | collective-permute-start | bytes 393224 | tf_op jit(solution)/shard_map/ppermute | solution.py:35
  6.4 18.3 %collective-permute-start.2 = (bf16[384,512]{1,0:T(8,128)(2,1)S(1)}, bf16[384,512]{1,0:T(8,128)(2,1)S(1)}, u32[]{:S(2)}, u32[]{:S(2)}) collective-permute-start(bf16[384,512]{1,0:T(8,128)(2,1)S(1)} %constant_dynamic-update-slice_fusion.refs_3_.refs_9_), channel_id=1, source_target_pairs={{0,2},{1,3},{2,4},{3,5},{4,6},{5,7},{6,0},{7,1},{8,10},{9,11},{10,... | collective-permute-start | bytes 1179656 | tf_op jit(solution)/shard_map/ppermute | solution.py:35
  9.4 21.7 %collective-permute-start.3 = (bf16[384,512]{1,0:T(8,128)(2,1)S(1)}, bf16[384,512]{1,0:T(8,128)(2,1)S(1)}, u32[]{:S(2)}, u32[]{:S(2)}) collective-permute-start(bf16[384,512]{1,0:T(8,128)(2,1)S(1)} %constant_dynamic-update-slice_fusion.refs_3_.refs_9_), channel_id=1, source_target_pairs={{0,6},{1,7},{2,0},{3,1},{4,2},{5,3},{6,4},{7,5},{8,14},{9,15},{10,... | collective-permute-start | bytes 1179656 | tf_op jit(solution)/shard_map/ppermute | solution.py:35
  12.4 10.5 %collective-permute-start.8 = (bf16[384,512]{1,0:T(8,128)(2,1)S(1)}, bf16[384,512]{1,0:T(8,128)(2,1)S(1)}, u32[]{:S(2)}, u32[]{:S(2)}) collective-permute-start(bf16[384,512]{1,0:T(8,128)(2,1)S(1)} %constant_dynamic-update-slice_fusion.refs_3_.refs_9_), channel_id=1, source_target_pairs={{0,24},{1,25},{2,26},{3,27},{4,28},{5,29},{6,30},{7,31},{8,0},{9,1... | collective-permute-start | bytes 1179656 | tf_op jit(solution)/shard_map/ppermute | solution.py:35
  14.2 5.2 %collective-permute-start.17 = (bf16[128,512]{1,0:T(8,128)(2,1)S(1)}, bf16[128,512]{1,0:T(8,128)(2,1)S(1)}, u32[]{:S(2)}, u32[]{:S(2)}) collective-permute-start(bf16[128,512]{1,0:T(8,128)(2,1)S(1)} %collective-permute-done.5), channel_id=1, source_target_pairs={{0,8},{1,9},{2,10},{3,11},{4,12},{5,13},{6,14},{7,15},{8,16},{9,17... | collective-permute-start | bytes 393224 | tf_op jit(solution)/shard_map/ppermute | solution.py:35
  19.3 16.7 %collective-permute-start.7 = (bf16[384,512]{1,0:T(8,128)(2,1)S(1)}, bf16[384,512]{1,0:T(8,128)(2,1)S(1)}, u32[]{:S(2)}, u32[]{:S(2)}) collective-permute-start(bf16[384,512]{1,0:T(8,128)(2,1)S(1)} %constant_dynamic-update-slice_fusion.refs_3_.refs_9_), channel_id=1, source_target_pairs={{0,8},{1,9},{2,10},{3,11},{4,12},{5,13},{6,14},{7,15},{8,16},{9,17... | collective-permute-start | bytes 1179656 | tf_op jit(solution)/shard_map/ppermute | solution.py:35
  19.5 57.1 %copy-start = (bf16[512,512]{1,0:T(8,128)(2,1)}, bf16[512,512]{1,0:T(8,128)(2,1)S(1)}, u32[]{:S(2)}) copy-start(bf16[512,512]{1,0:T(8,128)(2,1)S(1)} %constant_dynamic-update-slice_fusion.2.refs_6_.refs_23_) | copy-start | bytes 1572868
  23.0 22.6 %copy-start.3 = (bf16[384,512]{1,0:T(8,128)(2,1)}, bf16[384,512]{1,0:T(8,128)(2,1)S(1)}, u32[]{:S(2)}) copy-start(bf16[384,512]{1,0:T(8,128)(2,1)S(1)} %collective-permute-done.8.refs_5_.refs_11_) | copy-start | bytes 1179652
  23.0 13.6 %collective-permute-start.9 = (bf16[384,512]{1,0:T(8,128)(2,1)S(1)}, bf16[384,512]{1,0:T(8,128)(2,1)S(1)}, u32[]{:S(2)}, u32[]{:S(2)}) collective-permute-start(bf16[384,512]{1,0:T(8,128)(2,1)S(1)} %collective-permute-done.8.refs_5_.refs_11_), channel_id=1, source_target_pairs={{0,24},{1,25},{2,26},{3,27},{4,28},{5,29},{6,30},{7,31},{8,0},{9,1... | collective-permute-start | bytes 1179656 | tf_op jit(solution)/shard_map/ppermute | solution.py:35
  24.7 6.4 %copy-start.14 = (bf16[384,512]{1,0:T(8,128)(2,1)}, bf16[384,512]{1,0:T(8,128)(2,1)S(1)}, u32[]{:S(2)}) copy-start(bf16[384,512]{1,0:T(8,128)(2,1)S(1)} %collective-permute-done.2.refs_0_) | copy-start | bytes 1179652
  31.8 10.8 %collective-permute-start.10 = (bf16[384,512]{1,0:T(8,128)(2,1)}, bf16[384,512]{1,0:T(8,128)(2,1)S(1)}, u32[]{:S(2)}, u32[]{:S(2)}) collective-permute-start(bf16[384,512]{1,0:T(8,128)(2,1)} %get-tuple-element.37.refs_4_.refs_13_), channel_id=1, source_target_pairs={{0,8},{1,9},{2,10},{3,11},{4,12},{5,13},{6,14},{7,15},{8,16},{9,17... | collective-permute-start | bytes 1179656 | tf_op jit(solution)/shard_map/ppermute | solution.py:35
  33.3 16.6 %copy-start.17 = (bf16[384,512]{1,0:T(8,128)(2,1)S(1)}, bf16[384,512]{1,0:T(8,128)(2,1)}, u32[]{:S(2)}) copy-start(bf16[384,512]{1,0:T(8,128)(2,1)} %get-tuple-element.38.refs_4_.refs_17_) | copy-start | bytes 1179652
  33.3 31.2 %copy-start.15 = (bf16[384,512]{1,0:T(8,128)(2,1)S(1)}, bf16[384,512]{1,0:T(8,128)(2,1)}, u32[]{:S(2)}) copy-start(bf16[384,512]{1,0:T(8,128)(2,1)} %get-tuple-element.37.refs_4_.refs_13_) | copy-start | bytes 1179652
  33.3 25.5 %collective-permute-start.18 = (bf16[512,512]{1,0:T(8,128)(2,1)S(1)}, bf16[512,512]{1,0:T(8,128)(2,1)S(1)}, u32[]{:S(2)}, u32[]{:S(2)}) collective-permute-start(bf16[512,512]{1,0:T(8,128)(2,1)S(1)} %constant_dynamic-update-slice_fusion.2.refs_6_.refs_23_), channel_id=1, source_target_pairs={{0,6},{1,7},{2,0},{3,1},{4,2},{5,3},{6,4},{7,5},{8,14},{9,15},{10,... | collective-permute-start | bytes 1572872 | tf_op jit(solution)/shard_map/ppermute | solution.py:35
  36.0 13.9 %copy-start.4 = (bf16[384,512]{1,0:T(8,128)(2,1)}, bf16[384,512]{1,0:T(8,128)(2,1)S(1)}, u32[]{:S(2)}) copy-start(bf16[384,512]{1,0:T(8,128)(2,1)S(1)} %collective-permute-done.7.refs_4_.refs_10_) | copy-start | bytes 1179652
  36.0 13.9 %collective-permute-start.11 = (bf16[384,512]{1,0:T(8,128)(2,1)}, bf16[384,512]{1,0:T(8,128)(2,1)S(1)}, u32[]{:S(2)}, u32[]{:S(2)}) collective-permute-start(bf16[384,512]{1,0:T(8,128)(2,1)} %get-tuple-element.38.refs_4_.refs_17_), channel_id=1, source_target_pairs={{0,24},{1,25},{2,26},{3,27},{4,28},{5,29},{6,30},{7,31},{8,0},{9,1... | collective-permute-start | bytes 1179656 | tf_op jit(solution)/shard_map/ppermute | solution.py:35
  36.6 13.3 %copy-start.5 = (bf16[384,512]{1,0:T(8,128)(2,1)}, bf16[384,512]{1,0:T(8,128)(2,1)S(1)}, u32[]{:S(2)}) copy-start(bf16[384,512]{1,0:T(8,128)(2,1)S(1)} %collective-permute-done.9.refs_6_.refs_12_) | copy-start | bytes 1179652
  36.6 18.6 %collective-permute-start.4 = (bf16[384,512]{1,0:T(8,128)(2,1)}, bf16[384,512]{1,0:T(8,128)(2,1)S(1)}, u32[]{:S(2)}, u32[]{:S(2)}) collective-permute-start(bf16[384,512]{1,0:T(8,128)(2,1)} %get-tuple-element.37.refs_4_.refs_13_), channel_id=1, source_target_pairs={{0,2},{1,3},{2,4},{3,5},{4,6},{5,7},{6,0},{7,1},{8,10},{9,11},{10,... | collective-permute-start | bytes 1179656 | tf_op jit(solution)/shard_map/ppermute | solution.py:35
  42.6 21.9 %copy-start.6 = (bf16[384,512]{1,0:T(8,128)(2,1)}, bf16[384,512]{1,0:T(8,128)(2,1)S(1)}, u32[]{:S(2)}) copy-start(bf16[384,512]{1,0:T(8,128)(2,1)S(1)} %collective-permute-done.10.refs_5_.refs_14_) | copy-start | bytes 1179652
  42.6 17.4 %collective-permute-start.13 = (bf16[384,512]{1,0:T(8,128)(2,1)}, bf16[384,512]{1,0:T(8,128)(2,1)S(1)}, u32[]{:S(2)}, u32[]{:S(2)}) collective-permute-start(bf16[384,512]{1,0:T(8,128)(2,1)} %get-tuple-element.37.refs_4_.refs_13_), channel_id=1, source_target_pairs={{0,24},{1,25},{2,26},{3,27},{4,28},{5,29},{6,30},{7,31},{8,0},{9,1... | collective-permute-start | bytes 1179656 | tf_op jit(solution)/shard_map/ppermute | solution.py:35
  45.6 17.9 %collective-permute-start.14 = (bf16[384,512]{1,0:T(8,128)(2,1)S(1)}, bf16[384,512]{1,0:T(8,128)(2,1)S(1)}, u32[]{:S(2)}, u32[]{:S(2)}) collective-permute-start(bf16[384,512]{1,0:T(8,128)(2,1)S(1)} %collective-permute-done.10.refs_5_.refs_14_), channel_id=1, source_target_pairs={{0,8},{1,9},{2,10},{3,11},{4,12},{5,13},{6,14},{7,15},{8,16},{9,17... | collective-permute-start | bytes 1179656 | tf_op jit(solution)/shard_map/ppermute | solution.py:35
  49.9 21.1 %copy-start.7 = (bf16[384,512]{1,0:T(8,128)(2,1)}, bf16[384,512]{1,0:T(8,128)(2,1)S(1)}, u32[]{:S(2)}) copy-start(bf16[384,512]{1,0:T(8,128)(2,1)S(1)} %collective-permute-done.11.refs_6_.refs_19_) | copy-start | bytes 1179652
  49.9 19.1 %collective-permute-start.15 = (bf16[384,512]{1,0:T(8,128)(2,1)S(1)}, bf16[384,512]{1,0:T(8,128)(2,1)S(1)}, u32[]{:S(2)}, u32[]{:S(2)}) collective-permute-start(bf16[384,512]{1,0:T(8,128)(2,1)S(1)} %copy-done.17), channel_id=1, source_target_pairs={{0,8},{1,9},{2,10},{3,11},{4,12},{5,13},{6,14},{7,15},{8,16},{9,17... | collective-permute-start | bytes 1179656 | tf_op jit(solution)/shard_map/ppermute | solution.py:35
  55.1 21.5 %copy-start.8 = (bf16[384,512]{1,0:T(8,128)(2,1)}, bf16[384,512]{1,0:T(8,128)(2,1)S(1)}, u32[]{:S(2)}) copy-start(bf16[384,512]{1,0:T(8,128)(2,1)S(1)} %collective-permute-done.4.refs_4_.refs_21_) | copy-start | bytes 1179652
  55.1 15.9 %collective-permute-start.16 = (bf16[384,512]{1,0:T(8,128)(2,1)S(1)}, bf16[384,512]{1,0:T(8,128)(2,1)S(1)}, u32[]{:S(2)}, u32[]{:S(2)}) collective-permute-start(bf16[384,512]{1,0:T(8,128)(2,1)S(1)} %collective-permute-done.11.refs_6_.refs_19_), channel_id=1, source_target_pairs={{0,24},{1,25},{2,26},{3,27},{4,28},{5,29},{6,30},{7,31},{8,0},{9,1... | collective-permute-start | bytes 1179656 | tf_op jit(solution)/shard_map/ppermute | solution.py:35
  58.8 17.9 %copy-start.2 = (bf16[512,512]{1,0:T(8,128)(2,1)}, bf16[512,512]{1,0:T(8,128)(2,1)S(1)}, u32[]{:S(2)}) copy-start(bf16[512,512]{1,0:T(8,128)(2,1)S(1)} %collective-permute-done.18.refs_7_.refs_24_) | copy-start | bytes 1572868
  58.8 16.8 %collective-permute-start.12 = (bf16[384,512]{1,0:T(8,128)(2,1)S(1)}, bf16[384,512]{1,0:T(8,128)(2,1)S(1)}, u32[]{:S(2)}, u32[]{:S(2)}) collective-permute-start(bf16[384,512]{1,0:T(8,128)(2,1)S(1)} %collective-permute-done.4.refs_4_.refs_21_), channel_id=1, source_target_pairs={{0,8},{1,9},{2,10},{3,11},{4,12},{5,13},{6,14},{7,15},{8,16},{9,17... | collective-permute-start | bytes 1179656 | tf_op jit(solution)/shard_map/ppermute | solution.py:35
  60.0 9.0 %copy-start.9 = (bf16[384,512]{1,0:T(8,128)(2,1)}, bf16[384,512]{1,0:T(8,128)(2,1)S(1)}, u32[]{:S(2)}) copy-start(bf16[384,512]{1,0:T(8,128)(2,1)S(1)} %collective-permute-done.13.refs_6_.refs_15_) | copy-start | bytes 1179652
  60.0 22.3 %collective-permute-start.22 = (bf16[512,512]{1,0:T(8,128)(2,1)S(1)}, bf16[512,512]{1,0:T(8,128)(2,1)S(1)}, u32[]{:S(2)}, u32[]{:S(2)}) collective-permute-start(bf16[512,512]{1,0:T(8,128)(2,1)S(1)} %collective-permute-done.18.refs_7_.refs_24_), channel_id=1, source_target_pairs={{0,6},{1,7},{2,0},{3,1},{4,2},{5,3},{6,4},{7,5},{8,14},{9,15},{10,... | collective-permute-start | bytes 1572872 | tf_op jit(solution)/shard_map/ppermute | solution.py:35
  63.5 5.5 %copy-start.10 = (bf16[384,512]{1,0:T(8,128)(2,1)}, bf16[384,512]{1,0:T(8,128)(2,1)S(1)}, u32[]{:S(2)}) copy-start(bf16[384,512]{1,0:T(8,128)(2,1)S(1)} %collective-permute-done.14.refs_7_.refs_16_) | copy-start | bytes 1179652
  63.5 18.8 %collective-permute-start.21 = (bf16[512,512]{1,0:T(8,128)(2,1)S(1)}, bf16[512,512]{1,0:T(8,128)(2,1)S(1)}, u32[]{:S(2)}, u32[]{:S(2)}) collective-permute-start(bf16[512,512]{1,0:T(8,128)(2,1)S(1)} %constant_dynamic-update-slice_fusion.2.refs_6_.refs_23_), channel_id=1, source_target_pairs={{0,2},{1,3},{2,4},{3,5},{4,6},{5,7},{6,0},{7,1},{8,10},{9,11},{10,... | collective-permute-start | bytes 1572872 | tf_op jit(solution)/shard_map/ppermute | solution.py:35
  69.0 7.6 %copy-start.23 = (bf16[1,2,24,256]{3,2,1,0:T(8,128)(2,1)S(1)}, bf16[1,2,24,256]{3,2,1,0:T(8,128)(2,1)}, u32[]{:S(2)}) copy-start(bf16[1,2,24,256]{3,2,1,0:T(8,128)(2,1)} %param.10) | copy-start | bytes 73732
  69.0 6.5 %copy-start.11 = (bf16[384,512]{1,0:T(8,128)(2,1)}, bf16[384,512]{1,0:T(8,128)(2,1)S(1)}, u32[]{:S(2)}) copy-start(bf16[384,512]{1,0:T(8,128)(2,1)S(1)} %collective-permute-done.15.refs_5_.refs_18_) | copy-start | bytes 1179652
  69.0 13.3 %collective-permute-start.19 = (bf16[384,512]{1,0:T(8,128)(2,1)S(1)}, bf16[384,512]{1,0:T(8,128)(2,1)S(1)}, u32[]{:S(2)}, u32[]{:S(2)}) collective-permute-start(bf16[384,512]{1,0:T(8,128)(2,1)S(1)} %collective-permute-done.4.refs_4_.refs_21_), channel_id=1, source_target_pairs={{0,24},{1,25},{2,26},{3,27},{4,28},{5,29},{6,30},{7,31},{8,0},{9,1... | collective-permute-start | bytes 1179656 | tf_op jit(solution)/shard_map/ppermute | solution.py:35
  75.6 6.0 %copy-start.13 = (bf16[384,512]{1,0:T(8,128)(2,1)}, bf16[384,512]{1,0:T(8,128)(2,1)S(1)}, u32[]{:S(2)}) copy-start(bf16[384,512]{1,0:T(8,128)(2,1)S(1)} %collective-permute-done.12.refs_5_.refs_22_) | copy-start | bytes 1179652
  75.6 8.5 %collective-permute-start.20 = (bf16[384,512]{1,0:T(8,128)(2,1)S(1)}, bf16[384,512]{1,0:T(8,128)(2,1)S(1)}, u32[]{:S(2)}, u32[]{:S(2)}) collective-permute-start(bf16[384,512]{1,0:T(8,128)(2,1)S(1)} %collective-permute-done.12.refs_5_.refs_22_), channel_id=1, source_target_pairs={{0,8},{1,9},{2,10},{3,11},{4,12},{5,13},{6,14},{7,15},{8,16},{9,17... | collective-permute-start | bytes 1179656 | tf_op jit(solution)/shard_map/ppermute | solution.py:35
  91.8 1.5 %collective-permute-start.28 = (bf16[384,256]{1,0:T(8,128)(2,1)S(1)}, bf16[384,256]{1,0:T(8,128)(2,1)S(1)}, u32[]{:S(2)}, u32[]{:S(2)}) collective-permute-start(bf16[384,256]{1,0:T(8,128)(2,1)S(1)} %get-tuple-element.49), channel_id=1, source_target_pairs={{0,1},{1,0},{2,3},{3,2},{4,5},{5,4},{6,7},{7,6},{8,9},{9,8},{10,11... | collective-permute-start | bytes 589832 | tf_op jit(solution)/shard_map/ppermute | solution.py:35
  91.9 14.6 %collective-permute-start.23 = (f32[4,64,256]{2,1,0:T(8,128)S(1)}, f32[4,64,256]{2,1,0:T(8,128)S(1)}, u32[]{:S(2)}, u32[]{:S(2)}) collective-permute-start(f32[4,64,256]{2,1,0:T(8,128)S(1)} %get-tuple-element.44), channel_id=1, source_target_pairs={{0,128},{32,160},{64,192},{96,224},{128,0},{160,32},{192,64},{224,... | collective-permute-start | bytes 786440 | tf_op jit(solution)/shard_map/ppermute | solution.py:455
  94.1 39.6 %copy-start.18 = (s32[3]{0:T(128)S(1)}, s32[3]{0:T(128)}, u32[]{:S(2)}) copy-start(s32[3]{0:T(128)} %widths.3) | copy-start | bytes 40
  94.1 26.3 %all-to-all-start = ((f32[16,24,256]{2,1,0:T(8,128)}), f32[16,24,256]{2,1,0:T(8,128)S(1)}, u32[]{:S(2)}, u32[]{:S(2)}) async-start(f32[16,24,256]{2,1,0:T(8,128)} %bitcast.11), calls=%async_computation | async-start | bytes 786432 | tf_op jit(solution)/shard_map/all_to_all | solution.py:454
  106.5 4.8 %collective-permute-start.24 = (f32[64,256]{1,0:T(8,128)S(1)}, f32[64,256]{1,0:T(8,128)S(1)}, u32[]{:S(2)}, u32[]{:S(2)}) collective-permute-start(f32[64,256]{1,0:T(8,128)S(1)} %get-tuple-element.52), channel_id=1, source_target_pairs={{0,32},{32,0},{64,96},{96,64},{128,160},{160,128},{192,224},{224,1... | collective-permute-start | bytes 196616 | tf_op jit(solution)/shard_map/ppermute | solution.py:458
  107.9 6.1 %collective-permute-start.25 = (f32[64,256]{1,0:T(8,128)S(1)}, f32[64,256]{1,0:T(8,128)S(1)}, u32[]{:S(2)}, u32[]{:S(2)}) collective-permute-start(f32[64,256]{1,0:T(8,128)S(1)} %get-tuple-element.54), channel_id=1, source_target_pairs={{0,64},{32,96},{64,0},{96,32},{128,192},{160,224},{192,128},{224,1... | collective-permute-start | bytes 196616 | tf_op jit(solution)/shard_map/ppermute | solution.py:458
  111.0 5.5 %collective-permute-start.26 = (f32[64,256]{1,0:T(8,128)S(1)}, f32[64,256]{1,0:T(8,128)S(1)}, u32[]{:S(2)}, u32[]{:S(2)}) collective-permute-start(f32[64,256]{1,0:T(8,128)S(1)} %get-tuple-element.53), channel_id=1, source_target_pairs={{0,96},{32,64},{64,32},{96,0},{128,224},{160,192},{192,160},{224,1... | collective-permute-start | bytes 196616 | tf_op jit(solution)/shard_map/ppermute | solution.py:458
  116.5 3.9 %collective-permute-start.27 = (bf16[32,256]{1,0:T(8,128)(2,1)S(1)}, bf16[32,256]{1,0:T(8,128)(2,1)S(1)}, u32[]{:S(2)}, u32[]{:S(2)}) collective-permute-start(bf16[32,256]{1,0:T(8,128)(2,1)S(1)} %get-tuple-element.56), channel_id=1, source_target_pairs={{0,1},{1,0},{2,3},{3,2},{4,5},{5,4},{6,7},{7,6},{8,9},{9,8},{10,11... | collective-permute-start | bytes 49160 | tf_op jit(solution)/shard_map/ppermute | solution.py:35
  (6 other events, 11.2 us)
